TPU v7x, 512 devices: a whole 4x4x16 slice. The times are simulated.
512 devices in a mesh: seq: 32 (over z, core), head: 16 (over y, x).
Axes of the slice: x: 4, y: 4, z: 16, core: 2. Of those that a mesh axis runs over, the one named last changes fastest.
Arguments:
- context: bfloat16 [65536, 1024], P('seq', 'head'), may hold values from -6.6 to 6.6
- latents: bfloat16 [2048, 1024], P('seq', 'head'), may hold values from -6.6 to 6.6
- ctx_pos: int32 [65536], P('seq'), may hold values from 0 to 67583, as said below
- lat_pos: int32 [2048], replicated, may hold values from 0 to 67583, as said below
- input_gain: float32 [1024], replicated, may hold values from 0.1 to 1.9
- w_query: bfloat16 [1024, 1024], P(None, 'head'), may hold values from -12.5 to 12.5
- w_key: bfloat16 [1024, 1024], P(None, 'head'), may hold values from -0.2375 to 0.2375
- w_value: bfloat16 [1024, 1024], P(None, 'head'), may hold values from -0.1875 to 0.1875
- w_out: bfloat16 [1024, 1024], P('head'), may hold values from -0.1875 to 0.1875
- mlp_gain: float32 [1024], replicated, may hold values from 0.1 to 1.9
- w_up: bfloat16 [1024, 4096], P(None, 'head'), may hold values from -0.1875 to 0.1875
- w_down: bfloat16 [4096, 1024], P('head'), may hold values from -0.09375 to 0.09375
Outputs:
- updated: bfloat16 [2048, 1024], P('seq', 'head')
Inputs may be any that keep to these rules, and one draw needn't show every extreme that they name: ctx_pos and lat_pos together hold each of 0 to 67583 exactly once. ctx_pos and lat_pos together hold each of 0 to 67583 exactly once.
All inputs are finite; a program needn't handle non-finite values.
Results may differ from a plain program's by a relative error of at most 0.02.
Values may be sent and summed in bfloat16 or wider, within the bound.
No kernel may reach another device: no remote copies, remote signals or barrier semaphores. Data moves between devices by JAX's collectives and lax.ppermute only.
A program may use at most 128 MiB of HBM per device.

v0:
```python
import jax
import jax.numpy as jnp
from jax import lax
from jax.sharding import PartitionSpec as P

HD = 64


EPSILON = 1e-06
NEGATIVE = -1e30


def normalize(rows, gain):
    values_f = rows.astype(jnp.float32)
    inverse = lax.rsqrt(jnp.mean(values_f * values_f, axis=-1, keepdims=True) + EPSILON)
    return (values_f * inverse * gain).astype(jnp.bfloat16)


def body(
    context,
    latents,
    ctx_pos,
    lat_pos,
    input_gain,
    w_query,
    w_key,
    w_value,
    w_out,
    mlp_gain,
    w_up,
    w_down,
):
    lat_rows = latents.shape[0]
    head_cols = w_query.shape[1]
    heads_here = head_cols // HD
    score_scale = HD ** (-0.5)
    full_context = lax.all_gather(context, "head", axis=1, tiled=True)
    normed_context = normalize(full_context, input_gain)
    key_value_proj = jnp.concatenate([w_key, w_value], axis=1)
    context_kv = jnp.dot(normed_context, key_value_proj, preferred_element_type=jnp.float32).astype(
        jnp.bfloat16
    )
    full_latents = lax.all_gather(latents, "head", axis=1, tiled=True)
    normed_latents = normalize(full_latents, input_gain)
    all_proj = jnp.concatenate([w_query, w_key, w_value], axis=1)
    latent_qkv = jnp.dot(normed_latents, all_proj, preferred_element_type=jnp.float32).astype(
        jnp.bfloat16
    )
    query_rows = latent_qkv[:, :head_cols]
    queries = lax.all_gather(query_rows, "seq", axis=0, tiled=True)
    key_rows = jnp.concatenate(
        [context_kv[:, :head_cols], latent_qkv[:, head_cols : 2 * head_cols]], axis=0
    )
    value_rows = jnp.concatenate(
        [context_kv[:, head_cols:], latent_qkv[:, 2 * head_cols :]], axis=0
    )
    row_start = lax.axis_index("seq") * lat_rows
    own_pos = lax.dynamic_slice_in_dim(lat_pos, row_start, lat_rows)
    key_pos = jnp.concatenate([ctx_pos, own_pos])
    total_queries = queries.shape[0]
    block_rows = 512
    block_count = total_queries // block_rows
    keys_split = key_rows.reshape(-1, heads_here, HD)
    values_split = value_rows.reshape(-1, heads_here, HD)
    query_blocks = queries.reshape(block_count, block_rows, heads_here, HD)
    pos_blocks = lat_pos.reshape(block_count, block_rows)

    def attend(pieces):
        query_block, pos_block = pieces
        scores = (
            jnp.einsum("qhd,khd->qhk", query_block, keys_split, preferred_element_type=jnp.float32)
            * score_scale
        )
        visible = (key_pos[None, :] <= pos_block[:, None])[:, None, :]
        scores = jnp.where(visible, scores, NEGATIVE)
        row_top = jnp.max(scores, axis=-1)
        weights = jnp.where(visible, jnp.exp(scores - row_top[..., None]), 0.0).astype(jnp.bfloat16)
        row_total = jnp.sum(weights.astype(jnp.float32), axis=-1)
        mixed = jnp.einsum(
            "qhk,khd->qhd", weights, values_split, preferred_element_type=jnp.float32
        )
        return (row_top, row_total, mixed)

    tops, totals, mixes = lax.map(attend, (query_blocks, pos_blocks))
    tops = tops.reshape(total_queries, heads_here)
    totals = totals.reshape(total_queries, heads_here)
    mixes = mixes.reshape(total_queries, heads_here, HD)
    global_top = lax.pmax(tops, "seq")
    factors = jnp.exp(tops - global_top)
    own_mixed, own_total = (
        lax.psum_scatter(
            (mixes * factors[..., None]).astype(jnp.bfloat16),
            "seq",
            scatter_dimension=0,
            tiled=True,
        ).astype(jnp.float32),
        lax.psum_scatter(
            (totals * factors).astype(jnp.bfloat16), "seq", scatter_dimension=0, tiled=True
        ).astype(jnp.float32),
    )
    attended = (own_mixed / own_total[..., None]).astype(jnp.bfloat16).reshape(lat_rows, head_cols)
    partial_value = jnp.dot(attended, w_out, preferred_element_type=jnp.float32)
    latent_float = full_latents.astype(jnp.float32)
    col_start = lax.axis_index("head") * head_cols
    head_sum = lax.psum(partial_value.astype(jnp.bfloat16), "head").astype(jnp.float32)
    projected = latent_float + head_sum
    normed_mid = normalize(projected, mlp_gain)
    own_proj = lax.dynamic_slice_in_dim(projected, col_start, head_cols, 1)
    hidden = jax.nn.gelu(jnp.dot(normed_mid, w_up, preferred_element_type=jnp.float32)).astype(
        jnp.bfloat16
    )
    down_terms = jnp.dot(hidden, w_down, preferred_element_type=jnp.float32)
    down_share = lax.psum_scatter(
        down_terms.astype(jnp.bfloat16), "head", scatter_dimension=1, tiled=True
    ).astype(jnp.float32)
    return (own_proj + down_share).astype(jnp.bfloat16)


def solution(mesh):
    placed = (
        P("seq", "head"),
        P("seq", "head"),
        P("seq"),
        P(),
        P(),
        P(None, "head"),
        P(None, "head"),
        P(None, "head"),
        P("head", None),
        P(),
        P(None, "head"),
        P("head", None),
    )
    return jax.shard_map(
        body, mesh=mesh, in_specs=placed, out_specs=P("seq", "head"), check_vma=False
    )
```

profile of v0, /device:TPU:32, one launch (start us, length us, event | category | flops | bytes accessed | tf_op | source)
XLA Modules:
  0.0 582.4 jit_solution(13008936980843425707)
XLA Ops:
  6.6 0.7 all-gather.2.cloned.1.call-update
  7.4 0.8 copy.23
  8.2 24.0 %all_gather.9 = bf16[64,1024]{0,1:T(8,128)(2,1)S(1)} all-gather(bf16[64,64]{0,1:T(8,128)(2,1)S(1)} %copy.23), channel_id=1, replica_groups=mesh['seq'=32,'head'=16] {'head'}, dimensions={1}, use_global_device_ids=true | all-gather | bytes 139264 | tf_op jit(solution)/shard_map/all_gather | solution.py:43
  32.5 1.4 convolution_convert_fusion.2
  34.1 0.7 reshape.173
  34.9 0.8 dynamic_slice.14
  35.6 35.6 %all_gather.10 = bf16[2048,64]{1,0:T(8,128)(2,1)S(1)} all-gather(bf16[64,64]{1,0:T(8,128)(2,1)S(1)} %get-tuple-element.116), channel_id=1, replica_groups=mesh['seq'=32,'head'=16] {'seq'}, dimensions={0}, use_global_device_ids=true | all-gather | bytes 270336 | tf_op jit(solution)/shard_map/all_gather | solution.py:50
  71.2 0.2 copy.27
  71.4 0.7 pad_add_fusion
  72.1 9.3 %all-gather.2.cloned.1.call-done = bf16[2048,1024]{0,1:T(8,128)(2,1)} async-done(((bf16[2048,64]{0,1:T(8,128)(2,1)}), bf16[2048,1024]{0,1:T(8,128)(2,1)}) %all-gather.2.cloned.1.call-update) | async-done | bytes 4194320 | tf_op jit(solution)/shard_map/all_gather | solution.py:37
  81.4 3.1 fusion.12
  84.5 3.6 fusion.19
  88.2 17.2 %while.14 = (s32[]{:T(128)}, f32[4,512,1]{1,2,0:T(1,128)S(1)}, f32[4,512,1]{1,2,0:T(1,128)S(1)}, f32[4,512,1,64]{1,0,3,2:T(4,128)S(1)}, s32[2112]{0:T(1024)S(1)}...) while((s32[]{:T(128)}, f32[4,512,1]{1,2,0:T(1,128)S(1)}, ...), condition=%wide.region_5.6_spmd, body=%wide.region_2.5_spmd.sunk | while | flops 287636480 | bytes 14289277 | solution.py:84
  88.2 0.9 fusion.74
  89.2 1.4 convert_reduce_fusion.2
  90.6 0.5 fusion.75
  91.0 0.1 copy.44
  91.2 1.3 dynamic_update_slice.16
  92.5 0.9 fusion.74
  93.5 1.4 convert_reduce_fusion.2
  94.8 0.5 fusion.75
  95.5 1.3 dynamic_update_slice.16
  96.8 0.9 fusion.74
  97.7 1.4 convert_reduce_fusion.2
  99.1 0.5 fusion.75
  99.6 0.1 copy.44
  99.8 1.3 dynamic_update_slice.16
  101.1 0.9 fusion.74
  102.0 1.4 convert_reduce_fusion.2
  103.4 0.5 fusion.75
  103.9 0.1 copy.44
  104.1 1.3 dynamic_update_slice.16
  105.4 47.4 %pmax.7 = f32[2048,1]{0,1:T(1,128)S(1)} all-reduce(f32[2048,1]{0,1:T(1,128)S(1)} %bitcast.87), channel_id=1, replica_groups=mesh['seq'=32,'head'=16] {'seq'}, use_global_device_ids=true, to_apply=%region_6.7 | all-reduce | flops 2048 | bytes 16384 | tf_op jit(solution)/shard_map/pmax | solution.py:88
  152.8 0.4 reshape.177
  153.2 1.1 copy.32
  154.3 1.0 copy.36
  155.4 102.7 %reduce-scatter.12.cloned.1.call-done = bf16[64,1]{1,0:T(8,128)(2,1)} async-done(((bf16[2048,1]{1,0:T(8,128)(2,1)}), bf16[64,1]{1,0:T(8,128)(2,1)}) %reduce-scatter.12.cloned.1.call-update) | async-done | bytes 144
  258.1 0.8 copy.33
  258.9 107.1 %reduce-scatter.10.cloned.1.call-done = bf16[64,64]{1,0:T(8,128)(2,1)} async-done(((bf16[2048,64]{1,0:T(8,128)(2,1)}), bf16[64,64]{1,0:T(8,128)(2,1)}) %reduce-scatter.10.cloned.1.call-update) | async-done | bytes 8208
  366.0 0.8 copy.37
  366.9 0.9 convolution_convert_fusion.1
  367.8 115.2 %all-reduce.2.cloned.1.call-done = bf16[64,1024]{1,0:T(8,128)(2,1)} async-done(((bf16[64,1024]{1,0:T(8,128)(2,1)}), bf16[64,1024]{1,0:T(8,128)(2,1)}) %all-reduce.2.cloned.1.call-update) | async-done | bytes 131088 | tf_op jit(solution)/shard_map/psum | solution.py:105
  483.1 1.0 convert_add_fusion
  484.2 1.5 convolution_convert_fusion
  485.6 0.8 copy.34
  486.5 87.9 %reduce-scatter.14.cloned.1.call-done = bf16[64,64]{1,0:T(8,128)(2,1)} async-done(((bf16[1024,64]{1,0:T(8,128)(2,1)}), bf16[64,64]{1,0:T(8,128)(2,1)}) %reduce-scatter.14.cloned.1.call-update) | async-done | bytes 8208
  574.4 0.8 copy.35
  575.2 0.7 add_convert_fusion
  (49 shorter events, 1.3 us)
Async XLA Ops:
  6.5 477.6 %copy-start = (bf16[256,1024]{1,0:T(8,128)(2,1)S(1)}, bf16[256,1024]{1,0:T(8,128)(2,1)}, u32[]{:S(2)}) copy-start(bf16[256,1024]{1,0:T(8,128)(2,1)} %param.25) | copy-start | bytes 1572868
  6.5 77.9 %copy-start.6 = (f32[1024]{0:T(1024)S(1)}, f32[1024]{0:T(1024)}, u32[]{:S(2)}) copy-start(f32[1024]{0:T(1024)} %param.18) | copy-start | bytes 12292
  6.5 77.9 %copy-start.5 = (bf16[1024,64]{0,1:T(8,128)(2,1)S(1)}, bf16[1024,64]{0,1:T(8,128)(2,1)}, u32[]{:S(2)}) copy-start(bf16[1024,64]{0,1:T(8,128)(2,1)} %param.20) | copy-start | bytes 393220
  6.5 78.0 %copy-start.4 = (bf16[1024,64]{0,1:T(8,128)(2,1)S(1)}, bf16[1024,64]{0,1:T(8,128)(2,1)}, u32[]{:S(2)}) copy-start(bf16[1024,64]{0,1:T(8,128)(2,1)} %param.21) | copy-start | bytes 393220
  6.5 74.9 %all-gather.2.cloned.1.call-start = ((), (), s32[]{:S(2)}) async-start(), calls=%async_computation.3 | async-start | bytes 4456448 | tf_op jit(solution)/shard_map/all_gather | solution.py:37
  7.3 250.8 %reduce-scatter.12.cloned.1.call-start = ((), (), s32[]{:S(2)}) async-start(), calls=%async_computation.6 | async-start | bytes 540672
  105.4 261.5 %copy-start.2 = (bf16[64,1024]{1,0:T(8,128)(2,1)S(1)}, bf16[64,1024]{1,0:T(8,128)(2,1)}, u32[]{:S(2)}) copy-start(bf16[64,1024]{1,0:T(8,128)(2,1)} %param.22) | copy-start | bytes 393220
  105.4 378.8 %copy-start.1 = (bf16[1024,256]{1,0:T(8,128)(2,1)S(1)}, bf16[1024,256]{1,0:T(8,128)(2,1)}, u32[]{:S(2)}) copy-start(bf16[1024,256]{1,0:T(8,128)(2,1)} %param.24) | copy-start | bytes 1572868
  105.4 378.8 %copy-start.3 = (f32[1024]{0:T(1024)S(1)}, f32[1024]{0:T(1024)}, u32[]{:S(2)}) copy-start(f32[1024]{0:T(1024)} %param.23) | copy-start | bytes 12292
  154.3 211.7 %reduce-scatter.10.cloned.1.call-start = ((), (), s32[]{:S(2)}) async-start(), calls=%async_computation.5 | async-start | bytes 540672
  155.4 327.7 %all-reduce.2.cloned.1.call-start = ((), (), s32[]{:S(2)}) async-start(), calls=%async_computation.4 | async-start | bytes 262144 | tf_op jit(solution)/shard_map/psum | solution.py:105
  367.8 206.6 %reduce-scatter.14.cloned.1.call-start = ((), (), s32[]{:S(2)}) async-start(), calls=%async_computation.7 | async-start | bytes 278528
Sparse Core Ops, SparseCore 0:
  10.4 70.9 all-gather.1
  154.4 103.6 reduce-scatter.11
  261.1 104.8 reduce-scatter.9
  369.0 114.0 all-reduce.1
  487.5 86.8 reduce-scatter.13
where the time goes:
time: 583 us; the launch traced here: 582 us
  waiting for transfers between devices  423 us (73%)
  blocking collectives  107 us (18%)
  local copies, waits for them, and re-layouts  14.3 us (2%)
  between operations  13.4 us (2%)
  matrix products  13 us (2%)
  other arithmetic  11.3 us (2%)
    unnamed x8, waiting for transfers between devices  298 us
    psum x1, waiting for transfers between devices, body(): lax.psum(partial_value.astype(jnp.bfloat16), 'head').astype(jnp.float32)  115 us
    pmax x1, blocking collectives, body(): global_top = lax.pmax(tops, 'seq')  47.4 us
    all_gather x1, blocking collectives, body(): queries = lax.all_gather(query_rows, 'seq', axis=0, tiled=True)  35.6 us
    all_gather x1, blocking collectives, body(): full_latents = lax.all_gather(latents, 'head', axis=1, tiled=True)  24 us
  transfers between devices with their start and end apart: 5, of which 5 were waited for; matrix products, arithmetic and copies ran while one was open for 1% of the time, Pallas kernels for 0%

commit v1 on v0

v1 whole, which is shorter than its diff:
```python
import jax
import jax.numpy as jnp
from jax import lax
from jax.sharding import PartitionSpec as P

HD = 64


EPSILON = 1e-06
NEGATIVE = -1e30
LOWEST = -1e29


def normalize(rows, gain):
    values_f = rows.astype(jnp.float32)
    inverse = lax.rsqrt(jnp.mean(values_f * values_f, axis=-1, keepdims=True) + EPSILON)
    return (values_f * inverse * gain).astype(jnp.bfloat16)


def gather_by_exchange(rows, axis, size):
    return lax.all_to_all(jnp.broadcast_to(rows[None], (size, *rows.shape)), axis, 0, 0)


def three_terms(values):
    first = values.astype(jnp.bfloat16)
    rest = values - first.astype(jnp.float32)
    second = rest.astype(jnp.bfloat16)
    third = (rest - second.astype(jnp.float32)).astype(jnp.bfloat16)
    return first, second, third


def body(
    context,
    latents,
    ctx_pos,
    lat_pos,
    input_gain,
    w_query,
    w_key,
    w_value,
    w_out,
    mlp_gain,
    w_up,
    w_down,
):
    seq_size = lax.axis_size("seq")
    head_size = lax.axis_size("head")
    lat_rows = latents.shape[0]
    head_cols = w_query.shape[1]
    score_scale = HD ** (-0.5)
    full_context = lax.all_gather(context, "head", axis=1, tiled=True)
    lat_blocks = gather_by_exchange(latents, "head", head_size)
    full_latents = lat_blocks.transpose(1, 0, 2).reshape(lat_rows, -1)
    normed_latents = normalize(full_latents, input_gain)
    all_proj = jnp.concatenate([w_query, w_key, w_value], axis=1)
    latent_qkv = jnp.dot(normed_latents, all_proj, preferred_element_type=jnp.float32).astype(
        jnp.bfloat16
    )
    query_rows = latent_qkv[:, :head_cols]
    half = lat_rows // 2
    packed_rows = jnp.concatenate([query_rows[:half], query_rows[half:]], axis=1)
    packed = gather_by_exchange(packed_rows, "seq", seq_size)
    queries = jnp.concatenate([packed[:, :, :head_cols], packed[:, :, head_cols:]], axis=1)
    queries = queries.reshape(-1, head_cols)

    normed_context = normalize(full_context, input_gain)
    key_value_proj = jnp.concatenate([w_key, w_value], axis=1)
    context_kv = jnp.dot(normed_context, key_value_proj, preferred_element_type=jnp.float32).astype(
        jnp.bfloat16
    )
    key_rows = jnp.concatenate(
        [context_kv[:, :head_cols], latent_qkv[:, head_cols : 2 * head_cols]], axis=0
    )
    value_rows = jnp.concatenate(
        [context_kv[:, head_cols:], latent_qkv[:, 2 * head_cols :]], axis=0
    )
    row_start = lax.axis_index("seq") * lat_rows
    own_pos = lax.dynamic_slice_in_dim(lat_pos, row_start, lat_rows)
    key_pos = jnp.concatenate([ctx_pos, own_pos])
    total_queries = queries.shape[0]
    block_rows = 512
    block_count = total_queries // block_rows
    query_blocks = queries.reshape(block_count, block_rows, HD)
    pos_blocks = lat_pos.reshape(block_count, block_rows)

    def attend(pieces):
        query_block, pos_block = pieces
        scores = (
            jnp.einsum("qd,kd->qk", query_block, key_rows, preferred_element_type=jnp.float32)
            * score_scale
        )
        visible = key_pos[None, :] <= pos_block[:, None]
        scores = jnp.where(visible, scores, NEGATIVE)
        row_top = jnp.maximum(jnp.max(scores, axis=-1), LOWEST)
        weights = jnp.exp(scores - row_top[..., None]).astype(jnp.bfloat16)
        row_total = jnp.sum(weights.astype(jnp.float32), axis=-1)
        mixed = jnp.einsum("qk,kd->qd", weights, value_rows, preferred_element_type=jnp.float32)
        floor = jnp.maximum(row_total, 1e-30)
        return ((mixed / floor[:, None]).astype(jnp.bfloat16), row_top + jnp.log(floor))

    mixes, levels = lax.map(attend, (query_blocks, pos_blocks))
    mixes = mixes.reshape(seq_size, 2, half, head_cols)
    mixes = jnp.concatenate([mixes[:, 0], mixes[:, 1]], axis=2)
    terms = jnp.stack(three_terms(levels.reshape(seq_size, lat_rows)), axis=1)
    terms = jnp.pad(terms, ((0, 0), (0, 5), (0, 2 * head_cols - lat_rows)))
    message = jnp.concatenate([mixes, terms], axis=1)
    arrived = lax.all_to_all(message, "seq", 0, 0)
    level = jnp.sum(arrived[:, half : half + 3, :lat_rows].astype(jnp.float32), axis=1)
    factors = jnp.exp(level - jnp.max(level, axis=0, keepdims=True))
    parts = jnp.concatenate(
        [arrived[:, :half, :head_cols], arrived[:, :half, head_cols:]], axis=1
    ).astype(jnp.float32)
    attended = jnp.sum(parts * factors[:, :, None], axis=0) / jnp.sum(factors, axis=0)[:, None]
    attended = attended.astype(jnp.bfloat16)

    def head_sum(terms_here):
        blocks = terms_here.astype(jnp.bfloat16).reshape(lat_rows, head_size, -1).transpose(1, 0, 2)
        return jnp.sum(lax.all_to_all(blocks, "head", 0, 0).astype(jnp.float32), axis=0)

    own_latents = latents.astype(jnp.float32)
    own_proj = own_latents + head_sum(jnp.dot(attended, w_out, preferred_element_type=jnp.float32))
    projected = gather_by_exchange(own_proj, "head", head_size)
    projected = projected.transpose(1, 0, 2).reshape(lat_rows, -1)
    normed_mid = normalize(projected, mlp_gain)
    hidden = jax.nn.gelu(jnp.dot(normed_mid, w_up, preferred_element_type=jnp.float32)).astype(
        jnp.bfloat16
    )
    down_share = head_sum(jnp.dot(hidden, w_down, preferred_element_type=jnp.float32))
    return (own_proj + down_share).astype(jnp.bfloat16)


def solution(mesh):
    placed = (
        P("seq", "head"),
        P("seq", "head"),
        P("seq"),
        P(),
        P(),
        P(None, "head"),
        P(None, "head"),
        P(None, "head"),
        P("head", None),
        P(),
        P(None, "head"),
        P("head", None),
    )
    return jax.shard_map(
        body, mesh=mesh, in_specs=placed, out_specs=P("seq", "head"), check_vma=False
    )
```

time: 583 us -> 186 us (0.32)
  the two profiles are of different devices: /device:TPU:32 before, /device:TPU:2 now
where the time goes in v1:
time: 186 us; the launch traced here: 185 us
  blocking collectives  87.7 us (47%)
  waiting for transfers between devices  41.9 us (23%)
  starting transfers between devices  14.4 us (8%)
  between operations  13.9 us (7%)
  matrix products  10.6 us (6%)
  other arithmetic  9.11 us (5%)
  local copies, waits for them, and re-layouts  7.31 us (4%)
    all_to_all x1, blocking collectives, body(): arrived = lax.all_to_all(message, 'seq', 0, 0)  37.8 us
    all_to_all x2, blocking collectives, gather_by_exchange(): lax.all_to_all(jnp.broadcast_to(rows[None], (size, *rows.shape)), axis, 0...  26.8 us
    all_to_all x2, blocking collectives, head_sum(): lax.all_to_all(blocks, 'head', 0, 0).astype(jnp.float32)  23 us
    all_to_all x1, waiting for transfers between devices, gather_by_exchange(): lax.all_to_all(jnp.broadcast_to(rows[None], (size, *rows.shape)), axis, 0...  22.3 us
    all_gather x1, waiting for transfers between devices, body(): full_context = lax.all_gather(context, 'head', axis=1, tiled=True)  18.9 us
    all_to_all x1, starting transfers between devices, gather_by_exchange(): lax.all_to_all(jnp.broadcast_to(rows[None], (size, *rows.shape)), axis, 0...  14.4 us
  transfers between devices with their start and end apart: 2, of which 2 were waited for; matrix products, arithmetic and copies ran while one was open for 2% of the time, Pallas kernels for 0%

profile of v1, /device:TPU:2, one launch (start us, length us, event | category | flops | bytes accessed | tf_op | source)
XLA Modules:
  0.0 185.1 jit_solution(17351735262215548543)
XLA Ops:
  6.6 0.7 all-gather.2.cloned.1.call-update
  7.3 0.8 broadcast_in_dim.20
  8.1 0.2 reshape.153
  8.3 15.0 %all_to_all.30 = bf16[16,2,2048]{2,1,0:T(2,128)(2,1)S(1)} all-to-all(bf16[16,2,2048]{2,1,0:T(2,128)(2,1)S(1)} %reshape.153), channel_id=1, replica_groups=mesh['seq'=32,'head'=16] {'head'}, dimensions={0} | all-to-all | bytes 262144 | tf_op jit(solution)/shard_map/all_to_all | solution.py:21
  23.3 0.2 reshape.154
  23.6 0.3 copy.25
  24.3 0.3 convolution_convert_fusion.2
  24.7 0.7 broadcast_in_dim.22
  25.4 14.4 %all-to-all-start.1 = ((bf16[32,32,128]{2,1,0:T(8,128)(2,1)}), bf16[32,32,128]{2,1,0:T(8,128)(2,1)S(1)}, u32[]{:S(2)}, u32[]{:S(2)}) async-start(bf16[32,32,128]{2,1,0:T(8,128)(2,1)} %broadcast_in_dim.22), calls=%async_computation.1 | async-start | bytes 524288 | tf_op jit(solution)/shard_map/all_to_all | solution.py:21
  40.2 22.3 %all-to-all-done.1 = bf16[32,32,128]{2,1,0:T(8,128)(2,1)S(1)} async-done(((bf16[32,32,128]{2,1,0:T(8,128)(2,1)}), bf16[32,32,128]{2,1,0:T(8,128)(2,1)S(1)}, u32[]{:S(2)}, u32[]{:S(2)}) %all-to-all-start.1) | async-done | bytes 262176 | tf_op jit(solution)/shard_map/all_to_all | solution.py:21
  62.8 18.9 %all-gather.2.cloned.1.call-done = bf16[2048,1024]{0,1:T(8,128)(2,1)} async-done(((bf16[2048,64]{0,1:T(8,128)(2,1)}), bf16[2048,1024]{0,1:T(8,128)(2,1)}) %all-gather.2.cloned.1.call-update) | async-done | bytes 4194320 | tf_op jit(solution)/shard_map/all_gather | solution.py:51
  81.7 3.1 %fusion.7 = f32[2048]{0:T(1024)S(1)} fusion(bf16[2048,1024]{0,1:T(8,128)(2,1)} %all-gather.2.cloned.1.call-done), kind=kLoop, calls=%fused_computation.17 | loop fusion | flops 6289408 | bytes 4202496 | tf_op jit(solution)/shard_map/reduce_sum | solution.py:16
  84.8 3.6 %fusion.14 = bf16[2048,128]{0,1:T(8,128)(2,1)S(1)} fusion(bf16[2048,1024]{0,1:T(8,128)(2,1)} %all-gather.2.cloned.1.call-done, f32[1024]{0:T(1024)S(1)} %copy-done.10, f32[2048]{0:T(1024)S(1)} %add_rsqrt_fusion, bf16[1024,64]{0,1:T(8,128)(2,1)S(1)} %copy-done.8, bf16[1024,64]{0,1:T(8,128)(2,1)S(1)} %copy-done.9), kind=kOutput, calls=%fused_computation.23 | convolution fusion | flops 546045952 | bytes 4993024 | tf_op jit(solution)/shard_map/dot_general | solution.py:68
  88.5 0.3 copy.28
  88.8 0.3 copy.29
  89.1 9.1 %while.12 = (s32[]{:T(128)}, bf16[4,512,64]{1,2,0:T(8,128)(2,1)S(1)}, f32[4,512]{1,0:T(4,128)S(1)}, s32[2112]{0:T(1024)S(1)}, s32[4,512]{1,0:T(4,128)S(1)}, /*in...) while((s32[]{:T(128)}, ...), condition=%wide.region_5.6_spmd, body=%wide.region_2.5_spmd.sunk | while | flops 287704064 | bytes 14299253 | solution.py:101
  89.1 0.8 fusion.79
  89.9 0.7 convert_reduce_fusion.5
  90.5 0.8 fusion.80
  91.4 0.8 fusion.79
  92.1 0.7 convert_reduce_fusion.5
  92.8 0.8 fusion.80
  93.6 0.8 fusion.79
  94.4 0.7 convert_reduce_fusion.5
  95.1 0.8 fusion.80
  95.9 0.8 fusion.79
  96.7 0.7 convert_reduce_fusion.5
  97.3 0.8 fusion.80
  98.3 0.3 copy.30
  98.9 37.8 %all_to_all.31 = bf16[32,40,128]{2,1,0:T(8,128)(2,1)S(1)} all-to-all(bf16[32,40,128]{2,1,0:T(8,128)(2,1)S(1)} %pad_maximum_fusion.1), channel_id=1, replica_groups=mesh['seq'=32,'head'=16] {'seq'}, dimensions={0} | all-to-all | bytes 655360 | tf_op jit(solution)/shard_map/all_to_all | solution.py:107
  137.0 0.3 multiply_reduce_fusion
  137.4 0.2 convolution_convert_fusion.1
  137.6 0.2 reshape.149
  137.9 0.2 reshape.155
  138.1 12.1 %all_to_all.32 = bf16[16,2,2048]{2,1,0:T(2,128)(2,1)S(1)} all-to-all(bf16[16,2,2048]{2,1,0:T(2,128)(2,1)S(1)} %reshape.155), channel_id=1, replica_groups=mesh['seq'=32,'head'=16] {'head'}, dimensions={0} | all-to-all | bytes 262144 | tf_op jit(solution)/shard_map/all_to_all | solution.py:118
  150.3 0.2 reshape.156
  150.6 0.3 reshape.157
  150.9 11.8 %all_to_all.33 = f32[16,1,4096]{2,1,0:T(1,128)S(1)} all-to-all(f32[16,1,4096]{2,1,0:T(1,128)S(1)} %reshape.157), channel_id=1, replica_groups=mesh['seq'=32,'head'=16] {'head'}, dimensions={0} | all-to-all | bytes 524288 | tf_op jit(solution)/shard_map/all_to_all | solution.py:21
  162.7 0.5 broadcast.118
  163.2 1.3 reduce.3
  164.5 0.2 reshape.158
  164.9 0.3 copy.33
  165.4 0.6 convolution_convert_fusion
  166.0 0.2 reshape.151
  166.2 0.2 reshape.159
  166.5 10.9 %all_to_all.34 = bf16[16,2,2048]{2,1,0:T(2,128)(2,1)S(1)} all-to-all(bf16[16,2,2048]{2,1,0:T(2,128)(2,1)S(1)} %reshape.159), channel_id=1, replica_groups=mesh['seq'=32,'head'=16] {'head'}, dimensions={0} | all-to-all | bytes 262144 | tf_op jit(solution)/shard_map/all_to_all | solution.py:118
  177.4 0.2 reshape.160
  177.6 0.6 add_convert_fusion
  (76 shorter events, 2.9 us)
Async XLA Ops:
  6.5 158.8 %copy-start = (bf16[256,1024]{1,0:T(8,128)(2,1)S(1)}, bf16[256,1024]{1,0:T(8,128)(2,1)}, u32[]{:S(2)}) copy-start(bf16[256,1024]{1,0:T(8,128)(2,1)} %param.25) | copy-start | bytes 1572868
  6.5 17.7 %copy-start.10 = (f32[1024]{0:T(1024)S(1)}, f32[1024]{0:T(1024)}, u32[]{:S(2)}) copy-start(f32[1024]{0:T(1024)} %param.18) | copy-start | bytes 12292
  6.5 17.8 %copy-start.7 = (bf16[1024,64]{0,1:T(8,128)(2,1)S(1)}, bf16[1024,64]{0,1:T(8,128)(2,1)}, u32[]{:S(2)}) copy-start(bf16[1024,64]{0,1:T(8,128)(2,1)} %param.19) | copy-start | bytes 393220
  6.5 17.8 %copy-start.9 = (bf16[1024,64]{0,1:T(8,128)(2,1)S(1)}, bf16[1024,64]{0,1:T(8,128)(2,1)}, u32[]{:S(2)}) copy-start(bf16[1024,64]{0,1:T(8,128)(2,1)} %param.20) | copy-start | bytes 393220
  6.5 17.8 %copy-start.8 = (bf16[1024,64]{0,1:T(8,128)(2,1)S(1)}, bf16[1024,64]{0,1:T(8,128)(2,1)}, u32[]{:S(2)}) copy-start(bf16[1024,64]{0,1:T(8,128)(2,1)} %param.21) | copy-start | bytes 393220
  6.5 33.3 %copy-start.4 = (s32[2048]{0:T(1024)S(1)}, s32[2048]{0:T(1024)}, u32[]{:S(2)}) copy-start(s32[2048]{0:T(1024)} %param.17) | copy-start | bytes 24580
  6.6 33.3 %copy-start.5 = (s32[2048]{0:T(1024)S(1)}, s32[2048]{0:T(1024)}, u32[]{:S(2)}) copy-start(s32[2048]{0:T(1024)} %param.16) | copy-start | bytes 24580
  6.6 75.2 %all-gather.2.cloned.1.call-start = ((), (), s32[]{:S(2)}) async-start(), calls=%async_computation.6 | async-start | bytes 4456448 | tf_op jit(solution)/shard_map/all_gather | solution.py:51
  25.4 37.1 %all-to-all-start.1 = ((bf16[32,32,128]{2,1,0:T(8,128)(2,1)}), bf16[32,32,128]{2,1,0:T(8,128)(2,1)S(1)}, u32[]{:S(2)}, u32[]{:S(2)}) async-start(bf16[32,32,128]{2,1,0:T(8,128)(2,1)} %broadcast_in_dim.22), calls=%async_computation.1 | async-start | bytes 524288 | tf_op jit(solution)/shard_map/all_to_all | solution.py:21
  98.2 39.2 %copy-start.2 = (bf16[64,1024]{1,0:T(8,128)(2,1)S(1)}, bf16[64,1024]{1,0:T(8,128)(2,1)}, u32[]{:S(2)}) copy-start(bf16[64,1024]{1,0:T(8,128)(2,1)} %param.22) | copy-start | bytes 393220
  98.2 52.4 %copy-start.3 = (bf16[64,64]{1,0:T(8,128)(2,1)S(1)}, bf16[64,64]{1,0:T(8,128)(2,1)}, u32[]{:S(2)}) copy-start(bf16[64,64]{1,0:T(8,128)(2,1)} %param.15) | copy-start | bytes 24580
  137.0 28.4 %copy-start.1 = (bf16[1024,256]{1,0:T(8,128)(2,1)S(1)}, bf16[1024,256]{1,0:T(8,128)(2,1)}, u32[]{:S(2)}) copy-start(bf16[1024,256]{1,0:T(8,128)(2,1)} %param.24) | copy-start | bytes 1572868
  137.0 28.4 %copy-start.6 = (f32[1024]{0:T(1024)S(1)}, f32[1024]{0:T(1024)}, u32[]{:S(2)}) copy-start(f32[1024]{0:T(1024)} %param.23) | copy-start | bytes 12292
Sparse Core Ops, SparseCore 0:
  10.4 71.2 all-gather.1

commit v2 on v1

--- a/solution.py
+++ b/solution.py
@@ -1,3 +1,5 @@
+import math
+
 import jax
 import jax.numpy as jnp
 from jax import lax
@@ -9,6 +11,8 @@
 EPSILON = 1e-06
 NEGATIVE = -1e30
 LOWEST = -1e29
+BOTH = ("seq", "head")
+SHIFTS = (0, 1, 3, 2)
 
 
 def normalize(rows, gain):
@@ -27,6 +31,34 @@
     second = rest.astype(jnp.bfloat16)
     third = (rest - second.astype(jnp.float32)).astype(jnp.bfloat16)
     return first, second, third
+
+
+def line_shift(seq_size, side, phase, step):
+    pairs = []
+    for s in range(seq_size):
+        along_x = (s % 2 == 0) == (phase == 0)
+        for y in range(side):
+            for x in range(side):
+                target = (y, (x + step) % side) if along_x else ((y + step) % side, x)
+                base = s * side * side
+                pairs.append((base + y * side + x, base + target[0] * side + target[1]))
+    return pairs
+
+
+def pack_rows(mixes, levels):
+    half = mixes.shape[1] // 2
+    values = jnp.concatenate([mixes[:, :half], mixes[:, half:]], axis=2).astype(jnp.bfloat16)
+    terms = jnp.stack(three_terms(levels), axis=1)
+    terms = jnp.pad(terms, ((0, 0), (0, 5), (0, values.shape[2] - levels.shape[1])))
+    return jnp.concatenate([values, terms], axis=1)
+
+
+def unpack_rows(block, rows):
+    half = rows // 2
+    cols = block.shape[2] // 2
+    mixes = jnp.concatenate([block[:, :half, :cols], block[:, :half, cols:]], axis=1)
+    levels = jnp.sum(block[:, half : half + 3, :rows].astype(jnp.float32), axis=1)
+    return mixes.astype(jnp.float32), levels
 
 
 def body(
@@ -45,10 +77,26 @@
 ):
     seq_size = lax.axis_size("seq")
     head_size = lax.axis_size("head")
+    side = math.isqrt(head_size)
     lat_rows = latents.shape[0]
     head_cols = w_query.shape[1]
-    score_scale = HD ** (-0.5)
-    full_context = lax.all_gather(context, "head", axis=1, tiled=True)
+    half = lat_rows // 2
+    core = lax.axis_index("seq") % 2
+    planes = seq_size // 2
+    along_z = [[2 * z + c for z in range(planes)] for c in range(2)]
+    swap = [(s, s ^ 1) for s in range(seq_size)]
+
+    own = context.T
+    line = jnp.concatenate(
+        [own]
+        + [lax.ppermute(own, BOTH, line_shift(seq_size, side, 0, k)) for k in SHIFTS[1:]],
+        axis=0,
+    )
+    line, latents = lax.optimization_barrier((line, latents))
+    lines = [line] + [
+        lax.ppermute(line, BOTH, line_shift(seq_size, side, 1, k)) for k in SHIFTS[1:]
+    ]
+
     lat_blocks = gather_by_exchange(latents, "head", head_size)
     full_latents = lat_blocks.transpose(1, 0, 2).reshape(lat_rows, -1)
     normed_latents = normalize(full_latents, input_gain)
@@ -56,18 +104,39 @@
     latent_qkv = jnp.dot(normed_latents, all_proj, preferred_element_type=jnp.float32).astype(
         jnp.bfloat16
     )
-    query_rows = latent_qkv[:, :head_cols]
-    half = lat_rows // 2
+    query_rows = latent_qkv[:, :head_cols] * jnp.bfloat16(HD ** (-0.5))
     packed_rows = jnp.concatenate([query_rows[:half], query_rows[half:]], axis=1)
-    packed = gather_by_exchange(packed_rows, "seq", seq_size)
-    queries = jnp.concatenate([packed[:, :, :head_cols], packed[:, :, head_cols:]], axis=1)
-    queries = queries.reshape(-1, head_cols)
-
-    normed_context = normalize(full_context, input_gain)
+    own_queries = lax.all_to_all(
+        jnp.broadcast_to(packed_rows[None], (planes, *packed_rows.shape)),
+        "seq",
+        0,
+        0,
+        axis_index_groups=along_z,
+    )
+    other_queries = lax.ppermute(own_queries, "seq", swap)
+
+    full_context = jnp.concatenate(lines, axis=0)
+    place = lax.axis_index("head")
+    y, x = place // side, place % side
+    shifts = jnp.array(SHIFTS, jnp.int32)
+    first, second = shifts[None, :], shifts[:, None]
+    by_x = ((y - second) % side) * side + (x - first) % side
+    by_y = ((y - first) % side) * side + (x - second) % side
+    order = jnp.where(core == 0, by_x, by_y).reshape(-1)
     key_value_proj = jnp.concatenate([w_key, w_value], axis=1)
-    context_kv = jnp.dot(normed_context, key_value_proj, preferred_element_type=jnp.float32).astype(
-        jnp.bfloat16
-    )
+    key_value_proj = (input_gain[:, None] * key_value_proj.astype(jnp.float32)).astype(jnp.bfloat16)
+    key_value_proj = jnp.take(
+        key_value_proj.reshape(head_size, -1, 2 * head_cols), order, axis=0
+    ).reshape(-1, 2 * head_cols)
+    context_f = full_context.astype(jnp.float32)
+    inverse = lax.rsqrt(jnp.mean(context_f * context_f, axis=0) + EPSILON)
+    context_kv = lax.dot_general(
+        full_context,
+        key_value_proj,
+        (((0,), (0,)), ((), ())),
+        preferred_element_type=jnp.float32,
+    )
+    context_kv = (context_kv * inverse[:, None]).astype(jnp.bfloat16)
     key_rows = jnp.concatenate(
         [context_kv[:, :head_cols], latent_qkv[:, head_cols : 2 * head_cols]], axis=0
     )
@@ -77,18 +146,10 @@
     row_start = lax.axis_index("seq") * lat_rows
     own_pos = lax.dynamic_slice_in_dim(lat_pos, row_start, lat_rows)
     key_pos = jnp.concatenate([ctx_pos, own_pos])
-    total_queries = queries.shape[0]
-    block_rows = 512
-    block_count = total_queries // block_rows
-    query_blocks = queries.reshape(block_count, block_rows, HD)
-    pos_blocks = lat_pos.reshape(block_count, block_rows)
-
-    def attend(pieces):
-        query_block, pos_block = pieces
-        scores = (
-            jnp.einsum("qd,kd->qk", query_block, key_rows, preferred_element_type=jnp.float32)
-            * score_scale
-        )
+    pos_by_core = lat_pos.reshape(planes, 2, lat_rows)
+
+    def attend(query_block, pos_block):
+        scores = jnp.einsum("qd,kd->qk", query_block, key_rows, preferred_element_type=jnp.float32)
         visible = key_pos[None, :] <= pos_block[:, None]
         scores = jnp.where(visible, scores, NEGATIVE)
         row_top = jnp.maximum(jnp.max(scores, axis=-1), LOWEST)
@@ -96,20 +157,31 @@
         row_total = jnp.sum(weights.astype(jnp.float32), axis=-1)
         mixed = jnp.einsum("qk,kd->qd", weights, value_rows, preferred_element_type=jnp.float32)
         floor = jnp.maximum(row_total, 1e-30)
-        return ((mixed / floor[:, None]).astype(jnp.bfloat16), row_top + jnp.log(floor))
-
-    mixes, levels = lax.map(attend, (query_blocks, pos_blocks))
-    mixes = mixes.reshape(seq_size, 2, half, head_cols)
-    mixes = jnp.concatenate([mixes[:, 0], mixes[:, 1]], axis=2)
-    terms = jnp.stack(three_terms(levels.reshape(seq_size, lat_rows)), axis=1)
-    terms = jnp.pad(terms, ((0, 0), (0, 5), (0, 2 * head_cols - lat_rows)))
-    message = jnp.concatenate([mixes, terms], axis=1)
-    arrived = lax.all_to_all(message, "seq", 0, 0)
-    level = jnp.sum(arrived[:, half : half + 3, :lat_rows].astype(jnp.float32), axis=1)
+        return mixed / floor[:, None], row_top + jnp.log(floor)
+
+    def attend_half(packed, which):
+        rows = jnp.concatenate([packed[:, :, :head_cols], packed[:, :, head_cols:]], axis=1)
+        pos = lax.dynamic_index_in_dim(pos_by_core, which, 1, keepdims=False)
+        parts = 2
+        rows = rows.reshape(parts, -1, head_cols)
+        pos = pos.reshape(parts, -1)
+        results = [attend(rows[i], pos[i]) for i in range(parts)]
+        mixes = jnp.concatenate([r[0] for r in results]).reshape(planes, lat_rows, head_cols)
+        levels = jnp.concatenate([r[1] for r in results]).reshape(planes, lat_rows)
+        return mixes, levels
+
+    theirs = pack_rows(*attend_half(other_queries, 1 - core))
+    from_sibling = lax.ppermute(theirs, "seq", swap)
+    own_mixes, own_levels = attend_half(own_queries, core)
+    mixes_b, levels_b = unpack_rows(from_sibling, lat_rows)
+    top = jnp.maximum(own_levels, levels_b)
+    share_a, share_b = jnp.exp(own_levels - top), jnp.exp(levels_b - top)
+    total = share_a + share_b
+    joined = (own_mixes * share_a[..., None] + mixes_b * share_b[..., None]) / total[..., None]
+    message = pack_rows(joined, top + jnp.log(total))
+    arrived = lax.all_to_all(message, "seq", 0, 0, axis_index_groups=along_z)
+    parts, level = unpack_rows(arrived, lat_rows)
     factors = jnp.exp(level - jnp.max(level, axis=0, keepdims=True))
-    parts = jnp.concatenate(
-        [arrived[:, :half, :head_cols], arrived[:, :half, head_cols:]], axis=1
-    ).astype(jnp.float32)
     attended = jnp.sum(parts * factors[:, :, None], axis=0) / jnp.sum(factors, axis=0)[:, None]
     attended = attended.astype(jnp.bfloat16)
 

time: 186 us -> 183 us (0.984)
  the two profiles are of different devices: /device:TPU:2 before, /device:TPU:32 now
where the time goes in v2:
time: 183 us; the launch traced here: 182 us
  blocking collectives  62.3 us (34%)
  starting transfers between devices  44.3 us (24%)
  waiting for transfers between devices  25.8 us (14%)
  local copies, waits for them, and re-layouts  24.1 us (13%)
  matrix products  12.8 us (7%)
  other arithmetic  11.9 us (7%)
    all_to_all x1, blocking collectives, body(): arrived = lax.all_to_all(message, 'seq', 0, 0, axis_index_groups=along_z)  27.2 us
    all_to_all x2, blocking collectives, head_sum(): lax.all_to_all(blocks, 'head', 0, 0).astype(jnp.float32)  23.3 us
    all_to_all x1, starting transfers between devices, body(): lax.all_to_all(jnp.broadcast_to(packed_rows[None], (planes, *packed_rows....  15.2 us
    unnamed x48, local copies, waits for them, and re-layouts  15.2 us
    ppermute x3, waiting for transfers between devices, body(): lax.ppermute(line, BOTH, line_shift(seq_size, side, 1, k))  14.1 us
    all_to_all x1, blocking collectives, gather_by_exchange(): lax.all_to_all(jnp.broadcast_to(rows[None], (size, *rows.shape)), axis, 0...  11.8 us
    ppermute x3, starting transfers between devices, body(): lax.ppermute(own, BOTH, line_shift(seq_size, side, 0, k))  10.9 us
    ppermute x3, starting transfers between devices, body(): lax.ppermute(line, BOTH, line_shift(seq_size, side, 1, k))  9.36 us
  transfers between devices with their start and end apart: 10, of which 6 were waited for; matrix products, arithmetic and copies ran while one was open for 9% of the time, Pallas kernels for 0%

profile of v2, /device:TPU:32, one launch (start us, length us, event | category | flops | bytes accessed | tf_op | source)
XLA Modules:
  0.0 182.1 jit_solution(9426799052191639938)
XLA Ops:
  0.0 5.1 %collective-permute-start.2 = (bf16[64,2048]{1,0:T(8,128)(2,1)}, bf16[64,2048]{1,0:T(8,128)(2,1)S(1)}, u32[]{:S(2)}, u32[]{:S(2)}) collective-permute-start(bf16[64,2048]{1,0:T(8,128)(2,1)} %bitcast.70), channel_id=1, source_target_pairs={{0,2},{1,3},{2,0},{3,1},{4,6},{5,7},{6,4},{7,5},{8,10},{9,11},{10,... | collective-permute-start | bytes 786440 | tf_op jit(solution)/shard_map/ppermute | solution.py:92
  5.1 3.1 %collective-permute-start.1 = (bf16[64,2048]{1,0:T(8,128)(2,1)}, bf16[64,2048]{1,0:T(8,128)(2,1)S(1)}, u32[]{:S(2)}, u32[]{:S(2)}) collective-permute-start(bf16[64,2048]{1,0:T(8,128)(2,1)} %bitcast.71), channel_id=1, source_target_pairs={{0,3},{1,0},{2,1},{3,2},{4,7},{5,4},{6,5},{7,6},{8,11},{9,8},{10,9... | collective-permute-start | bytes 786440 | tf_op jit(solution)/shard_map/ppermute | solution.py:92
  8.1 2.8 %collective-permute-start = (bf16[64,2048]{1,0:T(8,128)(2,1)}, bf16[64,2048]{1,0:T(8,128)(2,1)S(1)}, u32[]{:S(2)}, u32[]{:S(2)}) collective-permute-start(bf16[64,2048]{1,0:T(8,128)(2,1)} %bitcast.72), channel_id=1, source_target_pairs={{0,1},{1,2},{2,3},{3,0},{4,5},{5,6},{6,7},{7,4},{8,9},{9,10},{10,1... | collective-permute-start | bytes 786440 | tf_op jit(solution)/shard_map/ppermute | solution.py:92
  11.0 0.8 fusion.49
  12.1 0.8 mul.132
  12.8 1.1 copy.125
  13.9 1.1 copy.126
  15.3 2.5 %collective-permute-done = bf16[64,2048]{1,0:T(8,128)(2,1)S(1)} collective-permute-done((bf16[64,2048]{1,0:T(8,128)(2,1)}, bf16[64,2048]{1,0:T(8,128)(2,1)S(1)}, u32[]{:S(2)}, u32[]{:S(2)}) %collective-permute-start) | collective-permute-done | bytes 262176 | tf_op jit(solution)/shard_map/ppermute | solution.py:92
  17.8 1.0 pad_maximum_fusion
  18.9 0.8 broadcast_in_dim.27
  19.6 0.9 reshape.627
  20.5 4.6 %all-to-all-start = ((bf16[16,2,2048]{2,1,0:T(2,128)(2,1)}), bf16[16,2,2048]{2,1,0:T(2,128)(2,1)S(1)}, u32[]{:S(2)}, u32[]{:S(2)}) async-start(bf16[16,2,2048]{2,1,0:T(2,128)(2,1)} %reshape.627), calls=%async_computation | async-start | bytes 262144 | tf_op jit(solution)/shard_map/all_to_all | solution.py:25
  26.4 6.7 %all-to-all-done = bf16[16,2,2048]{2,1,0:T(2,128)(2,1)S(1)} async-done(((bf16[16,2,2048]{2,1,0:T(2,128)(2,1)}), bf16[16,2,2048]{2,1,0:T(2,128)(2,1)S(1)}, u32[]{:S(2)}, u32[]{:S(2)}) %all-to-all-start) | async-done | bytes 131104 | tf_op jit(solution)/shard_map/all_to_all | solution.py:25
  34.5 0.7 broadcast_in_dim.28
  35.2 15.2 %all-to-all-start.1 = ((bf16[16,32,128]{2,1,0:T(8,128)(2,1)}), bf16[16,32,128]{2,1,0:T(8,128)(2,1)S(1)}, u32[]{:S(2)}, u32[]{:S(2)}) async-start(bf16[16,32,128]{2,1,0:T(8,128)(2,1)} %broadcast_in_dim.28), calls=%async_computation.1 | async-start | bytes 262144 | tf_op jit(solution)/shard_map/all_to_all | solution.py:109
  50.6 2.2 %collective-permute-start.3 = (bf16[256,2048]{1,0:T(8,128)(2,1)S(1)}, bf16[256,2048]{1,0:T(8,128)(2,1)}, u32[]{:S(2)}, u32[]{:S(2)}) collective-permute-start(bf16[256,2048]{1,0:T(8,128)(2,1)S(1)} %pad_maximum_fusion), channel_id=1, source_target_pairs={{0,4},{1,5},{2,6},{3,7},{4,8},{5,9},{6,10},{7,11},{8,12},{9,13},{1... | collective-permute-start | bytes 3145736 | tf_op jit(solution)/shard_map/ppermute | solution.py:97
  52.8 4.0 %collective-permute-start.5 = (bf16[256,2048]{1,0:T(8,128)(2,1)S(1)}, bf16[256,2048]{1,0:T(8,128)(2,1)S(1)}, u32[]{:S(2)}, u32[]{:S(2)}) collective-permute-start(bf16[256,2048]{1,0:T(8,128)(2,1)S(1)} %pad_maximum_fusion), channel_id=1, source_target_pairs={{0,8},{1,9},{2,10},{3,11},{4,12},{5,13},{6,14},{7,15},{8,0},{9,1},... | collective-permute-start | bytes 3145736 | tf_op jit(solution)/shard_map/ppermute | solution.py:97
  56.8 3.2 %collective-permute-start.4 = (bf16[256,2048]{1,0:T(8,128)(2,1)S(1)}, bf16[256,2048]{1,0:T(8,128)(2,1)}, u32[]{:S(2)}, u32[]{:S(2)}) collective-permute-start(bf16[256,2048]{1,0:T(8,128)(2,1)S(1)} %pad_maximum_fusion), channel_id=1, source_target_pairs={{0,12},{1,13},{2,14},{3,15},{4,0},{5,1},{6,2},{7,3},{8,4},{9,5},{1... | collective-permute-start | bytes 3145736 | tf_op jit(solution)/shard_map/ppermute | solution.py:97
  60.0 1.1 constant_dynamic-update-slice_fusion.3
  61.3 1.5 all-to-all-done.1
  62.8 2.1 %collective-permute-start.6 = (bf16[16,32,128]{2,1,0:T(8,128)(2,1)S(1)}, bf16[16,32,128]{2,1,0:T(8,128)(2,1)S(1)}, u32[]{:S(2)}, u32[]{:S(2)}) collective-permute-start(bf16[16,32,128]{2,1,0:T(8,128)(2,1)S(1)} %all-to-all-done.1), channel_id=1, source_target_pairs={{0,16},{16,0},{32,48},{48,32},{64,80},{80,64},{96,112},{112,96},{1... | collective-permute-start | bytes 393224 | tf_op jit(solution)/shard_map/ppermute | solution.py:116
  65.0 1.0 collective-permute-done.6
  66.2 13.7 %collective-permute-done.3 = bf16[256,2048]{1,0:T(8,128)(2,1)} collective-permute-done((bf16[256,2048]{1,0:T(8,128)(2,1)S(1)}, bf16[256,2048]{1,0:T(8,128)(2,1)}, u32[]{:S(2)}, u32[]{:S(2)}) %collective-permute-start.3) | collective-permute-done | bytes 1048608 | tf_op jit(solution)/shard_map/ppermute | solution.py:97
  79.8 2.4 %constant_dynamic-update-slice_fusion.2 = bf16[1024,2048]{1,0:T(8,128)(2,1)} fusion(bf16[1024,2048]{1,0:T(8,128)(2,1)} %constant_dynamic-update-slice_fusion.3, bf16[256,2048]{1,0:T(8,128)(2,1)} %collective-permute-done.3), kind=kLoop, calls=%fused_computation.96 | loop fusion | bytes 2097152
  82.7 2.3 %constant_dynamic-update-slice_fusion.1 = bf16[1024,2048]{1,0:T(8,128)(2,1)} fusion(bf16[1024,2048]{1,0:T(8,128)(2,1)} %constant_dynamic-update-slice_fusion.2, bf16[256,2048]{1,0:T(8,128)(2,1)} %collective-permute-done.4), kind=kLoop, calls=%fused_computation.95 | loop fusion | bytes 2097152
  85.0 1.1 constant_dynamic-update-slice_fusion
  86.1 3.1 %multiply_reduce_fusion = f32[2048]{0:T(1024)S(1)} fusion(bf16[1024,2048]{1,0:T(8,128)(2,1)} %constant_dynamic-update-slice_fusion), kind=kLoop, calls=%fused_computation.1 | loop fusion | flops 6289408 | bytes 4202496 | tf_op jit(solution)/shard_map/reduce_sum | solution.py:132
  89.1 3.0 %fusion = bf16[2048,128]{0,1:T(8,128)(2,1)S(1)} fusion(bf16[1024,2048]{1,0:T(8,128)(2,1)} %constant_dynamic-update-slice_fusion, bf16[1024,128]{1,0:T(8,128)(2,1)S(1)} %bitcast_select_fusion, f32[2048]{0:T(1024)S(1)} %add_rsqrt_fusion), kind=kOutput, calls=%fused_computation.15 | convolution fusion | flops 537395200 | bytes 4988928 | tf_op jit(solution)/shard_map/dot_general | solution.py:133
  92.2 0.9 fusion.75
  93.0 2.0 %copy-done.1 = f32[512,2112]{0,1:T(8,128)} copy-done((f32[512,2112]{0,1:T(8,128)}, f32[512,2112]{0,1:T(8,128)S(1)}, u32[]{:S(2)}) %copy-start.1) | copy-done | bytes 4325400
  95.8 0.9 fusion.74
  96.7 2.0 %copy-done.2 = f32[512,2112]{0,1:T(8,128)} copy-done((f32[512,2112]{0,1:T(8,128)}, f32[512,2112]{0,1:T(8,128)S(1)}, u32[]{:S(2)}) %copy-start.2) | copy-done | bytes 4325400
  98.7 0.7 convert_reduce_fusion.2
  99.4 0.9 fusion.73
  100.3 0.7 convert_reduce_fusion.1
  101.0 0.7 slice-done
  101.6 0.8 convolution_divide_fusion.2
  102.4 0.8 convolution_divide_fusion.1
  103.3 0.9 fusion.72
  104.2 0.7 convert_reduce_fusion
  104.9 0.8 convolution_divide_fusion
  106.2 2.1 %collective-permute-start.7 = (bf16[16,40,128]{2,0,1:T(8,128)(2,1)S(1)}, bf16[16,40,128]{2,0,1:T(8,128)(2,1)S(1)}, u32[]{:S(2)}, u32[]{:S(2)}) collective-permute-start(bf16[16,40,128]{2,0,1:T(8,128)(2,1)S(1)} %pad_maximum_fusion.4), channel_id=1, source_target_pairs={{0,16},{16,0},{32,48},{48,32},{64,80},{80,64},{96,112},{112,96},{1... | collective-permute-start | bytes 491528 | tf_op jit(solution)/shard_map/ppermute | solution.py:174
  108.3 3.0 %convolution_divide_fusion.3 = f32[512,64]{0,1:T(8,128)S(1)} fusion(f32[512,2112]{0,1:T(8,128)} %copy-done.1, f32[512]{0:T(512)S(1)} %broadcast_maximum_fusion.7, f32[512]{0:T(512)S(1)} %get-tuple-element.47, bf16[64,64]{0,1:T(8,128)(2,1)S(1)} %copy.128, bf16[2048,64]{0,1:T(8,128)(2,1)S(1)} %get-tuple-element.18), kind=kOutput, calls=%fused_computation.21 | convolution fusion | flops 141148160 | bytes 4730880 | tf_op jit(solution)/shard_map/qk,kd->qd/dot_general | solution.py:158
  113.2 27.2 %all_to_all.30 = bf16[16,40,128]{2,1,0:T(8,128)(2,1)S(1)} all-to-all(bf16[16,40,128]{2,1,0:T(8,128)(2,1)S(1)} %fusion.8), channel_id=1, replica_groups={{0,32,64,96,128,160,192,224,256,288,320,352,384,416,448,480},{16,48,80,..., dimensions={0} | all-to-all | bytes 327680 | tf_op jit(solution)/shard_map/all_to_all | solution.py:182
  141.7 12.4 %all_to_all.31 = bf16[16,2,2048]{2,1,0:T(2,128)(2,1)S(1)} all-to-all(bf16[16,2,2048]{2,1,0:T(2,128)(2,1)S(1)} %reshape.629), channel_id=1, replica_groups=mesh['seq'=32,'head'=16] {'head'}, dimensions={0} | all-to-all | bytes 262144 | tf_op jit(solution)/shard_map/all_to_all | solution.py:190
  154.8 11.8 %all_to_all.32 = f32[16,1,4096]{2,1,0:T(1,128)S(1)} all-to-all(f32[16,1,4096]{2,1,0:T(1,128)S(1)} %reshape.631), channel_id=1, replica_groups=mesh['seq'=32,'head'=16] {'head'}, dimensions={0} | all-to-all | bytes 524288 | tf_op jit(solution)/shard_map/all_to_all | solution.py:25
  167.1 1.3 reduce.19
  170.3 10.9 %all_to_all.33 = bf16[16,2,2048]{2,1,0:T(2,128)(2,1)S(1)} all-to-all(bf16[16,2,2048]{2,1,0:T(2,128)(2,1)S(1)} %reshape.633), channel_id=1, replica_groups=mesh['seq'=32,'head'=16] {'head'}, dimensions={0} | all-to-all | bytes 262144 | tf_op jit(solution)/shard_map/all_to_all | solution.py:190
  (145 shorter events, 12.7 us)
Async XLA Ops:
  0.0 169.2 %copy-start = (bf16[256,1024]{1,0:T(8,128)(2,1)S(1)}, bf16[256,1024]{1,0:T(8,128)(2,1)}, u32[]{:S(2)}) copy-start(bf16[256,1024]{1,0:T(8,128)(2,1)} %param.24) | copy-start | bytes 1572868
  0.0 25.1 %copy-start.8 = (s32[2048]{0:T(1024)S(1)}, s32[2048]{0:T(1024)}, u32[]{:S(2)}) copy-start(s32[2048]{0:T(1024)} %param.16) | copy-start | bytes 24580
  0.0 15.3 %collective-permute-start.2 = (bf16[64,2048]{1,0:T(8,128)(2,1)}, bf16[64,2048]{1,0:T(8,128)(2,1)S(1)}, u32[]{:S(2)}, u32[]{:S(2)}) collective-permute-start(bf16[64,2048]{1,0:T(8,128)(2,1)} %bitcast.70), channel_id=1, source_target_pairs={{0,2},{1,3},{2,0},{3,1},{4,6},{5,7},{6,4},{7,5},{8,10},{9,11},{10,... | collective-permute-start | bytes 786440 | tf_op jit(solution)/shard_map/ppermute | solution.py:92
  5.1 10.2 %collective-permute-start.1 = (bf16[64,2048]{1,0:T(8,128)(2,1)}, bf16[64,2048]{1,0:T(8,128)(2,1)S(1)}, u32[]{:S(2)}, u32[]{:S(2)}) collective-permute-start(bf16[64,2048]{1,0:T(8,128)(2,1)} %bitcast.71), channel_id=1, source_target_pairs={{0,3},{1,0},{2,1},{3,2},{4,7},{5,4},{6,5},{7,6},{8,11},{9,8},{10,9... | collective-permute-start | bytes 786440 | tf_op jit(solution)/shard_map/ppermute | solution.py:92
  8.1 9.7 %collective-permute-start = (bf16[64,2048]{1,0:T(8,128)(2,1)}, bf16[64,2048]{1,0:T(8,128)(2,1)S(1)}, u32[]{:S(2)}, u32[]{:S(2)}) collective-permute-start(bf16[64,2048]{1,0:T(8,128)(2,1)} %bitcast.72), channel_id=1, source_target_pairs={{0,1},{1,2},{2,3},{3,0},{4,5},{5,6},{6,7},{7,4},{8,9},{9,10},{10,1... | collective-permute-start | bytes 786440 | tf_op jit(solution)/shard_map/ppermute | solution.py:92
  10.9 23.1 %copy-start.4 = (bf16[1024,64]{0,1:T(8,128)(2,1)S(1)}, bf16[1024,64]{0,1:T(8,128)(2,1)}, u32[]{:S(2)}) copy-start(bf16[1024,64]{0,1:T(8,128)(2,1)} %param.20) | copy-start | bytes 393220
  10.9 23.1 %copy-start.5 = (bf16[1024,64]{0,1:T(8,128)(2,1)S(1)}, bf16[1024,64]{0,1:T(8,128)(2,1)}, u32[]{:S(2)}) copy-start(bf16[1024,64]{0,1:T(8,128)(2,1)} %param.19) | copy-start | bytes 393220
  11.0 23.1 %copy-start.11 = (f32[1024]{0:T(1024)S(1)}, f32[1024]{0:T(1024)}, u32[]{:S(2)}) copy-start(f32[1024]{0:T(1024)} %param.17) | copy-start | bytes 12292
  11.0 23.1 %copy-start.12 = (bf16[1024,64]{0,1:T(8,128)(2,1)S(1)}, bf16[1024,64]{0,1:T(8,128)(2,1)}, u32[]{:S(2)}) copy-start(bf16[1024,64]{0,1:T(8,128)(2,1)} %param.18) | copy-start | bytes 393220
  15.3 37.6 %copy-start.9 = (s32[2048]{0:T(1024)S(1)}, s32[2048]{0:T(1024)}, u32[]{:S(2)}) copy-start(s32[2048]{0:T(1024)} %param.15) | copy-start | bytes 24580
  20.5 12.6 %all-to-all-start = ((bf16[16,2,2048]{2,1,0:T(2,128)(2,1)}), bf16[16,2,2048]{2,1,0:T(2,128)(2,1)S(1)}, u32[]{:S(2)}, u32[]{:S(2)}) async-start(bf16[16,2,2048]{2,1,0:T(2,128)(2,1)} %reshape.627), calls=%async_computation | async-start | bytes 262144 | tf_op jit(solution)/shard_map/all_to_all | solution.py:25
  35.2 27.6 %all-to-all-start.1 = ((bf16[16,32,128]{2,1,0:T(8,128)(2,1)}), bf16[16,32,128]{2,1,0:T(8,128)(2,1)S(1)}, u32[]{:S(2)}, u32[]{:S(2)}) async-start(bf16[16,32,128]{2,1,0:T(8,128)(2,1)} %broadcast_in_dim.28), calls=%async_computation.1 | async-start | bytes 262144 | tf_op jit(solution)/shard_map/all_to_all | solution.py:109
  50.6 29.2 %collective-permute-start.3 = (bf16[256,2048]{1,0:T(8,128)(2,1)S(1)}, bf16[256,2048]{1,0:T(8,128)(2,1)}, u32[]{:S(2)}, u32[]{:S(2)}) collective-permute-start(bf16[256,2048]{1,0:T(8,128)(2,1)S(1)} %pad_maximum_fusion), channel_id=1, source_target_pairs={{0,4},{1,5},{2,6},{3,7},{4,8},{5,9},{6,10},{7,11},{8,12},{9,13},{1... | collective-permute-start | bytes 3145736 | tf_op jit(solution)/shard_map/ppermute | solution.py:97
  52.8 32.2 %collective-permute-start.5 = (bf16[256,2048]{1,0:T(8,128)(2,1)S(1)}, bf16[256,2048]{1,0:T(8,128)(2,1)S(1)}, u32[]{:S(2)}, u32[]{:S(2)}) collective-permute-start(bf16[256,2048]{1,0:T(8,128)(2,1)S(1)} %pad_maximum_fusion), channel_id=1, source_target_pairs={{0,8},{1,9},{2,10},{3,11},{4,12},{5,13},{6,14},{7,15},{8,0},{9,1},... | collective-permute-start | bytes 3145736 | tf_op jit(solution)/shard_map/ppermute | solution.py:97
  56.8 25.9 %collective-permute-start.4 = (bf16[256,2048]{1,0:T(8,128)(2,1)S(1)}, bf16[256,2048]{1,0:T(8,128)(2,1)}, u32[]{:S(2)}, u32[]{:S(2)}) collective-permute-start(bf16[256,2048]{1,0:T(8,128)(2,1)S(1)} %pad_maximum_fusion), channel_id=1, source_target_pairs={{0,12},{1,13},{2,14},{3,15},{4,0},{5,1},{6,2},{7,3},{8,4},{9,5},{1... | collective-permute-start | bytes 3145736 | tf_op jit(solution)/shard_map/ppermute | solution.py:97
  62.8 3.2 %collective-permute-start.6 = (bf16[16,32,128]{2,1,0:T(8,128)(2,1)S(1)}, bf16[16,32,128]{2,1,0:T(8,128)(2,1)S(1)}, u32[]{:S(2)}, u32[]{:S(2)}) collective-permute-start(bf16[16,32,128]{2,1,0:T(8,128)(2,1)S(1)} %all-to-all-done.1), channel_id=1, source_target_pairs={{0,16},{16,0},{32,48},{48,32},{64,80},{80,64},{96,112},{112,96},{1... | collective-permute-start | bytes 393224 | tf_op jit(solution)/shard_map/ppermute | solution.py:116
  93.0 2.0 %copy-start.1 = (f32[512,2112]{0,1:T(8,128)}, f32[512,2112]{0,1:T(8,128)S(1)}, u32[]{:S(2)}) copy-start(f32[512,2112]{0,1:T(8,128)S(1)} %get-tuple-element.64) | copy-start | bytes 12976132
  96.7 2.0 %copy-start.2 = (f32[512,2112]{0,1:T(8,128)}, f32[512,2112]{0,1:T(8,128)S(1)}, u32[]{:S(2)}) copy-start(f32[512,2112]{0,1:T(8,128)S(1)} %get-tuple-element.62) | copy-start | bytes 12976132
  99.4 2.2 %slice-start = ((s8[4325376]{0:T(1024)(128)(4,1)}), s8[4194304]{0:T(1024)(128)(4,1)S(1)}, s32[]{:S(2)}) async-start(s8[4325376]{0:T(1024)(128)(4,1)} %bitcast.58), calls=%async_computation.6 | async-start | bytes 8388608
  99.4 2.2 %slice-start.1 = ((s8[4325376]{0:T(1024)(128)(4,1)}), s8[131072]{0:T(1024)(128)(4,1)S(1)}, s32[]{:S(2)}) async-start(s8[4325376]{0:T(1024)(128)(4,1)} %bitcast.58), calls=%async_computation.7 | async-start | bytes 262144
  106.2 5.8 %collective-permute-start.7 = (bf16[16,40,128]{2,0,1:T(8,128)(2,1)S(1)}, bf16[16,40,128]{2,0,1:T(8,128)(2,1)S(1)}, u32[]{:S(2)}, u32[]{:S(2)}) collective-permute-start(bf16[16,40,128]{2,0,1:T(8,128)(2,1)S(1)} %pad_maximum_fusion.4), channel_id=1, source_target_pairs={{0,16},{16,0},{32,48},{48,32},{64,80},{80,64},{96,112},{112,96},{1... | collective-permute-start | bytes 491528 | tf_op jit(solution)/shard_map/ppermute | solution.py:174
  111.4 29.6 %copy-start.6 = (bf16[64,1024]{1,0:T(8,128)(2,1)S(1)}, bf16[64,1024]{1,0:T(8,128)(2,1)}, u32[]{:S(2)}) copy-start(bf16[64,1024]{1,0:T(8,128)(2,1)} %param.21) | copy-start | bytes 393220
  111.6 42.7 %copy-start.7 = (bf16[64,64]{1,0:T(8,128)(2,1)S(1)}, bf16[64,64]{1,0:T(8,128)(2,1)}, u32[]{:S(2)}) copy-start(bf16[64,64]{1,0:T(8,128)(2,1)} %param.14) | copy-start | bytes 24580
  140.6 28.6 %copy-start.3 = (bf16[1024,256]{1,0:T(8,128)(2,1)S(1)}, bf16[1024,256]{1,0:T(8,128)(2,1)}, u32[]{:S(2)}) copy-start(bf16[1024,256]{1,0:T(8,128)(2,1)} %param.23) | copy-start | bytes 1572868
  140.6 28.6 %copy-start.10 = (f32[1024]{0:T(1024)S(1)}, f32[1024]{0:T(1024)}, u32[]{:S(2)}) copy-start(f32[1024]{0:T(1024)} %param.22) | copy-start | bytes 12292

commit v3 on v1

v3 whole, which is shorter than its diff:
```python
import functools
import math

import jax
import jax.numpy as jnp
from jax import lax
from jax.experimental import pallas as pl
from jax.experimental.pallas import tpu as pltpu
from jax.sharding import PartitionSpec as P

HD = 64
EPSILON = 1e-06
NEGATIVE = -1e30
LOWEST = -1e29
BOTH = ("seq", "head")
SHIFTS = (0, 1, 3, 2)
F32 = jnp.float32
BF16 = jnp.bfloat16
MIB = 1 << 20


def dot(a, b, dims):
    return lax.dot_general(a, b, (dims, ((), ())), preferred_element_type=F32)


NN = ((1,), (0,))
NT = ((1,), (1,))
TN = ((0,), (0,))


def line_shift(seq_size, side, phase, step):
    pairs = []
    for s in range(seq_size):
        along_x = (s % 2 == 0) == (phase == 0)
        for y in range(side):
            for x in range(side):
                target = (y, (x + step) % side) if along_x else ((y + step) % side, x)
                base = s * side * side
                pairs.append((base + y * side + x, base + target[0] * side + target[1]))
    return pairs


def low_half(shape):
    return lax.broadcasted_iota(jnp.int32, shape, len(shape) - 1) < shape[-1] // 2


def pack_columns(low_rows, high_rows, out_ref):
    for g in range(low_rows.shape[1] // 128):
        a = low_rows[:, 128 * g : 128 * g + 128]
        b = high_rows[:, 128 * g : 128 * g + 128]
        low = low_half(a.shape)
        out_ref[2 * g] = jnp.where(low, a, pltpu.roll(b, 64, 1)).astype(out_ref.dtype)
        out_ref[2 * g + 1] = jnp.where(low, pltpu.roll(a, 64, 1), b).astype(out_ref.dtype)


def unpack_columns(ref):
    tops, bottoms = [], []
    for g in range(ref.shape[0] // 2):
        a = ref[2 * g].astype(F32)
        b = ref[2 * g + 1].astype(F32)
        low = low_half(a.shape)
        tops.append(jnp.where(low, a, pltpu.roll(b, 64, 1)))
        bottoms.append(jnp.where(low, pltpu.roll(a, 64, 1), b))
    return jnp.concatenate(
        [jnp.concatenate(tops, axis=1), jnp.concatenate(bottoms, axis=1)], axis=0
    )


def normalize(rows, gain):
    inverse = lax.rsqrt(jnp.mean(rows * rows, axis=-1, keepdims=True) + EPSILON)
    return (rows * inverse * gain).astype(BF16)


def weights_kernel(order_ref, wk_ref, wv_ref, gain_ref, out_ref, scratch):
    both = jnp.concatenate([wk_ref[...], wv_ref[...]], axis=0).astype(F32) * gain_ref[...]
    scratch[...] = both.T.reshape(scratch.shape)
    for b in range(scratch.shape[0]):
        out_ref[b] = scratch[order_ref[b]].astype(BF16)


def queries_kernel(lat_ref, wq_ref, wk_ref, wv_ref, gain_ref, q_ref, kv_ref):
    normed = normalize(unpack_columns(lat_ref), gain_ref[...])
    q = dot(normed, wq_ref[...], NT).astype(BF16).astype(F32) * HD ** (-0.5)
    half = q.shape[0] // 2
    packed = jnp.concatenate([q[:half], q[half:]], axis=1).astype(BF16)
    q_ref[...] = jnp.broadcast_to(packed[None], q_ref.shape)
    rows = jnp.concatenate([dot(wk_ref[...], normed, NT), dot(wv_ref[...], normed, NT)], axis=0)
    kv_ref[...] = jnp.concatenate([rows, jnp.zeros_like(rows)], axis=1).astype(BF16)


def keys_kernel(*refs):
    *line_refs, w_ref, lat_ref, ka_ref, kb_ref, va_ref, vb_ref = refs
    tokens = line_refs[0].shape[1]
    width = 256
    for c in range(tokens // width):
        cols = slice(c * width, c * width + width)
        total = jnp.zeros((128, width), F32)
        squares = jnp.zeros((1, width), F32)
        for i, line in enumerate(line_refs):
            piece = line[:, cols]
            w = w_ref[4 * i : 4 * i + 4].reshape(-1, 128)
            total = total + dot(w, piece, TN)
            wide = piece.astype(F32)
            squares = squares + jnp.sum(wide * wide, axis=0, keepdims=True)
        inverse = lax.rsqrt(squares * (1.0 / 1024) + EPSILON)
        put_keys((total * inverse).astype(BF16), cols, ka_ref, kb_ref, va_ref, vb_ref)
    put_keys(lat_ref[...], slice(tokens, tokens + 128), ka_ref, kb_ref, va_ref, vb_ref)


def put_keys(both, cols, ka_ref, kb_ref, va_ref, vb_ref):
    keys, values = both[:64], both[64:]
    none = jnp.zeros_like(keys)
    ka_ref[:, cols] = jnp.concatenate([keys, none], axis=0)
    kb_ref[:, cols] = jnp.concatenate([none, keys], axis=0)
    ones = jnp.ones(values.shape, F32)
    va_ref[cols, :] = jnp.concatenate([values.astype(F32), ones], axis=0).T.astype(BF16)
    vb_ref[cols, :] = jnp.concatenate([ones, values.astype(F32)], axis=0).T.astype(BF16)


def attend_rows(q, pos_a, pos_b, kp, ka_ref, kb_ref, va_ref, vb_ref):
    def one(k_ref, v_ref, pos):
        scores = jnp.where(kp <= pos, dot(q, k_ref[...], NN), NEGATIVE)
        top = jnp.maximum(jnp.max(scores, axis=1, keepdims=True), LOWEST)
        weights = jnp.exp(scores - top).astype(BF16)
        return dot(weights, v_ref[...], NN), top

    out_a, top_a = one(ka_ref, va_ref, pos_a)
    out_b, top_b = one(kb_ref, vb_ref, pos_b)
    low = low_half(out_a.shape)
    above = jnp.where(low, out_a, out_b)
    below = jnp.maximum(pltpu.roll(jnp.where(low, out_b, out_a), 64, 1), 1e-30)
    return above / below, jnp.where(low, top_a, top_b) + jnp.log(below)


def put_message(mixed, level, out_ref, group):
    out_ref[group, :32] = mixed.astype(BF16)
    lane = lax.broadcasted_iota(jnp.int32, level.shape, 1) % 64
    row = lax.broadcasted_iota(jnp.int32, level.shape, 0)
    once = jnp.sum(jnp.where(lane == row, level, 0.0), axis=0, keepdims=True)
    first = once.astype(BF16).astype(F32)
    second = (once - first).astype(BF16).astype(F32)
    third = once - first - second
    rest = jnp.zeros((13, 128), F32)
    out_ref[group, 32:] = jnp.concatenate([first, second, third, rest], axis=0).astype(BF16)


def get_message(ref):
    groups = ref.shape[0]
    values = ref[:, :32].astype(F32).reshape(groups * 32, 128)
    lane = lax.broadcasted_iota(jnp.int32, (32, 128), 1) % 64
    row = lax.broadcasted_iota(jnp.int32, (32, 128), 0)
    terms = []
    for g in range(groups):
        tail = ref[g, 32:].astype(F32)
        terms.append(
            jnp.concatenate(
                [jnp.where(lane == row, tail[t : t + 1], 0.0) for t in range(3)], axis=1
            )
        )
    spread = jnp.concatenate(terms, axis=0).astype(BF16)
    i = lax.broadcasted_iota(jnp.int32, (384, 128), 0) // 64 % 2
    j = lax.broadcasted_iota(jnp.int32, (384, 128), 1) // 64
    levels = dot(spread, jnp.where(i == j, 1.0, 0.0).astype(BF16), NN)
    return values, levels


def other_kernel(q_ref, pos_ref, kp_ref, ka_ref, kb_ref, va_ref, vb_ref, out_ref):
    kp = kp_ref[...]

    @pl.loop(0, q_ref.shape[0] // 128)
    def _(i):
        rows = pl.ds(pl.multiple_of(i * 128, 128), 128)
        pos = pos_ref[rows, :]
        mixed, level = attend_rows(
            q_ref[rows, :], pos[:, 0:1], pos[:, 1:2], kp, ka_ref, kb_ref, va_ref, vb_ref
        )
        for g in range(4):
            part = slice(32 * g, 32 * g + 32)
            put_message(mixed[part], level[part], out_ref, i * 4 + g)


def own_kernel(q_ref, pos_ref, kp_ref, ka_ref, kb_ref, va_ref, vb_ref, mix_ref, lev_ref):
    kp = kp_ref[...]

    @pl.loop(0, q_ref.shape[0] // 128)
    def _(i):
        rows = pl.ds(pl.multiple_of(i * 128, 128), 128)
        pos = pos_ref[rows, :]
        mixed, level = attend_rows(
            q_ref[rows, :], pos[:, 2:3], pos[:, 3:4], kp, ka_ref, kb_ref, va_ref, vb_ref
        )
        mix_ref[rows, :] = mixed
        lev_ref[rows, :] = level


def join_kernel(mix_ref, lev_ref, arrived_ref, out_ref):
    values, levels = get_message(arrived_ref)
    mine = lev_ref[...]
    top = jnp.maximum(mine, levels)
    a, b = jnp.exp(mine - top), jnp.exp(levels - top)
    total = a + b
    mixed = (mix_ref[...] * a + values * b) / total
    level = top + jnp.log(total)
    for g in range(out_ref.shape[0]):
        part = slice(32 * g, 32 * g + 32)
        put_message(mixed[part], level[part], out_ref, g)


def project_kernel(arrived_ref, w_ref, out_ref):
    values, levels = get_message(arrived_ref)
    groups = arrived_ref.shape[0]
    values = values.reshape(groups, 32, 128)
    levels = levels.reshape(groups, 32, 128)
    factors = jnp.exp(levels - jnp.max(levels, axis=0, keepdims=True))
    attended = jnp.sum(values * factors, axis=0) / jnp.sum(factors, axis=0)
    low = low_half(attended.shape)
    w = w_ref[...]
    twice = jnp.concatenate([w, w], axis=0)
    top = dot(jnp.where(low, attended, 0.0).astype(BF16), twice, NN)
    bottom = dot(jnp.where(low, 0.0, attended).astype(BF16), twice, NN)
    pack_columns(top, bottom, out_ref)


def add_kernel(arrived_ref, lat_ref, own_ref, out_ref):
    own = jnp.sum(arrived_ref[...].astype(F32), axis=0) + lat_ref[...].astype(F32)
    own_ref[...] = own
    out_ref[...] = jnp.broadcast_to(own.astype(BF16)[None], out_ref.shape)


def mlp_kernel(arrived_ref, gain_ref, up_ref, down_ref, out_ref):
    normed = normalize(unpack_columns(arrived_ref), gain_ref[...])
    hidden = jax.nn.gelu(dot(normed, up_ref[...], NN), approximate=True).astype(BF16)
    share = dot(hidden, down_ref[...], NN)
    half = share.shape[0] // 2
    pack_columns(share[:half], share[half:], out_ref)


def last_kernel(arrived_ref, own_ref, out_ref):
    out_ref[...] = (jnp.sum(arrived_ref[...].astype(F32), axis=0) + own_ref[...]).astype(BF16)


def call(kernel, outs, cost=1000, **kwargs):
    shapes = [jax.ShapeDtypeStruct(s, t) for s, t in outs]
    return pl.pallas_call(
        kernel,
        out_shape=shapes if len(shapes) > 1 else shapes[0],
        compiler_params=pltpu.CompilerParams(vmem_limit_bytes=40 * MIB),
        cost_estimate=pl.CostEstimate(flops=cost, bytes_accessed=cost, transcendentals=0),
        **kwargs,
    )


def body(
    context,
    latents,
    ctx_pos,
    lat_pos,
    input_gain,
    w_query,
    w_key,
    w_value,
    w_out,
    mlp_gain,
    w_up,
    w_down,
):
    seq_size = lax.axis_size("seq")
    head_size = lax.axis_size("head")
    side = math.isqrt(head_size)
    lat_rows, cols = latents.shape
    tokens = context.shape[0]
    half = lat_rows // 2
    seq_place = lax.axis_index("seq")
    core = seq_place % 2
    planes = seq_size // 2
    along_z = [[2 * z + c for z in range(planes)] for c in range(2)]
    swap = [(s, s ^ 1) for s in range(seq_size)]
    block = (half, 2 * cols)
    row_gain = input_gain.reshape(1, -1)
    wq_t, wk_t, wv_t = w_query.T, w_key.T, w_value.T

    place = lax.axis_index("head")
    y, x = place // side, place % side
    shifts = jnp.array(SHIFTS, jnp.int32)
    first, second = shifts[None, :], shifts[:, None]
    by_x = ((y - second) % side) * side + (x - first) % side
    by_y = ((y - first) % side) * side + (x - second) % side
    order = jnp.where(core == 0, by_x, by_y).reshape(-1)

    own = context.T
    line = jnp.concatenate(
        [own]
        + [lax.ppermute(own, BOTH, line_shift(seq_size, side, 0, k)) for k in SHIFTS[1:]],
        axis=0,
    )
    line, latents = lax.optimization_barrier((line, latents))
    lines = [line] + [
        lax.ppermute(line, BOTH, line_shift(seq_size, side, 1, k)) for k in SHIFTS[1:]
    ]

    packed_latents = jnp.concatenate([latents[:half], latents[half:]], axis=1)
    lat_blocks = lax.all_to_all(
        jnp.broadcast_to(packed_latents[None], (head_size, *block)), "head", 0, 0
    )
    queries, latent_kv = call(
        queries_kernel, [((planes, *block), BF16), ((2 * cols, 2 * lat_rows), BF16)]
    )(lat_blocks, wq_t, wk_t, wv_t, row_gain)
    own_queries = lax.all_to_all(queries, "seq", 0, 0, axis_index_groups=along_z)
    other_queries = lax.ppermute(own_queries, "seq", swap)

    key_weights = call(
        weights_kernel,
        [((head_size, cols, 2 * cols), BF16)],
        in_specs=[pl.BlockSpec(memory_space=pltpu.SMEM)]
        + [pl.BlockSpec(memory_space=pltpu.VMEM)] * 3,
        scratch_shapes=[pltpu.VMEM((head_size, cols, 2 * cols), F32)],
    )(order, wk_t, wv_t, row_gain)
    key_count = tokens + 2 * lat_rows
    operands = call(
        keys_kernel,
        [((128, key_count), BF16)] * 2 + [((key_count, 128), BF16)] * 2,
        cost=10**9,
    )(*lines, key_weights, latent_kv)

    own_pos = lax.dynamic_slice_in_dim(lat_pos, seq_place * lat_rows, lat_rows)
    never = jnp.full((lat_rows,), jnp.iinfo(jnp.int32).max, jnp.int32)
    key_pos = jnp.concatenate([ctx_pos, own_pos, never]).reshape(1, -1)
    by_core = lat_pos.reshape(planes, 2, 2, half)
    mine = lax.dynamic_index_in_dim(by_core, core, 1, keepdims=False)
    theirs = lax.dynamic_index_in_dim(by_core, 1 - core, 1, keepdims=False)
    query_pos = jnp.stack([theirs[:, 0], theirs[:, 1], mine[:, 0], mine[:, 1]], axis=-1)
    query_pos = query_pos.reshape(-1, 4)

    rows = planes * half
    message = (planes, 48, 2 * cols)
    to_sibling = call(other_kernel, [(message, BF16)])(
        other_queries.reshape(rows, -1), query_pos, key_pos, *operands
    )
    from_sibling = lax.ppermute(to_sibling, "seq", swap)
    mixed, level = call(own_kernel, [((rows, 2 * cols), F32)] * 2)(
        own_queries.reshape(rows, -1), query_pos, key_pos, *operands
    )
    joined = call(join_kernel, [(message, BF16)])(mixed, level, from_sibling)
    arrived = lax.all_to_all(joined, "seq", 0, 0, axis_index_groups=along_z)
    shares = call(project_kernel, [((head_size, *block), BF16)])(arrived, w_out)
    arrived = lax.all_to_all(shares, "head", 0, 0)
    own_proj, copies = call(add_kernel, [(block, F32), ((head_size, *block), BF16)])(
        arrived, packed_latents
    )
    arrived = lax.all_to_all(copies, "head", 0, 0)
    shares = call(mlp_kernel, [((head_size, *block), BF16)])(
        arrived, mlp_gain.reshape(1, -1), w_up, w_down
    )
    arrived = lax.all_to_all(shares, "head", 0, 0)
    packed = call(last_kernel, [(block, BF16)])(arrived, own_proj)
    return jnp.concatenate([packed[:, :cols], packed[:, cols:]], axis=0)


def solution(mesh):
    placed = (
        P("seq", "head"),
        P("seq", "head"),
        P("seq"),
        P(),
        P(),
        P(None, "head"),
        P(None, "head"),
        P(None, "head"),
        P("head", None),
        P(),
        P(None, "head"),
        P("head", None),
    )
    return jax.shard_map(
        body, mesh=mesh, in_specs=placed, out_specs=P("seq", "head"), check_vma=False
    )
```

time: 186 us -> 170 us (0.914)
  the two profiles are of different devices: /device:TPU:2 before, /device:TPU:32 now
where the time goes in v3:
time: 170 us; the launch traced here: 169 us
  blocking collectives  55.8 us (33%)
  starting transfers between devices  45.4 us (27%)
  waiting for transfers between devices  30.5 us (18%)
  Pallas kernels  18.1 us (11%)
  local copies, waits for them, and re-layouts  14.1 us (8%)
  other arithmetic  4.3 us (3%)
    all_to_all x2, blocking collectives, body(): arrived = lax.all_to_all(shares, 'head', 0, 0)  24.3 us
    all_to_all x1, blocking collectives, body(): arrived = lax.all_to_all(joined, 'seq', 0, 0, axis_index_groups=along_z)  20.5 us
    all_to_all x1, waiting for transfers between devices, body(): lax.all_to_all(jnp.broadcast_to(packed_latents[None], (head_size, *block)...  15.8 us
    all_to_all x1, starting transfers between devices, body(): lax.all_to_all(queries, 'seq', 0, 0, axis_index_groups=along_z)  15.2 us
    all_to_all x1, blocking collectives, body(): arrived = lax.all_to_all(copies, 'head', 0, 0)  11.1 us
    ppermute x3, starting transfers between devices, body(): lax.ppermute(line, BOTH, line_shift(seq_size, side, 1, k))  10.9 us
    ppermute x3, starting transfers between devices, body(): lax.ppermute(own, BOTH, line_shift(seq_size, side, 0, k))  10.8 us
    all_to_all x1, waiting for transfers between devices, body(): lax.all_to_all(queries, 'seq', 0, 0, axis_index_groups=along_z)  9.93 us
  transfers between devices with their start and end apart: 10, of which 3 were waited for; matrix products, arithmetic and copies ran while one was open for 6% of the time, Pallas kernels for 6%

profile of v3, /device:TPU:32, one launch (start us, length us, event | category | flops | bytes accessed | tf_op | source)
XLA Modules:
  0.0 168.6 jit_solution(766146003007066316)
XLA Ops:
  0.0 3.4 %collective-permute-start = (bf16[64,2048]{1,0:T(8,128)(2,1)}, bf16[64,2048]{1,0:T(8,128)(2,1)S(1)}, u32[]{:S(2)}, u32[]{:S(2)}) collective-permute-start(bf16[64,2048]{1,0:T(8,128)(2,1)} %bitcast.29), channel_id=1, source_target_pairs={{0,1},{1,2},{2,3},{3,0},{4,5},{5,6},{6,7},{7,4},{8,9},{9,10},{10,1... | collective-permute-start | bytes 786440 | tf_op jit(solution)/shard_map/ppermute | solution.py:293
  3.4 3.7 %collective-permute-start.1 = (bf16[64,2048]{1,0:T(8,128)(2,1)}, bf16[64,2048]{1,0:T(8,128)(2,1)S(1)}, u32[]{:S(2)}, u32[]{:S(2)}) collective-permute-start(bf16[64,2048]{1,0:T(8,128)(2,1)} %bitcast.30), channel_id=1, source_target_pairs={{0,3},{1,0},{2,1},{3,2},{4,7},{5,4},{6,5},{7,6},{8,11},{9,8},{10,9... | collective-permute-start | bytes 786440 | tf_op jit(solution)/shard_map/ppermute | solution.py:293
  7.1 3.7 %collective-permute-start.2 = (bf16[64,2048]{1,0:T(8,128)(2,1)}, bf16[64,2048]{1,0:T(8,128)(2,1)S(1)}, u32[]{:S(2)}, u32[]{:S(2)}) collective-permute-start(bf16[64,2048]{1,0:T(8,128)(2,1)} %bitcast.31), channel_id=1, source_target_pairs={{0,2},{1,3},{2,0},{3,1},{4,6},{5,7},{6,4},{7,5},{8,10},{9,11},{10,... | collective-permute-start | bytes 786440 | tf_op jit(solution)/shard_map/ppermute | solution.py:293
  10.8 0.8 reshape.73
  11.7 0.6 copy_bitcast_fusion
  12.3 4.7 %collective-permute-done.2 = bf16[64,2048]{1,0:T(8,128)(2,1)S(1)} collective-permute-done((bf16[64,2048]{1,0:T(8,128)(2,1)}, bf16[64,2048]{1,0:T(8,128)(2,1)S(1)}, u32[]{:S(2)}, u32[]{:S(2)}) %collective-permute-start.2) | collective-permute-done | bytes 262176 | tf_op jit(solution)/shard_map/ppermute | solution.py:293
  17.0 1.0 pad_maximum_fusion.refs_0_
  18.1 3.5 %collective-permute-start.3 = (bf16[256,2048]{1,0:T(8,128)(2,1)S(1)}, bf16[256,2048]{1,0:T(8,128)(2,1)S(1)}, u32[]{:S(2)}, u32[]{:S(2)}) collective-permute-start(bf16[256,2048]{1,0:T(8,128)(2,1)S(1)} %pad_maximum_fusion.refs_0_), channel_id=1, source_target_pairs={{0,4},{1,5},{2,6},{3,7},{4,8},{5,9},{6,10},{7,11},{8,12},{9,13},{1... | collective-permute-start | bytes 3145736 | tf_op jit(solution)/shard_map/ppermute | solution.py:298
  21.6 3.6 %collective-permute-start.4 = (bf16[256,2048]{1,0:T(8,128)(2,1)S(1)}, bf16[256,2048]{1,0:T(8,128)(2,1)S(1)}, u32[]{:S(2)}, u32[]{:S(2)}) collective-permute-start(bf16[256,2048]{1,0:T(8,128)(2,1)S(1)} %pad_maximum_fusion.refs_0_), channel_id=1, source_target_pairs={{0,12},{1,13},{2,14},{3,15},{4,0},{5,1},{6,2},{7,3},{8,4},{9,5},{1... | collective-permute-start | bytes 3145736 | tf_op jit(solution)/shard_map/ppermute | solution.py:298
  25.2 3.9 %collective-permute-start.5 = (bf16[256,2048]{1,0:T(8,128)(2,1)S(1)}, bf16[256,2048]{1,0:T(8,128)(2,1)}, u32[]{:S(2)}, u32[]{:S(2)}) collective-permute-start(bf16[256,2048]{1,0:T(8,128)(2,1)S(1)} %pad_maximum_fusion.refs_0_), channel_id=1, source_target_pairs={{0,8},{1,9},{2,10},{3,11},{4,12},{5,13},{6,14},{7,15},{8,0},{9,1},... | collective-permute-start | bytes 3145736 | tf_op jit(solution)/shard_map/ppermute | solution.py:298
  29.2 0.7 broadcast_in_dim.4
  29.9 4.2 %all-to-all-start = ((bf16[16,32,128]{2,1,0:T(8,128)(2,1)}), bf16[16,32,128]{2,1,0:T(8,128)(2,1)S(1)}, u32[]{:S(2)}, u32[]{:S(2)}) async-start(bf16[16,32,128]{2,1,0:T(8,128)(2,1)} %broadcast_in_dim.4), calls=%async_computation | async-start | bytes 262144 | tf_op jit(solution)/shard_map/all_to_all | solution.py:302
  34.0 1.2 fusion.1
  35.2 15.8 %all-to-all-done.lat_ref = bf16[16,32,128]{2,1,0:T(8,128)(2,1)S(1)} async-done(((bf16[16,32,128]{2,1,0:T(8,128)(2,1)}), bf16[16,32,128]{2,1,0:T(8,128)(2,1)S(1)}, u32[]{:S(2)}, u32[]{:S(2)}) %all-to-all-start) | async-done | bytes 131104 | tf_op jit(solution)/shard_map/all_to_all | solution.py:302
  51.1 0.9 copy-done.10
  52.0 0.4 shard_map.127
  52.4 0.6 copy-done.9
  53.1 0.6 copy-done.11
  53.7 15.2 %all-to-all-start.1 = ((bf16[16,32,128]{2,1,0:T(8,128)(2,1)}), bf16[16,32,128]{2,1,0:T(8,128)(2,1)S(1)}, u32[]{:S(2)}, u32[]{:S(2)}) async-start(bf16[16,32,128]{2,1,0:T(8,128)(2,1)} %copy-done.9), calls=%async_computation.1 | async-start | bytes 262144 | tf_op jit(solution)/shard_map/all_to_all | solution.py:308
  68.9 0.8 add_select_fusion
  69.6 0.1 select_n.67.order_ref
  69.7 0.7 fusion.3
  70.6 0.7 fusion.4
  71.5 9.9 %all-to-all-done.1 = bf16[16,32,128]{2,1,0:T(8,128)(2,1)S(1)} async-done(((bf16[16,32,128]{2,1,0:T(8,128)(2,1)}), bf16[16,32,128]{2,1,0:T(8,128)(2,1)S(1)}, u32[]{:S(2)}, u32[]{:S(2)}) %all-to-all-start.1) | async-done | bytes 131104 | tf_op jit(solution)/shard_map/all_to_all | solution.py:308
  81.4 1.9 %collective-permute-start.6 = (bf16[16,32,128]{2,1,0:T(8,128)(2,1)S(1)}, bf16[16,32,128]{2,1,0:T(8,128)(2,1)}, u32[]{:S(2)}, u32[]{:S(2)}) collective-permute-start(bf16[16,32,128]{2,1,0:T(8,128)(2,1)S(1)} %all-to-all-done.1), channel_id=1, source_target_pairs={{0,16},{16,0},{32,48},{48,32},{64,80},{80,64},{96,112},{112,96},{1... | collective-permute-start | bytes 393224 | tf_op jit(solution)/shard_map/ppermute | solution.py:309
  83.3 0.6 pad_add_fusion
  83.9 0.9 copy-done.5
  84.8 0.9 copy-done.7
  85.8 0.8 shard_map.128.refs_4_
  86.5 0.7 copy-done
  87.2 0.8 copy.26.pos_ref
  88.1 0.8 dynamic_slice.12
  88.8 1.4 concatenate.15
  90.2 0.7 reshape.74.kp_ref
  90.9 0.9 copy-done.1
  91.9 0.8 copy-done.12
  92.6 3.3 %shard_map.129 = (bf16[128,2176]{1,0:T(8,128)(2,1)S(1)}, bf16[128,2176]{1,0:T(8,128)(2,1)S(1)}, bf16[2176,128]{1,0:T(8,128)(2,1)S(1)}, bf16[2176,128]{1,0:T(8,128)(2,1)S(1)}) custom-call(bf16[256,2048]{1,0:T(8,128)(2,1)S(1)} %pad_maximum_fusion.refs_0_, bf16[256,2048]{1,0:T(8,128)(2,1)S(1)} %collective-permute-done.3.refs_1_, ...), custom_call_target="tpu_custom_call" | custom-call | flops 1000000000 | bytes 1000000000 | tf_op jit(solution)/shard_map/pallas_call | solution.py:319
  95.9 6.4 %shard_map.131 = bf16[16,48,128]{2,1,0:T(8,128)(2,1)S(1)} custom-call(bf16[512,128]{1,0:T(8,128)(2,1)} %bitcast.8.q_ref, s32[512,4]{1,0:T(8,128)S(1)} %copy.26.pos_ref, s32[1,2176]{1,0:T(1,128)S(1)} %reshape.74.kp_ref, bf16[128,2176]{1,0:T(8,128)(2,1)S(1)} %get-tuple-element.21.ka_ref, bf16[128,2176]{1,0:T(8,128)(2,1)S(1)} %get-tuple-element.22.kb_ref, ...), custom_call_target="tpu_custom_call" | custom-call | flops 1000 | bytes 1000 | tf_op jit(solution)/shard_map/pallas_call | solution.py:336
  102.3 2.4 %collective-permute-start.7 = (bf16[16,48,128]{2,1,0:T(8,128)(2,1)S(1)}, bf16[16,48,128]{2,1,0:T(8,128)(2,1)S(1)}, u32[]{:S(2)}, u32[]{:S(2)}) collective-permute-start(bf16[16,48,128]{2,1,0:T(8,128)(2,1)S(1)} %shard_map.131), channel_id=1, source_target_pairs={{0,16},{16,0},{32,48},{48,32},{64,80},{80,64},{96,112},{112,96},{1... | collective-permute-start | bytes 589832 | tf_op jit(solution)/shard_map/ppermute | solution.py:339
  104.7 5.4 %shard_map.130 = (f32[512,128]{1,0:T(8,128)S(1)}, f32[512,128]{1,0:T(8,128)S(1)}) custom-call(bf16[512,128]{1,0:T(8,128)(2,1)S(1)} %bitcast.20, s32[512,4]{1,0:T(8,128)S(1)} %copy.26.pos_ref, s32[1,2176]{1,0:T(1,128)S(1)} %reshape.74.kp_ref, bf16[128,2176]{1,0:T(8,128)(2,1)S(1)} %get-tuple-element.21.ka_ref, bf16[128,2176]{1,0:T(8,128)(2,1)S(1)} %get-tuple-element.22.kb_ref, ...), custom_call_target="tpu_custom_call" | custom-call | flops 1000 | bytes 1000 | tf_op jit(solution)/shard_map/pallas_call | solution.py:340
  110.2 0.4 shard_map.132
  110.6 20.5 %all_to_all.30.arrived_ref = bf16[16,48,128]{2,1,0:T(8,128)(2,1)S(1)} all-to-all(bf16[16,48,128]{2,1,0:T(8,128)(2,1)S(1)} %shard_map.132), channel_id=1, replica_groups={{0,32,64,96,128,160,192,224,256,288,320,352,384,416,448,480},{16,48,80,..., dimensions={0} | all-to-all | bytes 393216 | tf_op jit(solution)/shard_map/all_to_all | solution.py:344
  131.1 0.7 shard_map.133
  131.8 13.2 %all_to_all.31.arrived_ref = bf16[16,32,128]{2,1,0:T(8,128)(2,1)S(1)} all-to-all(bf16[16,32,128]{2,1,0:T(8,128)(2,1)S(1)} %shard_map.133), channel_id=1, replica_groups=mesh['seq'=32,'head'=16] {'head'}, dimensions={0} | all-to-all | bytes 262144 | tf_op jit(solution)/shard_map/all_to_all | solution.py:346
  145.0 11.1 %all_to_all.32.arrived_ref = bf16[16,32,128]{2,1,0:T(8,128)(2,1)S(1)} all-to-all(bf16[16,32,128]{2,1,0:T(8,128)(2,1)S(1)} %get-tuple-element.27), channel_id=1, replica_groups=mesh['seq'=32,'head'=16] {'head'}, dimensions={0} | all-to-all | bytes 262144 | tf_op jit(solution)/shard_map/all_to_all | solution.py:350
  156.1 0.7 shard_map.135
  156.8 11.1 %all_to_all.33.arrived_ref = bf16[16,32,128]{2,1,0:T(8,128)(2,1)S(1)} all-to-all(bf16[16,32,128]{2,1,0:T(8,128)(2,1)S(1)} %shard_map.135), channel_id=1, replica_groups=mesh['seq'=32,'head'=16] {'head'}, dimensions={0} | all-to-all | bytes 262144 | tf_op jit(solution)/shard_map/all_to_all | solution.py:354
  168.0 0.6 pad_maximum_fusion.1
  (42 shorter events, 0.6 us)
Async XLA Ops:
  0.0 12.3 %collective-permute-start = (bf16[64,2048]{1,0:T(8,128)(2,1)}, bf16[64,2048]{1,0:T(8,128)(2,1)S(1)}, u32[]{:S(2)}, u32[]{:S(2)}) collective-permute-start(bf16[64,2048]{1,0:T(8,128)(2,1)} %bitcast.29), channel_id=1, source_target_pairs={{0,1},{1,2},{2,3},{3,0},{4,5},{5,6},{6,7},{7,4},{8,9},{9,10},{10,1... | collective-permute-start | bytes 786440 | tf_op jit(solution)/shard_map/ppermute | solution.py:293
  3.4 8.9 %collective-permute-start.1 = (bf16[64,2048]{1,0:T(8,128)(2,1)}, bf16[64,2048]{1,0:T(8,128)(2,1)S(1)}, u32[]{:S(2)}, u32[]{:S(2)}) collective-permute-start(bf16[64,2048]{1,0:T(8,128)(2,1)} %bitcast.30), channel_id=1, source_target_pairs={{0,3},{1,0},{2,1},{3,2},{4,7},{5,4},{6,5},{7,6},{8,11},{9,8},{10,9... | collective-permute-start | bytes 786440 | tf_op jit(solution)/shard_map/ppermute | solution.py:293
  7.1 10.0 %collective-permute-start.2 = (bf16[64,2048]{1,0:T(8,128)(2,1)}, bf16[64,2048]{1,0:T(8,128)(2,1)S(1)}, u32[]{:S(2)}, u32[]{:S(2)}) collective-permute-start(bf16[64,2048]{1,0:T(8,128)(2,1)} %bitcast.31), channel_id=1, source_target_pairs={{0,2},{1,3},{2,0},{3,1},{4,6},{5,7},{6,4},{7,5},{8,10},{9,11},{10,... | collective-permute-start | bytes 786440 | tf_op jit(solution)/shard_map/ppermute | solution.py:293
  12.3 16.8 %copy-start.15 = (bf16[64,64]{1,0:T(8,128)(2,1)S(1)}, bf16[64,64]{1,0:T(8,128)(2,1)}, u32[]{:S(2)}) copy-start(bf16[64,64]{1,0:T(8,128)(2,1)} %param.14) | copy-start | bytes 24580
  12.3 38.8 %copy-start.4 = (bf16[1024,64]{0,1:T(8,128)(2,1)S(1)}, bf16[1024,64]{0,1:T(8,128)(2,1)}, u32[]{:S(2)}) copy-start(bf16[1024,64]{0,1:T(8,128)(2,1)} %param.19) | copy-start | bytes 393220
  12.3 38.8 %copy-start.6 = (bf16[1024,64]{0,1:T(8,128)(2,1)S(1)}, bf16[1024,64]{0,1:T(8,128)(2,1)}, u32[]{:S(2)}) copy-start(bf16[1024,64]{0,1:T(8,128)(2,1)} %param.20) | copy-start | bytes 393220
  12.3 38.8 %copy-start.13 = (f32[1024]{0:T(1024)S(1)}, f32[1024]{0:T(1024)}, u32[]{:S(2)}) copy-start(f32[1024]{0:T(1024)} %param.17) | copy-start | bytes 12292
  18.1 72.8 %collective-permute-start.3 = (bf16[256,2048]{1,0:T(8,128)(2,1)S(1)}, bf16[256,2048]{1,0:T(8,128)(2,1)S(1)}, u32[]{:S(2)}, u32[]{:S(2)}) collective-permute-start(bf16[256,2048]{1,0:T(8,128)(2,1)S(1)} %pad_maximum_fusion.refs_0_), channel_id=1, source_target_pairs={{0,4},{1,5},{2,6},{3,7},{4,8},{5,9},{6,10},{7,11},{8,12},{9,13},{1... | collective-permute-start | bytes 3145736 | tf_op jit(solution)/shard_map/ppermute | solution.py:298
  21.6 69.3 %collective-permute-start.4 = (bf16[256,2048]{1,0:T(8,128)(2,1)S(1)}, bf16[256,2048]{1,0:T(8,128)(2,1)S(1)}, u32[]{:S(2)}, u32[]{:S(2)}) collective-permute-start(bf16[256,2048]{1,0:T(8,128)(2,1)S(1)} %pad_maximum_fusion.refs_0_), channel_id=1, source_target_pairs={{0,12},{1,13},{2,14},{3,15},{4,0},{5,1},{6,2},{7,3},{8,4},{9,5},{1... | collective-permute-start | bytes 3145736 | tf_op jit(solution)/shard_map/ppermute | solution.py:298
  25.2 65.8 %collective-permute-start.5 = (bf16[256,2048]{1,0:T(8,128)(2,1)S(1)}, bf16[256,2048]{1,0:T(8,128)(2,1)}, u32[]{:S(2)}, u32[]{:S(2)}) collective-permute-start(bf16[256,2048]{1,0:T(8,128)(2,1)S(1)} %pad_maximum_fusion.refs_0_), channel_id=1, source_target_pairs={{0,8},{1,9},{2,10},{3,11},{4,12},{5,13},{6,14},{7,15},{8,0},{9,1},... | collective-permute-start | bytes 3145736 | tf_op jit(solution)/shard_map/ppermute | solution.py:298
  29.9 21.2 %all-to-all-start = ((bf16[16,32,128]{2,1,0:T(8,128)(2,1)}), bf16[16,32,128]{2,1,0:T(8,128)(2,1)S(1)}, u32[]{:S(2)}, u32[]{:S(2)}) async-start(bf16[16,32,128]{2,1,0:T(8,128)(2,1)} %broadcast_in_dim.4), calls=%async_computation | async-start | bytes 262144 | tf_op jit(solution)/shard_map/all_to_all | solution.py:302
  51.1 0.9 copy-start.10
  52.4 0.7 copy-start.9
  53.1 0.6 copy-start.11
  53.7 27.7 %all-to-all-start.1 = ((bf16[16,32,128]{2,1,0:T(8,128)(2,1)}), bf16[16,32,128]{2,1,0:T(8,128)(2,1)S(1)}, u32[]{:S(2)}, u32[]{:S(2)}) async-start(bf16[16,32,128]{2,1,0:T(8,128)(2,1)} %copy-done.9), calls=%async_computation.1 | async-start | bytes 262144 | tf_op jit(solution)/shard_map/all_to_all | solution.py:308
  81.4 14.5 %collective-permute-start.6 = (bf16[16,32,128]{2,1,0:T(8,128)(2,1)S(1)}, bf16[16,32,128]{2,1,0:T(8,128)(2,1)}, u32[]{:S(2)}, u32[]{:S(2)}) collective-permute-start(bf16[16,32,128]{2,1,0:T(8,128)(2,1)S(1)} %all-to-all-done.1), channel_id=1, source_target_pairs={{0,16},{16,0},{32,48},{48,32},{64,80},{80,64},{96,112},{112,96},{1... | collective-permute-start | bytes 393224 | tf_op jit(solution)/shard_map/ppermute | solution.py:309
  83.9 0.9 copy-start.5
  84.8 0.9 copy-start.7
  86.5 0.7 copy-start
  90.9 1.0 copy-start.1
  91.9 0.8 copy-start.12
  102.3 7.8 %collective-permute-start.7 = (bf16[16,48,128]{2,1,0:T(8,128)(2,1)S(1)}, bf16[16,48,128]{2,1,0:T(8,128)(2,1)S(1)}, u32[]{:S(2)}, u32[]{:S(2)}) collective-permute-start(bf16[16,48,128]{2,1,0:T(8,128)(2,1)S(1)} %shard_map.131), channel_id=1, source_target_pairs={{0,16},{16,0},{32,48},{48,32},{64,80},{80,64},{96,112},{112,96},{1... | collective-permute-start | bytes 589832 | tf_op jit(solution)/shard_map/ppermute | solution.py:339
  110.1 21.0 %copy-start.8 = (bf16[64,1024]{1,0:T(8,128)(2,1)S(1)}, bf16[64,1024]{1,0:T(8,128)(2,1)}, u32[]{:S(2)}) copy-start(bf16[64,1024]{1,0:T(8,128)(2,1)} %w_ref.1) | copy-start | bytes 393220
  110.1 45.9 %copy-start.2 = (bf16[1024,256]{1,0:T(8,128)(2,1)S(1)}, bf16[1024,256]{1,0:T(8,128)(2,1)}, u32[]{:S(2)}) copy-start(bf16[1024,256]{1,0:T(8,128)(2,1)} %up_ref.1) | copy-start | bytes 1572868
  110.2 45.9 %copy-start.3 = (bf16[256,1024]{1,0:T(8,128)(2,1)S(1)}, bf16[256,1024]{1,0:T(8,128)(2,1)}, u32[]{:S(2)}) copy-start(bf16[256,1024]{1,0:T(8,128)(2,1)} %down_ref.1) | copy-start | bytes 1572868
  110.2 45.9 %copy-start.14 = (f32[1024]{0:T(1024)S(1)}, f32[1024]{0:T(1024)}, u32[]{:S(2)}) copy-start(f32[1024]{0:T(1024)} %param.22) | copy-start | bytes 12292

commit v4 on v3

--- a/solution.py
+++ b/solution.py
@@ -74,8 +74,37 @@
 def weights_kernel(order_ref, wk_ref, wv_ref, gain_ref, out_ref, scratch):
     both = jnp.concatenate([wk_ref[...], wv_ref[...]], axis=0).astype(F32) * gain_ref[...]
     scratch[...] = both.T.reshape(scratch.shape)
-    for b in range(scratch.shape[0]):
-        out_ref[b] = scratch[order_ref[b]].astype(BF16)
+    for i in range(out_ref.shape[0]):
+        line = jnp.concatenate([scratch[order_ref[4 * i + j]] for j in range(4)], axis=0)
+        out_ref[i] = line.T.astype(BF16)
+
+
+def latents_kernel(lat_ref, out_ref):
+    half = lat_ref.shape[0] // 2
+    packed = jnp.concatenate([lat_ref[:half, :], lat_ref[half:, :]], axis=1)
+    out_ref[...] = jnp.broadcast_to(packed[None], out_ref.shape)
+
+
+def positions_kernel(place_ref, ctx_ref, lat_ref, kp_ref, pos_ref):
+    plane, core = place_ref[0], place_ref[1]
+    for i in range(ctx_ref.shape[0]):
+        kp_ref[:, 128 * i : 128 * i + 128] = ctx_ref[i : i + 1, :]
+    own = lat_ref[pl.ds(plane, 1), :]
+    own = jnp.where(core == 0, own, pltpu.roll(own, 64, 1))
+    last = 128 * ctx_ref.shape[0]
+    kp_ref[:, last : last + 128] = jnp.where(low_half(own.shape), own, jnp.iinfo(jnp.int32).max)
+    planes = lat_ref.shape[0]
+    lat = lat_ref[...]
+    swapped = pltpu.roll(lat, 64, 1)
+    mine = jnp.where(core == 0, lat, swapped)
+    theirs = jnp.where(core == 0, swapped, lat)
+    wide = jnp.concatenate([theirs, mine, jnp.zeros((128 - 2 * planes, 128), jnp.int32)], axis=0)
+    columns = wide.T
+    for k in range(4):
+        part = columns[32 * (k % 2) : 32 * (k % 2) + 32]
+        for z in range(planes):
+            lane = (k // 2) * planes + z
+            pos_ref[k, 32 * z : 32 * z + 32] = jnp.broadcast_to(part[:, lane : lane + 1], (32, 128))
 
 
 def queries_kernel(lat_ref, wq_ref, wk_ref, wv_ref, gain_ref, q_ref, kv_ref):
@@ -89,22 +118,33 @@
 
 
 def keys_kernel(*refs):
-    *line_refs, w_ref, lat_ref, ka_ref, kb_ref, va_ref, vb_ref = refs
+    *line_refs, w_ref, lat_ref, ka_ref, kb_ref, va_ref, vb_ref, held, sems = refs
     tokens = line_refs[0].shape[1]
-    width = 256
+    width = 512
+    copies = []
+    for c in range(tokens // width):
+        cols = slice(c * width, c * width + width)
+        copies.append(
+            [
+                pltpu.make_async_copy(line.at[:, cols], held.at[i, :, cols], sems.at[c, i])
+                for i, line in enumerate(line_refs)
+            ]
+        )
+        for copy in copies[c]:
+            copy.start()
+    put_keys(lat_ref[...], slice(tokens, tokens + 128), ka_ref, kb_ref, va_ref, vb_ref)
     for c in range(tokens // width):
         cols = slice(c * width, c * width + width)
         total = jnp.zeros((128, width), F32)
         squares = jnp.zeros((1, width), F32)
-        for i, line in enumerate(line_refs):
-            piece = line[:, cols]
-            w = w_ref[4 * i : 4 * i + 4].reshape(-1, 128)
-            total = total + dot(w, piece, TN)
+        for i in range(len(line_refs)):
+            copies[c][i].wait()
+            piece = held[i, :, cols]
+            total = total + dot(w_ref[i], piece, NN)
             wide = piece.astype(F32)
             squares = squares + jnp.sum(wide * wide, axis=0, keepdims=True)
         inverse = lax.rsqrt(squares * (1.0 / 1024) + EPSILON)
         put_keys((total * inverse).astype(BF16), cols, ka_ref, kb_ref, va_ref, vb_ref)
-    put_keys(lat_ref[...], slice(tokens, tokens + 128), ka_ref, kb_ref, va_ref, vb_ref)
 
 
 def put_keys(both, cols, ka_ref, kb_ref, va_ref, vb_ref):
@@ -167,27 +207,39 @@
 def other_kernel(q_ref, pos_ref, kp_ref, ka_ref, kb_ref, va_ref, vb_ref, out_ref):
     kp = kp_ref[...]
 
-    @pl.loop(0, q_ref.shape[0] // 128)
+    @pl.loop(0, q_ref.shape[0] // 256)
     def _(i):
-        rows = pl.ds(pl.multiple_of(i * 128, 128), 128)
-        pos = pos_ref[rows, :]
+        rows = pl.ds(pl.multiple_of(i * 256, 256), 256)
         mixed, level = attend_rows(
-            q_ref[rows, :], pos[:, 0:1], pos[:, 1:2], kp, ka_ref, kb_ref, va_ref, vb_ref
+            q_ref[rows, :],
+            pos_ref[0, rows, 0:1],
+            pos_ref[1, rows, 0:1],
+            kp,
+            ka_ref,
+            kb_ref,
+            va_ref,
+            vb_ref,
         )
-        for g in range(4):
+        for g in range(8):
             part = slice(32 * g, 32 * g + 32)
-            put_message(mixed[part], level[part], out_ref, i * 4 + g)
+            put_message(mixed[part], level[part], out_ref, i * 8 + g)
 
 
 def own_kernel(q_ref, pos_ref, kp_ref, ka_ref, kb_ref, va_ref, vb_ref, mix_ref, lev_ref):
     kp = kp_ref[...]
 
-    @pl.loop(0, q_ref.shape[0] // 128)
+    @pl.loop(0, q_ref.shape[0] // 256)
     def _(i):
-        rows = pl.ds(pl.multiple_of(i * 128, 128), 128)
-        pos = pos_ref[rows, :]
+        rows = pl.ds(pl.multiple_of(i * 256, 256), 256)
         mixed, level = attend_rows(
-            q_ref[rows, :], pos[:, 2:3], pos[:, 3:4], kp, ka_ref, kb_ref, va_ref, vb_ref
+            q_ref[rows, :],
+            pos_ref[2, rows, 0:1],
+            pos_ref[3, rows, 0:1],
+            kp,
+            ka_ref,
+            kb_ref,
+            va_ref,
+            vb_ref,
         )
         mix_ref[rows, :] = mixed
         lev_ref[rows, :] = level
@@ -222,7 +274,9 @@
 
 
 def add_kernel(arrived_ref, lat_ref, own_ref, out_ref):
-    own = jnp.sum(arrived_ref[...].astype(F32), axis=0) + lat_ref[...].astype(F32)
+    half = lat_ref.shape[0] // 2
+    packed = jnp.concatenate([lat_ref[:half, :], lat_ref[half:, :]], axis=1)
+    own = jnp.sum(arrived_ref[...].astype(F32), axis=0) + packed.astype(F32)
     own_ref[...] = own
     out_ref[...] = jnp.broadcast_to(own.astype(BF16)[None], out_ref.shape)
 
@@ -236,7 +290,9 @@
 
 
 def last_kernel(arrived_ref, own_ref, out_ref):
-    out_ref[...] = (jnp.sum(arrived_ref[...].astype(F32), axis=0) + own_ref[...]).astype(BF16)
+    packed = jnp.sum(arrived_ref[...].astype(F32), axis=0) + own_ref[...]
+    cols = packed.shape[1] // 2
+    out_ref[...] = jnp.concatenate([packed[:, :cols], packed[:, cols:]], axis=0).astype(BF16)
 
 
 def call(kernel, outs, cost=1000, **kwargs):
@@ -293,15 +349,13 @@
         + [lax.ppermute(own, BOTH, line_shift(seq_size, side, 0, k)) for k in SHIFTS[1:]],
         axis=0,
     )
-    line, latents = lax.optimization_barrier((line, latents))
+    copies = call(latents_kernel, [((head_size, *block), BF16)])(latents)
+    lat_blocks = lax.all_to_all(copies, "head", 0, 0)
+    line, lat_blocks = lax.optimization_barrier((line, lat_blocks))
     lines = [line] + [
         lax.ppermute(line, BOTH, line_shift(seq_size, side, 1, k)) for k in SHIFTS[1:]
     ]
 
-    packed_latents = jnp.concatenate([latents[:half], latents[half:]], axis=1)
-    lat_blocks = lax.all_to_all(
-        jnp.broadcast_to(packed_latents[None], (head_size, *block)), "head", 0, 0
-    )
     queries, latent_kv = call(
         queries_kernel, [((planes, *block), BF16), ((2 * cols, 2 * lat_rows), BF16)]
     )(lat_blocks, wq_t, wk_t, wv_t, row_gain)
@@ -310,7 +364,7 @@
 
     key_weights = call(
         weights_kernel,
-        [((head_size, cols, 2 * cols), BF16)],
+        [((side, 2 * cols, side * cols), BF16)],
         in_specs=[pl.BlockSpec(memory_space=pltpu.SMEM)]
         + [pl.BlockSpec(memory_space=pltpu.VMEM)] * 3,
         scratch_shapes=[pltpu.VMEM((head_size, cols, 2 * cols), F32)],
@@ -320,18 +374,26 @@
         keys_kernel,
         [((128, key_count), BF16)] * 2 + [((key_count, 128), BF16)] * 2,
         cost=10**9,
+        in_specs=[pl.BlockSpec(memory_space=pl.ANY)] * side
+        + [pl.BlockSpec(memory_space=pltpu.VMEM)] * 2,
+        scratch_shapes=[
+            pltpu.VMEM((side, side * cols, tokens), BF16),
+            pltpu.SemaphoreType.DMA((4, side)),
+        ],
     )(*lines, key_weights, latent_kv)
 
-    own_pos = lax.dynamic_slice_in_dim(lat_pos, seq_place * lat_rows, lat_rows)
-    never = jnp.full((lat_rows,), jnp.iinfo(jnp.int32).max, jnp.int32)
-    key_pos = jnp.concatenate([ctx_pos, own_pos, never]).reshape(1, -1)
-    by_core = lat_pos.reshape(planes, 2, 2, half)
-    mine = lax.dynamic_index_in_dim(by_core, core, 1, keepdims=False)
-    theirs = lax.dynamic_index_in_dim(by_core, 1 - core, 1, keepdims=False)
-    query_pos = jnp.stack([theirs[:, 0], theirs[:, 1], mine[:, 0], mine[:, 1]], axis=-1)
-    query_pos = query_pos.reshape(-1, 4)
-
     rows = planes * half
+    key_pos, query_pos = call(
+        positions_kernel,
+        [((1, key_count), jnp.int32), ((4, rows, 2 * cols), jnp.int32)],
+        in_specs=[pl.BlockSpec(memory_space=pltpu.SMEM)]
+        + [pl.BlockSpec(memory_space=pltpu.VMEM)] * 2,
+    )(
+        jnp.stack([seq_place // 2, core]),
+        ctx_pos.reshape(-1, 128),
+        lat_pos.reshape(-1, 2 * lat_rows),
+    )
+
     message = (planes, 48, 2 * cols)
     to_sibling = call(other_kernel, [(message, BF16)])(
         other_queries.reshape(rows, -1), query_pos, key_pos, *operands
@@ -345,15 +407,14 @@
     shares = call(project_kernel, [((head_size, *block), BF16)])(arrived, w_out)
     arrived = lax.all_to_all(shares, "head", 0, 0)
     own_proj, copies = call(add_kernel, [(block, F32), ((head_size, *block), BF16)])(
-        arrived, packed_latents
+        arrived, latents
     )
     arrived = lax.all_to_all(copies, "head", 0, 0)
     shares = call(mlp_kernel, [((head_size, *block), BF16)])(
         arrived, mlp_gain.reshape(1, -1), w_up, w_down
     )
     arrived = lax.all_to_all(shares, "head", 0, 0)
-    packed = call(last_kernel, [(block, BF16)])(arrived, own_proj)
-    return jnp.concatenate([packed[:, :cols], packed[:, cols:]], axis=0)
+    return call(last_kernel, [((lat_rows, cols), BF16)])(arrived, own_proj)
 
 
 def solution(mesh):

time: 170 us -> 145 us (0.85)
  waiting for transfers between devices: 30.5 us -> 17.7 us
  local copies, waits for them, and re-layouts: 14.1 us -> 5.12 us
  other arithmetic: 4.3 us -> 1.9 us
    all_to_all x1, waiting for transfers between devices: 15.8 us -> 6.73 us  [body(): lat_blocks = lax.all_to_all(copies, 'head', 0, 0)]
    ppermute x3, waiting for transfers between devices: 4.74 us -> 0.01 us  [body(): lax.ppermute(own, BOTH, line_shift(seq_size, side, 0, k))]
    pallas_call x2 -> x4, Pallas kernels: 0.79 us -> 3.4 us  [the longest x1 1.08 us: body(): call(positions_kernel, [((1, key_count), jnp.int32), ((4, rows, 2 * cols)...]
    unnamed x32, local copies, waits for them, and re-layouts: 6.38 us -> 4.36 us
    ppermute x3, starting transfers between devices: 10.9 us -> 8.96 us  [body(): lax.ppermute(line, BOTH, line_shift(seq_size, side, 1, k))]
    pallas_call x1, Pallas kernels: 6.36 us -> 4.41 us  [body(): call(other_kernel, [(message, BF16)])]
  transfers between devices with their start and end apart: 10 -> 10, of which waited for: 3 -> 2; matrix products, arithmetic and copies ran while one was open for 6% -> 2% of each run, Pallas kernels for 6% -> 7%
where the time goes in v4:
time: 145 us; the launch traced here: 144 us
  blocking collectives  56.1 us (39%)
  starting transfers between devices  45 us (31%)
  Pallas kernels  17.7 us (12%)
  waiting for transfers between devices  17.7 us (12%)
  local copies, waits for them, and re-layouts  5.12 us (4%)
  other arithmetic  1.9 us (1%)
    all_to_all x2, blocking collectives, body(): arrived = lax.all_to_all(shares, 'head', 0, 0)  24.4 us
    all_to_all x1, blocking collectives, body(): arrived = lax.all_to_all(joined, 'seq', 0, 0, axis_index_groups=along_z)  20.6 us
    all_to_all x1, starting transfers between devices, body(): lax.all_to_all(queries, 'seq', 0, 0, axis_index_groups=along_z)  15.2 us
    all_to_all x1, blocking collectives, body(): arrived = lax.all_to_all(copies, 'head', 0, 0)  11.1 us
    all_to_all x1, waiting for transfers between devices, body(): lax.all_to_all(queries, 'seq', 0, 0, axis_index_groups=along_z)  10.9 us
    ppermute x3, starting transfers between devices, body(): lax.ppermute(own, BOTH, line_shift(seq_size, side, 0, k))  10.8 us
    ppermute x3, starting transfers between devices, body(): lax.ppermute(line, BOTH, line_shift(seq_size, side, 1, k))  8.96 us
    all_to_all x1, waiting for transfers between devices, body(): lat_blocks = lax.all_to_all(copies, 'head', 0, 0)  6.73 us
  transfers between devices with their start and end apart: 10, of which 2 were waited for; matrix products, arithmetic and copies ran while one was open for 2% of the time, Pallas kernels for 7%

profile of v4, /device:TPU:32, one launch (start us, length us, event | category | flops | bytes accessed | tf_op | source)
XLA Modules:
  0.0 143.8 jit_solution(13597822553199144439)
XLA Ops:
  0.0 3.4 %collective-permute-start = (bf16[64,2048]{1,0:T(8,128)(2,1)}, bf16[64,2048]{1,0:T(8,128)(2,1)S(1)}, u32[]{:S(2)}, u32[]{:S(2)}) collective-permute-start(bf16[64,2048]{1,0:T(8,128)(2,1)} %bitcast.24), channel_id=1, source_target_pairs={{0,1},{1,2},{2,3},{3,0},{4,5},{5,6},{6,7},{7,4},{8,9},{9,10},{10,1... | collective-permute-start | bytes 786440 | tf_op jit(solution)/shard_map/ppermute | solution.py:349
  3.4 3.7 %collective-permute-start.1 = (bf16[64,2048]{1,0:T(8,128)(2,1)}, bf16[64,2048]{1,0:T(8,128)(2,1)S(1)}, u32[]{:S(2)}, u32[]{:S(2)}) collective-permute-start(bf16[64,2048]{1,0:T(8,128)(2,1)} %bitcast.25), channel_id=1, source_target_pairs={{0,3},{1,0},{2,1},{3,2},{4,7},{5,4},{6,5},{7,6},{8,11},{9,8},{10,9... | collective-permute-start | bytes 786440 | tf_op jit(solution)/shard_map/ppermute | solution.py:349
  7.1 3.7 %collective-permute-start.2 = (bf16[64,2048]{1,0:T(8,128)(2,1)}, bf16[64,2048]{1,0:T(8,128)(2,1)S(1)}, u32[]{:S(2)}, u32[]{:S(2)}) collective-permute-start(bf16[64,2048]{1,0:T(8,128)(2,1)} %bitcast.26), channel_id=1, source_target_pairs={{0,2},{1,3},{2,0},{3,1},{4,6},{5,7},{6,4},{7,5},{8,10},{9,11},{10,... | collective-permute-start | bytes 786440 | tf_op jit(solution)/shard_map/ppermute | solution.py:349
  10.8 0.0 copy-start.7
  10.8 0.7 copy-done.7
  11.5 0.7 shard_map.127
  12.3 5.7 %all-to-all-start = ((bf16[16,32,128]{2,1,0:T(8,128)(2,1)}), bf16[16,32,128]{2,1,0:T(8,128)(2,1)S(1)}, u32[]{:S(2)}, u32[]{:S(2)}) async-start(bf16[16,32,128]{2,1,0:T(8,128)(2,1)} %shard_map.127), calls=%async_computation | async-start | bytes 262144 | tf_op jit(solution)/shard_map/all_to_all | solution.py:353
  18.0 0.0 copy-start.2
  18.0 0.0 copy-start.3
  18.0 0.0 copy-start.11
  18.0 0.0 copy-start.15
  18.1 0.0 copy-start.12
  18.1 1.2 pad_maximum_fusion.refs_0_
  19.2 6.7 %all-to-all-done.lat_ref = bf16[16,32,128]{2,1,0:T(8,128)(2,1)S(1)} async-done(((bf16[16,32,128]{2,1,0:T(8,128)(2,1)}), bf16[16,32,128]{2,1,0:T(8,128)(2,1)S(1)}, u32[]{:S(2)}, u32[]{:S(2)}) %all-to-all-start) | async-done | bytes 131104 | tf_op jit(solution)/shard_map/all_to_all | solution.py:353
  26.0 2.2 %collective-permute-start.3 = (bf16[256,2048]{1,0:T(8,128)(2,1)S(1)}, bf16[256,2048]{1,0:T(8,128)(2,1)S(1)}, u32[]{:S(2)}, u32[]{:S(2)}) collective-permute-start(bf16[256,2048]{1,0:T(8,128)(2,1)S(1)} %pad_maximum_fusion.refs_0_), channel_id=1, source_target_pairs={{0,4},{1,5},{2,6},{3,7},{4,8},{5,9},{6,10},{7,11},{8,12},{9,13},{1... | collective-permute-start | bytes 3145736 | tf_op jit(solution)/shard_map/ppermute | solution.py:356
  28.2 4.8 %collective-permute-start.4 = (bf16[256,2048]{1,0:T(8,128)(2,1)S(1)}, bf16[256,2048]{1,0:T(8,128)(2,1)S(1)}, u32[]{:S(2)}, u32[]{:S(2)}) collective-permute-start(bf16[256,2048]{1,0:T(8,128)(2,1)S(1)} %pad_maximum_fusion.refs_0_), channel_id=1, source_target_pairs={{0,12},{1,13},{2,14},{3,15},{4,0},{5,1},{6,2},{7,3},{8,4},{9,5},{1... | collective-permute-start | bytes 3145736 | tf_op jit(solution)/shard_map/ppermute | solution.py:356
  33.0 1.9 %collective-permute-start.5 = (bf16[256,2048]{1,0:T(8,128)(2,1)S(1)}, bf16[256,2048]{1,0:T(8,128)(2,1)}, u32[]{:S(2)}, u32[]{:S(2)}) collective-permute-start(bf16[256,2048]{1,0:T(8,128)(2,1)S(1)} %pad_maximum_fusion.refs_0_), channel_id=1, source_target_pairs={{0,8},{1,9},{2,10},{3,11},{4,12},{5,13},{6,14},{7,15},{8,0},{9,1},... | collective-permute-start | bytes 3145736 | tf_op jit(solution)/shard_map/ppermute | solution.py:356
  35.0 0.9 copy-done.6
  35.9 0.4 shard_map.128
  36.3 0.6 copy-done.5
  37.0 0.6 copy-done.9
  37.6 15.2 %all-to-all-start.1 = ((bf16[16,32,128]{2,1,0:T(8,128)(2,1)}), bf16[16,32,128]{2,1,0:T(8,128)(2,1)S(1)}, u32[]{:S(2)}, u32[]{:S(2)}) async-start(bf16[16,32,128]{2,1,0:T(8,128)(2,1)} %copy-done.5), calls=%async_computation.1 | async-start | bytes 262144 | tf_op jit(solution)/shard_map/all_to_all | solution.py:362
  52.8 0.7 add_select_fusion
  53.5 0.8 select_n.58.order_ref
  54.2 10.9 %all-to-all-done.1 = bf16[16,32,128]{2,1,0:T(8,128)(2,1)S(1)} async-done(((bf16[16,32,128]{2,1,0:T(8,128)(2,1)}), bf16[16,32,128]{2,1,0:T(8,128)(2,1)S(1)}, u32[]{:S(2)}, u32[]{:S(2)}) %all-to-all-start.1) | async-done | bytes 131104 | tf_op jit(solution)/shard_map/all_to_all | solution.py:362
  65.2 1.9 %collective-permute-start.6 = (bf16[16,32,128]{2,1,0:T(8,128)(2,1)S(1)}, bf16[16,32,128]{2,1,0:T(8,128)(2,1)S(1)}, u32[]{:S(2)}, u32[]{:S(2)}) collective-permute-start(bf16[16,32,128]{2,1,0:T(8,128)(2,1)S(1)} %all-to-all-done.1), channel_id=1, source_target_pairs={{0,16},{16,0},{32,48},{48,32},{64,80},{80,64},{96,112},{112,96},{1... | collective-permute-start | bytes 393224 | tf_op jit(solution)/shard_map/ppermute | solution.py:363
  67.1 0.1 pad_add_fusion.place_ref
  67.2 0.9 shard_map.130.refs_4_
  68.1 0.0 copy-start.13
  68.1 0.7 copy-done.13
  68.8 1.1 shard_map.129
  69.9 0.7 copy-done.10
  70.7 3.1 %shard_map.131 = (bf16[128,2176]{1,0:T(8,128)(2,1)S(1)}, bf16[128,2176]{1,0:T(8,128)(2,1)S(1)}, bf16[2176,128]{1,0:T(8,128)(2,1)S(1)}, bf16[2176,128]{1,0:T(8,128)(2,1)S(1)}) custom-call(bf16[256,2048]{1,0:T(8,128)(2,1)S(1)} %pad_maximum_fusion.refs_0_, bf16[256,2048]{1,0:T(8,128)(2,1)S(1)} %collective-permute-done.3.refs_1_, ...), custom_call_target="tpu_custom_call" | custom-call | flops 1000000000 | bytes 1000000000 | tf_op jit(solution)/shard_map/pallas_call | solution.py:373
  73.8 4.4 %shard_map.133 = bf16[16,48,128]{2,1,0:T(8,128)(2,1)S(1)} custom-call(bf16[512,128]{1,0:T(8,128)(2,1)S(1)} %bitcast.17, s32[4,512,128]{2,1,0:T(8,128)S(1)} %get-tuple-element.21.pos_ref, s32[1,2176]{1,0:T(1,128)S(1)} %get-tuple-element.22.kp_ref, bf16[128,2176]{1,0:T(8,128)(2,1)S(1)} %get-tuple-element.25.ka_ref, ...), custom_call_target="tpu_custom_call" | custom-call | flops 1000 | bytes 1000 | tf_op jit(solution)/shard_map/pallas_call | solution.py:398
  78.2 2.4 %collective-permute-start.7 = (bf16[16,48,128]{2,1,0:T(8,128)(2,1)S(1)}, bf16[16,48,128]{2,1,0:T(8,128)(2,1)S(1)}, u32[]{:S(2)}, u32[]{:S(2)}) collective-permute-start(bf16[16,48,128]{2,1,0:T(8,128)(2,1)S(1)} %shard_map.133), channel_id=1, source_target_pairs={{0,16},{16,0},{32,48},{48,32},{64,80},{80,64},{96,112},{112,96},{1... | collective-permute-start | bytes 589832 | tf_op jit(solution)/shard_map/ppermute | solution.py:401
  80.6 4.4 %shard_map.132 = (f32[512,128]{1,0:T(8,128)S(1)}, f32[512,128]{1,0:T(8,128)S(1)}) custom-call(bf16[512,128]{1,0:T(8,128)(2,1)S(1)} %bitcast.12, s32[4,512,128]{2,1,0:T(8,128)S(1)} %get-tuple-element.21.pos_ref, s32[1,2176]{1,0:T(1,128)S(1)} %get-tuple-element.22.kp_ref, bf16[128,2176]{1,0:T(8,128)(2,1)S(1)} %get-tuple-element.25.ka_ref, ...), custom_call_target="tpu_custom_call" | custom-call | flops 1000 | bytes 1000 | tf_op jit(solution)/shard_map/pallas_call | solution.py:402
  85.0 0.0 copy-start.8
  85.1 0.0 copy-start.1
  85.1 0.0 copy-start.14
  85.1 0.4 shard_map.134
  85.5 20.6 %all_to_all.30.arrived_ref = bf16[16,48,128]{2,1,0:T(8,128)(2,1)S(1)} all-to-all(bf16[16,48,128]{2,1,0:T(8,128)(2,1)S(1)} %shard_map.134), channel_id=1, replica_groups={{0,32,64,96,128,160,192,224,256,288,320,352,384,416,448,480},{16,48,80,..., dimensions={0} | all-to-all | bytes 393216 | tf_op jit(solution)/shard_map/all_to_all | solution.py:406
  106.2 0.7 shard_map.135
  106.8 13.3 %all_to_all.31.arrived_ref = bf16[16,32,128]{2,1,0:T(8,128)(2,1)S(1)} all-to-all(bf16[16,32,128]{2,1,0:T(8,128)(2,1)S(1)} %shard_map.135), channel_id=1, replica_groups=mesh['seq'=32,'head'=16] {'head'}, dimensions={0} | all-to-all | bytes 262144 | tf_op jit(solution)/shard_map/all_to_all | solution.py:408
  120.1 0.1 shard_map.136
  120.2 11.1 %all_to_all.32.arrived_ref = bf16[16,32,128]{2,1,0:T(8,128)(2,1)S(1)} all-to-all(bf16[16,32,128]{2,1,0:T(8,128)(2,1)S(1)} %get-tuple-element.31), channel_id=1, replica_groups=mesh['seq'=32,'head'=16] {'head'}, dimensions={0} | all-to-all | bytes 262144 | tf_op jit(solution)/shard_map/all_to_all | solution.py:412
  131.3 0.7 shard_map.137
  132.0 11.1 %all_to_all.33.arrived_ref = bf16[16,32,128]{2,1,0:T(8,128)(2,1)S(1)} all-to-all(bf16[16,32,128]{2,1,0:T(8,128)(2,1)S(1)} %shard_map.137), channel_id=1, replica_groups=mesh['seq'=32,'head'=16] {'head'}, dimensions={0} | all-to-all | bytes 262144 | tf_op jit(solution)/shard_map/all_to_all | solution.py:416
  143.1 0.7 shard_map.138
  (25 shorter events, 0.1 us)
Async XLA Ops:
  0.0 18.0 %collective-permute-start = (bf16[64,2048]{1,0:T(8,128)(2,1)}, bf16[64,2048]{1,0:T(8,128)(2,1)S(1)}, u32[]{:S(2)}, u32[]{:S(2)}) collective-permute-start(bf16[64,2048]{1,0:T(8,128)(2,1)} %bitcast.24), channel_id=1, source_target_pairs={{0,1},{1,2},{2,3},{3,0},{4,5},{5,6},{6,7},{7,4},{8,9},{9,10},{10,1... | collective-permute-start | bytes 786440 | tf_op jit(solution)/shard_map/ppermute | solution.py:349
  3.4 14.7 %collective-permute-start.1 = (bf16[64,2048]{1,0:T(8,128)(2,1)}, bf16[64,2048]{1,0:T(8,128)(2,1)S(1)}, u32[]{:S(2)}, u32[]{:S(2)}) collective-permute-start(bf16[64,2048]{1,0:T(8,128)(2,1)} %bitcast.25), channel_id=1, source_target_pairs={{0,3},{1,0},{2,1},{3,2},{4,7},{5,4},{6,5},{7,6},{8,11},{9,8},{10,9... | collective-permute-start | bytes 786440 | tf_op jit(solution)/shard_map/ppermute | solution.py:349
  7.1 11.0 %collective-permute-start.2 = (bf16[64,2048]{1,0:T(8,128)(2,1)}, bf16[64,2048]{1,0:T(8,128)(2,1)S(1)}, u32[]{:S(2)}, u32[]{:S(2)}) collective-permute-start(bf16[64,2048]{1,0:T(8,128)(2,1)} %bitcast.26), channel_id=1, source_target_pairs={{0,2},{1,3},{2,0},{3,1},{4,6},{5,7},{6,4},{7,5},{8,10},{9,11},{10,... | collective-permute-start | bytes 786440 | tf_op jit(solution)/shard_map/ppermute | solution.py:349
  10.8 0.7 copy-start.7
  12.3 13.7 %all-to-all-start = ((bf16[16,32,128]{2,1,0:T(8,128)(2,1)}), bf16[16,32,128]{2,1,0:T(8,128)(2,1)S(1)}, u32[]{:S(2)}, u32[]{:S(2)}) async-start(bf16[16,32,128]{2,1,0:T(8,128)(2,1)} %shard_map.127), calls=%async_computation | async-start | bytes 262144 | tf_op jit(solution)/shard_map/all_to_all | solution.py:353
  18.0 17.0 %copy-start.2 = (bf16[1024,64]{0,1:T(8,128)(2,1)S(1)}, bf16[1024,64]{0,1:T(8,128)(2,1)}, u32[]{:S(2)}) copy-start(bf16[1024,64]{0,1:T(8,128)(2,1)} %param.19) | copy-start | bytes 393220
  18.0 17.0 %copy-start.3 = (bf16[1024,64]{0,1:T(8,128)(2,1)S(1)}, bf16[1024,64]{0,1:T(8,128)(2,1)}, u32[]{:S(2)}) copy-start(bf16[1024,64]{0,1:T(8,128)(2,1)} %param.20) | copy-start | bytes 393220
  18.0 17.0 %copy-start.11 = (f32[1024]{0:T(1024)S(1)}, f32[1024]{0:T(1024)}, u32[]{:S(2)}) copy-start(f32[1024]{0:T(1024)} %param.17) | copy-start | bytes 12292
  18.0 34.8 %copy-start.15 = (s32[4]{0:T(128)S(1)}, s32[4]{0:T(128)}, u32[]{:S(2)}) copy-start(s32[4]{0:T(128)} %constant.79) | copy-start | bytes 52
  18.1 50.0 %copy-start.12 = (s32[2048]{0:T(1024)S(1)}, s32[2048]{0:T(1024)}, u32[]{:S(2)}) copy-start(s32[2048]{0:T(1024)} %param.15) | copy-start | bytes 24580
  26.0 43.9 %collective-permute-start.3 = (bf16[256,2048]{1,0:T(8,128)(2,1)S(1)}, bf16[256,2048]{1,0:T(8,128)(2,1)S(1)}, u32[]{:S(2)}, u32[]{:S(2)}) collective-permute-start(bf16[256,2048]{1,0:T(8,128)(2,1)S(1)} %pad_maximum_fusion.refs_0_), channel_id=1, source_target_pairs={{0,4},{1,5},{2,6},{3,7},{4,8},{5,9},{6,10},{7,11},{8,12},{9,13},{1... | collective-permute-start | bytes 3145736 | tf_op jit(solution)/shard_map/ppermute | solution.py:356
  28.2 41.7 %collective-permute-start.4 = (bf16[256,2048]{1,0:T(8,128)(2,1)S(1)}, bf16[256,2048]{1,0:T(8,128)(2,1)S(1)}, u32[]{:S(2)}, u32[]{:S(2)}) collective-permute-start(bf16[256,2048]{1,0:T(8,128)(2,1)S(1)} %pad_maximum_fusion.refs_0_), channel_id=1, source_target_pairs={{0,12},{1,13},{2,14},{3,15},{4,0},{5,1},{6,2},{7,3},{8,4},{9,5},{1... | collective-permute-start | bytes 3145736 | tf_op jit(solution)/shard_map/ppermute | solution.py:356
  33.0 36.9 %collective-permute-start.5 = (bf16[256,2048]{1,0:T(8,128)(2,1)S(1)}, bf16[256,2048]{1,0:T(8,128)(2,1)}, u32[]{:S(2)}, u32[]{:S(2)}) collective-permute-start(bf16[256,2048]{1,0:T(8,128)(2,1)S(1)} %pad_maximum_fusion.refs_0_), channel_id=1, source_target_pairs={{0,8},{1,9},{2,10},{3,11},{4,12},{5,13},{6,14},{7,15},{8,0},{9,1},... | collective-permute-start | bytes 3145736 | tf_op jit(solution)/shard_map/ppermute | solution.py:356
  35.0 0.9 copy-start.6
  36.3 0.7 copy-start.5
  37.0 0.6 copy-start.9
  37.6 27.6 %all-to-all-start.1 = ((bf16[16,32,128]{2,1,0:T(8,128)(2,1)}), bf16[16,32,128]{2,1,0:T(8,128)(2,1)S(1)}, u32[]{:S(2)}, u32[]{:S(2)}) async-start(bf16[16,32,128]{2,1,0:T(8,128)(2,1)} %copy-done.5), calls=%async_computation.1 | async-start | bytes 262144 | tf_op jit(solution)/shard_map/all_to_all | solution.py:362
  65.2 8.6 %collective-permute-start.6 = (bf16[16,32,128]{2,1,0:T(8,128)(2,1)S(1)}, bf16[16,32,128]{2,1,0:T(8,128)(2,1)S(1)}, u32[]{:S(2)}, u32[]{:S(2)}) collective-permute-start(bf16[16,32,128]{2,1,0:T(8,128)(2,1)S(1)} %all-to-all-done.1), channel_id=1, source_target_pairs={{0,16},{16,0},{32,48},{48,32},{64,80},{80,64},{96,112},{112,96},{1... | collective-permute-start | bytes 393224 | tf_op jit(solution)/shard_map/ppermute | solution.py:363
  68.1 0.7 copy-start.13
  69.9 0.8 copy-start.10
  78.2 6.8 %collective-permute-start.7 = (bf16[16,48,128]{2,1,0:T(8,128)(2,1)S(1)}, bf16[16,48,128]{2,1,0:T(8,128)(2,1)S(1)}, u32[]{:S(2)}, u32[]{:S(2)}) collective-permute-start(bf16[16,48,128]{2,1,0:T(8,128)(2,1)S(1)} %shard_map.133), channel_id=1, source_target_pairs={{0,16},{16,0},{32,48},{48,32},{64,80},{80,64},{96,112},{112,96},{1... | collective-permute-start | bytes 589832 | tf_op jit(solution)/shard_map/ppermute | solution.py:401
  85.0 21.1 %copy-start.4 = (bf16[64,1024]{1,0:T(8,128)(2,1)S(1)}, bf16[64,1024]{1,0:T(8,128)(2,1)}, u32[]{:S(2)}) copy-start(bf16[64,1024]{1,0:T(8,128)(2,1)} %w_ref.1) | copy-start | bytes 393220
  85.0 35.1 %copy-start.8 = (bf16[64,64]{1,0:T(8,128)(2,1)S(1)}, bf16[64,64]{1,0:T(8,128)(2,1)}, u32[]{:S(2)}) copy-start(bf16[64,64]{1,0:T(8,128)(2,1)} %lat_ref.3) | copy-start | bytes 24580
  85.1 46.2 %copy-start = (bf16[1024,256]{1,0:T(8,128)(2,1)S(1)}, bf16[1024,256]{1,0:T(8,128)(2,1)}, u32[]{:S(2)}) copy-start(bf16[1024,256]{1,0:T(8,128)(2,1)} %up_ref.1) | copy-start | bytes 1572868
  85.1 46.2 %copy-start.1 = (bf16[256,1024]{1,0:T(8,128)(2,1)S(1)}, bf16[256,1024]{1,0:T(8,128)(2,1)}, u32[]{:S(2)}) copy-start(bf16[256,1024]{1,0:T(8,128)(2,1)} %down_ref.1) | copy-start | bytes 1572868
  85.1 46.2 %copy-start.14 = (f32[1024]{0:T(1024)S(1)}, f32[1024]{0:T(1024)}, u32[]{:S(2)}) copy-start(f32[1024]{0:T(1024)} %param.22) | copy-start | bytes 12292

commit v5 on v4

--- a/solution.py
+++ b/solution.py
@@ -13,7 +13,6 @@
 NEGATIVE = -1e30
 LOWEST = -1e29
 BOTH = ("seq", "head")
-SHIFTS = (0, 1, 3, 2)
 F32 = jnp.float32
 BF16 = jnp.bfloat16
 MIB = 1 << 20
@@ -28,15 +27,13 @@
 TN = ((0,), (0,))
 
 
-def line_shift(seq_size, side, phase, step):
+def partners(seq_size, side, phase, step):
     pairs = []
     for s in range(seq_size):
         along_x = (s % 2 == 0) == (phase == 0)
-        for y in range(side):
-            for x in range(side):
-                target = (y, (x + step) % side) if along_x else ((y + step) % side, x)
-                base = s * side * side
-                pairs.append((base + y * side + x, base + target[0] * side + target[1]))
+        for place in range(side * side):
+            other = place ^ (step if along_x else side * step)
+            pairs.append((s * side * side + place, s * side * side + other))
     return pairs
 
 
@@ -71,22 +68,31 @@
     return (rows * inverse * gain).astype(BF16)
 
 
-def weights_kernel(order_ref, wk_ref, wv_ref, gain_ref, out_ref, scratch):
-    both = jnp.concatenate([wk_ref[...], wv_ref[...]], axis=0).astype(F32) * gain_ref[...]
-    scratch[...] = both.T.reshape(scratch.shape)
-    for i in range(out_ref.shape[0]):
-        line = jnp.concatenate([scratch[order_ref[4 * i + j]] for j in range(4)], axis=0)
-        out_ref[i] = line.T.astype(BF16)
-
-
 def latents_kernel(lat_ref, out_ref):
     half = lat_ref.shape[0] // 2
     packed = jnp.concatenate([lat_ref[:half, :], lat_ref[half:, :]], axis=1)
     out_ref[...] = jnp.broadcast_to(packed[None], out_ref.shape)
 
 
-def positions_kernel(place_ref, ctx_ref, lat_ref, kp_ref, pos_ref):
-    plane, core = place_ref[0], place_ref[1]
+def prepare_kernel(*refs):
+    given, outs, held, scratch, sems = refs[:6], refs[6:10], refs[10:16], refs[16], refs[17]
+    w_ref, all_ref, kp_ref, pos_ref = outs
+    copies = [pltpu.make_async_copy(a, b, sems.at[i]) for i, (a, b) in enumerate(zip(given, held))]
+    for copy in copies:
+        copy.start()
+    for copy in copies:
+        copy.wait()
+    wq_ref, wk_ref, wv_ref, gain_ref, ctx_ref, lat_ref = held
+    seq_place, place = lax.axis_index("seq"), lax.axis_index("head")
+    plane, core = seq_place // 2, seq_place % 2
+    weights = jnp.concatenate([wq_ref[...], wk_ref[...], wv_ref[...]], axis=0).astype(F32)
+    weights = weights * gain_ref[...]
+    all_ref[...] = weights.astype(BF16)
+    scratch[...] = weights[64:].T.reshape(scratch.shape)
+    for i in range(w_ref.shape[0]):
+        blocks = [scratch[place ^ jnp.where(core == 0, 4 * i + j, 4 * j + i)] for j in range(4)]
+        w_ref[i] = jnp.concatenate(blocks, axis=0).T.astype(BF16)
+
     for i in range(ctx_ref.shape[0]):
         kp_ref[:, 128 * i : 128 * i + 128] = ctx_ref[i : i + 1, :]
     own = lat_ref[pl.ds(plane, 1), :]
@@ -107,14 +113,16 @@
             pos_ref[k, 32 * z : 32 * z + 32] = jnp.broadcast_to(part[:, lane : lane + 1], (32, 128))
 
 
-def queries_kernel(lat_ref, wq_ref, wk_ref, wv_ref, gain_ref, q_ref, kv_ref):
-    normed = normalize(unpack_columns(lat_ref), gain_ref[...])
-    q = dot(normed, wq_ref[...], NT).astype(BF16).astype(F32) * HD ** (-0.5)
+def queries_kernel(lat_ref, w_ref, q_ref, kv_ref):
+    rows = unpack_columns(lat_ref)
+    inverse = lax.rsqrt(jnp.mean(rows * rows, axis=-1, keepdims=True) + EPSILON)
+    normed = (rows * inverse).astype(BF16)
+    q = dot(normed, w_ref[:64], NT).astype(BF16).astype(F32) * HD ** (-0.5)
     half = q.shape[0] // 2
     packed = jnp.concatenate([q[:half], q[half:]], axis=1).astype(BF16)
     q_ref[...] = jnp.broadcast_to(packed[None], q_ref.shape)
-    rows = jnp.concatenate([dot(wk_ref[...], normed, NT), dot(wv_ref[...], normed, NT)], axis=0)
-    kv_ref[...] = jnp.concatenate([rows, jnp.zeros_like(rows)], axis=1).astype(BF16)
+    both = dot(w_ref[64:], normed, NT)
+    kv_ref[...] = jnp.concatenate([both, jnp.zeros_like(both)], axis=1).astype(BF16)
 
 
 def keys_kernel(*refs):
@@ -326,73 +334,69 @@
     lat_rows, cols = latents.shape
     tokens = context.shape[0]
     half = lat_rows // 2
-    seq_place = lax.axis_index("seq")
-    core = seq_place % 2
     planes = seq_size // 2
     along_z = [[2 * z + c for z in range(planes)] for c in range(2)]
     swap = [(s, s ^ 1) for s in range(seq_size)]
     block = (half, 2 * cols)
-    row_gain = input_gain.reshape(1, -1)
-    wq_t, wk_t, wv_t = w_query.T, w_key.T, w_value.T
-
-    place = lax.axis_index("head")
-    y, x = place // side, place % side
-    shifts = jnp.array(SHIFTS, jnp.int32)
-    first, second = shifts[None, :], shifts[:, None]
-    by_x = ((y - second) % side) * side + (x - first) % side
-    by_y = ((y - first) % side) * side + (x - second) % side
-    order = jnp.where(core == 0, by_x, by_y).reshape(-1)
+    vmem = pl.BlockSpec(memory_space=pltpu.VMEM)
+    key_count = tokens + 2 * lat_rows
+    rows = planes * half
+
+    def swap_lines(piece, phase, step):
+        return lax.ppermute(piece, BOTH, partners(seq_size, side, phase, step))
 
     own = context.T
-    line = jnp.concatenate(
-        [own]
-        + [lax.ppermute(own, BOTH, line_shift(seq_size, side, 0, k)) for k in SHIFTS[1:]],
-        axis=0,
-    )
+    pair = jnp.concatenate([own, swap_lines(own, 0, 1)], axis=0)
     copies = call(latents_kernel, [((head_size, *block), BF16)])(latents)
+    pair, copies = lax.optimization_barrier((pair, copies))
     lat_blocks = lax.all_to_all(copies, "head", 0, 0)
-    line, lat_blocks = lax.optimization_barrier((line, lat_blocks))
-    lines = [line] + [
-        lax.ppermute(line, BOTH, line_shift(seq_size, side, 1, k)) for k in SHIFTS[1:]
-    ]
+    line = jnp.concatenate([pair, swap_lines(pair, 0, 2)], axis=0)
+    anywhere = pl.BlockSpec(memory_space=pl.ANY)
+    prepared = call(
+        prepare_kernel,
+        [
+            ((side, 2 * cols, side * cols), BF16),
+            ((3 * cols, head_size * cols), BF16),
+            ((1, key_count), jnp.int32),
+            ((4, rows, 2 * cols), jnp.int32),
+        ],
+        in_specs=[anywhere] * 6,
+        scratch_shapes=[pltpu.VMEM((cols, head_size * cols), BF16)] * 3
+        + [
+            pltpu.VMEM((1, head_size * cols), F32),
+            pltpu.VMEM((tokens // 128, 128), jnp.int32),
+            pltpu.VMEM((planes, 2 * lat_rows), jnp.int32),
+            pltpu.VMEM((head_size, cols, 2 * cols), F32),
+            pltpu.SemaphoreType.DMA((6,)),
+        ],
+    )(
+        w_query.T,
+        w_key.T,
+        w_value.T,
+        input_gain.reshape(1, -1),
+        ctx_pos.reshape(-1, 128),
+        lat_pos.reshape(-1, 2 * lat_rows),
+    )
+    line, lat_blocks, prepared = lax.optimization_barrier((line, lat_blocks, prepared))
+    key_weights, all_weights, key_pos, query_pos = prepared
+    lines = [line] + [swap_lines(line, 1, step) for step in range(1, side)]
 
     queries, latent_kv = call(
         queries_kernel, [((planes, *block), BF16), ((2 * cols, 2 * lat_rows), BF16)]
-    )(lat_blocks, wq_t, wk_t, wv_t, row_gain)
+    )(lat_blocks, all_weights)
     own_queries = lax.all_to_all(queries, "seq", 0, 0, axis_index_groups=along_z)
     other_queries = lax.ppermute(own_queries, "seq", swap)
 
-    key_weights = call(
-        weights_kernel,
-        [((side, 2 * cols, side * cols), BF16)],
-        in_specs=[pl.BlockSpec(memory_space=pltpu.SMEM)]
-        + [pl.BlockSpec(memory_space=pltpu.VMEM)] * 3,
-        scratch_shapes=[pltpu.VMEM((head_size, cols, 2 * cols), F32)],
-    )(order, wk_t, wv_t, row_gain)
-    key_count = tokens + 2 * lat_rows
     operands = call(
         keys_kernel,
         [((128, key_count), BF16)] * 2 + [((key_count, 128), BF16)] * 2,
         cost=10**9,
-        in_specs=[pl.BlockSpec(memory_space=pl.ANY)] * side
-        + [pl.BlockSpec(memory_space=pltpu.VMEM)] * 2,
+        in_specs=[anywhere] * side + [vmem] * 2,
         scratch_shapes=[
             pltpu.VMEM((side, side * cols, tokens), BF16),
             pltpu.SemaphoreType.DMA((4, side)),
         ],
     )(*lines, key_weights, latent_kv)
-
-    rows = planes * half
-    key_pos, query_pos = call(
-        positions_kernel,
-        [((1, key_count), jnp.int32), ((4, rows, 2 * cols), jnp.int32)],
-        in_specs=[pl.BlockSpec(memory_space=pltpu.SMEM)]
-        + [pl.BlockSpec(memory_space=pltpu.VMEM)] * 2,
-    )(
-        jnp.stack([seq_place // 2, core]),
-        ctx_pos.reshape(-1, 128),
-        lat_pos.reshape(-1, 2 * lat_rows),
-    )
 
     message = (planes, 48, 2 * cols)
     to_sibling = call(other_kernel, [(message, BF16)])(

time: 145 us -> 147 us (1.014)
  blocking collectives: 56.1 us -> 87.9 us
  starting transfers between devices: 45 us -> 28.4 us
  waiting for transfers between devices: 17.7 us -> 10.5 us
  local copies, waits for them, and re-layouts: 5.12 us -> 0.77 us
    all_to_all x0 -> x1, blocking collectives: none -> 27.7 us  [body(): lax.all_to_all(queries, 'seq', 0, 0, axis_index_groups=along_z)]
    all_to_all x1 -> x0, starting transfers between devices: 15.2 us -> none  [body(): lax.all_to_all(queries, 'seq', 0, 0, axis_index_groups=along_z)]
    all_to_all x1 -> x0, waiting for transfers between devices: 10.9 us -> none  [body(): lax.all_to_all(queries, 'seq', 0, 0, axis_index_groups=along_z)]
    all_to_all x1, blocking collectives: 20.6 us -> 25.9 us  [body(): arrived = lax.all_to_all(joined, 'seq', 0, 0, axis_index_groups=along_z)]
    ppermute x6 -> x5, waiting for transfers between devices: 0.02 us -> 4.74 us  [swap_lines(): return lax.ppermute(piece, BOTH, partners(seq_size, side, phase, step))]
    unnamed x32 -> x24, local copies, waits for them, and re-layouts: 4.36 us -> 0.77 us
    ppermute x6 -> x5, starting transfers between devices: 19.7 us -> 18.9 us  [swap_lines(): return lax.ppermute(piece, BOTH, partners(seq_size, side, phase, step))]
  transfers between devices with their start and end apart: 10 -> 8, of which waited for: 2 -> 3; matrix products, arithmetic and copies ran while one was open for 2% -> 1% of each run, Pallas kernels for 7% -> 7%
where the time goes in v5:
time: 147 us
  blocking collectives  87.9 us (60%)
  starting transfers between devices  28.4 us (19%)
  Pallas kernels  16.7 us (11%)
  waiting for transfers between devices  10.5 us (7%)
  other arithmetic  2.09 us (1%)
    all_to_all x1, blocking collectives, body(): lax.all_to_all(queries, 'seq', 0, 0, axis_index_groups=along_z)  27.7 us
    all_to_all x1, blocking collectives, body(): arrived = lax.all_to_all(joined, 'seq', 0, 0, axis_index_groups=along_z)  25.9 us
    all_to_all x2, blocking collectives, body(): arrived = lax.all_to_all(shares, 'head', 0, 0)  23.2 us
    ppermute x5, starting transfers between devices, swap_lines(): return lax.ppermute(piece, BOTH, partners(seq_size, side, phase, step))  18.9 us
    all_to_all x1, blocking collectives, body(): arrived = lax.all_to_all(copies, 'head', 0, 0)  11.1 us
    all_to_all x1, waiting for transfers between devices, body(): lat_blocks = lax.all_to_all(copies, 'head', 0, 0)  5.74 us
    all_to_all x1, starting transfers between devices, body(): lat_blocks = lax.all_to_all(copies, 'head', 0, 0)  5.16 us
    ppermute x5, waiting for transfers between devices, swap_lines(): return lax.ppermute(piece, BOTH, partners(seq_size, side, phase, step))  4.74 us
  transfers between devices with their start and end apart: 8, of which 3 were waited for; matrix products, arithmetic and copies ran while one was open for 1% of the time, Pallas kernels for 7%

profile of v5, /device:TPU:32, one launch (start us, length us, event | category | flops | bytes accessed | tf_op | source)
XLA Modules:
  0.0 146.6 jit_solution(17040985136531040244)
XLA Ops:
  0.0 3.5 %collective-permute-start = (bf16[64,2048]{1,0:T(8,128)(2,1)}, bf16[64,2048]{1,0:T(8,128)(2,1)S(1)}, u32[]{:S(2)}, u32[]{:S(2)}) collective-permute-start(bf16[64,2048]{1,0:T(8,128)(2,1)} %bitcast.19), channel_id=1, source_target_pairs={{0,1},{1,0},{2,3},{3,2},{4,5},{5,4},{6,7},{7,6},{8,9},{9,8},{10,11... | collective-permute-start | bytes 786440 | tf_op jit(solution)/shard_map/ppermute | solution.py:346
  3.6 0.0 copy-start.6
  3.6 0.7 copy-done.6
  4.3 0.7 shard_map.118
  5.0 3.6 %collective-permute-done = bf16[64,2048]{1,0:T(8,128)(2,1)S(1)} collective-permute-done((bf16[64,2048]{1,0:T(8,128)(2,1)}, bf16[64,2048]{1,0:T(8,128)(2,1)S(1)}, u32[]{:S(2)}, u32[]{:S(2)}) %collective-permute-start) | collective-permute-done | bytes 262176 | tf_op jit(solution)/shard_map/ppermute | solution.py:346
  8.6 1.0 pad_maximum_fusion.1
  9.6 4.9 %collective-permute-start.1 = (bf16[128,2048]{1,0:T(8,128)(2,1)S(1)}, bf16[128,2048]{1,0:T(8,128)(2,1)}, u32[]{:S(2)}, u32[]{:S(2)}) collective-permute-start(bf16[128,2048]{1,0:T(8,128)(2,1)S(1)} %pad_maximum_fusion.1), channel_id=1, source_target_pairs={{0,2},{1,3},{2,0},{3,1},{4,6},{5,7},{6,4},{7,5},{8,10},{9,11},{10,... | collective-permute-start | bytes 1572872 | tf_op jit(solution)/shard_map/ppermute | solution.py:346
  14.5 0.0 copy-done.2
  14.6 0.0 copy-done.3
  14.6 0.0 copy-done.4
  14.6 0.0 copy-done.8
  14.6 0.0 copy-done.9
  14.6 0.0 copy-done.10
  14.6 1.4 shard_map.119
  16.0 5.2 %all-to-all-start = ((bf16[16,32,128]{2,1,0:T(8,128)(2,1)}), bf16[16,32,128]{2,1,0:T(8,128)(2,1)S(1)}, u32[]{:S(2)}, u32[]{:S(2)}) async-start(bf16[16,32,128]{2,1,0:T(8,128)(2,1)} %shard_map.118), calls=%async_computation | async-start | bytes 262144 | tf_op jit(solution)/shard_map/all_to_all | solution.py:352
  21.2 1.1 collective-permute-done.1
  22.3 1.1 pad_maximum_fusion.refs_0_
  23.4 5.7 %all-to-all-done.lat_ref = bf16[16,32,128]{2,1,0:T(8,128)(2,1)S(1)} async-done(((bf16[16,32,128]{2,1,0:T(8,128)(2,1)}), bf16[16,32,128]{2,1,0:T(8,128)(2,1)S(1)}, u32[]{:S(2)}, u32[]{:S(2)}) %all-to-all-start) | async-done | bytes 131104 | tf_op jit(solution)/shard_map/all_to_all | solution.py:352
  29.2 2.2 %collective-permute-start.2 = (bf16[256,2048]{1,0:T(8,128)(2,1)S(1)}, bf16[256,2048]{1,0:T(8,128)(2,1)S(1)}, u32[]{:S(2)}, u32[]{:S(2)}) collective-permute-start(bf16[256,2048]{1,0:T(8,128)(2,1)S(1)} %pad_maximum_fusion.refs_0_), channel_id=1, source_target_pairs={{0,4},{1,5},{2,6},{3,7},{4,0},{5,1},{6,2},{7,3},{8,12},{9,13},{10,... | collective-permute-start | bytes 3145736 | tf_op jit(solution)/shard_map/ppermute | solution.py:346
  31.4 4.0 %collective-permute-start.3 = (bf16[256,2048]{1,0:T(8,128)(2,1)S(1)}, bf16[256,2048]{1,0:T(8,128)(2,1)S(1)}, u32[]{:S(2)}, u32[]{:S(2)}) collective-permute-start(bf16[256,2048]{1,0:T(8,128)(2,1)S(1)} %pad_maximum_fusion.refs_0_), channel_id=1, source_target_pairs={{0,8},{1,9},{2,10},{3,11},{4,12},{5,13},{6,14},{7,15},{8,0},{9,1},... | collective-permute-start | bytes 3145736 | tf_op jit(solution)/shard_map/ppermute | solution.py:346
  35.3 4.2 %collective-permute-start.4 = (bf16[256,2048]{1,0:T(8,128)(2,1)S(1)}, bf16[256,2048]{1,0:T(8,128)(2,1)S(1)}, u32[]{:S(2)}, u32[]{:S(2)}) collective-permute-start(bf16[256,2048]{1,0:T(8,128)(2,1)S(1)} %pad_maximum_fusion.refs_0_), channel_id=1, source_target_pairs={{0,12},{1,13},{2,14},{3,15},{4,8},{5,9},{6,10},{7,11},{8,4},{9,5},... | collective-permute-start | bytes 3145736 | tf_op jit(solution)/shard_map/ppermute | solution.py:346
  39.6 0.4 shard_map.120
  40.0 27.7 %all_to_all.30 = bf16[16,32,128]{2,1,0:T(8,128)(2,1)S(1)} all-to-all(bf16[16,32,128]{2,1,0:T(8,128)(2,1)S(1)} %get-tuple-element.35), channel_id=1, replica_groups={{0,32,64,96,128,160,192,224,256,288,320,352,384,416,448,480},{16,48,80,..., dimensions={0} | all-to-all | bytes 262144 | tf_op jit(solution)/shard_map/all_to_all | solution.py:387
  67.8 1.9 %collective-permute-start.5 = (bf16[16,32,128]{2,1,0:T(8,128)(2,1)S(1)}, bf16[16,32,128]{2,1,0:T(8,128)(2,1)S(1)}, u32[]{:S(2)}, u32[]{:S(2)}) collective-permute-start(bf16[16,32,128]{2,1,0:T(8,128)(2,1)S(1)} %all_to_all.30), channel_id=1, source_target_pairs={{0,16},{16,0},{32,48},{48,32},{64,80},{80,64},{96,112},{112,96},{1... | collective-permute-start | bytes 393224 | tf_op jit(solution)/shard_map/ppermute | solution.py:388
  69.7 0.0 collective-permute-done.2.refs_1_
  69.7 0.0 collective-permute-done.3.refs_2_
  69.7 0.0 collective-permute-done.4.refs_3_
  69.7 2.9 %shard_map.121 = (bf16[128,2176]{1,0:T(8,128)(2,1)S(1)}, bf16[128,2176]{1,0:T(8,128)(2,1)S(1)}, bf16[2176,128]{1,0:T(8,128)(2,1)S(1)}, bf16[2176,128]{1,0:T(8,128)(2,1)S(1)}) custom-call(bf16[256,2048]{1,0:T(8,128)(2,1)S(1)} %pad_maximum_fusion.refs_0_, bf16[256,2048]{1,0:T(8,128)(2,1)S(1)} %collective-permute-done.2.refs_1_, ...), custom_call_target="tpu_custom_call" | custom-call | flops 1000000000 | bytes 1000000000 | tf_op jit(solution)/shard_map/pallas_call | solution.py:390
  72.7 0.0 collective-permute-done.5
  72.7 4.3 %shard_map.123 = bf16[16,48,128]{2,1,0:T(8,128)(2,1)S(1)} custom-call(bf16[512,128]{1,0:T(8,128)(2,1)S(1)} %bitcast.14, s32[4,512,128]{2,1,0:T(8,128)S(1)} %get-tuple-element.36.pos_ref, s32[1,2176]{1,0:T(1,128)S(1)} %get-tuple-element.37.kp_ref, bf16[128,2176]{1,0:T(8,128)(2,1)S(1)} %get-tuple-element.41.ka_ref, ...), custom_call_target="tpu_custom_call" | custom-call | flops 1000 | bytes 1000 | tf_op jit(solution)/shard_map/pallas_call | solution.py:402
  77.0 2.4 %collective-permute-start.6 = (bf16[16,48,128]{2,1,0:T(8,128)(2,1)S(1)}, bf16[16,48,128]{2,1,0:T(8,128)(2,1)S(1)}, u32[]{:S(2)}, u32[]{:S(2)}) collective-permute-start(bf16[16,48,128]{2,1,0:T(8,128)(2,1)S(1)} %shard_map.123), channel_id=1, source_target_pairs={{0,16},{16,0},{32,48},{48,32},{64,80},{80,64},{96,112},{112,96},{1... | collective-permute-start | bytes 589832 | tf_op jit(solution)/shard_map/ppermute | solution.py:405
  79.4 4.3 %shard_map.122 = (f32[512,128]{1,0:T(8,128)S(1)}, f32[512,128]{1,0:T(8,128)S(1)}) custom-call(bf16[512,128]{1,0:T(8,128)(2,1)S(1)} %bitcast.10, s32[4,512,128]{2,1,0:T(8,128)S(1)} %get-tuple-element.36.pos_ref, s32[1,2176]{1,0:T(1,128)S(1)} %get-tuple-element.37.kp_ref, bf16[128,2176]{1,0:T(8,128)(2,1)S(1)} %get-tuple-element.41.ka_ref, ...), custom_call_target="tpu_custom_call" | custom-call | flops 1000 | bytes 1000 | tf_op jit(solution)/shard_map/pallas_call | solution.py:406
  83.7 0.0 copy-start.5
  83.7 0.0 copy-start.7
  83.7 0.0 collective-permute-done.6.arrived_ref
  83.7 0.0 copy-start
  83.7 0.0 copy-start.1
  83.8 0.0 copy-start.11
  83.8 0.4 shard_map.124
  84.2 25.9 %all_to_all.31.arrived_ref = bf16[16,48,128]{2,1,0:T(8,128)(2,1)S(1)} all-to-all(bf16[16,48,128]{2,1,0:T(8,128)(2,1)S(1)} %shard_map.124), channel_id=1, replica_groups={{0,32,64,96,128,160,192,224,256,288,320,352,384,416,448,480},{16,48,80,..., dimensions={0} | all-to-all | bytes 393216 | tf_op jit(solution)/shard_map/all_to_all | solution.py:410
  110.1 0.0 copy-done.5
  110.1 0.7 shard_map.125
  110.8 12.2 %all_to_all.32.arrived_ref = bf16[16,32,128]{2,1,0:T(8,128)(2,1)S(1)} all-to-all(bf16[16,32,128]{2,1,0:T(8,128)(2,1)S(1)} %shard_map.125), channel_id=1, replica_groups=mesh['seq'=32,'head'=16] {'head'}, dimensions={0} | all-to-all | bytes 262144 | tf_op jit(solution)/shard_map/all_to_all | solution.py:412
  122.9 0.1 shard_map.126
  123.0 11.1 %all_to_all.33.arrived_ref = bf16[16,32,128]{2,1,0:T(8,128)(2,1)S(1)} all-to-all(bf16[16,32,128]{2,1,0:T(8,128)(2,1)S(1)} %get-tuple-element.47), channel_id=1, replica_groups=mesh['seq'=32,'head'=16] {'head'}, dimensions={0} | all-to-all | bytes 262144 | tf_op jit(solution)/shard_map/all_to_all | solution.py:416
  134.1 0.7 shard_map.127
  134.8 11.1 %all_to_all.34.arrived_ref = bf16[16,32,128]{2,1,0:T(8,128)(2,1)S(1)} all-to-all(bf16[16,32,128]{2,1,0:T(8,128)(2,1)S(1)} %shard_map.127), channel_id=1, replica_groups=mesh['seq'=32,'head'=16] {'head'}, dimensions={0} | all-to-all | bytes 262144 | tf_op jit(solution)/shard_map/all_to_all | solution.py:420
  145.9 0.7 shard_map.128
  (10 shorter events, 0.0 us)
Async XLA Ops:
  0.0 14.6 %copy-start.2 = (bf16[1024,64]{0,1:T(8,128)(2,1)S(1)}, bf16[1024,64]{0,1:T(8,128)(2,1)}, u32[]{:S(2)}) copy-start(bf16[1024,64]{0,1:T(8,128)(2,1)} %param.17) | copy-start | bytes 393220
  0.0 14.6 %copy-start.3 = (bf16[1024,64]{0,1:T(8,128)(2,1)S(1)}, bf16[1024,64]{0,1:T(8,128)(2,1)}, u32[]{:S(2)}) copy-start(bf16[1024,64]{0,1:T(8,128)(2,1)} %param.18) | copy-start | bytes 393220
  0.0 14.6 %copy-start.4 = (bf16[1024,64]{0,1:T(8,128)(2,1)S(1)}, bf16[1024,64]{0,1:T(8,128)(2,1)}, u32[]{:S(2)}) copy-start(bf16[1024,64]{0,1:T(8,128)(2,1)} %param.19) | copy-start | bytes 393220
  0.0 8.6 %collective-permute-start = (bf16[64,2048]{1,0:T(8,128)(2,1)}, bf16[64,2048]{1,0:T(8,128)(2,1)S(1)}, u32[]{:S(2)}, u32[]{:S(2)}) collective-permute-start(bf16[64,2048]{1,0:T(8,128)(2,1)} %bitcast.19), channel_id=1, source_target_pairs={{0,1},{1,0},{2,3},{3,2},{4,5},{5,4},{6,7},{7,6},{8,9},{9,8},{10,11... | collective-permute-start | bytes 786440 | tf_op jit(solution)/shard_map/ppermute | solution.py:346
  3.6 0.7 copy-start.6
  4.3 10.3 %copy-start.8 = (s32[2048]{0:T(1024)S(1)}, s32[2048]{0:T(1024)}, u32[]{:S(2)}) copy-start(s32[2048]{0:T(1024)} %param.14) | copy-start | bytes 24580
  4.3 10.3 %copy-start.9 = (s32[2048]{0:T(1024)S(1)}, s32[2048]{0:T(1024)}, u32[]{:S(2)}) copy-start(s32[2048]{0:T(1024)} %param.15) | copy-start | bytes 24580
  4.3 10.3 %copy-start.10 = (f32[1024]{0:T(1024)S(1)}, f32[1024]{0:T(1024)}, u32[]{:S(2)}) copy-start(f32[1024]{0:T(1024)} %param.16) | copy-start | bytes 12292
  9.6 12.7 %collective-permute-start.1 = (bf16[128,2048]{1,0:T(8,128)(2,1)S(1)}, bf16[128,2048]{1,0:T(8,128)(2,1)}, u32[]{:S(2)}, u32[]{:S(2)}) collective-permute-start(bf16[128,2048]{1,0:T(8,128)(2,1)S(1)} %pad_maximum_fusion.1), channel_id=1, source_target_pairs={{0,2},{1,3},{2,0},{3,1},{4,6},{5,7},{6,4},{7,5},{8,10},{9,11},{10,... | collective-permute-start | bytes 1572872 | tf_op jit(solution)/shard_map/ppermute | solution.py:346
  16.0 13.2 %all-to-all-start = ((bf16[16,32,128]{2,1,0:T(8,128)(2,1)}), bf16[16,32,128]{2,1,0:T(8,128)(2,1)S(1)}, u32[]{:S(2)}, u32[]{:S(2)}) async-start(bf16[16,32,128]{2,1,0:T(8,128)(2,1)} %shard_map.118), calls=%async_computation | async-start | bytes 262144 | tf_op jit(solution)/shard_map/all_to_all | solution.py:352
  29.2 40.5 %collective-permute-start.2 = (bf16[256,2048]{1,0:T(8,128)(2,1)S(1)}, bf16[256,2048]{1,0:T(8,128)(2,1)S(1)}, u32[]{:S(2)}, u32[]{:S(2)}) collective-permute-start(bf16[256,2048]{1,0:T(8,128)(2,1)S(1)} %pad_maximum_fusion.refs_0_), channel_id=1, source_target_pairs={{0,4},{1,5},{2,6},{3,7},{4,0},{5,1},{6,2},{7,3},{8,12},{9,13},{10,... | collective-permute-start | bytes 3145736 | tf_op jit(solution)/shard_map/ppermute | solution.py:346
  31.4 38.3 %collective-permute-start.3 = (bf16[256,2048]{1,0:T(8,128)(2,1)S(1)}, bf16[256,2048]{1,0:T(8,128)(2,1)S(1)}, u32[]{:S(2)}, u32[]{:S(2)}) collective-permute-start(bf16[256,2048]{1,0:T(8,128)(2,1)S(1)} %pad_maximum_fusion.refs_0_), channel_id=1, source_target_pairs={{0,8},{1,9},{2,10},{3,11},{4,12},{5,13},{6,14},{7,15},{8,0},{9,1},... | collective-permute-start | bytes 3145736 | tf_op jit(solution)/shard_map/ppermute | solution.py:346
  35.3 34.4 %collective-permute-start.4 = (bf16[256,2048]{1,0:T(8,128)(2,1)S(1)}, bf16[256,2048]{1,0:T(8,128)(2,1)S(1)}, u32[]{:S(2)}, u32[]{:S(2)}) collective-permute-start(bf16[256,2048]{1,0:T(8,128)(2,1)S(1)} %pad_maximum_fusion.refs_0_), channel_id=1, source_target_pairs={{0,12},{1,13},{2,14},{3,15},{4,8},{5,9},{6,10},{7,11},{8,4},{9,5},... | collective-permute-start | bytes 3145736 | tf_op jit(solution)/shard_map/ppermute | solution.py:346
  67.8 4.9 %collective-permute-start.5 = (bf16[16,32,128]{2,1,0:T(8,128)(2,1)S(1)}, bf16[16,32,128]{2,1,0:T(8,128)(2,1)S(1)}, u32[]{:S(2)}, u32[]{:S(2)}) collective-permute-start(bf16[16,32,128]{2,1,0:T(8,128)(2,1)S(1)} %all_to_all.30), channel_id=1, source_target_pairs={{0,16},{16,0},{32,48},{48,32},{64,80},{80,64},{96,112},{112,96},{1... | collective-permute-start | bytes 393224 | tf_op jit(solution)/shard_map/ppermute | solution.py:388
  77.0 6.7 %collective-permute-start.6 = (bf16[16,48,128]{2,1,0:T(8,128)(2,1)S(1)}, bf16[16,48,128]{2,1,0:T(8,128)(2,1)S(1)}, u32[]{:S(2)}, u32[]{:S(2)}) collective-permute-start(bf16[16,48,128]{2,1,0:T(8,128)(2,1)S(1)} %shard_map.123), channel_id=1, source_target_pairs={{0,16},{16,0},{32,48},{48,32},{64,80},{80,64},{96,112},{112,96},{1... | collective-permute-start | bytes 589832 | tf_op jit(solution)/shard_map/ppermute | solution.py:405
  83.7 26.4 %copy-start.5 = (bf16[64,1024]{1,0:T(8,128)(2,1)S(1)}, bf16[64,1024]{1,0:T(8,128)(2,1)}, u32[]{:S(2)}) copy-start(bf16[64,1024]{1,0:T(8,128)(2,1)} %w_ref.1) | copy-start | bytes 393220
  83.7 39.2 %copy-start.7 = (bf16[64,64]{1,0:T(8,128)(2,1)S(1)}, bf16[64,64]{1,0:T(8,128)(2,1)}, u32[]{:S(2)}) copy-start(bf16[64,64]{1,0:T(8,128)(2,1)} %lat_ref.3) | copy-start | bytes 24580
  83.7 50.4 %copy-start = (bf16[1024,256]{1,0:T(8,128)(2,1)S(1)}, bf16[1024,256]{1,0:T(8,128)(2,1)}, u32[]{:S(2)}) copy-start(bf16[1024,256]{1,0:T(8,128)(2,1)} %up_ref.1) | copy-start | bytes 1572868
  83.7 50.4 %copy-start.1 = (bf16[256,1024]{1,0:T(8,128)(2,1)S(1)}, bf16[256,1024]{1,0:T(8,128)(2,1)}, u32[]{:S(2)}) copy-start(bf16[256,1024]{1,0:T(8,128)(2,1)} %down_ref.1) | copy-start | bytes 1572868
  83.8 50.3 %copy-start.11 = (f32[1024]{0:T(1024)S(1)}, f32[1024]{0:T(1024)}, u32[]{:S(2)}) copy-start(f32[1024]{0:T(1024)} %param.21) | copy-start | bytes 12292

commit v6 on v5

--- a/solution.py
+++ b/solution.py
@@ -13,6 +13,7 @@
 NEGATIVE = -1e30
 LOWEST = -1e29
 BOTH = ("seq", "head")
+STEPS = (0, 1, 3, 2)
 F32 = jnp.float32
 BF16 = jnp.bfloat16
 MIB = 1 << 20
@@ -90,7 +91,7 @@
     all_ref[...] = weights.astype(BF16)
     scratch[...] = weights[64:].T.reshape(scratch.shape)
     for i in range(w_ref.shape[0]):
-        blocks = [scratch[place ^ jnp.where(core == 0, 4 * i + j, 4 * j + i)] for j in range(4)]
+        blocks = [scratch[place ^ jnp.where(core == 0, 4 * STEPS[i] + STEPS[j], 4 * STEPS[j] + STEPS[i])] for j in range(4)]
         w_ref[i] = jnp.concatenate(blocks, axis=0).T.astype(BF16)
 
     for i in range(ctx_ref.shape[0]):
@@ -346,11 +347,10 @@
         return lax.ppermute(piece, BOTH, partners(seq_size, side, phase, step))
 
     own = context.T
-    pair = jnp.concatenate([own, swap_lines(own, 0, 1)], axis=0)
+    line = jnp.concatenate([own] + [swap_lines(own, 0, step) for step in STEPS[1:]], axis=0)
+    line, input_gain = lax.optimization_barrier((line, input_gain))
     copies = call(latents_kernel, [((head_size, *block), BF16)])(latents)
-    pair, copies = lax.optimization_barrier((pair, copies))
     lat_blocks = lax.all_to_all(copies, "head", 0, 0)
-    line = jnp.concatenate([pair, swap_lines(pair, 0, 2)], axis=0)
     anywhere = pl.BlockSpec(memory_space=pl.ANY)
     prepared = call(
         prepare_kernel,
@@ -379,7 +379,7 @@
     )
     line, lat_blocks, prepared = lax.optimization_barrier((line, lat_blocks, prepared))
     key_weights, all_weights, key_pos, query_pos = prepared
-    lines = [line] + [swap_lines(line, 1, step) for step in range(1, side)]
+    lines = [line] + [swap_lines(line, 1, step) for step in STEPS[1:]]
 
     queries, latent_kv = call(
         queries_kernel, [((planes, *block), BF16), ((2 * cols, 2 * lat_rows), BF16)]

time: 147 us -> 140 us (0.952)
  waiting for transfers between devices: 10.5 us -> 5.28 us
  blocking collectives: 87.9 us -> 83.7 us
  starting transfers between devices: 28.4 us -> 31.6 us
    ppermute x5 -> x6, waiting for transfers between devices: 4.74 us -> 0.02 us  [swap_lines(): return lax.ppermute(piece, BOTH, partners(seq_size, side, phase, step))]
    all_to_all x1, blocking collectives: 25.9 us -> 22.7 us  [body(): arrived = lax.all_to_all(joined, 'seq', 0, 0, axis_index_groups=along_z)]
    all_to_all x1, starting transfers between devices: 5.16 us -> 7.56 us  [body(): lat_blocks = lax.all_to_all(copies, 'head', 0, 0)]
    ppermute x5 -> x6, starting transfers between devices: 18.9 us -> 19.7 us  [swap_lines(): return lax.ppermute(piece, BOTH, partners(seq_size, side, phase, step))]
  transfers between devices with their start and end apart: 8 -> 9, of which waited for: 3 -> 1; matrix products, arithmetic and copies ran while one was open for 1% -> 1% of each run, Pallas kernels for 7% -> 7%
where the time goes in v6:
time: 140 us
  blocking collectives  83.7 us (60%)
  starting transfers between devices  31.6 us (23%)
  Pallas kernels  16.7 us (12%)
  waiting for transfers between devices  5.28 us (4%)
    all_to_all x1, blocking collectives, body(): lax.all_to_all(queries, 'seq', 0, 0, axis_index_groups=along_z)  27.6 us
    all_to_all x1, blocking collectives, body(): arrived = lax.all_to_all(joined, 'seq', 0, 0, axis_index_groups=along_z)  22.7 us
    all_to_all x2, blocking collectives, body(): arrived = lax.all_to_all(shares, 'head', 0, 0)  22.4 us
    ppermute x6, starting transfers between devices, swap_lines(): return lax.ppermute(piece, BOTH, partners(seq_size, side, phase, step))  19.7 us
    all_to_all x1, blocking collectives, body(): arrived = lax.all_to_all(copies, 'head', 0, 0)  11.1 us
    all_to_all x1, starting transfers between devices, body(): lat_blocks = lax.all_to_all(copies, 'head', 0, 0)  7.56 us
    all_to_all x1, waiting for transfers between devices, body(): lat_blocks = lax.all_to_all(copies, 'head', 0, 0)  5.25 us
    pallas_call x1, Pallas kernels, body(): call(other_kernel, [(message, BF16)])  4.33 us
  transfers between devices with their start and end apart: 9, of which 1 were waited for; matrix products, arithmetic and copies ran while one was open for 1% of the time, Pallas kernels for 7%

profile of v6, /device:TPU:32, one launch (start us, length us, event | category | flops | bytes accessed | tf_op | source)
XLA Modules:
  0.0 139.6 jit_solution(8948144071667430053)
XLA Ops:
  0.0 4.9 %collective-permute-start.2 = (bf16[64,2048]{1,0:T(8,128)(2,1)}, bf16[64,2048]{1,0:T(8,128)(2,1)S(1)}, u32[]{:S(2)}, u32[]{:S(2)}) collective-permute-start(bf16[64,2048]{1,0:T(8,128)(2,1)} %bitcast.19), channel_id=1, source_target_pairs={{0,2},{1,3},{2,0},{3,1},{4,6},{5,7},{6,4},{7,5},{8,10},{9,11},{10,... | collective-permute-start | bytes 786440 | tf_op jit(solution)/shard_map/ppermute | solution.py:347
  4.9 3.1 %collective-permute-start.1 = (bf16[64,2048]{1,0:T(8,128)(2,1)}, bf16[64,2048]{1,0:T(8,128)(2,1)S(1)}, u32[]{:S(2)}, u32[]{:S(2)}) collective-permute-start(bf16[64,2048]{1,0:T(8,128)(2,1)} %bitcast.20), channel_id=1, source_target_pairs={{0,3},{1,2},{2,1},{3,0},{4,7},{5,6},{6,5},{7,4},{8,11},{9,10},{10,... | collective-permute-start | bytes 786440 | tf_op jit(solution)/shard_map/ppermute | solution.py:347
  8.0 1.9 %collective-permute-start = (bf16[64,2048]{1,0:T(8,128)(2,1)}, bf16[64,2048]{1,0:T(8,128)(2,1)S(1)}, u32[]{:S(2)}, u32[]{:S(2)}) collective-permute-start(bf16[64,2048]{1,0:T(8,128)(2,1)} %bitcast.21), channel_id=1, source_target_pairs={{0,1},{1,0},{2,3},{3,2},{4,5},{5,4},{6,7},{7,6},{8,9},{9,8},{10,11... | collective-permute-start | bytes 786440 | tf_op jit(solution)/shard_map/ppermute | solution.py:347
  9.9 0.0 copy-start.6
  9.9 0.7 copy-done.6
  10.6 0.7 shard_map.118
  11.4 7.6 %all-to-all-start = ((bf16[16,32,128]{2,1,0:T(8,128)(2,1)}), bf16[16,32,128]{2,1,0:T(8,128)(2,1)S(1)}, u32[]{:S(2)}, u32[]{:S(2)}) async-start(bf16[16,32,128]{2,1,0:T(8,128)(2,1)} %shard_map.118), calls=%async_computation | async-start | bytes 262144 | tf_op jit(solution)/shard_map/all_to_all | solution.py:353
  18.9 0.0 copy-start.2
  19.0 0.0 copy-start.3
  19.0 0.0 copy-start.4
  19.0 0.0 copy-start.8
  19.0 0.0 copy-start.9
  19.0 0.0 copy-start.10
  19.0 0.0 collective-permute-done.2
  19.0 0.0 collective-permute-done.1
  19.0 0.0 collective-permute-done
  19.0 1.2 pad_maximum_fusion.refs_0_
  20.3 1.4 shard_map.119
  21.7 5.3 %all-to-all-done.lat_ref = bf16[16,32,128]{2,1,0:T(8,128)(2,1)S(1)} async-done(((bf16[16,32,128]{2,1,0:T(8,128)(2,1)}), bf16[16,32,128]{2,1,0:T(8,128)(2,1)S(1)}, u32[]{:S(2)}, u32[]{:S(2)}) %all-to-all-start) | async-done | bytes 131104 | tf_op jit(solution)/shard_map/all_to_all | solution.py:353
  26.9 2.2 %collective-permute-start.3 = (bf16[256,2048]{1,0:T(8,128)(2,1)S(1)}, bf16[256,2048]{1,0:T(8,128)(2,1)S(1)}, u32[]{:S(2)}, u32[]{:S(2)}) collective-permute-start(bf16[256,2048]{1,0:T(8,128)(2,1)S(1)} %pad_maximum_fusion.refs_0_), channel_id=1, source_target_pairs={{0,4},{1,5},{2,6},{3,7},{4,0},{5,1},{6,2},{7,3},{8,12},{9,13},{10,... | collective-permute-start | bytes 3145736 | tf_op jit(solution)/shard_map/ppermute | solution.py:347
  29.1 3.2 %collective-permute-start.4 = (bf16[256,2048]{1,0:T(8,128)(2,1)S(1)}, bf16[256,2048]{1,0:T(8,128)(2,1)S(1)}, u32[]{:S(2)}, u32[]{:S(2)}) collective-permute-start(bf16[256,2048]{1,0:T(8,128)(2,1)S(1)} %pad_maximum_fusion.refs_0_), channel_id=1, source_target_pairs={{0,12},{1,13},{2,14},{3,15},{4,8},{5,9},{6,10},{7,11},{8,4},{9,5},... | collective-permute-start | bytes 3145736 | tf_op jit(solution)/shard_map/ppermute | solution.py:347
  32.3 4.4 %collective-permute-start.5 = (bf16[256,2048]{1,0:T(8,128)(2,1)S(1)}, bf16[256,2048]{1,0:T(8,128)(2,1)S(1)}, u32[]{:S(2)}, u32[]{:S(2)}) collective-permute-start(bf16[256,2048]{1,0:T(8,128)(2,1)S(1)} %pad_maximum_fusion.refs_0_), channel_id=1, source_target_pairs={{0,8},{1,9},{2,10},{3,11},{4,12},{5,13},{6,14},{7,15},{8,0},{9,1},... | collective-permute-start | bytes 3145736 | tf_op jit(solution)/shard_map/ppermute | solution.py:347
  36.8 0.5 shard_map.120
  37.2 27.6 %all_to_all.30 = bf16[16,32,128]{2,1,0:T(8,128)(2,1)S(1)} all-to-all(bf16[16,32,128]{2,1,0:T(8,128)(2,1)S(1)} %get-tuple-element.35), channel_id=1, replica_groups={{0,32,64,96,128,160,192,224,256,288,320,352,384,416,448,480},{16,48,80,..., dimensions={0} | all-to-all | bytes 262144 | tf_op jit(solution)/shard_map/all_to_all | solution.py:387
  64.8 1.9 %collective-permute-start.6 = (bf16[16,32,128]{2,1,0:T(8,128)(2,1)S(1)}, bf16[16,32,128]{2,1,0:T(8,128)(2,1)S(1)}, u32[]{:S(2)}, u32[]{:S(2)}) collective-permute-start(bf16[16,32,128]{2,1,0:T(8,128)(2,1)S(1)} %all_to_all.30), channel_id=1, source_target_pairs={{0,16},{16,0},{32,48},{48,32},{64,80},{80,64},{96,112},{112,96},{1... | collective-permute-start | bytes 393224 | tf_op jit(solution)/shard_map/ppermute | solution.py:388
  66.7 0.0 collective-permute-done.3.refs_1_
  66.7 0.0 collective-permute-done.4.refs_2_
  66.7 0.0 collective-permute-done.5.refs_3_
  66.7 2.9 %shard_map.121 = (bf16[128,2176]{1,0:T(8,128)(2,1)S(1)}, bf16[128,2176]{1,0:T(8,128)(2,1)S(1)}, bf16[2176,128]{1,0:T(8,128)(2,1)S(1)}, bf16[2176,128]{1,0:T(8,128)(2,1)S(1)}) custom-call(bf16[256,2048]{1,0:T(8,128)(2,1)S(1)} %pad_maximum_fusion.refs_0_, bf16[256,2048]{1,0:T(8,128)(2,1)S(1)} %collective-permute-done.3.refs_1_, ...), custom_call_target="tpu_custom_call" | custom-call | flops 1000000000 | bytes 1000000000 | tf_op jit(solution)/shard_map/pallas_call | solution.py:390
  69.7 0.0 collective-permute-done.6
  69.7 4.3 %shard_map.123 = bf16[16,48,128]{2,1,0:T(8,128)(2,1)S(1)} custom-call(bf16[512,128]{1,0:T(8,128)(2,1)S(1)} %bitcast.14, s32[4,512,128]{2,1,0:T(8,128)S(1)} %get-tuple-element.36.pos_ref, s32[1,2176]{1,0:T(1,128)S(1)} %get-tuple-element.37.kp_ref, bf16[128,2176]{1,0:T(8,128)(2,1)S(1)} %get-tuple-element.41.ka_ref, ...), custom_call_target="tpu_custom_call" | custom-call | flops 1000 | bytes 1000 | tf_op jit(solution)/shard_map/pallas_call | solution.py:402
  74.0 2.4 %collective-permute-start.7 = (bf16[16,48,128]{2,1,0:T(8,128)(2,1)S(1)}, bf16[16,48,128]{2,1,0:T(8,128)(2,1)S(1)}, u32[]{:S(2)}, u32[]{:S(2)}) collective-permute-start(bf16[16,48,128]{2,1,0:T(8,128)(2,1)S(1)} %shard_map.123), channel_id=1, source_target_pairs={{0,16},{16,0},{32,48},{48,32},{64,80},{80,64},{96,112},{112,96},{1... | collective-permute-start | bytes 589832 | tf_op jit(solution)/shard_map/ppermute | solution.py:405
  76.4 4.3 %shard_map.122 = (f32[512,128]{1,0:T(8,128)S(1)}, f32[512,128]{1,0:T(8,128)S(1)}) custom-call(bf16[512,128]{1,0:T(8,128)(2,1)S(1)} %bitcast.10, s32[4,512,128]{2,1,0:T(8,128)S(1)} %get-tuple-element.36.pos_ref, s32[1,2176]{1,0:T(1,128)S(1)} %get-tuple-element.37.kp_ref, bf16[128,2176]{1,0:T(8,128)(2,1)S(1)} %get-tuple-element.41.ka_ref, ...), custom_call_target="tpu_custom_call" | custom-call | flops 1000 | bytes 1000 | tf_op jit(solution)/shard_map/pallas_call | solution.py:406
  80.7 0.0 copy-start.5
  80.7 0.0 copy-start.7
  80.7 0.0 collective-permute-done.7.arrived_ref
  80.7 0.0 copy-start
  80.7 0.0 copy-start.1
  80.8 0.0 copy-start.11
  80.8 0.4 shard_map.124
  81.2 22.7 %all_to_all.31.arrived_ref = bf16[16,48,128]{2,1,0:T(8,128)(2,1)S(1)} all-to-all(bf16[16,48,128]{2,1,0:T(8,128)(2,1)S(1)} %shard_map.124), channel_id=1, replica_groups={{0,32,64,96,128,160,192,224,256,288,320,352,384,416,448,480},{16,48,80,..., dimensions={0} | all-to-all | bytes 393216 | tf_op jit(solution)/shard_map/all_to_all | solution.py:410
  103.9 0.7 shard_map.125
  104.6 11.3 %all_to_all.32.arrived_ref = bf16[16,32,128]{2,1,0:T(8,128)(2,1)S(1)} all-to-all(bf16[16,32,128]{2,1,0:T(8,128)(2,1)S(1)} %shard_map.125), channel_id=1, replica_groups=mesh['seq'=32,'head'=16] {'head'}, dimensions={0} | all-to-all | bytes 262144 | tf_op jit(solution)/shard_map/all_to_all | solution.py:412
  115.9 0.1 shard_map.126
  116.0 11.1 %all_to_all.33.arrived_ref = bf16[16,32,128]{2,1,0:T(8,128)(2,1)S(1)} all-to-all(bf16[16,32,128]{2,1,0:T(8,128)(2,1)S(1)} %get-tuple-element.47), channel_id=1, replica_groups=mesh['seq'=32,'head'=16] {'head'}, dimensions={0} | all-to-all | bytes 262144 | tf_op jit(solution)/shard_map/all_to_all | solution.py:416
  127.1 0.7 shard_map.127
  127.8 11.1 %all_to_all.34.arrived_ref = bf16[16,32,128]{2,1,0:T(8,128)(2,1)S(1)} all-to-all(bf16[16,32,128]{2,1,0:T(8,128)(2,1)S(1)} %shard_map.127), channel_id=1, replica_groups=mesh['seq'=32,'head'=16] {'head'}, dimensions={0} | all-to-all | bytes 262144 | tf_op jit(solution)/shard_map/all_to_all | solution.py:420
  138.9 0.7 shard_map.128
  (11 shorter events, 0.0 us)
Async XLA Ops:
  0.0 19.0 %collective-permute-start.2 = (bf16[64,2048]{1,0:T(8,128)(2,1)}, bf16[64,2048]{1,0:T(8,128)(2,1)S(1)}, u32[]{:S(2)}, u32[]{:S(2)}) collective-permute-start(bf16[64,2048]{1,0:T(8,128)(2,1)} %bitcast.19), channel_id=1, source_target_pairs={{0,2},{1,3},{2,0},{3,1},{4,6},{5,7},{6,4},{7,5},{8,10},{9,11},{10,... | collective-permute-start | bytes 786440 | tf_op jit(solution)/shard_map/ppermute | solution.py:347
  4.9 14.1 %collective-permute-start.1 = (bf16[64,2048]{1,0:T(8,128)(2,1)}, bf16[64,2048]{1,0:T(8,128)(2,1)S(1)}, u32[]{:S(2)}, u32[]{:S(2)}) collective-permute-start(bf16[64,2048]{1,0:T(8,128)(2,1)} %bitcast.20), channel_id=1, source_target_pairs={{0,3},{1,2},{2,1},{3,0},{4,7},{5,6},{6,5},{7,4},{8,11},{9,10},{10,... | collective-permute-start | bytes 786440 | tf_op jit(solution)/shard_map/ppermute | solution.py:347
  8.0 11.1 %collective-permute-start = (bf16[64,2048]{1,0:T(8,128)(2,1)}, bf16[64,2048]{1,0:T(8,128)(2,1)S(1)}, u32[]{:S(2)}, u32[]{:S(2)}) collective-permute-start(bf16[64,2048]{1,0:T(8,128)(2,1)} %bitcast.21), channel_id=1, source_target_pairs={{0,1},{1,0},{2,3},{3,2},{4,5},{5,4},{6,7},{7,6},{8,9},{9,8},{10,11... | collective-permute-start | bytes 786440 | tf_op jit(solution)/shard_map/ppermute | solution.py:347
  9.9 0.7 copy-start.6
  11.4 15.6 %all-to-all-start = ((bf16[16,32,128]{2,1,0:T(8,128)(2,1)}), bf16[16,32,128]{2,1,0:T(8,128)(2,1)S(1)}, u32[]{:S(2)}, u32[]{:S(2)}) async-start(bf16[16,32,128]{2,1,0:T(8,128)(2,1)} %shard_map.118), calls=%async_computation | async-start | bytes 262144 | tf_op jit(solution)/shard_map/all_to_all | solution.py:353
  18.9 1.3 copy-start.2
  19.0 1.3 copy-start.3
  19.0 1.3 copy-start.4
  19.0 1.3 copy-start.8
  19.0 1.3 copy-start.9
  19.0 1.3 copy-start.10
  26.9 39.8 %collective-permute-start.3 = (bf16[256,2048]{1,0:T(8,128)(2,1)S(1)}, bf16[256,2048]{1,0:T(8,128)(2,1)S(1)}, u32[]{:S(2)}, u32[]{:S(2)}) collective-permute-start(bf16[256,2048]{1,0:T(8,128)(2,1)S(1)} %pad_maximum_fusion.refs_0_), channel_id=1, source_target_pairs={{0,4},{1,5},{2,6},{3,7},{4,0},{5,1},{6,2},{7,3},{8,12},{9,13},{10,... | collective-permute-start | bytes 3145736 | tf_op jit(solution)/shard_map/ppermute | solution.py:347
  29.1 37.6 %collective-permute-start.4 = (bf16[256,2048]{1,0:T(8,128)(2,1)S(1)}, bf16[256,2048]{1,0:T(8,128)(2,1)S(1)}, u32[]{:S(2)}, u32[]{:S(2)}) collective-permute-start(bf16[256,2048]{1,0:T(8,128)(2,1)S(1)} %pad_maximum_fusion.refs_0_), channel_id=1, source_target_pairs={{0,12},{1,13},{2,14},{3,15},{4,8},{5,9},{6,10},{7,11},{8,4},{9,5},... | collective-permute-start | bytes 3145736 | tf_op jit(solution)/shard_map/ppermute | solution.py:347
  32.3 34.4 %collective-permute-start.5 = (bf16[256,2048]{1,0:T(8,128)(2,1)S(1)}, bf16[256,2048]{1,0:T(8,128)(2,1)S(1)}, u32[]{:S(2)}, u32[]{:S(2)}) collective-permute-start(bf16[256,2048]{1,0:T(8,128)(2,1)S(1)} %pad_maximum_fusion.refs_0_), channel_id=1, source_target_pairs={{0,8},{1,9},{2,10},{3,11},{4,12},{5,13},{6,14},{7,15},{8,0},{9,1},... | collective-permute-start | bytes 3145736 | tf_op jit(solution)/shard_map/ppermute | solution.py:347
  64.8 4.9 %collective-permute-start.6 = (bf16[16,32,128]{2,1,0:T(8,128)(2,1)S(1)}, bf16[16,32,128]{2,1,0:T(8,128)(2,1)S(1)}, u32[]{:S(2)}, u32[]{:S(2)}) collective-permute-start(bf16[16,32,128]{2,1,0:T(8,128)(2,1)S(1)} %all_to_all.30), channel_id=1, source_target_pairs={{0,16},{16,0},{32,48},{48,32},{64,80},{80,64},{96,112},{112,96},{1... | collective-permute-start | bytes 393224 | tf_op jit(solution)/shard_map/ppermute | solution.py:388
  74.0 6.7 %collective-permute-start.7 = (bf16[16,48,128]{2,1,0:T(8,128)(2,1)S(1)}, bf16[16,48,128]{2,1,0:T(8,128)(2,1)S(1)}, u32[]{:S(2)}, u32[]{:S(2)}) collective-permute-start(bf16[16,48,128]{2,1,0:T(8,128)(2,1)S(1)} %shard_map.123), channel_id=1, source_target_pairs={{0,16},{16,0},{32,48},{48,32},{64,80},{80,64},{96,112},{112,96},{1... | collective-permute-start | bytes 589832 | tf_op jit(solution)/shard_map/ppermute | solution.py:405
  80.7 23.2 %copy-start.5 = (bf16[64,1024]{1,0:T(8,128)(2,1)S(1)}, bf16[64,1024]{1,0:T(8,128)(2,1)}, u32[]{:S(2)}) copy-start(bf16[64,1024]{1,0:T(8,128)(2,1)} %w_ref.1) | copy-start | bytes 393220
  80.7 35.2 %copy-start.7 = (bf16[64,64]{1,0:T(8,128)(2,1)S(1)}, bf16[64,64]{1,0:T(8,128)(2,1)}, u32[]{:S(2)}) copy-start(bf16[64,64]{1,0:T(8,128)(2,1)} %lat_ref.3) | copy-start | bytes 24580
  80.7 46.3 %copy-start = (bf16[1024,256]{1,0:T(8,128)(2,1)S(1)}, bf16[1024,256]{1,0:T(8,128)(2,1)}, u32[]{:S(2)}) copy-start(bf16[1024,256]{1,0:T(8,128)(2,1)} %up_ref.1) | copy-start | bytes 1572868
  80.7 46.3 %copy-start.1 = (bf16[256,1024]{1,0:T(8,128)(2,1)S(1)}, bf16[256,1024]{1,0:T(8,128)(2,1)}, u32[]{:S(2)}) copy-start(bf16[256,1024]{1,0:T(8,128)(2,1)} %down_ref.1) | copy-start | bytes 1572868
  80.8 46.3 %copy-start.11 = (f32[1024]{0:T(1024)S(1)}, f32[1024]{0:T(1024)}, u32[]{:S(2)}) copy-start(f32[1024]{0:T(1024)} %param.21) | copy-start | bytes 12292

commit v7 on v6

--- a/solution.py
+++ b/solution.py
@@ -28,12 +28,11 @@
 TN = ((0,), (0,))
 
 
-def partners(seq_size, side, phase, step):
+def partners(seq_size, side, step):
     pairs = []
     for s in range(seq_size):
-        along_x = (s % 2 == 0) == (phase == 0)
         for place in range(side * side):
-            other = place ^ (step if along_x else side * step)
+            other = place ^ (side * step if s % 2 == 0 else step)
             pairs.append((s * side * side + place, s * side * side + other))
     return pairs
 
@@ -51,11 +50,9 @@
         out_ref[2 * g + 1] = jnp.where(low, pltpu.roll(a, 64, 1), b).astype(out_ref.dtype)
 
 
-def unpack_columns(ref):
+def unpack_columns(blocks):
     tops, bottoms = [], []
-    for g in range(ref.shape[0] // 2):
-        a = ref[2 * g].astype(F32)
-        b = ref[2 * g + 1].astype(F32)
+    for a, b in zip(blocks[::2], blocks[1::2]):
         low = low_half(a.shape)
         tops.append(jnp.where(low, a, pltpu.roll(b, 64, 1)))
         bottoms.append(jnp.where(low, pltpu.roll(a, 64, 1), b))
@@ -69,15 +66,35 @@
     return (rows * inverse * gain).astype(BF16)
 
 
-def latents_kernel(lat_ref, out_ref):
-    half = lat_ref.shape[0] // 2
-    packed = jnp.concatenate([lat_ref[:half, :], lat_ref[half:, :]], axis=1)
-    out_ref[...] = jnp.broadcast_to(packed[None], out_ref.shape)
+def context_kernel(ctx_any, lat_any, out_ref, ctx_ref, lat_ref, sems):
+    copies = [
+        pltpu.make_async_copy(lat_any, lat_ref, sems.at[0]),
+        pltpu.make_async_copy(ctx_any, ctx_ref, sems.at[1]),
+    ]
+    for copy in copies:
+        copy.start()
+    for copy in copies:
+        copy.wait()
+    count, height, width = out_ref.shape
+    rows, cols = lat_ref.shape
+    lat = lat_ref[...].astype(F32)
+    packed = jnp.concatenate([lat[: rows // 2], lat[rows // 2 :]], axis=1)
+    tail = jnp.concatenate([packed[8 * k : 8 * k + 8] for k in range(4)], axis=1).astype(BF16)
+
+    def fill(quarter_of):
+        for p in range(count):
+            q = quarter_of(p)
+            out_ref[p, :cols] = ctx_ref[:, q * width : q * width + width]
+            out_ref[p, cols:] = tail
+
+    core = lax.axis_index("seq") % 2
+    pl.when(core == 0)(lambda: fill(lambda p: p // 4))
+    pl.when(core == 1)(lambda: fill(lambda p: p % 4))
 
 
 def prepare_kernel(*refs):
-    given, outs, held, scratch, sems = refs[:6], refs[6:10], refs[10:16], refs[16], refs[17]
-    w_ref, all_ref, kp_ref, pos_ref = outs
+    given, outs, held, sems = refs[:6], refs[6:9], refs[9:15], refs[15]
+    all_ref, kp_ref, pos_ref = outs
     copies = [pltpu.make_async_copy(a, b, sems.at[i]) for i, (a, b) in enumerate(zip(given, held))]
     for copy in copies:
         copy.start()
@@ -87,15 +104,14 @@
     seq_place, place = lax.axis_index("seq"), lax.axis_index("head")
     plane, core = seq_place // 2, seq_place % 2
     weights = jnp.concatenate([wq_ref[...], wk_ref[...], wv_ref[...]], axis=0).astype(F32)
-    weights = weights * gain_ref[...]
-    all_ref[...] = weights.astype(BF16)
-    scratch[...] = weights[64:].T.reshape(scratch.shape)
-    for i in range(w_ref.shape[0]):
-        blocks = [scratch[place ^ jnp.where(core == 0, 4 * STEPS[i] + STEPS[j], 4 * STEPS[j] + STEPS[i])] for j in range(4)]
-        w_ref[i] = jnp.concatenate(blocks, axis=0).T.astype(BF16)
-
-    for i in range(ctx_ref.shape[0]):
-        kp_ref[:, 128 * i : 128 * i + 128] = ctx_ref[i : i + 1, :]
+    all_ref[...] = (weights * gain_ref[...]).astype(BF16)
+    quarter = jnp.where(core == 0, place // 4, place % 4)
+    each = ctx_ref.shape[0] // 4
+    for i in range(4):
+        for r in range(each):
+            first = 128 * (each * i + r)
+            row = (quarter ^ STEPS[i]) * each + r
+            kp_ref[:, first : first + 128] = ctx_ref[pl.ds(row, 1), :]
     own = lat_ref[pl.ds(plane, 1), :]
     own = jnp.where(core == 0, own, pltpu.roll(own, 64, 1))
     last = 128 * ctx_ref.shape[0]
@@ -114,8 +130,14 @@
             pos_ref[k, 32 * z : 32 * z + 32] = jnp.broadcast_to(part[:, lane : lane + 1], (32, 128))
 
 
-def queries_kernel(lat_ref, w_ref, q_ref, kv_ref):
-    rows = unpack_columns(lat_ref)
+def queries_kernel(arrived_ref, w_ref, q_ref, kv_ref):
+    blocks = []
+    for p in range(arrived_ref.shape[0]):
+        tail = arrived_ref[p, 64:].astype(F32)
+        blocks.append(
+            jnp.concatenate([tail[:, 128 * k : 128 * k + 128] for k in range(4)], axis=0)
+        )
+    rows = unpack_columns(blocks)
     inverse = lax.rsqrt(jnp.mean(rows * rows, axis=-1, keepdims=True) + EPSILON)
     normed = (rows * inverse).astype(BF16)
     q = dot(normed, w_ref[:64], NT).astype(BF16).astype(F32) * HD ** (-0.5)
@@ -127,33 +149,26 @@
 
 
 def keys_kernel(*refs):
-    *line_refs, w_ref, lat_ref, ka_ref, kb_ref, va_ref, vb_ref, held, sems = refs
-    tokens = line_refs[0].shape[1]
-    width = 512
-    copies = []
-    for c in range(tokens // width):
-        cols = slice(c * width, c * width + width)
-        copies.append(
-            [
-                pltpu.make_async_copy(line.at[:, cols], held.at[i, :, cols], sems.at[c, i])
-                for i, line in enumerate(line_refs)
-            ]
-        )
-        for copy in copies[c]:
-            copy.start()
-    put_keys(lat_ref[...], slice(tokens, tokens + 128), ka_ref, kb_ref, va_ref, vb_ref)
-    for c in range(tokens // width):
-        cols = slice(c * width, c * width + width)
-        total = jnp.zeros((128, width), F32)
-        squares = jnp.zeros((1, width), F32)
-        for i in range(len(line_refs)):
-            copies[c][i].wait()
-            piece = held[i, :, cols]
-            total = total + dot(w_ref[i], piece, NN)
-            wide = piece.astype(F32)
-            squares = squares + jnp.sum(wide * wide, axis=0, keepdims=True)
+    *quarter_refs, w_ref, lat_ref, ka_ref, kb_ref, va_ref, vb_ref, held, sems = refs
+    width = quarter_refs[0].shape[1]
+    copies = [
+        pltpu.make_async_copy(quarter, held.at[i], sems.at[i])
+        for i, quarter in enumerate(quarter_refs)
+    ]
+    for copy in copies:
+        copy.start()
+    last = width * len(copies)
+    put_keys(lat_ref[...], slice(last, last + 128), ka_ref, kb_ref, va_ref, vb_ref)
+    weights = w_ref[64:]
+    for i, copy in enumerate(copies):
+        copy.wait()
+        piece = held[i]
+        wide = piece.astype(F32)
+        squares = jnp.sum(wide * wide, axis=0, keepdims=True)
         inverse = lax.rsqrt(squares * (1.0 / 1024) + EPSILON)
-        put_keys((total * inverse).astype(BF16), cols, ka_ref, kb_ref, va_ref, vb_ref)
+        both = (dot(weights, piece, NN) * inverse).astype(BF16)
+        cols = slice(i * width, i * width + width)
+        put_keys(both, cols, ka_ref, kb_ref, va_ref, vb_ref)
 
 
 def put_keys(both, cols, ka_ref, kb_ref, va_ref, vb_ref):
@@ -189,7 +204,7 @@
     first = once.astype(BF16).astype(F32)
     second = (once - first).astype(BF16).astype(F32)
     third = once - first - second
-    rest = jnp.zeros((13, 128), F32)
+    rest = jnp.zeros((5, 128), F32)
     out_ref[group, 32:] = jnp.concatenate([first, second, third, rest], axis=0).astype(BF16)
 
 
@@ -291,7 +306,9 @@
 
 
 def mlp_kernel(arrived_ref, gain_ref, up_ref, down_ref, out_ref):
-    normed = normalize(unpack_columns(arrived_ref), gain_ref[...])
+    normed = normalize(
+        unpack_columns([arrived_ref[p].astype(F32) for p in range(arrived_ref.shape[0])]), gain_ref[...]
+    )
     hidden = jax.nn.gelu(dot(normed, up_ref[...], NN), approximate=True).astype(BF16)
     share = dot(hidden, down_ref[...], NN)
     half = share.shape[0] // 2
@@ -343,19 +360,23 @@
     key_count = tokens + 2 * lat_rows
     rows = planes * half
 
-    def swap_lines(piece, phase, step):
-        return lax.ppermute(piece, BOTH, partners(seq_size, side, phase, step))
-
-    own = context.T
-    line = jnp.concatenate([own] + [swap_lines(own, 0, step) for step in STEPS[1:]], axis=0)
-    line, input_gain = lax.optimization_barrier((line, input_gain))
-    copies = call(latents_kernel, [((head_size, *block), BF16)])(latents)
-    lat_blocks = lax.all_to_all(copies, "head", 0, 0)
     anywhere = pl.BlockSpec(memory_space=pl.ANY)
-    prepared = call(
+    quarter = tokens // side
+    sent = call(
+        context_kernel,
+        [((head_size, cols + 8, quarter), BF16)],
+        in_specs=[anywhere] * 2,
+        scratch_shapes=[
+            pltpu.VMEM((cols, tokens), BF16),
+            pltpu.VMEM((lat_rows, cols), BF16),
+            pltpu.SemaphoreType.DMA((2,)),
+        ],
+    )(context.T, latents)
+    first = lax.all_to_all(sent, "head", 0, 0)
+    first, input_gain = lax.optimization_barrier((first, input_gain))
+    all_weights, key_pos, query_pos = call(
         prepare_kernel,
         [
-            ((side, 2 * cols, side * cols), BF16),
             ((3 * cols, head_size * cols), BF16),
             ((1, key_count), jnp.int32),
             ((4, rows, 2 * cols), jnp.int32),
@@ -366,7 +387,6 @@
             pltpu.VMEM((1, head_size * cols), F32),
             pltpu.VMEM((tokens // 128, 128), jnp.int32),
             pltpu.VMEM((planes, 2 * lat_rows), jnp.int32),
-            pltpu.VMEM((head_size, cols, 2 * cols), F32),
             pltpu.SemaphoreType.DMA((6,)),
         ],
     )(
@@ -377,13 +397,14 @@
         ctx_pos.reshape(-1, 128),
         lat_pos.reshape(-1, 2 * lat_rows),
     )
-    line, lat_blocks, prepared = lax.optimization_barrier((line, lat_blocks, prepared))
-    key_weights, all_weights, key_pos, query_pos = prepared
-    lines = [line] + [swap_lines(line, 1, step) for step in STEPS[1:]]
+    own = first[:, :cols].reshape(head_size * cols, quarter)
+    quarters = [own] + [
+        lax.ppermute(own, BOTH, partners(seq_size, side, step)) for step in STEPS[1:]
+    ]
 
     queries, latent_kv = call(
         queries_kernel, [((planes, *block), BF16), ((2 * cols, 2 * lat_rows), BF16)]
-    )(lat_blocks, all_weights)
+    )(first, all_weights)
     own_queries = lax.all_to_all(queries, "seq", 0, 0, axis_index_groups=along_z)
     other_queries = lax.ppermute(own_queries, "seq", swap)
 
@@ -393,12 +414,12 @@
         cost=10**9,
         in_specs=[anywhere] * side + [vmem] * 2,
         scratch_shapes=[
-            pltpu.VMEM((side, side * cols, tokens), BF16),
-            pltpu.SemaphoreType.DMA((4, side)),
+            pltpu.VMEM((side, head_size * cols, quarter), BF16),
+            pltpu.SemaphoreType.DMA((side,)),
         ],
-    )(*lines, key_weights, latent_kv)
-
-    message = (planes, 48, 2 * cols)
+    )(*quarters, all_weights, latent_kv)
+
+    message = (planes, 40, 2 * cols)
     to_sibling = call(other_kernel, [(message, BF16)])(
         other_queries.reshape(rows, -1), query_pos, key_pos, *operands
     )

time: 140 us -> 139 us (level)
  blocking collectives: 83.7 us -> 107 us
  starting transfers between devices: 31.6 us -> 14.3 us
  waiting for transfers between devices: 5.28 us -> 0.01 us
  Pallas kernels: 16.7 us -> 15.2 us
    all_to_all x0 -> x1, blocking collectives: none -> 25.4 us  [body(): first = lax.all_to_all(sent, 'head', 0, 0)]
    ppermute x6 -> x3, starting transfers between devices: 19.7 us -> 9.95 us  [body(): lax.ppermute(own, BOTH, partners(seq_size, side, step))]
    all_to_all x1 -> x0, starting transfers between devices: 7.56 us -> none  [body(): lat_blocks = lax.all_to_all(copies, 'head', 0, 0)]
    all_to_all x1 -> x0, waiting for transfers between devices: 5.25 us -> none  [body(): lat_blocks = lax.all_to_all(copies, 'head', 0, 0)]
    all_to_all x1, blocking collectives: 22.7 us -> 20 us  [body(): arrived = lax.all_to_all(joined, 'seq', 0, 0, axis_index_groups=along_z)]
  transfers between devices with their start and end apart: 9 -> 5, of which waited for: 1 -> 0; matrix products, arithmetic and copies ran while one was open for 1% -> 0% of each run, Pallas kernels for 7% -> 6%
where the time goes in v7:
time: 139 us; the launch traced here: 138 us
  blocking collectives  107 us (77%)
  Pallas kernels  15.2 us (11%)
  starting transfers between devices  14.3 us (10%)
  local copies, waits for them, and re-layouts  1.83 us (1%)
    all_to_all x1, blocking collectives, body(): lax.all_to_all(queries, 'seq', 0, 0, axis_index_groups=along_z)  27.7 us
    all_to_all x1, blocking collectives, body(): first = lax.all_to_all(sent, 'head', 0, 0)  25.4 us
    all_to_all x2, blocking collectives, body(): arrived = lax.all_to_all(shares, 'head', 0, 0)  22.4 us
    all_to_all x1, blocking collectives, body(): arrived = lax.all_to_all(joined, 'seq', 0, 0, axis_index_groups=along_z)  20 us
    all_to_all x1, blocking collectives, body(): arrived = lax.all_to_all(copies, 'head', 0, 0)  11.1 us
    ppermute x3, starting transfers between devices, body(): lax.ppermute(own, BOTH, partners(seq_size, side, step))  9.95 us
    pallas_call x1, Pallas kernels, body(): call(other_kernel, [(message, BF16)])  4.33 us
    pallas_call x1, Pallas kernels, body(): call(own_kernel, [((rows, 2 * cols), F32)] * 2)  4.29 us
  transfers between devices with their start and end apart: 5, of which 0 were waited for; matrix products, arithmetic and copies ran while one was open for 0% of the time, Pallas kernels for 6%

profile of v7, /device:TPU:32, one launch (start us, length us, event | category | flops | bytes accessed | tf_op | source)
XLA Modules:
  0.0 138.2 jit_solution(2217842190510396358)
XLA Ops:
  0.0 0.9 copy-done.2
  1.0 0.7 copy-done.7
  1.7 0.1 shard_map.118
  1.8 25.4 %all_to_all.30.arrived_ref = bf16[16,72,512]{2,1,0:T(8,128)(2,1)S(1)} all-to-all(bf16[16,72,512]{2,1,0:T(8,128)(2,1)S(1)} %shard_map.118), channel_id=1, replica_groups=mesh['seq'=32,'head'=16] {'head'}, dimensions={0} | all-to-all | bytes 2359296 | tf_op jit(solution)/shard_map/all_to_all | solution.py:375
  27.3 0.0 copy-start.10
  27.3 0.0 copy-start.11
  27.3 0.1 slice.3
  27.4 2.3 %collective-permute-start = (bf16[1024,512]{1,0:T(8,128)(2,1)S(1)}, bf16[1024,512]{1,0:T(8,128)(2,1)S(1)}, u32[]{:S(2)}, u32[]{:S(2)}) collective-permute-start(bf16[1024,512]{1,0:T(8,128)(2,1)S(1)} %bitcast.11), channel_id=1, source_target_pairs={{0,4},{1,5},{2,6},{3,7},{4,0},{5,1},{6,2},{7,3},{8,12},{9,13},{10,... | collective-permute-start | bytes 3145736 | tf_op jit(solution)/shard_map/ppermute | solution.py:402
  29.7 3.2 %collective-permute-start.1 = (bf16[1024,512]{1,0:T(8,128)(2,1)S(1)}, bf16[1024,512]{1,0:T(8,128)(2,1)S(1)}, u32[]{:S(2)}, u32[]{:S(2)}) collective-permute-start(bf16[1024,512]{1,0:T(8,128)(2,1)S(1)} %bitcast.12), channel_id=1, source_target_pairs={{0,12},{1,13},{2,14},{3,15},{4,8},{5,9},{6,10},{7,11},{8,4},{9,5},... | collective-permute-start | bytes 3145736 | tf_op jit(solution)/shard_map/ppermute | solution.py:402
  32.9 4.5 %collective-permute-start.2 = (bf16[1024,512]{1,0:T(8,128)(2,1)S(1)}, bf16[1024,512]{1,0:T(8,128)(2,1)S(1)}, u32[]{:S(2)}, u32[]{:S(2)}) collective-permute-start(bf16[1024,512]{1,0:T(8,128)(2,1)S(1)} %bitcast.13), channel_id=1, source_target_pairs={{0,8},{1,9},{2,10},{3,11},{4,12},{5,13},{6,14},{7,15},{8,0},{9,1},... | collective-permute-start | bytes 3145736 | tf_op jit(solution)/shard_map/ppermute | solution.py:402
  37.4 0.0 copy-done.3
  37.4 0.0 copy-done.4
  37.4 0.0 copy-done.5
  37.4 0.0 copy-done.9
  37.4 0.0 copy-done.10
  37.4 0.0 copy-done.11
  37.4 1.2 shard_map.119
  38.7 0.5 shard_map.120
  39.1 27.7 %all_to_all.31 = bf16[16,32,128]{2,1,0:T(8,128)(2,1)S(1)} all-to-all(bf16[16,32,128]{2,1,0:T(8,128)(2,1)S(1)} %get-tuple-element.23), channel_id=1, replica_groups={{0,32,64,96,128,160,192,224,256,288,320,352,384,416,448,480},{16,48,80,..., dimensions={0} | all-to-all | bytes 262144 | tf_op jit(solution)/shard_map/all_to_all | solution.py:408
  66.8 1.9 %collective-permute-start.3 = (bf16[16,32,128]{2,1,0:T(8,128)(2,1)S(1)}, bf16[16,32,128]{2,1,0:T(8,128)(2,1)S(1)}, u32[]{:S(2)}, u32[]{:S(2)}) collective-permute-start(bf16[16,32,128]{2,1,0:T(8,128)(2,1)S(1)} %all_to_all.31), channel_id=1, source_target_pairs={{0,16},{16,0},{32,48},{48,32},{64,80},{80,64},{96,112},{112,96},{1... | collective-permute-start | bytes 393224 | tf_op jit(solution)/shard_map/ppermute | solution.py:409
  68.7 0.0 collective-permute-done.refs_1_
  68.8 0.0 collective-permute-done.1.refs_2_
  68.8 0.0 collective-permute-done.2.refs_3_
  68.8 2.2 %shard_map.121 = (bf16[128,2176]{1,0:T(8,128)(2,1)S(1)}, bf16[128,2176]{1,0:T(8,128)(2,1)S(1)}, bf16[2176,128]{1,0:T(8,128)(2,1)S(1)}, bf16[2176,128]{1,0:T(8,128)(2,1)S(1)}) custom-call(bf16[1024,512]{1,0:T(8,128)(2,1)S(1)} %bitcast.14, bf16[1024,512]{1,0:T(8,128)(2,1)S(1)} %collective-permute-done.refs_1_, ...), custom_call_target="tpu_custom_call" | custom-call | flops 1000000000 | bytes 1000000000 | tf_op jit(solution)/shard_map/pallas_call | solution.py:411
  71.0 0.0 collective-permute-done.3
  71.0 4.3 %shard_map.123 = bf16[16,40,128]{2,1,0:T(8,128)(2,1)S(1)} custom-call(bf16[512,128]{1,0:T(8,128)(2,1)S(1)} %bitcast.20, s32[4,512,128]{2,1,0:T(8,128)S(1)} %get-tuple-element.24.pos_ref, s32[1,2176]{1,0:T(1,128)S(1)} %get-tuple-element.25.kp_ref, bf16[128,2176]{1,0:T(8,128)(2,1)S(1)} %get-tuple-element.27.ka_ref, ...), custom_call_target="tpu_custom_call" | custom-call | flops 1000 | bytes 1000 | tf_op jit(solution)/shard_map/pallas_call | solution.py:423
  75.3 2.4 %collective-permute-start.4 = (bf16[16,40,128]{2,1,0:T(8,128)(2,1)S(1)}, bf16[16,40,128]{2,1,0:T(8,128)(2,1)S(1)}, u32[]{:S(2)}, u32[]{:S(2)}) collective-permute-start(bf16[16,40,128]{2,1,0:T(8,128)(2,1)S(1)} %shard_map.123), channel_id=1, source_target_pairs={{0,16},{16,0},{32,48},{48,32},{64,80},{80,64},{96,112},{112,96},{1... | collective-permute-start | bytes 491528 | tf_op jit(solution)/shard_map/ppermute | solution.py:426
  77.8 4.3 %shard_map.122 = (f32[512,128]{1,0:T(8,128)S(1)}, f32[512,128]{1,0:T(8,128)S(1)}) custom-call(bf16[512,128]{1,0:T(8,128)(2,1)S(1)} %bitcast.15, s32[4,512,128]{2,1,0:T(8,128)S(1)} %get-tuple-element.24.pos_ref, s32[1,2176]{1,0:T(1,128)S(1)} %get-tuple-element.25.kp_ref, bf16[128,2176]{1,0:T(8,128)(2,1)S(1)} %get-tuple-element.27.ka_ref, ...), custom_call_target="tpu_custom_call" | custom-call | flops 1000 | bytes 1000 | tf_op jit(solution)/shard_map/pallas_call | solution.py:427
  82.1 0.0 copy-start.6
  82.1 0.0 copy-start.8
  82.1 0.0 copy-start
  82.1 0.0 copy-start.1
  82.1 0.0 copy-start.12
  82.1 0.0 collective-permute-done.4.arrived_ref
  82.1 0.4 shard_map.124
  82.6 20.0 %all_to_all.32.arrived_ref = bf16[16,40,128]{2,1,0:T(8,128)(2,1)S(1)} all-to-all(bf16[16,40,128]{2,1,0:T(8,128)(2,1)S(1)} %shard_map.124), channel_id=1, replica_groups={{0,32,64,96,128,160,192,224,256,288,320,352,384,416,448,480},{16,48,80,..., dimensions={0} | all-to-all | bytes 327680 | tf_op jit(solution)/shard_map/all_to_all | solution.py:431
  102.6 0.0 copy-done.6
  102.6 0.7 shard_map.125
  103.2 11.4 %all_to_all.33.arrived_ref = bf16[16,32,128]{2,1,0:T(8,128)(2,1)S(1)} all-to-all(bf16[16,32,128]{2,1,0:T(8,128)(2,1)S(1)} %shard_map.125), channel_id=1, replica_groups=mesh['seq'=32,'head'=16] {'head'}, dimensions={0} | all-to-all | bytes 262144 | tf_op jit(solution)/shard_map/all_to_all | solution.py:433
  114.6 0.0 copy-done.8
  114.6 0.1 shard_map.126
  114.7 11.1 %all_to_all.34.arrived_ref = bf16[16,32,128]{2,1,0:T(8,128)(2,1)S(1)} all-to-all(bf16[16,32,128]{2,1,0:T(8,128)(2,1)S(1)} %get-tuple-element.33), channel_id=1, replica_groups=mesh['seq'=32,'head'=16] {'head'}, dimensions={0} | all-to-all | bytes 262144 | tf_op jit(solution)/shard_map/all_to_all | solution.py:437
  125.7 0.0 copy-done
  125.7 0.0 copy-done.1
  125.7 0.0 copy-done.12
  125.7 0.7 shard_map.127
  126.5 11.1 %all_to_all.35.arrived_ref = bf16[16,32,128]{2,1,0:T(8,128)(2,1)S(1)} all-to-all(bf16[16,32,128]{2,1,0:T(8,128)(2,1)S(1)} %shard_map.127), channel_id=1, replica_groups=mesh['seq'=32,'head'=16] {'head'}, dimensions={0} | all-to-all | bytes 262144 | tf_op jit(solution)/shard_map/all_to_all | solution.py:441
  137.5 0.7 shard_map.128
  (6 shorter events, 0.0 us)
Async XLA Ops:
  0.0 0.9 copy-start.2
  1.0 0.7 copy-start.7
  27.3 10.1 %copy-start.3 = (bf16[1024,64]{0,1:T(8,128)(2,1)S(1)}, bf16[1024,64]{0,1:T(8,128)(2,1)}, u32[]{:S(2)}) copy-start(bf16[1024,64]{0,1:T(8,128)(2,1)} %param.17) | copy-start | bytes 393220
  27.3 10.1 %copy-start.4 = (bf16[1024,64]{0,1:T(8,128)(2,1)S(1)}, bf16[1024,64]{0,1:T(8,128)(2,1)}, u32[]{:S(2)}) copy-start(bf16[1024,64]{0,1:T(8,128)(2,1)} %param.18) | copy-start | bytes 393220
  27.3 10.1 %copy-start.5 = (bf16[1024,64]{0,1:T(8,128)(2,1)S(1)}, bf16[1024,64]{0,1:T(8,128)(2,1)}, u32[]{:S(2)}) copy-start(bf16[1024,64]{0,1:T(8,128)(2,1)} %param.19) | copy-start | bytes 393220
  27.3 10.1 %copy-start.9 = (s32[2048]{0:T(1024)S(1)}, s32[2048]{0:T(1024)}, u32[]{:S(2)}) copy-start(s32[2048]{0:T(1024)} %param.14) | copy-start | bytes 24580
  27.3 10.1 %copy-start.10 = (s32[2048]{0:T(1024)S(1)}, s32[2048]{0:T(1024)}, u32[]{:S(2)}) copy-start(s32[2048]{0:T(1024)} %param.15) | copy-start | bytes 24580
  27.3 10.1 %copy-start.11 = (f32[1024]{0:T(1024)S(1)}, f32[1024]{0:T(1024)}, u32[]{:S(2)}) copy-start(f32[1024]{0:T(1024)} %param.16) | copy-start | bytes 12292
  27.4 41.3 %collective-permute-start = (bf16[1024,512]{1,0:T(8,128)(2,1)S(1)}, bf16[1024,512]{1,0:T(8,128)(2,1)S(1)}, u32[]{:S(2)}, u32[]{:S(2)}) collective-permute-start(bf16[1024,512]{1,0:T(8,128)(2,1)S(1)} %bitcast.11), channel_id=1, source_target_pairs={{0,4},{1,5},{2,6},{3,7},{4,0},{5,1},{6,2},{7,3},{8,12},{9,13},{10,... | collective-permute-start | bytes 3145736 | tf_op jit(solution)/shard_map/ppermute | solution.py:402
  29.7 39.0 %collective-permute-start.1 = (bf16[1024,512]{1,0:T(8,128)(2,1)S(1)}, bf16[1024,512]{1,0:T(8,128)(2,1)S(1)}, u32[]{:S(2)}, u32[]{:S(2)}) collective-permute-start(bf16[1024,512]{1,0:T(8,128)(2,1)S(1)} %bitcast.12), channel_id=1, source_target_pairs={{0,12},{1,13},{2,14},{3,15},{4,8},{5,9},{6,10},{7,11},{8,4},{9,5},... | collective-permute-start | bytes 3145736 | tf_op jit(solution)/shard_map/ppermute | solution.py:402
  32.9 35.9 %collective-permute-start.2 = (bf16[1024,512]{1,0:T(8,128)(2,1)S(1)}, bf16[1024,512]{1,0:T(8,128)(2,1)S(1)}, u32[]{:S(2)}, u32[]{:S(2)}) collective-permute-start(bf16[1024,512]{1,0:T(8,128)(2,1)S(1)} %bitcast.13), channel_id=1, source_target_pairs={{0,8},{1,9},{2,10},{3,11},{4,12},{5,13},{6,14},{7,15},{8,0},{9,1},... | collective-permute-start | bytes 3145736 | tf_op jit(solution)/shard_map/ppermute | solution.py:402
  66.8 4.2 %collective-permute-start.3 = (bf16[16,32,128]{2,1,0:T(8,128)(2,1)S(1)}, bf16[16,32,128]{2,1,0:T(8,128)(2,1)S(1)}, u32[]{:S(2)}, u32[]{:S(2)}) collective-permute-start(bf16[16,32,128]{2,1,0:T(8,128)(2,1)S(1)} %all_to_all.31), channel_id=1, source_target_pairs={{0,16},{16,0},{32,48},{48,32},{64,80},{80,64},{96,112},{112,96},{1... | collective-permute-start | bytes 393224 | tf_op jit(solution)/shard_map/ppermute | solution.py:409
  75.3 6.8 %collective-permute-start.4 = (bf16[16,40,128]{2,1,0:T(8,128)(2,1)S(1)}, bf16[16,40,128]{2,1,0:T(8,128)(2,1)S(1)}, u32[]{:S(2)}, u32[]{:S(2)}) collective-permute-start(bf16[16,40,128]{2,1,0:T(8,128)(2,1)S(1)} %shard_map.123), channel_id=1, source_target_pairs={{0,16},{16,0},{32,48},{48,32},{64,80},{80,64},{96,112},{112,96},{1... | collective-permute-start | bytes 491528 | tf_op jit(solution)/shard_map/ppermute | solution.py:426
  82.1 20.5 %copy-start.6 = (bf16[64,1024]{1,0:T(8,128)(2,1)S(1)}, bf16[64,1024]{1,0:T(8,128)(2,1)}, u32[]{:S(2)}) copy-start(bf16[64,1024]{1,0:T(8,128)(2,1)} %w_ref.1) | copy-start | bytes 393220
  82.1 32.5 %copy-start.8 = (bf16[64,64]{1,0:T(8,128)(2,1)S(1)}, bf16[64,64]{1,0:T(8,128)(2,1)}, u32[]{:S(2)}) copy-start(bf16[64,64]{1,0:T(8,128)(2,1)} %lat_ref.1) | copy-start | bytes 24580
  82.1 43.7 %copy-start = (bf16[1024,256]{1,0:T(8,128)(2,1)S(1)}, bf16[1024,256]{1,0:T(8,128)(2,1)}, u32[]{:S(2)}) copy-start(bf16[1024,256]{1,0:T(8,128)(2,1)} %up_ref.1) | copy-start | bytes 1572868
  82.1 43.7 %copy-start.1 = (bf16[256,1024]{1,0:T(8,128)(2,1)S(1)}, bf16[256,1024]{1,0:T(8,128)(2,1)}, u32[]{:S(2)}) copy-start(bf16[256,1024]{1,0:T(8,128)(2,1)} %down_ref.1) | copy-start | bytes 1572868
  82.1 43.6 %copy-start.12 = (f32[1024]{0:T(1024)S(1)}, f32[1024]{0:T(1024)}, u32[]{:S(2)}) copy-start(f32[1024]{0:T(1024)} %param.21) | copy-start | bytes 12292

commit v8 on v7

--- a/solution.py
+++ b/solution.py
@@ -93,17 +93,17 @@
 
 
 def prepare_kernel(*refs):
-    given, outs, held, sems = refs[:6], refs[6:9], refs[9:15], refs[15]
+    given, outs, held, sems = refs[:5], refs[5:8], refs[8:13], refs[13]
     all_ref, kp_ref, pos_ref = outs
     copies = [pltpu.make_async_copy(a, b, sems.at[i]) for i, (a, b) in enumerate(zip(given, held))]
     for copy in copies:
         copy.start()
     for copy in copies:
         copy.wait()
-    wq_ref, wk_ref, wv_ref, gain_ref, ctx_ref, lat_ref = held
+    wk_ref, wv_ref, gain_ref, ctx_ref, lat_ref = held
     seq_place, place = lax.axis_index("seq"), lax.axis_index("head")
     plane, core = seq_place // 2, seq_place % 2
-    weights = jnp.concatenate([wq_ref[...], wk_ref[...], wv_ref[...]], axis=0).astype(F32)
+    weights = jnp.concatenate([wk_ref[...], wv_ref[...]], axis=0).astype(F32)
     all_ref[...] = (weights * gain_ref[...]).astype(BF16)
     quarter = jnp.where(core == 0, place // 4, place % 4)
     each = ctx_ref.shape[0] // 4
@@ -130,21 +130,19 @@
             pos_ref[k, 32 * z : 32 * z + 32] = jnp.broadcast_to(part[:, lane : lane + 1], (32, 128))
 
 
-def queries_kernel(arrived_ref, w_ref, q_ref, kv_ref):
+def queries_kernel(arrived_ref, wq_ref, wk_ref, wv_ref, gain_ref, q_ref, kv_ref):
     blocks = []
     for p in range(arrived_ref.shape[0]):
         tail = arrived_ref[p, 64:].astype(F32)
         blocks.append(
             jnp.concatenate([tail[:, 128 * k : 128 * k + 128] for k in range(4)], axis=0)
         )
-    rows = unpack_columns(blocks)
-    inverse = lax.rsqrt(jnp.mean(rows * rows, axis=-1, keepdims=True) + EPSILON)
-    normed = (rows * inverse).astype(BF16)
-    q = dot(normed, w_ref[:64], NT).astype(BF16).astype(F32) * HD ** (-0.5)
+    normed = normalize(unpack_columns(blocks), gain_ref[...])
+    q = dot(normed, wq_ref[...], NT).astype(BF16).astype(F32) * HD ** (-0.5)
     half = q.shape[0] // 2
     packed = jnp.concatenate([q[:half], q[half:]], axis=1).astype(BF16)
     q_ref[...] = jnp.broadcast_to(packed[None], q_ref.shape)
-    both = dot(w_ref[64:], normed, NT)
+    both = jnp.concatenate([dot(wk_ref[...], normed, NT), dot(wv_ref[...], normed, NT)], axis=0)
     kv_ref[...] = jnp.concatenate([both, jnp.zeros_like(both)], axis=1).astype(BF16)
 
 
@@ -159,7 +157,7 @@
         copy.start()
     last = width * len(copies)
     put_keys(lat_ref[...], slice(last, last + 128), ka_ref, kb_ref, va_ref, vb_ref)
-    weights = w_ref[64:]
+    weights = w_ref[...]
     for i, copy in enumerate(copies):
         copy.wait()
         piece = held[i]
@@ -181,19 +179,39 @@
     vb_ref[cols, :] = jnp.concatenate([ones, values.astype(F32)], axis=0).T.astype(BF16)
 
 
-def attend_rows(q, pos_a, pos_b, kp, ka_ref, kb_ref, va_ref, vb_ref):
-    def one(k_ref, v_ref, pos):
-        scores = jnp.where(kp <= pos, dot(q, k_ref[...], NN), NEGATIVE)
+def attend_all(q_ref, pos_ref, first, kp_ref, key_refs, value_refs, put):
+    step = 256
+    kp = kp_ref[...]
+    pieces = [(i, h) for i in range(0, q_ref.shape[0], step) for h in range(2)]
+
+    def scores_of(piece):
+        i, h = piece
+        return dot(q_ref[i : i + step], key_refs[h][...], NN)
+
+    def finish(piece, weights, top):
+        i, h = piece
+        done[h] = (dot(weights, value_refs[h][...], NN), top)
+        if h == 1:
+            (out_a, top_a), (out_b, top_b) = done
+            low = low_half(out_a.shape)
+            above = jnp.where(low, out_a, out_b)
+            below = jnp.maximum(pltpu.roll(jnp.where(low, out_b, out_a), 64, 1), 1e-30)
+            put(i, above / below, jnp.where(low, top_a, top_b) + jnp.log(below))
+
+    done = [None, None]
+    waiting = None
+    scores = scores_of(pieces[0])
+    for n, (i, h) in enumerate(pieces):
+        following = scores_of(pieces[n + 1]) if n + 1 < len(pieces) else None
+        visible = kp <= pos_ref[first + h, i : i + step, 0:1]
+        scores = jnp.where(visible, scores, NEGATIVE)
         top = jnp.maximum(jnp.max(scores, axis=1, keepdims=True), LOWEST)
         weights = jnp.exp(scores - top).astype(BF16)
-        return dot(weights, v_ref[...], NN), top
-
-    out_a, top_a = one(ka_ref, va_ref, pos_a)
-    out_b, top_b = one(kb_ref, vb_ref, pos_b)
-    low = low_half(out_a.shape)
-    above = jnp.where(low, out_a, out_b)
-    below = jnp.maximum(pltpu.roll(jnp.where(low, out_b, out_a), 64, 1), 1e-30)
-    return above / below, jnp.where(low, top_a, top_b) + jnp.log(below)
+        if waiting is not None:
+            finish(*waiting)
+        waiting = ((i, h), weights, top)
+        scores = following
+    finish(*waiting)
 
 
 def put_message(mixed, level, out_ref, group):
@@ -229,44 +247,20 @@
 
 
 def other_kernel(q_ref, pos_ref, kp_ref, ka_ref, kb_ref, va_ref, vb_ref, out_ref):
-    kp = kp_ref[...]
-
-    @pl.loop(0, q_ref.shape[0] // 256)
-    def _(i):
-        rows = pl.ds(pl.multiple_of(i * 256, 256), 256)
-        mixed, level = attend_rows(
-            q_ref[rows, :],
-            pos_ref[0, rows, 0:1],
-            pos_ref[1, rows, 0:1],
-            kp,
-            ka_ref,
-            kb_ref,
-            va_ref,
-            vb_ref,
-        )
-        for g in range(8):
+    def put(row, mixed, level):
+        for g in range(mixed.shape[0] // 32):
             part = slice(32 * g, 32 * g + 32)
-            put_message(mixed[part], level[part], out_ref, i * 8 + g)
+            put_message(mixed[part], level[part], out_ref, row // 32 + g)
+
+    attend_all(q_ref, pos_ref, 0, kp_ref, (ka_ref, kb_ref), (va_ref, vb_ref), put)
 
 
 def own_kernel(q_ref, pos_ref, kp_ref, ka_ref, kb_ref, va_ref, vb_ref, mix_ref, lev_ref):
-    kp = kp_ref[...]
-
-    @pl.loop(0, q_ref.shape[0] // 256)
-    def _(i):
-        rows = pl.ds(pl.multiple_of(i * 256, 256), 256)
-        mixed, level = attend_rows(
-            q_ref[rows, :],
-            pos_ref[2, rows, 0:1],
-            pos_ref[3, rows, 0:1],
-            kp,
-            ka_ref,
-            kb_ref,
-            va_ref,
-            vb_ref,
-        )
-        mix_ref[rows, :] = mixed
-        lev_ref[rows, :] = level
+    def put(row, mixed, level):
+        mix_ref[row : row + mixed.shape[0]] = mixed
+        lev_ref[row : row + mixed.shape[0]] = level
+
+    attend_all(q_ref, pos_ref, 2, kp_ref, (ka_ref, kb_ref), (va_ref, vb_ref), put)
 
 
 def join_kernel(mix_ref, lev_ref, arrived_ref, out_ref):
@@ -321,12 +315,12 @@
     out_ref[...] = jnp.concatenate([packed[:, :cols], packed[:, cols:]], axis=0).astype(BF16)
 
 
-def call(kernel, outs, cost=1000, **kwargs):
+def call(kernel, outs, cost=1000, vmem_mib=40, **kwargs):
     shapes = [jax.ShapeDtypeStruct(s, t) for s, t in outs]
     return pl.pallas_call(
         kernel,
         out_shape=shapes if len(shapes) > 1 else shapes[0],
-        compiler_params=pltpu.CompilerParams(vmem_limit_bytes=40 * MIB),
+        compiler_params=pltpu.CompilerParams(vmem_limit_bytes=vmem_mib * MIB),
         cost_estimate=pl.CostEstimate(flops=cost, bytes_accessed=cost, transcendentals=0),
         **kwargs,
     )
@@ -362,9 +356,12 @@
 
     anywhere = pl.BlockSpec(memory_space=pl.ANY)
     quarter = tokens // side
+    row_gain = input_gain.reshape(1, -1)
+    wq_t, wk_t, wv_t = w_query.T, w_key.T, w_value.T
     sent = call(
         context_kernel,
         [((head_size, cols + 8, quarter), BF16)],
+        vmem_mib=60,
         in_specs=[anywhere] * 2,
         scratch_shapes=[
             pltpu.VMEM((cols, tokens), BF16),
@@ -373,41 +370,40 @@
         ],
     )(context.T, latents)
     first = lax.all_to_all(sent, "head", 0, 0)
-    first, input_gain = lax.optimization_barrier((first, input_gain))
-    all_weights, key_pos, query_pos = call(
+    own = first[:, :cols].reshape(head_size * cols, quarter)
+    quarters = [own] + [
+        lax.ppermute(own, BOTH, partners(seq_size, side, step)) for step in STEPS[1:]
+    ]
+
+    queries, latent_kv = call(
+        queries_kernel, [((planes, *block), BF16), ((2 * cols, 2 * lat_rows), BF16)]
+    )(first, wq_t, wk_t, wv_t, row_gain)
+    own_queries = lax.all_to_all(queries, "seq", 0, 0, axis_index_groups=along_z)
+    own_queries, late_gain = lax.optimization_barrier((own_queries, row_gain))
+    other_queries = lax.ppermute(own_queries, "seq", swap)
+
+    key_weights, key_pos, query_pos = call(
         prepare_kernel,
         [
-            ((3 * cols, head_size * cols), BF16),
+            ((2 * cols, head_size * cols), BF16),
             ((1, key_count), jnp.int32),
             ((4, rows, 2 * cols), jnp.int32),
         ],
-        in_specs=[anywhere] * 6,
-        scratch_shapes=[pltpu.VMEM((cols, head_size * cols), BF16)] * 3
+        in_specs=[anywhere] * 5,
+        scratch_shapes=[pltpu.VMEM((cols, head_size * cols), BF16)] * 2
         + [
             pltpu.VMEM((1, head_size * cols), F32),
             pltpu.VMEM((tokens // 128, 128), jnp.int32),
             pltpu.VMEM((planes, 2 * lat_rows), jnp.int32),
-            pltpu.SemaphoreType.DMA((6,)),
+            pltpu.SemaphoreType.DMA((5,)),
         ],
     )(
-        w_query.T,
-        w_key.T,
-        w_value.T,
-        input_gain.reshape(1, -1),
+        wk_t,
+        wv_t,
+        late_gain,
         ctx_pos.reshape(-1, 128),
         lat_pos.reshape(-1, 2 * lat_rows),
     )
-    own = first[:, :cols].reshape(head_size * cols, quarter)
-    quarters = [own] + [
-        lax.ppermute(own, BOTH, partners(seq_size, side, step)) for step in STEPS[1:]
-    ]
-
-    queries, latent_kv = call(
-        queries_kernel, [((planes, *block), BF16), ((2 * cols, 2 * lat_rows), BF16)]
-    )(first, all_weights)
-    own_queries = lax.all_to_all(queries, "seq", 0, 0, axis_index_groups=along_z)
-    other_queries = lax.ppermute(own_queries, "seq", swap)
-
     operands = call(
         keys_kernel,
         [((128, key_count), BF16)] * 2 + [((key_count, 128), BF16)] * 2,
@@ -417,7 +413,7 @@
             pltpu.VMEM((side, head_size * cols, quarter), BF16),
             pltpu.SemaphoreType.DMA((side,)),
         ],
-    )(*quarters, all_weights, latent_kv)
+    )(*quarters, key_weights, latent_kv)
 
     message = (planes, 40, 2 * cols)
     to_sibling = call(other_kernel, [(message, BF16)])(

time: 139 us -> 138 us (level)
  local copies, waits for them, and re-layouts: 1.83 us -> 0.16 us
    pallas_call x2, Pallas kernels: 1.34 us -> 3.11 us  [the longest x1 2.12 us: body(): call(context_kernel, [((head_size, cols + 8, quarter), BF16)], vmem_mib=6...]
    unnamed x26 -> x22, local copies, waits for them, and re-layouts: 1.73 us -> 0.06 us
  transfers between devices with their start and end apart: 5 -> 5, of which waited for: 0 -> 0; matrix products, arithmetic and copies ran while one was open for 0% -> 0% of each run, Pallas kernels for 6% -> 5%
where the time goes in v8:
time: 138 us
  blocking collectives  107 us (78%)
  Pallas kernels  15.7 us (11%)
  starting transfers between devices  14.3 us (10%)
    all_to_all x1, blocking collectives, body(): lax.all_to_all(queries, 'seq', 0, 0, axis_index_groups=along_z)  27.7 us
    all_to_all x1, blocking collectives, body(): first = lax.all_to_all(sent, 'head', 0, 0)  25.7 us
    all_to_all x2, blocking collectives, body(): arrived = lax.all_to_all(shares, 'head', 0, 0)  22.4 us
    all_to_all x1, blocking collectives, body(): arrived = lax.all_to_all(joined, 'seq', 0, 0, axis_index_groups=along_z)  20.2 us
    all_to_all x1, blocking collectives, body(): arrived = lax.all_to_all(copies, 'head', 0, 0)  11.1 us
    ppermute x3, starting transfers between devices, body(): lax.ppermute(own, BOTH, partners(seq_size, side, step))  9.95 us
    pallas_call x1, Pallas kernels, body(): call(other_kernel, [(message, BF16)])  3.71 us
    pallas_call x1, Pallas kernels, body(): call(own_kernel, [((rows, 2 * cols), F32)] * 2)  3.66 us
  transfers between devices with their start and end apart: 5, of which 0 were waited for; matrix products, arithmetic and copies ran while one was open for 0% of the time, Pallas kernels for 5%

profile of v8, /device:TPU:32, one launch (start us, length us, event | category | flops | bytes accessed | tf_op | source)
XLA Modules:
  0.0 137.5 jit_solution(17595601543835618368)
XLA Ops:
  0.0 2.1 %shard_map.118 = bf16[16,72,512]{2,1,0:T(8,128)(2,1)} custom-call(bf16[64,2048]{1,0:T(8,128)(2,1)} %bitcast.27, bf16[64,64]{1,0:T(8,128)(2,1)} %lat_ref.1), custom_call_target="tpu_custom_call" | custom-call | flops 1000 | bytes 1000 | tf_op jit(solution)/shard_map/pallas_call | solution.py:361
  2.1 25.7 %all_to_all.30.arrived_ref = bf16[16,72,512]{2,1,0:T(8,128)(2,1)S(1)} all-to-all(bf16[16,72,512]{2,1,0:T(8,128)(2,1)} %shard_map.118), channel_id=1, replica_groups=mesh['seq'=32,'head'=16] {'head'}, dimensions={0} | all-to-all | bytes 2359296 | tf_op jit(solution)/shard_map/all_to_all | solution.py:372
  27.8 0.0 copy-start
  27.8 0.0 copy-start.1
  27.8 0.1 slice.4
  27.9 0.0 copy-start.8
  27.9 0.0 copy-start.9
  27.9 2.3 %collective-permute-start = (bf16[1024,512]{1,0:T(8,128)(2,1)S(1)}, bf16[1024,512]{1,0:T(8,128)(2,1)S(1)}, u32[]{:S(2)}, u32[]{:S(2)}) collective-permute-start(bf16[1024,512]{1,0:T(8,128)(2,1)S(1)} %bitcast.11), channel_id=1, source_target_pairs={{0,4},{1,5},{2,6},{3,7},{4,0},{5,1},{6,2},{7,3},{8,12},{9,13},{10,... | collective-permute-start | bytes 3145736 | tf_op jit(solution)/shard_map/ppermute | solution.py:375
  30.2 3.2 %collective-permute-start.1 = (bf16[1024,512]{1,0:T(8,128)(2,1)S(1)}, bf16[1024,512]{1,0:T(8,128)(2,1)S(1)}, u32[]{:S(2)}, u32[]{:S(2)}) collective-permute-start(bf16[1024,512]{1,0:T(8,128)(2,1)S(1)} %bitcast.12), channel_id=1, source_target_pairs={{0,12},{1,13},{2,14},{3,15},{4,8},{5,9},{6,10},{7,11},{8,4},{9,5},... | collective-permute-start | bytes 3145736 | tf_op jit(solution)/shard_map/ppermute | solution.py:375
  33.4 4.5 %collective-permute-start.2 = (bf16[1024,512]{1,0:T(8,128)(2,1)S(1)}, bf16[1024,512]{1,0:T(8,128)(2,1)S(1)}, u32[]{:S(2)}, u32[]{:S(2)}) collective-permute-start(bf16[1024,512]{1,0:T(8,128)(2,1)S(1)} %bitcast.13), channel_id=1, source_target_pairs={{0,8},{1,9},{2,10},{3,11},{4,12},{5,13},{6,14},{7,15},{8,0},{9,1},... | collective-permute-start | bytes 3145736 | tf_op jit(solution)/shard_map/ppermute | solution.py:375
  37.9 0.0 copy-done
  37.9 0.0 copy-done.1
  37.9 0.0 copy-done.4
  37.9 0.0 copy-done.7
  37.9 0.4 shard_map.119
  38.4 27.7 %all_to_all.31 = bf16[16,32,128]{2,1,0:T(8,128)(2,1)S(1)} all-to-all(bf16[16,32,128]{2,1,0:T(8,128)(2,1)S(1)} %get-tuple-element.20), channel_id=1, replica_groups={{0,32,64,96,128,160,192,224,256,288,320,352,384,416,448,480},{16,48,80,..., dimensions={0} | all-to-all | bytes 262144 | tf_op jit(solution)/shard_map/all_to_all | solution.py:381
  66.1 1.9 %collective-permute-start.3 = (bf16[16,32,128]{2,1,0:T(8,128)(2,1)S(1)}, bf16[16,32,128]{2,1,0:T(8,128)(2,1)S(1)}, u32[]{:S(2)}, u32[]{:S(2)}) collective-permute-start(bf16[16,32,128]{2,1,0:T(8,128)(2,1)S(1)} %all_to_all.31), channel_id=1, source_target_pairs={{0,16},{16,0},{32,48},{48,32},{64,80},{80,64},{96,112},{112,96},{1... | collective-permute-start | bytes 393224 | tf_op jit(solution)/shard_map/ppermute | solution.py:383
  68.0 0.0 copy-done.8
  68.0 0.0 copy-done.9
  68.1 1.0 shard_map.120
  69.0 0.0 collective-permute-done.refs_1_
  69.1 0.0 collective-permute-done.1.refs_2_
  69.1 0.0 collective-permute-done.2.refs_3_
  69.1 2.2 %shard_map.121 = (bf16[128,2176]{1,0:T(8,128)(2,1)S(1)}, bf16[128,2176]{1,0:T(8,128)(2,1)S(1)}, bf16[2176,128]{1,0:T(8,128)(2,1)S(1)}, bf16[2176,128]{1,0:T(8,128)(2,1)S(1)}) custom-call(bf16[1024,512]{1,0:T(8,128)(2,1)S(1)} %bitcast.14, bf16[1024,512]{1,0:T(8,128)(2,1)S(1)} %collective-permute-done.refs_1_, ...), custom_call_target="tpu_custom_call" | custom-call | flops 1000000000 | bytes 1000000000 | tf_op jit(solution)/shard_map/pallas_call | solution.py:407
  71.3 0.0 collective-permute-done.3
  71.3 3.7 %shard_map.123 = bf16[16,40,128]{2,1,0:T(8,128)(2,1)S(1)} custom-call(bf16[512,128]{1,0:T(8,128)(2,1)S(1)} %bitcast.21, s32[4,512,128]{2,1,0:T(8,128)S(1)} %get-tuple-element.23.pos_ref, s32[1,2176]{1,0:T(1,128)S(1)} %get-tuple-element.24.kp_ref, bf16[128,2176]{1,0:T(8,128)(2,1)S(1)} %get-tuple-element.27.ka_ref, ...), custom_call_target="tpu_custom_call" | custom-call | flops 1000 | bytes 1000 | tf_op jit(solution)/shard_map/pallas_call | solution.py:419
  75.0 2.4 %collective-permute-start.4 = (bf16[16,40,128]{2,1,0:T(8,128)(2,1)S(1)}, bf16[16,40,128]{2,1,0:T(8,128)(2,1)S(1)}, u32[]{:S(2)}, u32[]{:S(2)}) collective-permute-start(bf16[16,40,128]{2,1,0:T(8,128)(2,1)S(1)} %shard_map.123), channel_id=1, source_target_pairs={{0,16},{16,0},{32,48},{48,32},{64,80},{80,64},{96,112},{112,96},{1... | collective-permute-start | bytes 491528 | tf_op jit(solution)/shard_map/ppermute | solution.py:422
  77.5 3.7 %shard_map.122 = (f32[512,128]{1,0:T(8,128)S(1)}, f32[512,128]{1,0:T(8,128)S(1)}) custom-call(bf16[512,128]{1,0:T(8,128)(2,1)S(1)} %bitcast.19, s32[4,512,128]{2,1,0:T(8,128)S(1)} %get-tuple-element.23.pos_ref, s32[1,2176]{1,0:T(1,128)S(1)} %get-tuple-element.24.kp_ref, bf16[128,2176]{1,0:T(8,128)(2,1)S(1)} %get-tuple-element.27.ka_ref, ...), custom_call_target="tpu_custom_call" | custom-call | flops 1000 | bytes 1000 | tf_op jit(solution)/shard_map/pallas_call | solution.py:423
  81.1 0.0 copy-start.5
  81.1 0.0 copy-start.6
  81.1 0.0 copy-start.2
  81.2 0.0 copy-start.3
  81.2 0.0 copy-start.10
  81.2 0.0 collective-permute-done.4.arrived_ref
  81.2 0.4 shard_map.124
  81.6 20.2 %all_to_all.32.arrived_ref = bf16[16,40,128]{2,1,0:T(8,128)(2,1)S(1)} all-to-all(bf16[16,40,128]{2,1,0:T(8,128)(2,1)S(1)} %shard_map.124), channel_id=1, replica_groups={{0,32,64,96,128,160,192,224,256,288,320,352,384,416,448,480},{16,48,80,..., dimensions={0} | all-to-all | bytes 327680 | tf_op jit(solution)/shard_map/all_to_all | solution.py:427
  101.8 0.0 copy-done.5
  101.8 0.7 shard_map.125
  102.5 11.4 %all_to_all.33.arrived_ref = bf16[16,32,128]{2,1,0:T(8,128)(2,1)S(1)} all-to-all(bf16[16,32,128]{2,1,0:T(8,128)(2,1)S(1)} %shard_map.125), channel_id=1, replica_groups=mesh['seq'=32,'head'=16] {'head'}, dimensions={0} | all-to-all | bytes 262144 | tf_op jit(solution)/shard_map/all_to_all | solution.py:429
  113.9 0.0 copy-done.6
  113.9 0.1 shard_map.126
  113.9 11.1 %all_to_all.34.arrived_ref = bf16[16,32,128]{2,1,0:T(8,128)(2,1)S(1)} all-to-all(bf16[16,32,128]{2,1,0:T(8,128)(2,1)S(1)} %get-tuple-element.33), channel_id=1, replica_groups=mesh['seq'=32,'head'=16] {'head'}, dimensions={0} | all-to-all | bytes 262144 | tf_op jit(solution)/shard_map/all_to_all | solution.py:433
  125.0 0.0 copy-done.2
  125.0 0.0 copy-done.3
  125.0 0.0 copy-done.10
  125.0 0.7 shard_map.127
  125.8 11.1 %all_to_all.35.arrived_ref = bf16[16,32,128]{2,1,0:T(8,128)(2,1)S(1)} all-to-all(bf16[16,32,128]{2,1,0:T(8,128)(2,1)S(1)} %shard_map.127), channel_id=1, replica_groups=mesh['seq'=32,'head'=16] {'head'}, dimensions={0} | all-to-all | bytes 262144 | tf_op jit(solution)/shard_map/all_to_all | solution.py:437
  136.8 0.7 shard_map.128
  (2 shorter events, 0.0 us)
Async XLA Ops:
  27.8 10.1 %copy-start = (bf16[1024,64]{0,1:T(8,128)(2,1)S(1)}, bf16[1024,64]{0,1:T(8,128)(2,1)}, u32[]{:S(2)}) copy-start(bf16[1024,64]{0,1:T(8,128)(2,1)} %param.18) | copy-start | bytes 393220
  27.8 10.1 %copy-start.1 = (bf16[1024,64]{0,1:T(8,128)(2,1)S(1)}, bf16[1024,64]{0,1:T(8,128)(2,1)}, u32[]{:S(2)}) copy-start(bf16[1024,64]{0,1:T(8,128)(2,1)} %param.19) | copy-start | bytes 393220
  27.8 10.1 %copy-start.4 = (bf16[1024,64]{0,1:T(8,128)(2,1)S(1)}, bf16[1024,64]{0,1:T(8,128)(2,1)}, u32[]{:S(2)}) copy-start(bf16[1024,64]{0,1:T(8,128)(2,1)} %param.17) | copy-start | bytes 393220
  27.8 10.1 %copy-start.7 = (f32[1024]{0:T(1024)S(1)}, f32[1024]{0:T(1024)}, u32[]{:S(2)}) copy-start(f32[1024]{0:T(1024)} %param.16) | copy-start | bytes 12292
  27.9 40.1 %copy-start.8 = (s32[2048]{0:T(1024)S(1)}, s32[2048]{0:T(1024)}, u32[]{:S(2)}) copy-start(s32[2048]{0:T(1024)} %param.14) | copy-start | bytes 24580
  27.9 40.1 %copy-start.9 = (s32[2048]{0:T(1024)S(1)}, s32[2048]{0:T(1024)}, u32[]{:S(2)}) copy-start(s32[2048]{0:T(1024)} %param.15) | copy-start | bytes 24580
  27.9 41.1 %collective-permute-start = (bf16[1024,512]{1,0:T(8,128)(2,1)S(1)}, bf16[1024,512]{1,0:T(8,128)(2,1)S(1)}, u32[]{:S(2)}, u32[]{:S(2)}) collective-permute-start(bf16[1024,512]{1,0:T(8,128)(2,1)S(1)} %bitcast.11), channel_id=1, source_target_pairs={{0,4},{1,5},{2,6},{3,7},{4,0},{5,1},{6,2},{7,3},{8,12},{9,13},{10,... | collective-permute-start | bytes 3145736 | tf_op jit(solution)/shard_map/ppermute | solution.py:375
  30.2 38.8 %collective-permute-start.1 = (bf16[1024,512]{1,0:T(8,128)(2,1)S(1)}, bf16[1024,512]{1,0:T(8,128)(2,1)S(1)}, u32[]{:S(2)}, u32[]{:S(2)}) collective-permute-start(bf16[1024,512]{1,0:T(8,128)(2,1)S(1)} %bitcast.12), channel_id=1, source_target_pairs={{0,12},{1,13},{2,14},{3,15},{4,8},{5,9},{6,10},{7,11},{8,4},{9,5},... | collective-permute-start | bytes 3145736 | tf_op jit(solution)/shard_map/ppermute | solution.py:375
  33.4 35.7 %collective-permute-start.2 = (bf16[1024,512]{1,0:T(8,128)(2,1)S(1)}, bf16[1024,512]{1,0:T(8,128)(2,1)S(1)}, u32[]{:S(2)}, u32[]{:S(2)}) collective-permute-start(bf16[1024,512]{1,0:T(8,128)(2,1)S(1)} %bitcast.13), channel_id=1, source_target_pairs={{0,8},{1,9},{2,10},{3,11},{4,12},{5,13},{6,14},{7,15},{8,0},{9,1},... | collective-permute-start | bytes 3145736 | tf_op jit(solution)/shard_map/ppermute | solution.py:375
  66.1 5.2 %collective-permute-start.3 = (bf16[16,32,128]{2,1,0:T(8,128)(2,1)S(1)}, bf16[16,32,128]{2,1,0:T(8,128)(2,1)S(1)}, u32[]{:S(2)}, u32[]{:S(2)}) collective-permute-start(bf16[16,32,128]{2,1,0:T(8,128)(2,1)S(1)} %all_to_all.31), channel_id=1, source_target_pairs={{0,16},{16,0},{32,48},{48,32},{64,80},{80,64},{96,112},{112,96},{1... | collective-permute-start | bytes 393224 | tf_op jit(solution)/shard_map/ppermute | solution.py:383
  75.0 6.2 %collective-permute-start.4 = (bf16[16,40,128]{2,1,0:T(8,128)(2,1)S(1)}, bf16[16,40,128]{2,1,0:T(8,128)(2,1)S(1)}, u32[]{:S(2)}, u32[]{:S(2)}) collective-permute-start(bf16[16,40,128]{2,1,0:T(8,128)(2,1)S(1)} %shard_map.123), channel_id=1, source_target_pairs={{0,16},{16,0},{32,48},{48,32},{64,80},{80,64},{96,112},{112,96},{1... | collective-permute-start | bytes 491528 | tf_op jit(solution)/shard_map/ppermute | solution.py:422
  81.1 20.7 %copy-start.5 = (bf16[64,1024]{1,0:T(8,128)(2,1)S(1)}, bf16[64,1024]{1,0:T(8,128)(2,1)}, u32[]{:S(2)}) copy-start(bf16[64,1024]{1,0:T(8,128)(2,1)} %w_ref.1) | copy-start | bytes 393220
  81.1 32.7 %copy-start.6 = (bf16[64,64]{1,0:T(8,128)(2,1)S(1)}, bf16[64,64]{1,0:T(8,128)(2,1)}, u32[]{:S(2)}) copy-start(bf16[64,64]{1,0:T(8,128)(2,1)} %lat_ref.1) | copy-start | bytes 24580
  81.1 43.9 %copy-start.2 = (bf16[1024,256]{1,0:T(8,128)(2,1)S(1)}, bf16[1024,256]{1,0:T(8,128)(2,1)}, u32[]{:S(2)}) copy-start(bf16[1024,256]{1,0:T(8,128)(2,1)} %up_ref.1) | copy-start | bytes 1572868
  81.2 43.9 %copy-start.3 = (bf16[256,1024]{1,0:T(8,128)(2,1)S(1)}, bf16[256,1024]{1,0:T(8,128)(2,1)}, u32[]{:S(2)}) copy-start(bf16[256,1024]{1,0:T(8,128)(2,1)} %down_ref.1) | copy-start | bytes 1572868
  81.2 43.9 %copy-start.10 = (f32[1024]{0:T(1024)S(1)}, f32[1024]{0:T(1024)}, u32[]{:S(2)}) copy-start(f32[1024]{0:T(1024)} %param.21) | copy-start | bytes 12292

commit v9 on v6

--- a/solution.py
+++ b/solution.py
@@ -90,9 +90,9 @@
     weights = weights * gain_ref[...]
     all_ref[...] = weights.astype(BF16)
     scratch[...] = weights[64:].T.reshape(scratch.shape)
-    for i in range(w_ref.shape[0]):
+    for i in range(4):
         blocks = [scratch[place ^ jnp.where(core == 0, 4 * STEPS[i] + STEPS[j], 4 * STEPS[j] + STEPS[i])] for j in range(4)]
-        w_ref[i] = jnp.concatenate(blocks, axis=0).T.astype(BF16)
+        w_ref[:, 256 * i : 256 * i + 256] = jnp.concatenate(blocks, axis=0).T.astype(BF16)
 
     for i in range(ctx_ref.shape[0]):
         kp_ref[:, 128 * i : 128 * i + 128] = ctx_ref[i : i + 1, :]
@@ -128,32 +128,33 @@
 
 def keys_kernel(*refs):
     *line_refs, w_ref, lat_ref, ka_ref, kb_ref, va_ref, vb_ref, held, sems = refs
-    tokens = line_refs[0].shape[1]
+    height, tokens = line_refs[0].shape
     width = 512
     copies = []
     for c in range(tokens // width):
         cols = slice(c * width, c * width + width)
         copies.append(
             [
-                pltpu.make_async_copy(line.at[:, cols], held.at[i, :, cols], sems.at[c, i])
+                pltpu.make_async_copy(
+                    line.at[:, cols], held.at[i * height : i * height + height, cols], sems.at[c, i]
+                )
                 for i, line in enumerate(line_refs)
             ]
         )
         for copy in copies[c]:
             copy.start()
     put_keys(lat_ref[...], slice(tokens, tokens + 128), ka_ref, kb_ref, va_ref, vb_ref)
+    weights = w_ref[...]
     for c in range(tokens // width):
         cols = slice(c * width, c * width + width)
-        total = jnp.zeros((128, width), F32)
-        squares = jnp.zeros((1, width), F32)
-        for i in range(len(line_refs)):
-            copies[c][i].wait()
-            piece = held[i, :, cols]
-            total = total + dot(w_ref[i], piece, NN)
-            wide = piece.astype(F32)
-            squares = squares + jnp.sum(wide * wide, axis=0, keepdims=True)
+        for copy in copies[c]:
+            copy.wait()
+        piece = held[:, cols]
+        wide = piece.astype(F32)
+        squares = jnp.sum(wide * wide, axis=0, keepdims=True)
         inverse = lax.rsqrt(squares * (1.0 / 1024) + EPSILON)
-        put_keys((total * inverse).astype(BF16), cols, ka_ref, kb_ref, va_ref, vb_ref)
+        both = (dot(weights, piece, NN) * inverse).astype(BF16)
+        put_keys(both, cols, ka_ref, kb_ref, va_ref, vb_ref)
 
 
 def put_keys(both, cols, ka_ref, kb_ref, va_ref, vb_ref):
@@ -166,19 +167,39 @@
     vb_ref[cols, :] = jnp.concatenate([ones, values.astype(F32)], axis=0).T.astype(BF16)
 
 
-def attend_rows(q, pos_a, pos_b, kp, ka_ref, kb_ref, va_ref, vb_ref):
-    def one(k_ref, v_ref, pos):
-        scores = jnp.where(kp <= pos, dot(q, k_ref[...], NN), NEGATIVE)
+def attend_all(q_ref, pos_ref, first, kp_ref, key_refs, value_refs, put):
+    step = 256
+    kp = kp_ref[...]
+    pieces = [(i, h) for i in range(0, q_ref.shape[0], step) for h in range(2)]
+
+    def scores_of(piece):
+        i, h = piece
+        return dot(q_ref[i : i + step], key_refs[h][...], NN)
+
+    def finish(piece, weights, top):
+        i, h = piece
+        done[h] = (dot(weights, value_refs[h][...], NN), top)
+        if h == 1:
+            (out_a, top_a), (out_b, top_b) = done
+            low = low_half(out_a.shape)
+            above = jnp.where(low, out_a, out_b)
+            below = jnp.maximum(pltpu.roll(jnp.where(low, out_b, out_a), 64, 1), 1e-30)
+            put(i, above / below, jnp.where(low, top_a, top_b) + jnp.log(below))
+
+    done = [None, None]
+    waiting = None
+    scores = scores_of(pieces[0])
+    for n, (i, h) in enumerate(pieces):
+        following = scores_of(pieces[n + 1]) if n + 1 < len(pieces) else None
+        visible = kp <= pos_ref[first + h, i : i + step, 0:1]
+        scores = jnp.where(visible, scores, NEGATIVE)
         top = jnp.maximum(jnp.max(scores, axis=1, keepdims=True), LOWEST)
         weights = jnp.exp(scores - top).astype(BF16)
-        return dot(weights, v_ref[...], NN), top
-
-    out_a, top_a = one(ka_ref, va_ref, pos_a)
-    out_b, top_b = one(kb_ref, vb_ref, pos_b)
-    low = low_half(out_a.shape)
-    above = jnp.where(low, out_a, out_b)
-    below = jnp.maximum(pltpu.roll(jnp.where(low, out_b, out_a), 64, 1), 1e-30)
-    return above / below, jnp.where(low, top_a, top_b) + jnp.log(below)
+        if waiting is not None:
+            finish(*waiting)
+        waiting = ((i, h), weights, top)
+        scores = following
+    finish(*waiting)
 
 
 def put_message(mixed, level, out_ref, group):
@@ -189,7 +210,7 @@
     first = once.astype(BF16).astype(F32)
     second = (once - first).astype(BF16).astype(F32)
     third = once - first - second
-    rest = jnp.zeros((13, 128), F32)
+    rest = jnp.zeros((5, 128), F32)
     out_ref[group, 32:] = jnp.concatenate([first, second, third, rest], axis=0).astype(BF16)
 
 
@@ -214,44 +235,20 @@
 
 
 def other_kernel(q_ref, pos_ref, kp_ref, ka_ref, kb_ref, va_ref, vb_ref, out_ref):
-    kp = kp_ref[...]
-
-    @pl.loop(0, q_ref.shape[0] // 256)
-    def _(i):
-        rows = pl.ds(pl.multiple_of(i * 256, 256), 256)
-        mixed, level = attend_rows(
-            q_ref[rows, :],
-            pos_ref[0, rows, 0:1],
-            pos_ref[1, rows, 0:1],
-            kp,
-            ka_ref,
-            kb_ref,
-            va_ref,
-            vb_ref,
-        )
-        for g in range(8):
+    def put(row, mixed, level):
+        for g in range(mixed.shape[0] // 32):
             part = slice(32 * g, 32 * g + 32)
-            put_message(mixed[part], level[part], out_ref, i * 8 + g)
+            put_message(mixed[part], level[part], out_ref, row // 32 + g)
+
+    attend_all(q_ref, pos_ref, 0, kp_ref, (ka_ref, kb_ref), (va_ref, vb_ref), put)
 
 
 def own_kernel(q_ref, pos_ref, kp_ref, ka_ref, kb_ref, va_ref, vb_ref, mix_ref, lev_ref):
-    kp = kp_ref[...]
-
-    @pl.loop(0, q_ref.shape[0] // 256)
-    def _(i):
-        rows = pl.ds(pl.multiple_of(i * 256, 256), 256)
-        mixed, level = attend_rows(
-            q_ref[rows, :],
-            pos_ref[2, rows, 0:1],
-            pos_ref[3, rows, 0:1],
-            kp,
-            ka_ref,
-            kb_ref,
-            va_ref,
-            vb_ref,
-        )
-        mix_ref[rows, :] = mixed
-        lev_ref[rows, :] = level
+    def put(row, mixed, level):
+        mix_ref[row : row + mixed.shape[0]] = mixed
+        lev_ref[row : row + mixed.shape[0]] = level
+
+    attend_all(q_ref, pos_ref, 2, kp_ref, (ka_ref, kb_ref), (va_ref, vb_ref), put)
 
 
 def join_kernel(mix_ref, lev_ref, arrived_ref, out_ref):
@@ -355,7 +352,7 @@
     prepared = call(
         prepare_kernel,
         [
-            ((side, 2 * cols, side * cols), BF16),
+            ((2 * cols, head_size * cols), BF16),
             ((3 * cols, head_size * cols), BF16),
             ((1, key_count), jnp.int32),
             ((4, rows, 2 * cols), jnp.int32),
@@ -393,12 +390,12 @@
         cost=10**9,
         in_specs=[anywhere] * side + [vmem] * 2,
         scratch_shapes=[
-            pltpu.VMEM((side, side * cols, tokens), BF16),
+            pltpu.VMEM((head_size * cols, tokens), BF16),
             pltpu.SemaphoreType.DMA((4, side)),
         ],
     )(*lines, key_weights, latent_kv)
 
-    message = (planes, 48, 2 * cols)
+    message = (planes, 40, 2 * cols)
     to_sibling = call(other_kernel, [(message, BF16)])(
         other_queries.reshape(rows, -1), query_pos, key_pos, *operands
     )

time: 140 us -> 137 us (0.979)
  Pallas kernels: 16.7 us -> 14.9 us
  transfers between devices with their start and end apart: 9 -> 9, of which waited for: 1 -> 1; matrix products, arithmetic and copies ran while one was open for 1% -> 1% of each run, Pallas kernels for 7% -> 6%
where the time goes in v9:
time: 137 us
  blocking collectives  82.5 us (60%)
  starting transfers between devices  31.6 us (23%)
  Pallas kernels  14.9 us (11%)
  waiting for transfers between devices  5.28 us (4%)
    all_to_all x1, blocking collectives, body(): lax.all_to_all(queries, 'seq', 0, 0, axis_index_groups=along_z)  27.6 us
    all_to_all x2, blocking collectives, body(): arrived = lax.all_to_all(shares, 'head', 0, 0)  22.4 us
    all_to_all x1, blocking collectives, body(): arrived = lax.all_to_all(joined, 'seq', 0, 0, axis_index_groups=along_z)  21.5 us
    ppermute x6, starting transfers between devices, swap_lines(): return lax.ppermute(piece, BOTH, partners(seq_size, side, phase, step))  19.7 us
    all_to_all x1, blocking collectives, body(): arrived = lax.all_to_all(copies, 'head', 0, 0)  11.1 us
    all_to_all x1, starting transfers between devices, body(): lat_blocks = lax.all_to_all(copies, 'head', 0, 0)  7.56 us
    all_to_all x1, waiting for transfers between devices, body(): lat_blocks = lax.all_to_all(copies, 'head', 0, 0)  5.25 us
    pallas_call x1, Pallas kernels, body(): call(other_kernel, [(message, BF16)])  3.59 us
  transfers between devices with their start and end apart: 9, of which 1 were waited for; matrix products, arithmetic and copies ran while one was open for 1% of the time, Pallas kernels for 6%

profile of v9, /device:TPU:32, one launch (start us, length us, event | category | flops | bytes accessed | tf_op | source)
XLA Modules:
  0.0 136.5 jit_solution(8325646658957907130)
XLA Ops:
  0.0 4.9 %collective-permute-start.2 = (bf16[64,2048]{1,0:T(8,128)(2,1)}, bf16[64,2048]{1,0:T(8,128)(2,1)S(1)}, u32[]{:S(2)}, u32[]{:S(2)}) collective-permute-start(bf16[64,2048]{1,0:T(8,128)(2,1)} %bitcast.19), channel_id=1, source_target_pairs={{0,2},{1,3},{2,0},{3,1},{4,6},{5,7},{6,4},{7,5},{8,10},{9,11},{10,... | collective-permute-start | bytes 786440 | tf_op jit(solution)/shard_map/ppermute | solution.py:344
  4.9 3.1 %collective-permute-start.1 = (bf16[64,2048]{1,0:T(8,128)(2,1)}, bf16[64,2048]{1,0:T(8,128)(2,1)S(1)}, u32[]{:S(2)}, u32[]{:S(2)}) collective-permute-start(bf16[64,2048]{1,0:T(8,128)(2,1)} %bitcast.20), channel_id=1, source_target_pairs={{0,3},{1,2},{2,1},{3,0},{4,7},{5,6},{6,5},{7,4},{8,11},{9,10},{10,... | collective-permute-start | bytes 786440 | tf_op jit(solution)/shard_map/ppermute | solution.py:344
  8.0 1.9 %collective-permute-start = (bf16[64,2048]{1,0:T(8,128)(2,1)}, bf16[64,2048]{1,0:T(8,128)(2,1)S(1)}, u32[]{:S(2)}, u32[]{:S(2)}) collective-permute-start(bf16[64,2048]{1,0:T(8,128)(2,1)} %bitcast.21), channel_id=1, source_target_pairs={{0,1},{1,0},{2,3},{3,2},{4,5},{5,4},{6,7},{7,6},{8,9},{9,8},{10,11... | collective-permute-start | bytes 786440 | tf_op jit(solution)/shard_map/ppermute | solution.py:344
  9.9 0.0 copy-start.6
  9.9 0.7 copy-done.6
  10.6 0.7 shard_map.118
  11.4 7.6 %all-to-all-start = ((bf16[16,32,128]{2,1,0:T(8,128)(2,1)}), bf16[16,32,128]{2,1,0:T(8,128)(2,1)S(1)}, u32[]{:S(2)}, u32[]{:S(2)}) async-start(bf16[16,32,128]{2,1,0:T(8,128)(2,1)} %shard_map.118), calls=%async_computation | async-start | bytes 262144 | tf_op jit(solution)/shard_map/all_to_all | solution.py:350
  18.9 0.0 copy-start.2
  19.0 0.0 copy-start.3
  19.0 0.0 copy-start.4
  19.0 0.0 copy-start.8
  19.0 0.0 copy-start.9
  19.0 0.0 copy-start.10
  19.0 0.0 collective-permute-done.2
  19.0 0.0 collective-permute-done.1
  19.0 0.0 collective-permute-done
  19.0 1.2 pad_maximum_fusion.refs_0_
  20.3 1.4 %shard_map.119 = (bf16[128,1024]{1,0:T(8,128)(2,1)S(1)}, bf16[192,1024]{1,0:T(8,128)(2,1)S(1)}, s32[1,2176]{1,0:T(1,128)S(1)}, s32[4,512,128]{2,1,0:T(8,128)S(1)}) custom-call(bf16[64,1024]{1,0:T(8,128)(2,1)S(1)} %bitcast.11, bf16[64,1024]{1,0:T(8,128)(2,1)S(1)} %bitcast.12, bf16[64,1024]{1,0:T(8,128)(2,1)S(1)} %bitcast.13, f32[1,1024]{1,0:T(1,128)S(1)} %bitcast.17, ...), custom_call_target="tpu_custom_call" | custom-call | flops 1000 | bytes 1000 | tf_op jit(solution)/shard_map/pallas_call | solution.py:352
  21.7 5.3 %all-to-all-done.lat_ref = bf16[16,32,128]{2,1,0:T(8,128)(2,1)S(1)} async-done(((bf16[16,32,128]{2,1,0:T(8,128)(2,1)}), bf16[16,32,128]{2,1,0:T(8,128)(2,1)S(1)}, u32[]{:S(2)}, u32[]{:S(2)}) %all-to-all-start) | async-done | bytes 131104 | tf_op jit(solution)/shard_map/all_to_all | solution.py:350
  26.9 2.2 %collective-permute-start.3 = (bf16[256,2048]{1,0:T(8,128)(2,1)S(1)}, bf16[256,2048]{1,0:T(8,128)(2,1)S(1)}, u32[]{:S(2)}, u32[]{:S(2)}) collective-permute-start(bf16[256,2048]{1,0:T(8,128)(2,1)S(1)} %pad_maximum_fusion.refs_0_), channel_id=1, source_target_pairs={{0,4},{1,5},{2,6},{3,7},{4,0},{5,1},{6,2},{7,3},{8,12},{9,13},{10,... | collective-permute-start | bytes 3145736 | tf_op jit(solution)/shard_map/ppermute | solution.py:344
  29.1 3.2 %collective-permute-start.4 = (bf16[256,2048]{1,0:T(8,128)(2,1)S(1)}, bf16[256,2048]{1,0:T(8,128)(2,1)S(1)}, u32[]{:S(2)}, u32[]{:S(2)}) collective-permute-start(bf16[256,2048]{1,0:T(8,128)(2,1)S(1)} %pad_maximum_fusion.refs_0_), channel_id=1, source_target_pairs={{0,12},{1,13},{2,14},{3,15},{4,8},{5,9},{6,10},{7,11},{8,4},{9,5},... | collective-permute-start | bytes 3145736 | tf_op jit(solution)/shard_map/ppermute | solution.py:344
  32.3 4.4 %collective-permute-start.5 = (bf16[256,2048]{1,0:T(8,128)(2,1)S(1)}, bf16[256,2048]{1,0:T(8,128)(2,1)S(1)}, u32[]{:S(2)}, u32[]{:S(2)}) collective-permute-start(bf16[256,2048]{1,0:T(8,128)(2,1)S(1)} %pad_maximum_fusion.refs_0_), channel_id=1, source_target_pairs={{0,8},{1,9},{2,10},{3,11},{4,12},{5,13},{6,14},{7,15},{8,0},{9,1},... | collective-permute-start | bytes 3145736 | tf_op jit(solution)/shard_map/ppermute | solution.py:344
  36.8 0.5 shard_map.120
  37.2 27.6 %all_to_all.30 = bf16[16,32,128]{2,1,0:T(8,128)(2,1)S(1)} all-to-all(bf16[16,32,128]{2,1,0:T(8,128)(2,1)S(1)} %get-tuple-element.35), channel_id=1, replica_groups={{0,32,64,96,128,160,192,224,256,288,320,352,384,416,448,480},{16,48,80,..., dimensions={0} | all-to-all | bytes 262144 | tf_op jit(solution)/shard_map/all_to_all | solution.py:384
  64.8 1.9 %collective-permute-start.6 = (bf16[16,32,128]{2,1,0:T(8,128)(2,1)S(1)}, bf16[16,32,128]{2,1,0:T(8,128)(2,1)S(1)}, u32[]{:S(2)}, u32[]{:S(2)}) collective-permute-start(bf16[16,32,128]{2,1,0:T(8,128)(2,1)S(1)} %all_to_all.30), channel_id=1, source_target_pairs={{0,16},{16,0},{32,48},{48,32},{64,80},{80,64},{96,112},{112,96},{1... | collective-permute-start | bytes 393224 | tf_op jit(solution)/shard_map/ppermute | solution.py:385
  66.7 0.0 collective-permute-done.3.refs_1_
  66.7 0.0 collective-permute-done.4.refs_2_
  66.7 0.0 collective-permute-done.5.refs_3_
  66.7 2.6 %shard_map.121 = (bf16[128,2176]{1,0:T(8,128)(2,1)S(1)}, bf16[128,2176]{1,0:T(8,128)(2,1)S(1)}, bf16[2176,128]{1,0:T(8,128)(2,1)S(1)}, bf16[2176,128]{1,0:T(8,128)(2,1)S(1)}) custom-call(bf16[256,2048]{1,0:T(8,128)(2,1)S(1)} %pad_maximum_fusion.refs_0_, bf16[256,2048]{1,0:T(8,128)(2,1)S(1)} %collective-permute-done.3.refs_1_, ...), custom_call_target="tpu_custom_call" | custom-call | flops 1000000000 | bytes 1000000000 | tf_op jit(solution)/shard_map/pallas_call | solution.py:387
  69.3 0.0 collective-permute-done.6
  69.4 3.6 %shard_map.123 = bf16[16,40,128]{2,1,0:T(8,128)(2,1)S(1)} custom-call(bf16[512,128]{1,0:T(8,128)(2,1)S(1)} %bitcast.14, s32[4,512,128]{2,1,0:T(8,128)S(1)} %get-tuple-element.36.pos_ref, s32[1,2176]{1,0:T(1,128)S(1)} %get-tuple-element.37.kp_ref, bf16[128,2176]{1,0:T(8,128)(2,1)S(1)} %get-tuple-element.41.ka_ref, ...), custom_call_target="tpu_custom_call" | custom-call | flops 1000 | bytes 1000 | tf_op jit(solution)/shard_map/pallas_call | solution.py:399
  73.0 2.4 %collective-permute-start.7 = (bf16[16,40,128]{2,1,0:T(8,128)(2,1)S(1)}, bf16[16,40,128]{2,1,0:T(8,128)(2,1)S(1)}, u32[]{:S(2)}, u32[]{:S(2)}) collective-permute-start(bf16[16,40,128]{2,1,0:T(8,128)(2,1)S(1)} %shard_map.123), channel_id=1, source_target_pairs={{0,16},{16,0},{32,48},{48,32},{64,80},{80,64},{96,112},{112,96},{1... | collective-permute-start | bytes 491528 | tf_op jit(solution)/shard_map/ppermute | solution.py:402
  75.4 3.5 %shard_map.122 = (f32[512,128]{1,0:T(8,128)S(1)}, f32[512,128]{1,0:T(8,128)S(1)}) custom-call(bf16[512,128]{1,0:T(8,128)(2,1)S(1)} %bitcast.10, s32[4,512,128]{2,1,0:T(8,128)S(1)} %get-tuple-element.36.pos_ref, s32[1,2176]{1,0:T(1,128)S(1)} %get-tuple-element.37.kp_ref, bf16[128,2176]{1,0:T(8,128)(2,1)S(1)} %get-tuple-element.41.ka_ref, ...), custom_call_target="tpu_custom_call" | custom-call | flops 1000 | bytes 1000 | tf_op jit(solution)/shard_map/pallas_call | solution.py:403
  78.9 0.0 copy-start.5
  78.9 0.0 copy-start.7
  78.9 0.0 collective-permute-done.7.arrived_ref
  78.9 0.0 copy-start
  78.9 0.0 copy-start.1
  78.9 0.0 copy-start.11
  78.9 0.4 shard_map.124
  79.4 21.5 %all_to_all.31.arrived_ref = bf16[16,40,128]{2,1,0:T(8,128)(2,1)S(1)} all-to-all(bf16[16,40,128]{2,1,0:T(8,128)(2,1)S(1)} %shard_map.124), channel_id=1, replica_groups={{0,32,64,96,128,160,192,224,256,288,320,352,384,416,448,480},{16,48,80,..., dimensions={0} | all-to-all | bytes 327680 | tf_op jit(solution)/shard_map/all_to_all | solution.py:407
  100.9 0.7 shard_map.125
  101.5 11.3 %all_to_all.32.arrived_ref = bf16[16,32,128]{2,1,0:T(8,128)(2,1)S(1)} all-to-all(bf16[16,32,128]{2,1,0:T(8,128)(2,1)S(1)} %shard_map.125), channel_id=1, replica_groups=mesh['seq'=32,'head'=16] {'head'}, dimensions={0} | all-to-all | bytes 262144 | tf_op jit(solution)/shard_map/all_to_all | solution.py:409
  112.9 0.1 shard_map.126
  112.9 11.1 %all_to_all.33.arrived_ref = bf16[16,32,128]{2,1,0:T(8,128)(2,1)S(1)} all-to-all(bf16[16,32,128]{2,1,0:T(8,128)(2,1)S(1)} %get-tuple-element.47), channel_id=1, replica_groups=mesh['seq'=32,'head'=16] {'head'}, dimensions={0} | all-to-all | bytes 262144 | tf_op jit(solution)/shard_map/all_to_all | solution.py:413
  124.0 0.7 shard_map.127
  124.8 11.1 %all_to_all.34.arrived_ref = bf16[16,32,128]{2,1,0:T(8,128)(2,1)S(1)} all-to-all(bf16[16,32,128]{2,1,0:T(8,128)(2,1)S(1)} %shard_map.127), channel_id=1, replica_groups=mesh['seq'=32,'head'=16] {'head'}, dimensions={0} | all-to-all | bytes 262144 | tf_op jit(solution)/shard_map/all_to_all | solution.py:417
  135.8 0.7 shard_map.128
  (11 shorter events, 0.0 us)
Async XLA Ops:
  0.0 19.0 %collective-permute-start.2 = (bf16[64,2048]{1,0:T(8,128)(2,1)}, bf16[64,2048]{1,0:T(8,128)(2,1)S(1)}, u32[]{:S(2)}, u32[]{:S(2)}) collective-permute-start(bf16[64,2048]{1,0:T(8,128)(2,1)} %bitcast.19), channel_id=1, source_target_pairs={{0,2},{1,3},{2,0},{3,1},{4,6},{5,7},{6,4},{7,5},{8,10},{9,11},{10,... | collective-permute-start | bytes 786440 | tf_op jit(solution)/shard_map/ppermute | solution.py:344
  4.9 14.1 %collective-permute-start.1 = (bf16[64,2048]{1,0:T(8,128)(2,1)}, bf16[64,2048]{1,0:T(8,128)(2,1)S(1)}, u32[]{:S(2)}, u32[]{:S(2)}) collective-permute-start(bf16[64,2048]{1,0:T(8,128)(2,1)} %bitcast.20), channel_id=1, source_target_pairs={{0,3},{1,2},{2,1},{3,0},{4,7},{5,6},{6,5},{7,4},{8,11},{9,10},{10,... | collective-permute-start | bytes 786440 | tf_op jit(solution)/shard_map/ppermute | solution.py:344
  8.0 11.1 %collective-permute-start = (bf16[64,2048]{1,0:T(8,128)(2,1)}, bf16[64,2048]{1,0:T(8,128)(2,1)S(1)}, u32[]{:S(2)}, u32[]{:S(2)}) collective-permute-start(bf16[64,2048]{1,0:T(8,128)(2,1)} %bitcast.21), channel_id=1, source_target_pairs={{0,1},{1,0},{2,3},{3,2},{4,5},{5,4},{6,7},{7,6},{8,9},{9,8},{10,11... | collective-permute-start | bytes 786440 | tf_op jit(solution)/shard_map/ppermute | solution.py:344
  9.9 0.7 copy-start.6
  11.4 15.6 %all-to-all-start = ((bf16[16,32,128]{2,1,0:T(8,128)(2,1)}), bf16[16,32,128]{2,1,0:T(8,128)(2,1)S(1)}, u32[]{:S(2)}, u32[]{:S(2)}) async-start(bf16[16,32,128]{2,1,0:T(8,128)(2,1)} %shard_map.118), calls=%async_computation | async-start | bytes 262144 | tf_op jit(solution)/shard_map/all_to_all | solution.py:350
  18.9 1.3 copy-start.2
  19.0 1.3 copy-start.3
  19.0 1.3 copy-start.4
  19.0 1.3 copy-start.8
  19.0 1.3 copy-start.9
  19.0 1.3 copy-start.10
  26.9 39.8 %collective-permute-start.3 = (bf16[256,2048]{1,0:T(8,128)(2,1)S(1)}, bf16[256,2048]{1,0:T(8,128)(2,1)S(1)}, u32[]{:S(2)}, u32[]{:S(2)}) collective-permute-start(bf16[256,2048]{1,0:T(8,128)(2,1)S(1)} %pad_maximum_fusion.refs_0_), channel_id=1, source_target_pairs={{0,4},{1,5},{2,6},{3,7},{4,0},{5,1},{6,2},{7,3},{8,12},{9,13},{10,... | collective-permute-start | bytes 3145736 | tf_op jit(solution)/shard_map/ppermute | solution.py:344
  29.1 37.6 %collective-permute-start.4 = (bf16[256,2048]{1,0:T(8,128)(2,1)S(1)}, bf16[256,2048]{1,0:T(8,128)(2,1)S(1)}, u32[]{:S(2)}, u32[]{:S(2)}) collective-permute-start(bf16[256,2048]{1,0:T(8,128)(2,1)S(1)} %pad_maximum_fusion.refs_0_), channel_id=1, source_target_pairs={{0,12},{1,13},{2,14},{3,15},{4,8},{5,9},{6,10},{7,11},{8,4},{9,5},... | collective-permute-start | bytes 3145736 | tf_op jit(solution)/shard_map/ppermute | solution.py:344
  32.3 34.4 %collective-permute-start.5 = (bf16[256,2048]{1,0:T(8,128)(2,1)S(1)}, bf16[256,2048]{1,0:T(8,128)(2,1)S(1)}, u32[]{:S(2)}, u32[]{:S(2)}) collective-permute-start(bf16[256,2048]{1,0:T(8,128)(2,1)S(1)} %pad_maximum_fusion.refs_0_), channel_id=1, source_target_pairs={{0,8},{1,9},{2,10},{3,11},{4,12},{5,13},{6,14},{7,15},{8,0},{9,1},... | collective-permute-start | bytes 3145736 | tf_op jit(solution)/shard_map/ppermute | solution.py:344
  64.8 4.6 %collective-permute-start.6 = (bf16[16,32,128]{2,1,0:T(8,128)(2,1)S(1)}, bf16[16,32,128]{2,1,0:T(8,128)(2,1)S(1)}, u32[]{:S(2)}, u32[]{:S(2)}) collective-permute-start(bf16[16,32,128]{2,1,0:T(8,128)(2,1)S(1)} %all_to_all.30), channel_id=1, source_target_pairs={{0,16},{16,0},{32,48},{48,32},{64,80},{80,64},{96,112},{112,96},{1... | collective-permute-start | bytes 393224 | tf_op jit(solution)/shard_map/ppermute | solution.py:385
  73.0 6.0 %collective-permute-start.7 = (bf16[16,40,128]{2,1,0:T(8,128)(2,1)S(1)}, bf16[16,40,128]{2,1,0:T(8,128)(2,1)S(1)}, u32[]{:S(2)}, u32[]{:S(2)}) collective-permute-start(bf16[16,40,128]{2,1,0:T(8,128)(2,1)S(1)} %shard_map.123), channel_id=1, source_target_pairs={{0,16},{16,0},{32,48},{48,32},{64,80},{80,64},{96,112},{112,96},{1... | collective-permute-start | bytes 491528 | tf_op jit(solution)/shard_map/ppermute | solution.py:402
  78.9 22.0 %copy-start.5 = (bf16[64,1024]{1,0:T(8,128)(2,1)S(1)}, bf16[64,1024]{1,0:T(8,128)(2,1)}, u32[]{:S(2)}) copy-start(bf16[64,1024]{1,0:T(8,128)(2,1)} %w_ref.1) | copy-start | bytes 393220
  78.9 34.0 %copy-start.7 = (bf16[64,64]{1,0:T(8,128)(2,1)S(1)}, bf16[64,64]{1,0:T(8,128)(2,1)}, u32[]{:S(2)}) copy-start(bf16[64,64]{1,0:T(8,128)(2,1)} %lat_ref.3) | copy-start | bytes 24580
  78.9 45.1 %copy-start = (bf16[1024,256]{1,0:T(8,128)(2,1)S(1)}, bf16[1024,256]{1,0:T(8,128)(2,1)}, u32[]{:S(2)}) copy-start(bf16[1024,256]{1,0:T(8,128)(2,1)} %up_ref.1) | copy-start | bytes 1572868
  78.9 45.1 %copy-start.1 = (bf16[256,1024]{1,0:T(8,128)(2,1)S(1)}, bf16[256,1024]{1,0:T(8,128)(2,1)}, u32[]{:S(2)}) copy-start(bf16[256,1024]{1,0:T(8,128)(2,1)} %down_ref.1) | copy-start | bytes 1572868
  78.9 45.1 %copy-start.11 = (f32[1024]{0:T(1024)S(1)}, f32[1024]{0:T(1024)}, u32[]{:S(2)}) copy-start(f32[1024]{0:T(1024)} %param.21) | copy-start | bytes 12292

commit v10 on v9

--- a/solution.py
+++ b/solution.py
@@ -13,7 +13,7 @@
 NEGATIVE = -1e30
 LOWEST = -1e29
 BOTH = ("seq", "head")
-STEPS = (0, 1, 3, 2)
+STEPS = (0, 2, 3, 1)
 F32 = jnp.float32
 BF16 = jnp.bfloat16
 MIB = 1 << 20

time: 137 us -> 135 us (0.985)
  no operation moved by 1% of the time
where the time goes in v10:
time: 135 us; the launch traced here: 134 us
  blocking collectives  81.4 us (60%)
  starting transfers between devices  30.4 us (23%)
  Pallas kernels  14.9 us (11%)
  waiting for transfers between devices  5.28 us (4%)
    all_to_all x1, blocking collectives, body(): lax.all_to_all(queries, 'seq', 0, 0, axis_index_groups=along_z)  27.5 us
    all_to_all x2, blocking collectives, body(): arrived = lax.all_to_all(shares, 'head', 0, 0)  22.6 us
    all_to_all x1, blocking collectives, body(): arrived = lax.all_to_all(joined, 'seq', 0, 0, axis_index_groups=along_z)  20.2 us
    ppermute x6, starting transfers between devices, swap_lines(): return lax.ppermute(piece, BOTH, partners(seq_size, side, phase, step))  19.2 us
    all_to_all x1, blocking collectives, body(): arrived = lax.all_to_all(copies, 'head', 0, 0)  11.1 us
    all_to_all x1, starting transfers between devices, body(): lat_blocks = lax.all_to_all(copies, 'head', 0, 0)  6.89 us
    all_to_all x1, waiting for transfers between devices, body(): lat_blocks = lax.all_to_all(copies, 'head', 0, 0)  5.25 us
    pallas_call x1, Pallas kernels, body(): call(other_kernel, [(message, BF16)])  3.59 us
  transfers between devices with their start and end apart: 9, of which 1 were waited for; matrix products, arithmetic and copies ran while one was open for 1% of the time, Pallas kernels for 6%

profile of v10, /device:TPU:32, one launch (start us, length us, event | category | flops | bytes accessed | tf_op | source)
XLA Modules:
  0.0 134.2 jit_solution(2875725506468990270)
XLA Ops:
  0.0 3.4 %collective-permute-start.2 = (bf16[64,2048]{1,0:T(8,128)(2,1)}, bf16[64,2048]{1,0:T(8,128)(2,1)S(1)}, u32[]{:S(2)}, u32[]{:S(2)}) collective-permute-start(bf16[64,2048]{1,0:T(8,128)(2,1)} %bitcast.19), channel_id=1, source_target_pairs={{0,1},{1,0},{2,3},{3,2},{4,5},{5,4},{6,7},{7,6},{8,9},{9,8},{10,11... | collective-permute-start | bytes 786440 | tf_op jit(solution)/shard_map/ppermute | solution.py:344
  3.4 4.0 %collective-permute-start.1 = (bf16[64,2048]{1,0:T(8,128)(2,1)}, bf16[64,2048]{1,0:T(8,128)(2,1)S(1)}, u32[]{:S(2)}, u32[]{:S(2)}) collective-permute-start(bf16[64,2048]{1,0:T(8,128)(2,1)} %bitcast.20), channel_id=1, source_target_pairs={{0,3},{1,2},{2,1},{3,0},{4,7},{5,6},{6,5},{7,4},{8,11},{9,10},{10,... | collective-permute-start | bytes 786440 | tf_op jit(solution)/shard_map/ppermute | solution.py:344
  7.4 2.6 %collective-permute-start = (bf16[64,2048]{1,0:T(8,128)(2,1)}, bf16[64,2048]{1,0:T(8,128)(2,1)S(1)}, u32[]{:S(2)}, u32[]{:S(2)}) collective-permute-start(bf16[64,2048]{1,0:T(8,128)(2,1)} %bitcast.21), channel_id=1, source_target_pairs={{0,2},{1,3},{2,0},{3,1},{4,6},{5,7},{6,4},{7,5},{8,10},{9,11},{10,... | collective-permute-start | bytes 786440 | tf_op jit(solution)/shard_map/ppermute | solution.py:344
  10.0 0.0 copy-start.6
  10.0 0.7 copy-done.6
  10.7 0.7 shard_map.118
  11.4 6.9 %all-to-all-start = ((bf16[16,32,128]{2,1,0:T(8,128)(2,1)}), bf16[16,32,128]{2,1,0:T(8,128)(2,1)S(1)}, u32[]{:S(2)}, u32[]{:S(2)}) async-start(bf16[16,32,128]{2,1,0:T(8,128)(2,1)} %shard_map.118), calls=%async_computation | async-start | bytes 262144 | tf_op jit(solution)/shard_map/all_to_all | solution.py:350
  18.3 0.0 copy-start.2
  18.4 0.0 copy-start.3
  18.4 0.0 copy-start.4
  18.4 0.0 copy-start.8
  18.4 0.0 copy-start.9
  18.4 0.0 copy-start.10
  18.4 0.0 collective-permute-done.2
  18.4 0.0 collective-permute-done.1
  18.4 0.0 collective-permute-done
  18.4 1.2 pad_maximum_fusion.refs_0_
  19.7 1.4 %shard_map.119 = (bf16[128,1024]{1,0:T(8,128)(2,1)S(1)}, bf16[192,1024]{1,0:T(8,128)(2,1)S(1)}, s32[1,2176]{1,0:T(1,128)S(1)}, s32[4,512,128]{2,1,0:T(8,128)S(1)}) custom-call(bf16[64,1024]{1,0:T(8,128)(2,1)S(1)} %bitcast.11, bf16[64,1024]{1,0:T(8,128)(2,1)S(1)} %bitcast.12, bf16[64,1024]{1,0:T(8,128)(2,1)S(1)} %bitcast.13, f32[1,1024]{1,0:T(1,128)S(1)} %bitcast.17, ...), custom_call_target="tpu_custom_call" | custom-call | flops 1000 | bytes 1000 | tf_op jit(solution)/shard_map/pallas_call | solution.py:352
  21.1 5.3 %all-to-all-done.lat_ref = bf16[16,32,128]{2,1,0:T(8,128)(2,1)S(1)} async-done(((bf16[16,32,128]{2,1,0:T(8,128)(2,1)}), bf16[16,32,128]{2,1,0:T(8,128)(2,1)S(1)}, u32[]{:S(2)}, u32[]{:S(2)}) %all-to-all-start) | async-done | bytes 131104 | tf_op jit(solution)/shard_map/all_to_all | solution.py:350
  26.3 2.9 %collective-permute-start.3 = (bf16[256,2048]{1,0:T(8,128)(2,1)S(1)}, bf16[256,2048]{1,0:T(8,128)(2,1)S(1)}, u32[]{:S(2)}, u32[]{:S(2)}) collective-permute-start(bf16[256,2048]{1,0:T(8,128)(2,1)S(1)} %pad_maximum_fusion.refs_0_), channel_id=1, source_target_pairs={{0,8},{1,9},{2,10},{3,11},{4,12},{5,13},{6,14},{7,15},{8,0},{9,1},... | collective-permute-start | bytes 3145736 | tf_op jit(solution)/shard_map/ppermute | solution.py:344
  29.2 3.9 %collective-permute-start.4 = (bf16[256,2048]{1,0:T(8,128)(2,1)S(1)}, bf16[256,2048]{1,0:T(8,128)(2,1)S(1)}, u32[]{:S(2)}, u32[]{:S(2)}) collective-permute-start(bf16[256,2048]{1,0:T(8,128)(2,1)S(1)} %pad_maximum_fusion.refs_0_), channel_id=1, source_target_pairs={{0,12},{1,13},{2,14},{3,15},{4,8},{5,9},{6,10},{7,11},{8,4},{9,5},... | collective-permute-start | bytes 3145736 | tf_op jit(solution)/shard_map/ppermute | solution.py:344
  33.1 2.4 %collective-permute-start.5 = (bf16[256,2048]{1,0:T(8,128)(2,1)S(1)}, bf16[256,2048]{1,0:T(8,128)(2,1)S(1)}, u32[]{:S(2)}, u32[]{:S(2)}) collective-permute-start(bf16[256,2048]{1,0:T(8,128)(2,1)S(1)} %pad_maximum_fusion.refs_0_), channel_id=1, source_target_pairs={{0,4},{1,5},{2,6},{3,7},{4,0},{5,1},{6,2},{7,3},{8,12},{9,13},{10,... | collective-permute-start | bytes 3145736 | tf_op jit(solution)/shard_map/ppermute | solution.py:344
  35.6 0.5 shard_map.120
  36.0 27.5 %all_to_all.30 = bf16[16,32,128]{2,1,0:T(8,128)(2,1)S(1)} all-to-all(bf16[16,32,128]{2,1,0:T(8,128)(2,1)S(1)} %get-tuple-element.35), channel_id=1, replica_groups={{0,32,64,96,128,160,192,224,256,288,320,352,384,416,448,480},{16,48,80,..., dimensions={0} | all-to-all | bytes 262144 | tf_op jit(solution)/shard_map/all_to_all | solution.py:384
  63.6 1.9 %collective-permute-start.6 = (bf16[16,32,128]{2,1,0:T(8,128)(2,1)S(1)}, bf16[16,32,128]{2,1,0:T(8,128)(2,1)S(1)}, u32[]{:S(2)}, u32[]{:S(2)}) collective-permute-start(bf16[16,32,128]{2,1,0:T(8,128)(2,1)S(1)} %all_to_all.30), channel_id=1, source_target_pairs={{0,16},{16,0},{32,48},{48,32},{64,80},{80,64},{96,112},{112,96},{1... | collective-permute-start | bytes 393224 | tf_op jit(solution)/shard_map/ppermute | solution.py:385
  65.5 0.0 collective-permute-done.3.refs_1_
  65.5 0.0 collective-permute-done.4.refs_2_
  65.5 0.0 collective-permute-done.5.refs_3_
  65.5 2.6 %shard_map.121 = (bf16[128,2176]{1,0:T(8,128)(2,1)S(1)}, bf16[128,2176]{1,0:T(8,128)(2,1)S(1)}, bf16[2176,128]{1,0:T(8,128)(2,1)S(1)}, bf16[2176,128]{1,0:T(8,128)(2,1)S(1)}) custom-call(bf16[256,2048]{1,0:T(8,128)(2,1)S(1)} %pad_maximum_fusion.refs_0_, bf16[256,2048]{1,0:T(8,128)(2,1)S(1)} %collective-permute-done.3.refs_1_, ...), custom_call_target="tpu_custom_call" | custom-call | flops 1000000000 | bytes 1000000000 | tf_op jit(solution)/shard_map/pallas_call | solution.py:387
  68.1 0.0 collective-permute-done.6
  68.1 3.6 %shard_map.123 = bf16[16,40,128]{2,1,0:T(8,128)(2,1)S(1)} custom-call(bf16[512,128]{1,0:T(8,128)(2,1)S(1)} %bitcast.14, s32[4,512,128]{2,1,0:T(8,128)S(1)} %get-tuple-element.36.pos_ref, s32[1,2176]{1,0:T(1,128)S(1)} %get-tuple-element.37.kp_ref, bf16[128,2176]{1,0:T(8,128)(2,1)S(1)} %get-tuple-element.41.ka_ref, ...), custom_call_target="tpu_custom_call" | custom-call | flops 1000 | bytes 1000 | tf_op jit(solution)/shard_map/pallas_call | solution.py:399
  71.7 2.4 %collective-permute-start.7 = (bf16[16,40,128]{2,1,0:T(8,128)(2,1)S(1)}, bf16[16,40,128]{2,1,0:T(8,128)(2,1)S(1)}, u32[]{:S(2)}, u32[]{:S(2)}) collective-permute-start(bf16[16,40,128]{2,1,0:T(8,128)(2,1)S(1)} %shard_map.123), channel_id=1, source_target_pairs={{0,16},{16,0},{32,48},{48,32},{64,80},{80,64},{96,112},{112,96},{1... | collective-permute-start | bytes 491528 | tf_op jit(solution)/shard_map/ppermute | solution.py:402
  74.1 3.5 %shard_map.122 = (f32[512,128]{1,0:T(8,128)S(1)}, f32[512,128]{1,0:T(8,128)S(1)}) custom-call(bf16[512,128]{1,0:T(8,128)(2,1)S(1)} %bitcast.10, s32[4,512,128]{2,1,0:T(8,128)S(1)} %get-tuple-element.36.pos_ref, s32[1,2176]{1,0:T(1,128)S(1)} %get-tuple-element.37.kp_ref, bf16[128,2176]{1,0:T(8,128)(2,1)S(1)} %get-tuple-element.41.ka_ref, ...), custom_call_target="tpu_custom_call" | custom-call | flops 1000 | bytes 1000 | tf_op jit(solution)/shard_map/pallas_call | solution.py:403
  77.7 0.0 copy-start.5
  77.7 0.0 copy-start.7
  77.7 0.0 collective-permute-done.7.arrived_ref
  77.7 0.0 copy-start
  77.7 0.0 copy-start.1
  77.7 0.0 copy-start.11
  77.7 0.4 shard_map.124
  78.2 20.2 %all_to_all.31.arrived_ref = bf16[16,40,128]{2,1,0:T(8,128)(2,1)S(1)} all-to-all(bf16[16,40,128]{2,1,0:T(8,128)(2,1)S(1)} %shard_map.124), channel_id=1, replica_groups={{0,32,64,96,128,160,192,224,256,288,320,352,384,416,448,480},{16,48,80,..., dimensions={0} | all-to-all | bytes 327680 | tf_op jit(solution)/shard_map/all_to_all | solution.py:407
  98.3 0.7 shard_map.125
  99.0 11.5 %all_to_all.32.arrived_ref = bf16[16,32,128]{2,1,0:T(8,128)(2,1)S(1)} all-to-all(bf16[16,32,128]{2,1,0:T(8,128)(2,1)S(1)} %shard_map.125), channel_id=1, replica_groups=mesh['seq'=32,'head'=16] {'head'}, dimensions={0} | all-to-all | bytes 262144 | tf_op jit(solution)/shard_map/all_to_all | solution.py:409
  110.5 0.1 shard_map.126
  110.6 11.1 %all_to_all.33.arrived_ref = bf16[16,32,128]{2,1,0:T(8,128)(2,1)S(1)} all-to-all(bf16[16,32,128]{2,1,0:T(8,128)(2,1)S(1)} %get-tuple-element.47), channel_id=1, replica_groups=mesh['seq'=32,'head'=16] {'head'}, dimensions={0} | all-to-all | bytes 262144 | tf_op jit(solution)/shard_map/all_to_all | solution.py:413
  121.7 0.7 shard_map.127
  122.4 11.1 %all_to_all.34.arrived_ref = bf16[16,32,128]{2,1,0:T(8,128)(2,1)S(1)} all-to-all(bf16[16,32,128]{2,1,0:T(8,128)(2,1)S(1)} %shard_map.127), channel_id=1, replica_groups=mesh['seq'=32,'head'=16] {'head'}, dimensions={0} | all-to-all | bytes 262144 | tf_op jit(solution)/shard_map/all_to_all | solution.py:417
  133.5 0.7 shard_map.128
  (11 shorter events, 0.0 us)
Async XLA Ops:
  0.0 18.4 %collective-permute-start.2 = (bf16[64,2048]{1,0:T(8,128)(2,1)}, bf16[64,2048]{1,0:T(8,128)(2,1)S(1)}, u32[]{:S(2)}, u32[]{:S(2)}) collective-permute-start(bf16[64,2048]{1,0:T(8,128)(2,1)} %bitcast.19), channel_id=1, source_target_pairs={{0,1},{1,0},{2,3},{3,2},{4,5},{5,4},{6,7},{7,6},{8,9},{9,8},{10,11... | collective-permute-start | bytes 786440 | tf_op jit(solution)/shard_map/ppermute | solution.py:344
  3.4 15.0 %collective-permute-start.1 = (bf16[64,2048]{1,0:T(8,128)(2,1)}, bf16[64,2048]{1,0:T(8,128)(2,1)S(1)}, u32[]{:S(2)}, u32[]{:S(2)}) collective-permute-start(bf16[64,2048]{1,0:T(8,128)(2,1)} %bitcast.20), channel_id=1, source_target_pairs={{0,3},{1,2},{2,1},{3,0},{4,7},{5,6},{6,5},{7,4},{8,11},{9,10},{10,... | collective-permute-start | bytes 786440 | tf_op jit(solution)/shard_map/ppermute | solution.py:344
  7.4 11.0 %collective-permute-start = (bf16[64,2048]{1,0:T(8,128)(2,1)}, bf16[64,2048]{1,0:T(8,128)(2,1)S(1)}, u32[]{:S(2)}, u32[]{:S(2)}) collective-permute-start(bf16[64,2048]{1,0:T(8,128)(2,1)} %bitcast.21), channel_id=1, source_target_pairs={{0,2},{1,3},{2,0},{3,1},{4,6},{5,7},{6,4},{7,5},{8,10},{9,11},{10,... | collective-permute-start | bytes 786440 | tf_op jit(solution)/shard_map/ppermute | solution.py:344
  10.0 0.7 copy-start.6
  11.4 14.9 %all-to-all-start = ((bf16[16,32,128]{2,1,0:T(8,128)(2,1)}), bf16[16,32,128]{2,1,0:T(8,128)(2,1)S(1)}, u32[]{:S(2)}, u32[]{:S(2)}) async-start(bf16[16,32,128]{2,1,0:T(8,128)(2,1)} %shard_map.118), calls=%async_computation | async-start | bytes 262144 | tf_op jit(solution)/shard_map/all_to_all | solution.py:350
  18.3 1.3 copy-start.2
  18.4 1.3 copy-start.3
  18.4 1.3 copy-start.4
  18.4 1.3 copy-start.8
  18.4 1.3 copy-start.9
  18.4 1.3 copy-start.10
  26.3 39.2 %collective-permute-start.3 = (bf16[256,2048]{1,0:T(8,128)(2,1)S(1)}, bf16[256,2048]{1,0:T(8,128)(2,1)S(1)}, u32[]{:S(2)}, u32[]{:S(2)}) collective-permute-start(bf16[256,2048]{1,0:T(8,128)(2,1)S(1)} %pad_maximum_fusion.refs_0_), channel_id=1, source_target_pairs={{0,8},{1,9},{2,10},{3,11},{4,12},{5,13},{6,14},{7,15},{8,0},{9,1},... | collective-permute-start | bytes 3145736 | tf_op jit(solution)/shard_map/ppermute | solution.py:344
  29.2 36.3 %collective-permute-start.4 = (bf16[256,2048]{1,0:T(8,128)(2,1)S(1)}, bf16[256,2048]{1,0:T(8,128)(2,1)S(1)}, u32[]{:S(2)}, u32[]{:S(2)}) collective-permute-start(bf16[256,2048]{1,0:T(8,128)(2,1)S(1)} %pad_maximum_fusion.refs_0_), channel_id=1, source_target_pairs={{0,12},{1,13},{2,14},{3,15},{4,8},{5,9},{6,10},{7,11},{8,4},{9,5},... | collective-permute-start | bytes 3145736 | tf_op jit(solution)/shard_map/ppermute | solution.py:344
  33.1 32.4 %collective-permute-start.5 = (bf16[256,2048]{1,0:T(8,128)(2,1)S(1)}, bf16[256,2048]{1,0:T(8,128)(2,1)S(1)}, u32[]{:S(2)}, u32[]{:S(2)}) collective-permute-start(bf16[256,2048]{1,0:T(8,128)(2,1)S(1)} %pad_maximum_fusion.refs_0_), channel_id=1, source_target_pairs={{0,4},{1,5},{2,6},{3,7},{4,0},{5,1},{6,2},{7,3},{8,12},{9,13},{10,... | collective-permute-start | bytes 3145736 | tf_op jit(solution)/shard_map/ppermute | solution.py:344
  63.6 4.6 %collective-permute-start.6 = (bf16[16,32,128]{2,1,0:T(8,128)(2,1)S(1)}, bf16[16,32,128]{2,1,0:T(8,128)(2,1)S(1)}, u32[]{:S(2)}, u32[]{:S(2)}) collective-permute-start(bf16[16,32,128]{2,1,0:T(8,128)(2,1)S(1)} %all_to_all.30), channel_id=1, source_target_pairs={{0,16},{16,0},{32,48},{48,32},{64,80},{80,64},{96,112},{112,96},{1... | collective-permute-start | bytes 393224 | tf_op jit(solution)/shard_map/ppermute | solution.py:385
  71.7 6.0 %collective-permute-start.7 = (bf16[16,40,128]{2,1,0:T(8,128)(2,1)S(1)}, bf16[16,40,128]{2,1,0:T(8,128)(2,1)S(1)}, u32[]{:S(2)}, u32[]{:S(2)}) collective-permute-start(bf16[16,40,128]{2,1,0:T(8,128)(2,1)S(1)} %shard_map.123), channel_id=1, source_target_pairs={{0,16},{16,0},{32,48},{48,32},{64,80},{80,64},{96,112},{112,96},{1... | collective-permute-start | bytes 491528 | tf_op jit(solution)/shard_map/ppermute | solution.py:402
  77.7 20.7 %copy-start.5 = (bf16[64,1024]{1,0:T(8,128)(2,1)S(1)}, bf16[64,1024]{1,0:T(8,128)(2,1)}, u32[]{:S(2)}) copy-start(bf16[64,1024]{1,0:T(8,128)(2,1)} %w_ref.1) | copy-start | bytes 393220
  77.7 32.9 %copy-start.7 = (bf16[64,64]{1,0:T(8,128)(2,1)S(1)}, bf16[64,64]{1,0:T(8,128)(2,1)}, u32[]{:S(2)}) copy-start(bf16[64,64]{1,0:T(8,128)(2,1)} %lat_ref.3) | copy-start | bytes 24580
  77.7 44.0 %copy-start = (bf16[1024,256]{1,0:T(8,128)(2,1)S(1)}, bf16[1024,256]{1,0:T(8,128)(2,1)}, u32[]{:S(2)}) copy-start(bf16[1024,256]{1,0:T(8,128)(2,1)} %up_ref.1) | copy-start | bytes 1572868
  77.7 44.0 %copy-start.1 = (bf16[256,1024]{1,0:T(8,128)(2,1)S(1)}, bf16[256,1024]{1,0:T(8,128)(2,1)}, u32[]{:S(2)}) copy-start(bf16[256,1024]{1,0:T(8,128)(2,1)} %down_ref.1) | copy-start | bytes 1572868
  77.7 44.0 %copy-start.11 = (f32[1024]{0:T(1024)S(1)}, f32[1024]{0:T(1024)}, u32[]{:S(2)}) copy-start(f32[1024]{0:T(1024)} %param.21) | copy-start | bytes 12292

commit v11 on v9

--- a/solution.py
+++ b/solution.py
@@ -17,6 +17,7 @@
 F32 = jnp.float32
 BF16 = jnp.bfloat16
 MIB = 1 << 20
+NEVER = (1 << 18) - 1
 
 
 def dot(a, b, dims):
@@ -76,8 +77,8 @@
 
 
 def prepare_kernel(*refs):
-    given, outs, held, scratch, sems = refs[:6], refs[6:10], refs[10:16], refs[16], refs[17]
-    w_ref, all_ref, kp_ref, pos_ref = outs
+    given, outs, held, scratch, sems = refs[:6], refs[6:11], refs[11:17], refs[17], refs[18]
+    w_ref, all_ref, kp_ref, digits_ref, pos_ref = outs
     copies = [pltpu.make_async_copy(a, b, sems.at[i]) for i, (a, b) in enumerate(zip(given, held))]
     for copy in copies:
         copy.start()
@@ -98,20 +99,22 @@
         kp_ref[:, 128 * i : 128 * i + 128] = ctx_ref[i : i + 1, :]
     own = lat_ref[pl.ds(plane, 1), :]
     own = jnp.where(core == 0, own, pltpu.roll(own, 64, 1))
+    own = jnp.where(low_half(own.shape), own, NEVER)
     last = 128 * ctx_ref.shape[0]
-    kp_ref[:, last : last + 128] = jnp.where(low_half(own.shape), own, jnp.iinfo(jnp.int32).max)
+    kp_ref[:, last : last + 128] = own
+    every = jnp.concatenate([ctx_ref[...], own, jnp.zeros((15, 128), jnp.int32)], axis=0)
+    for t in range(3):
+        digit = (every >> (6 * t)) & 63
+        digits_ref[32 * t : 32 * t + 32] = digit.astype(F32).astype(BF16)
     planes = lat_ref.shape[0]
     lat = lat_ref[...]
-    swapped = pltpu.roll(lat, 64, 1)
-    mine = jnp.where(core == 0, lat, swapped)
-    theirs = jnp.where(core == 0, swapped, lat)
-    wide = jnp.concatenate([theirs, mine, jnp.zeros((128 - 2 * planes, 128), jnp.int32)], axis=0)
+    mine = jnp.where(core == 0, lat, pltpu.roll(lat, 64, 1))
+    wide = jnp.concatenate([mine, jnp.zeros((128 - planes, 128), jnp.int32)], axis=0)
     columns = wide.T
-    for k in range(4):
-        part = columns[32 * (k % 2) : 32 * (k % 2) + 32]
+    for k in range(2):
+        part = columns[32 * k : 32 * k + 32]
         for z in range(planes):
-            lane = (k // 2) * planes + z
-            pos_ref[k, 32 * z : 32 * z + 32] = jnp.broadcast_to(part[:, lane : lane + 1], (32, 128))
+            pos_ref[k, 32 * z : 32 * z + 32] = jnp.broadcast_to(part[:, z : z + 1], (32, 128))
 
 
 def queries_kernel(lat_ref, w_ref, q_ref, kv_ref):
@@ -127,7 +130,7 @@
 
 
 def keys_kernel(*refs):
-    *line_refs, w_ref, lat_ref, ka_ref, kb_ref, va_ref, vb_ref, held, sems = refs
+    *line_refs, w_ref, lat_ref, digits_ref, k_ref, v_ref, kv_ref, held, sems = refs
     height, tokens = line_refs[0].shape
     width = 512
     copies = []
@@ -143,7 +146,8 @@
         )
         for copy in copies[c]:
             copy.start()
-    put_keys(lat_ref[...], slice(tokens, tokens + 128), ka_ref, kb_ref, va_ref, vb_ref)
+    put_keys(lat_ref[...], slice(tokens, tokens + 128), k_ref, v_ref, kv_ref)
+    kv_ref[tokens + 128 :] = digits_ref[...]
     weights = w_ref[...]
     for c in range(tokens // width):
         cols = slice(c * width, c * width + width)
@@ -154,36 +158,35 @@
         squares = jnp.sum(wide * wide, axis=0, keepdims=True)
         inverse = lax.rsqrt(squares * (1.0 / 1024) + EPSILON)
         both = (dot(weights, piece, NN) * inverse).astype(BF16)
-        put_keys(both, cols, ka_ref, kb_ref, va_ref, vb_ref)
-
-
-def put_keys(both, cols, ka_ref, kb_ref, va_ref, vb_ref):
+        put_keys(both, cols, k_ref, v_ref, kv_ref)
+
+
+def put_keys(both, cols, k_ref, v_ref, kv_ref):
     keys, values = both[:64], both[64:]
-    none = jnp.zeros_like(keys)
-    ka_ref[:, cols] = jnp.concatenate([keys, none], axis=0)
-    kb_ref[:, cols] = jnp.concatenate([none, keys], axis=0)
-    ones = jnp.ones(values.shape, F32)
-    va_ref[cols, :] = jnp.concatenate([values.astype(F32), ones], axis=0).T.astype(BF16)
-    vb_ref[cols, :] = jnp.concatenate([ones, values.astype(F32)], axis=0).T.astype(BF16)
-
-
-def attend_all(q_ref, pos_ref, first, kp_ref, key_refs, value_refs, put):
+    k_ref[:, cols] = jnp.concatenate([keys, keys], axis=0)
+    rows = jnp.concatenate([values, keys], axis=0).astype(F32).T
+    kv_ref[cols, :] = rows.astype(BF16)
+    v_ref[cols, :] = jnp.where(low_half(rows.shape), rows, 1.0).astype(BF16)
+
+
+def attend_all(q_ref, pos_ref, kp, k_ref, v_ref, put):
     step = 256
-    kp = kp_ref[...]
     pieces = [(i, h) for i in range(0, q_ref.shape[0], step) for h in range(2)]
+    low = low_half((step, 128))
 
     def scores_of(piece):
         i, h = piece
-        return dot(q_ref[i : i + step], key_refs[h][...], NN)
+        q = q_ref[i : i + step].astype(F32)
+        q = jnp.where(low, q, 0.0) if h == 0 else jnp.where(low, 0.0, q)
+        return dot(q.astype(BF16), k_ref[...], NN)
 
     def finish(piece, weights, top):
         i, h = piece
-        done[h] = (dot(weights, value_refs[h][...], NN), top)
+        done[h] = (dot(weights, v_ref[...], NN), top)
         if h == 1:
             (out_a, top_a), (out_b, top_b) = done
-            low = low_half(out_a.shape)
-            above = jnp.where(low, out_a, out_b)
-            below = jnp.maximum(pltpu.roll(jnp.where(low, out_b, out_a), 64, 1), 1e-30)
+            above = jnp.where(low, out_a, pltpu.roll(out_b, 64, 1))
+            below = jnp.maximum(jnp.where(low, pltpu.roll(out_a, 64, 1), out_b), 1e-30)
             put(i, above / below, jnp.where(low, top_a, top_b) + jnp.log(below))
 
     done = [None, None]
@@ -191,7 +194,7 @@
     scores = scores_of(pieces[0])
     for n, (i, h) in enumerate(pieces):
         following = scores_of(pieces[n + 1]) if n + 1 < len(pieces) else None
-        visible = kp <= pos_ref[first + h, i : i + step, 0:1]
+        visible = kp <= pos_ref[h, i : i + step, 0:1]
         scores = jnp.where(visible, scores, NEGATIVE)
         top = jnp.maximum(jnp.max(scores, axis=1, keepdims=True), LOWEST)
         weights = jnp.exp(scores - top).astype(BF16)
@@ -234,34 +237,39 @@
     return values, levels
 
 
-def other_kernel(q_ref, pos_ref, kp_ref, ka_ref, kb_ref, va_ref, vb_ref, out_ref):
+def own_kernel(q_ref, pos_ref, kp_ref, k_ref, v_ref, mix_ref, lev_ref):
     def put(row, mixed, level):
+        mix_ref[row : row + mixed.shape[0]] = mixed
+        lev_ref[row : row + mixed.shape[0]] = level
+
+    attend_all(q_ref, pos_ref, kp_ref[...], k_ref, v_ref, put)
+
+
+def sibling_kernel(q_ref, pos_ref, kv_ref, mix_ref, lev_ref, out_ref, k_ref, v_ref):
+    count = k_ref.shape[1]
+    digits = [kv_ref[count + 32 * t : count + 32 * t + 32].astype(F32) for t in range(3)]
+    places = (digits[0] + 64.0 * digits[1] + 4096.0 * digits[2]).astype(jnp.int32)
+    kp = jnp.concatenate([places[c : c + 1] for c in range(count // 128)], axis=1)
+    for c in range(count // 128):
+        part = slice(128 * c, 128 * c + 128)
+        rows = kv_ref[part].astype(F32)
+        keys = rows.T[64:]
+        k_ref[:, part] = jnp.concatenate([keys, keys], axis=0).astype(BF16)
+        v_ref[part] = jnp.where(low_half(rows.shape), rows, 1.0).astype(BF16)
+
+    def put(row, values, levels):
+        rows = slice(row, row + values.shape[0])
+        mine = lev_ref[rows]
+        top = jnp.maximum(mine, levels)
+        a, b = jnp.exp(mine - top), jnp.exp(levels - top)
+        total = a + b
+        mixed = (mix_ref[rows] * a + values * b) / total
+        level = top + jnp.log(total)
         for g in range(mixed.shape[0] // 32):
             part = slice(32 * g, 32 * g + 32)
             put_message(mixed[part], level[part], out_ref, row // 32 + g)
 
-    attend_all(q_ref, pos_ref, 0, kp_ref, (ka_ref, kb_ref), (va_ref, vb_ref), put)
-
-
-def own_kernel(q_ref, pos_ref, kp_ref, ka_ref, kb_ref, va_ref, vb_ref, mix_ref, lev_ref):
-    def put(row, mixed, level):
-        mix_ref[row : row + mixed.shape[0]] = mixed
-        lev_ref[row : row + mixed.shape[0]] = level
-
-    attend_all(q_ref, pos_ref, 2, kp_ref, (ka_ref, kb_ref), (va_ref, vb_ref), put)
-
-
-def join_kernel(mix_ref, lev_ref, arrived_ref, out_ref):
-    values, levels = get_message(arrived_ref)
-    mine = lev_ref[...]
-    top = jnp.maximum(mine, levels)
-    a, b = jnp.exp(mine - top), jnp.exp(levels - top)
-    total = a + b
-    mixed = (mix_ref[...] * a + values * b) / total
-    level = top + jnp.log(total)
-    for g in range(out_ref.shape[0]):
-        part = slice(32 * g, 32 * g + 32)
-        put_message(mixed[part], level[part], out_ref, g)
+    attend_all(q_ref, pos_ref, kp, k_ref, v_ref, put)
 
 
 def project_kernel(arrived_ref, w_ref, out_ref):
@@ -355,7 +363,8 @@
             ((2 * cols, head_size * cols), BF16),
             ((3 * cols, head_size * cols), BF16),
             ((1, key_count), jnp.int32),
-            ((4, rows, 2 * cols), jnp.int32),
+            ((96, 2 * cols), BF16),
+            ((2, rows, 2 * cols), jnp.int32),
         ],
         in_specs=[anywhere] * 6,
         scratch_shapes=[pltpu.VMEM((cols, head_size * cols), BF16)] * 3
@@ -375,35 +384,38 @@
         lat_pos.reshape(-1, 2 * lat_rows),
     )
     line, lat_blocks, prepared = lax.optimization_barrier((line, lat_blocks, prepared))
-    key_weights, all_weights, key_pos, query_pos = prepared
+    key_weights, all_weights, key_pos, digits, query_pos = prepared
     lines = [line] + [swap_lines(line, 1, step) for step in STEPS[1:]]
 
     queries, latent_kv = call(
         queries_kernel, [((planes, *block), BF16), ((2 * cols, 2 * lat_rows), BF16)]
     )(lat_blocks, all_weights)
     own_queries = lax.all_to_all(queries, "seq", 0, 0, axis_index_groups=along_z)
-    other_queries = lax.ppermute(own_queries, "seq", swap)
-
-    operands = call(
+    own_queries = own_queries.reshape(rows, -1)
+    own_queries, key_weights = lax.optimization_barrier((own_queries, key_weights))
+
+    keys, values, both = call(
         keys_kernel,
-        [((128, key_count), BF16)] * 2 + [((key_count, 128), BF16)] * 2,
+        [((128, key_count), BF16), ((key_count, 128), BF16), ((key_count + 96, 128), BF16)],
         cost=10**9,
-        in_specs=[anywhere] * side + [vmem] * 2,
+        in_specs=[anywhere] * side + [vmem] * 3,
         scratch_shapes=[
             pltpu.VMEM((head_size * cols, tokens), BF16),
             pltpu.SemaphoreType.DMA((4, side)),
         ],
-    )(*lines, key_weights, latent_kv)
-
-    message = (planes, 40, 2 * cols)
-    to_sibling = call(other_kernel, [(message, BF16)])(
-        other_queries.reshape(rows, -1), query_pos, key_pos, *operands
-    )
-    from_sibling = lax.ppermute(to_sibling, "seq", swap)
+    )(*lines, key_weights, latent_kv, digits)
+    from_sibling = lax.ppermute(both, "seq", swap)
     mixed, level = call(own_kernel, [((rows, 2 * cols), F32)] * 2)(
-        own_queries.reshape(rows, -1), query_pos, key_pos, *operands
-    )
-    joined = call(join_kernel, [(message, BF16)])(mixed, level, from_sibling)
+        own_queries, query_pos, key_pos, keys, values
+    )
+    joined = call(
+        sibling_kernel,
+        [((planes, 40, 2 * cols), BF16)],
+        scratch_shapes=[
+            pltpu.VMEM((128, key_count), BF16),
+            pltpu.VMEM((key_count, 128), BF16),
+        ],
+    )(own_queries, query_pos, from_sibling, mixed, level)
     arrived = lax.all_to_all(joined, "seq", 0, 0, axis_index_groups=along_z)
     shares = call(project_kernel, [((head_size, *block), BF16)])(arrived, w_out)
     arrived = lax.all_to_all(shares, "head", 0, 0)

time: 137 us -> 135 us (0.985)
  starting transfers between devices: 31.6 us -> 28.6 us
    ppermute x2 -> x1, starting transfers between devices: 4.31 us -> 1.92 us  [body(): from_sibling = lax.ppermute(both, 'seq', swap)]
    pallas_call x3 -> x2, Pallas kernels: 6.64 us -> 6.08 us  [the longest x1 3.85 us: body(): call(sibling_kernel, [((planes, 40, 2 * cols), BF16)], scratch_shapes=[pl...]
  transfers between devices with their start and end apart: 9 -> 8, of which waited for: 1 -> 1; matrix products, arithmetic and copies ran while one was open for 1% -> 1% of each run, Pallas kernels for 6% -> 5%
where the time goes in v11:
time: 135 us; the launch traced here: 134 us
  blocking collectives  83.5 us (62%)
  starting transfers between devices  28.6 us (21%)
  Pallas kernels  14.3 us (11%)
  waiting for transfers between devices  5.45 us (4%)
    all_to_all x1, blocking collectives, body(): lax.all_to_all(queries, 'seq', 0, 0, axis_index_groups=along_z)  27.6 us
    all_to_all x1, blocking collectives, body(): arrived = lax.all_to_all(joined, 'seq', 0, 0, axis_index_groups=along_z)  22.7 us
    all_to_all x2, blocking collectives, body(): arrived = lax.all_to_all(shares, 'head', 0, 0)  22.1 us
    ppermute x6, starting transfers between devices, swap_lines(): return lax.ppermute(piece, BOTH, partners(seq_size, side, phase, step))  19.1 us
    all_to_all x1, blocking collectives, body(): arrived = lax.all_to_all(copies, 'head', 0, 0)  11.1 us
    all_to_all x1, starting transfers between devices, body(): lat_blocks = lax.all_to_all(copies, 'head', 0, 0)  7.56 us
    all_to_all x1, waiting for transfers between devices, body(): lat_blocks = lax.all_to_all(copies, 'head', 0, 0)  5.43 us
    pallas_call x1, Pallas kernels, body(): call(sibling_kernel, [((planes, 40, 2 * cols), BF16)], scratch_shapes=[pl...  3.85 us
  transfers between devices with their start and end apart: 8, of which 1 were waited for; matrix products, arithmetic and copies ran while one was open for 1% of the time, Pallas kernels for 5%

profile of v11, /device:TPU:32, one launch (start us, length us, event | category | flops | bytes accessed | tf_op | source)
XLA Modules:
  0.0 134.1 jit_solution(16276556985144666080)
XLA Ops:
  0.0 4.9 %collective-permute-start.2 = (bf16[64,2048]{1,0:T(8,128)(2,1)}, bf16[64,2048]{1,0:T(8,128)(2,1)S(1)}, u32[]{:S(2)}, u32[]{:S(2)}) collective-permute-start(bf16[64,2048]{1,0:T(8,128)(2,1)} %bitcast.18), channel_id=1, source_target_pairs={{0,2},{1,3},{2,0},{3,1},{4,6},{5,7},{6,4},{7,5},{8,10},{9,11},{10,... | collective-permute-start | bytes 786440 | tf_op jit(solution)/shard_map/ppermute | solution.py:352
  4.9 3.1 %collective-permute-start.1 = (bf16[64,2048]{1,0:T(8,128)(2,1)}, bf16[64,2048]{1,0:T(8,128)(2,1)S(1)}, u32[]{:S(2)}, u32[]{:S(2)}) collective-permute-start(bf16[64,2048]{1,0:T(8,128)(2,1)} %bitcast.19), channel_id=1, source_target_pairs={{0,3},{1,2},{2,1},{3,0},{4,7},{5,6},{6,5},{7,4},{8,11},{9,10},{10,... | collective-permute-start | bytes 786440 | tf_op jit(solution)/shard_map/ppermute | solution.py:352
  8.0 1.9 %collective-permute-start = (bf16[64,2048]{1,0:T(8,128)(2,1)}, bf16[64,2048]{1,0:T(8,128)(2,1)S(1)}, u32[]{:S(2)}, u32[]{:S(2)}) collective-permute-start(bf16[64,2048]{1,0:T(8,128)(2,1)} %bitcast.20), channel_id=1, source_target_pairs={{0,1},{1,0},{2,3},{3,2},{4,5},{5,4},{6,7},{7,6},{8,9},{9,8},{10,11... | collective-permute-start | bytes 786440 | tf_op jit(solution)/shard_map/ppermute | solution.py:352
  9.9 0.0 copy-start.6
  9.9 0.7 copy-done.6
  10.6 0.7 shard_map.118
  11.4 7.6 %all-to-all-start = ((bf16[16,32,128]{2,1,0:T(8,128)(2,1)}), bf16[16,32,128]{2,1,0:T(8,128)(2,1)S(1)}, u32[]{:S(2)}, u32[]{:S(2)}) async-start(bf16[16,32,128]{2,1,0:T(8,128)(2,1)} %shard_map.118), calls=%async_computation | async-start | bytes 262144 | tf_op jit(solution)/shard_map/all_to_all | solution.py:358
  18.9 0.0 copy-start.2
  18.9 0.0 copy-start.3
  19.0 0.0 copy-start.4
  19.0 0.0 copy-start.8
  19.0 0.0 copy-start.9
  19.0 0.0 copy-start.10
  19.0 0.0 collective-permute-done.2
  19.0 0.0 collective-permute-done.1
  19.0 0.0 collective-permute-done
  19.0 1.2 pad_maximum_fusion.refs_0_
  20.2 0.0 copy-done.2
  20.2 0.0 copy-done.3
  20.2 0.0 copy-done.4
  20.3 1.2 shard_map.119
  21.5 5.4 %all-to-all-done.lat_ref = bf16[16,32,128]{2,1,0:T(8,128)(2,1)S(1)} async-done(((bf16[16,32,128]{2,1,0:T(8,128)(2,1)}), bf16[16,32,128]{2,1,0:T(8,128)(2,1)S(1)}, u32[]{:S(2)}, u32[]{:S(2)}) %all-to-all-start) | async-done | bytes 131104 | tf_op jit(solution)/shard_map/all_to_all | solution.py:358
  26.9 2.9 %collective-permute-start.5 = (bf16[256,2048]{1,0:T(8,128)(2,1)S(1)}, bf16[256,2048]{1,0:T(8,128)(2,1)S(1)}, u32[]{:S(2)}, u32[]{:S(2)}) collective-permute-start(bf16[256,2048]{1,0:T(8,128)(2,1)S(1)} %pad_maximum_fusion.refs_0_), channel_id=1, source_target_pairs={{0,8},{1,9},{2,10},{3,11},{4,12},{5,13},{6,14},{7,15},{8,0},{9,1},... | collective-permute-start | bytes 3145736 | tf_op jit(solution)/shard_map/ppermute | solution.py:352
  29.8 3.9 %collective-permute-start.4 = (bf16[256,2048]{1,0:T(8,128)(2,1)S(1)}, bf16[256,2048]{1,0:T(8,128)(2,1)S(1)}, u32[]{:S(2)}, u32[]{:S(2)}) collective-permute-start(bf16[256,2048]{1,0:T(8,128)(2,1)S(1)} %pad_maximum_fusion.refs_0_), channel_id=1, source_target_pairs={{0,12},{1,13},{2,14},{3,15},{4,8},{5,9},{6,10},{7,11},{8,4},{9,5},... | collective-permute-start | bytes 3145736 | tf_op jit(solution)/shard_map/ppermute | solution.py:352
  33.7 2.4 %collective-permute-start.3 = (bf16[256,2048]{1,0:T(8,128)(2,1)S(1)}, bf16[256,2048]{1,0:T(8,128)(2,1)S(1)}, u32[]{:S(2)}, u32[]{:S(2)}) collective-permute-start(bf16[256,2048]{1,0:T(8,128)(2,1)S(1)} %pad_maximum_fusion.refs_0_), channel_id=1, source_target_pairs={{0,4},{1,5},{2,6},{3,7},{4,0},{5,1},{6,2},{7,3},{8,12},{9,13},{10,... | collective-permute-start | bytes 3145736 | tf_op jit(solution)/shard_map/ppermute | solution.py:352
  36.1 0.4 shard_map.120
  36.6 27.6 %all_to_all.30 = bf16[16,32,128]{2,1,0:T(8,128)(2,1)S(1)} all-to-all(bf16[16,32,128]{2,1,0:T(8,128)(2,1)S(1)} %get-tuple-element.39), channel_id=1, replica_groups={{0,32,64,96,128,160,192,224,256,288,320,352,384,416,448,480},{16,48,80,..., dimensions={0} | all-to-all | bytes 262144 | tf_op jit(solution)/shard_map/all_to_all | solution.py:393
  64.2 0.0 collective-permute-done.5.refs_3_
  64.2 0.0 collective-permute-done.4.refs_2_
  64.2 0.0 collective-permute-done.3.refs_1_
  64.2 2.2 %shard_map.121 = (bf16[128,2176]{1,0:T(8,128)(2,1)S(1)}, bf16[2176,128]{1,0:T(8,128)(2,1)S(1)}, bf16[2272,128]{1,0:T(8,128)(2,1)S(1)}) custom-call(bf16[256,2048]{1,0:T(8,128)(2,1)S(1)} %pad_maximum_fusion.refs_0_, bf16[256,2048]{1,0:T(8,128)(2,1)S(1)} %collective-permute-done.3.refs_1_, bf16[256,2048]{1,0:T(8,128)(2,1)S(1)} %collective-permute-done.4.refs_2_, ...), custom_call_target="tpu_custom_call" | custom-call | flops 1000000000 | bytes 1000000000 | tf_op jit(solution)/shard_map/pallas_call | solution.py:397
  66.4 1.9 %collective-permute-start.6 = (bf16[2272,128]{1,0:T(8,128)(2,1)S(1)}, bf16[2272,128]{1,0:T(8,128)(2,1)S(1)}, u32[]{:S(2)}, u32[]{:S(2)}) collective-permute-start(bf16[2272,128]{1,0:T(8,128)(2,1)S(1)} %get-tuple-element.47), channel_id=1, source_target_pairs={{0,16},{16,0},{32,48},{48,32},{64,80},{80,64},{96,112},{112,96},{1... | collective-permute-start | bytes 1744904 | tf_op jit(solution)/shard_map/ppermute | solution.py:407
  68.3 3.7 %shard_map.122 = (f32[512,128]{1,0:T(8,128)S(1)}, f32[512,128]{1,0:T(8,128)S(1)}) custom-call(bf16[512,128]{1,0:T(8,128)(2,1)S(1)} %bitcast.9, s32[2,512,128]{2,1,0:T(8,128)S(1)} %get-tuple-element.42.pos_ref, s32[1,2176]{1,0:T(1,128)S(1)} %get-tuple-element.48.kp_ref, bf16[128,2176]{1,0:T(8,128)(2,1)S(1)} %get-tuple-element.49.k_ref, ...), custom_call_target="tpu_custom_call" | custom-call | flops 1000 | bytes 1000 | tf_op jit(solution)/shard_map/pallas_call | solution.py:408
  72.0 0.0 collective-permute-done.6.kv_ref
  72.1 0.0 copy-start.5
  72.1 0.0 copy-start.7
  72.1 3.8 %shard_map.123 = bf16[16,40,128]{2,1,0:T(8,128)(2,1)S(1)} custom-call(bf16[512,128]{1,0:T(8,128)(2,1)S(1)} %bitcast.10, s32[2,512,128]{2,1,0:T(8,128)S(1)} %get-tuple-element.42.pos_ref, bf16[2272,128]{1,0:T(8,128)(2,1)S(1)} %collective-permute-done.6.kv_ref, f32[512,128]{1,0:T(8,128)S(1)} %get-tuple-element.51.mix_ref, f32[512,128]{1,0:T(8,128)S(1)} %get-tuple-element.52.lev_ref), custom_call_target="tpu_custom_call" | custom-call | flops 1000 | bytes 1000 | tf_op jit(solution)/shard_map/pallas_call | solution.py:411
  75.9 0.0 copy-start
  75.9 0.0 copy-start.1
  75.9 0.0 copy-start.11
  76.0 22.7 %all_to_all.31.arrived_ref = bf16[16,40,128]{2,1,0:T(8,128)(2,1)S(1)} all-to-all(bf16[16,40,128]{2,1,0:T(8,128)(2,1)S(1)} %shard_map.123), channel_id=1, replica_groups={{0,32,64,96,128,160,192,224,256,288,320,352,384,416,448,480},{16,48,80,..., dimensions={0} | all-to-all | bytes 327680 | tf_op jit(solution)/shard_map/all_to_all | solution.py:419
  98.7 0.7 shard_map.124
  99.3 11.1 %all_to_all.32.arrived_ref = bf16[16,32,128]{2,1,0:T(8,128)(2,1)S(1)} all-to-all(bf16[16,32,128]{2,1,0:T(8,128)(2,1)S(1)} %shard_map.124), channel_id=1, replica_groups=mesh['seq'=32,'head'=16] {'head'}, dimensions={0} | all-to-all | bytes 262144 | tf_op jit(solution)/shard_map/all_to_all | solution.py:421
  110.4 0.1 shard_map.125
  110.5 11.1 %all_to_all.33.arrived_ref = bf16[16,32,128]{2,1,0:T(8,128)(2,1)S(1)} all-to-all(bf16[16,32,128]{2,1,0:T(8,128)(2,1)S(1)} %get-tuple-element.53), channel_id=1, replica_groups=mesh['seq'=32,'head'=16] {'head'}, dimensions={0} | all-to-all | bytes 262144 | tf_op jit(solution)/shard_map/all_to_all | solution.py:425
  121.6 0.7 shard_map.126
  122.3 11.1 %all_to_all.34.arrived_ref = bf16[16,32,128]{2,1,0:T(8,128)(2,1)S(1)} all-to-all(bf16[16,32,128]{2,1,0:T(8,128)(2,1)S(1)} %shard_map.126), channel_id=1, replica_groups=mesh['seq'=32,'head'=16] {'head'}, dimensions={0} | all-to-all | bytes 262144 | tf_op jit(solution)/shard_map/all_to_all | solution.py:429
  133.4 0.7 shard_map.127
  (8 shorter events, 0.0 us)
Async XLA Ops:
  0.0 19.0 %collective-permute-start.2 = (bf16[64,2048]{1,0:T(8,128)(2,1)}, bf16[64,2048]{1,0:T(8,128)(2,1)S(1)}, u32[]{:S(2)}, u32[]{:S(2)}) collective-permute-start(bf16[64,2048]{1,0:T(8,128)(2,1)} %bitcast.18), channel_id=1, source_target_pairs={{0,2},{1,3},{2,0},{3,1},{4,6},{5,7},{6,4},{7,5},{8,10},{9,11},{10,... | collective-permute-start | bytes 786440 | tf_op jit(solution)/shard_map/ppermute | solution.py:352
  4.9 14.1 %collective-permute-start.1 = (bf16[64,2048]{1,0:T(8,128)(2,1)}, bf16[64,2048]{1,0:T(8,128)(2,1)S(1)}, u32[]{:S(2)}, u32[]{:S(2)}) collective-permute-start(bf16[64,2048]{1,0:T(8,128)(2,1)} %bitcast.19), channel_id=1, source_target_pairs={{0,3},{1,2},{2,1},{3,0},{4,7},{5,6},{6,5},{7,4},{8,11},{9,10},{10,... | collective-permute-start | bytes 786440 | tf_op jit(solution)/shard_map/ppermute | solution.py:352
  8.0 11.0 %collective-permute-start = (bf16[64,2048]{1,0:T(8,128)(2,1)}, bf16[64,2048]{1,0:T(8,128)(2,1)S(1)}, u32[]{:S(2)}, u32[]{:S(2)}) collective-permute-start(bf16[64,2048]{1,0:T(8,128)(2,1)} %bitcast.20), channel_id=1, source_target_pairs={{0,1},{1,0},{2,3},{3,2},{4,5},{5,4},{6,7},{7,6},{8,9},{9,8},{10,11... | collective-permute-start | bytes 786440 | tf_op jit(solution)/shard_map/ppermute | solution.py:352
  9.9 0.7 copy-start.6
  11.4 15.6 %all-to-all-start = ((bf16[16,32,128]{2,1,0:T(8,128)(2,1)}), bf16[16,32,128]{2,1,0:T(8,128)(2,1)S(1)}, u32[]{:S(2)}, u32[]{:S(2)}) async-start(bf16[16,32,128]{2,1,0:T(8,128)(2,1)} %shard_map.118), calls=%async_computation | async-start | bytes 262144 | tf_op jit(solution)/shard_map/all_to_all | solution.py:358
  18.9 1.3 copy-start.2
  18.9 1.3 copy-start.3
  19.0 1.3 copy-start.4
  19.0 1.3 copy-start.8
  19.0 1.3 copy-start.9
  19.0 1.3 copy-start.10
  26.9 37.2 %collective-permute-start.5 = (bf16[256,2048]{1,0:T(8,128)(2,1)S(1)}, bf16[256,2048]{1,0:T(8,128)(2,1)S(1)}, u32[]{:S(2)}, u32[]{:S(2)}) collective-permute-start(bf16[256,2048]{1,0:T(8,128)(2,1)S(1)} %pad_maximum_fusion.refs_0_), channel_id=1, source_target_pairs={{0,8},{1,9},{2,10},{3,11},{4,12},{5,13},{6,14},{7,15},{8,0},{9,1},... | collective-permute-start | bytes 3145736 | tf_op jit(solution)/shard_map/ppermute | solution.py:352
  29.8 34.3 %collective-permute-start.4 = (bf16[256,2048]{1,0:T(8,128)(2,1)S(1)}, bf16[256,2048]{1,0:T(8,128)(2,1)S(1)}, u32[]{:S(2)}, u32[]{:S(2)}) collective-permute-start(bf16[256,2048]{1,0:T(8,128)(2,1)S(1)} %pad_maximum_fusion.refs_0_), channel_id=1, source_target_pairs={{0,12},{1,13},{2,14},{3,15},{4,8},{5,9},{6,10},{7,11},{8,4},{9,5},... | collective-permute-start | bytes 3145736 | tf_op jit(solution)/shard_map/ppermute | solution.py:352
  33.7 30.4 %collective-permute-start.3 = (bf16[256,2048]{1,0:T(8,128)(2,1)S(1)}, bf16[256,2048]{1,0:T(8,128)(2,1)S(1)}, u32[]{:S(2)}, u32[]{:S(2)}) collective-permute-start(bf16[256,2048]{1,0:T(8,128)(2,1)S(1)} %pad_maximum_fusion.refs_0_), channel_id=1, source_target_pairs={{0,4},{1,5},{2,6},{3,7},{4,0},{5,1},{6,2},{7,3},{8,12},{9,13},{10,... | collective-permute-start | bytes 3145736 | tf_op jit(solution)/shard_map/ppermute | solution.py:352
  66.4 5.6 %collective-permute-start.6 = (bf16[2272,128]{1,0:T(8,128)(2,1)S(1)}, bf16[2272,128]{1,0:T(8,128)(2,1)S(1)}, u32[]{:S(2)}, u32[]{:S(2)}) collective-permute-start(bf16[2272,128]{1,0:T(8,128)(2,1)S(1)} %get-tuple-element.47), channel_id=1, source_target_pairs={{0,16},{16,0},{32,48},{48,32},{64,80},{80,64},{96,112},{112,96},{1... | collective-permute-start | bytes 1744904 | tf_op jit(solution)/shard_map/ppermute | solution.py:407
  72.1 26.6 %copy-start.5 = (bf16[64,1024]{1,0:T(8,128)(2,1)S(1)}, bf16[64,1024]{1,0:T(8,128)(2,1)}, u32[]{:S(2)}) copy-start(bf16[64,1024]{1,0:T(8,128)(2,1)} %w_ref.1) | copy-start | bytes 393220
  72.1 38.3 %copy-start.7 = (bf16[64,64]{1,0:T(8,128)(2,1)S(1)}, bf16[64,64]{1,0:T(8,128)(2,1)}, u32[]{:S(2)}) copy-start(bf16[64,64]{1,0:T(8,128)(2,1)} %lat_ref.3) | copy-start | bytes 24580
  75.9 45.6 %copy-start = (bf16[1024,256]{1,0:T(8,128)(2,1)S(1)}, bf16[1024,256]{1,0:T(8,128)(2,1)}, u32[]{:S(2)}) copy-start(bf16[1024,256]{1,0:T(8,128)(2,1)} %up_ref.1) | copy-start | bytes 1572868
  75.9 45.6 %copy-start.1 = (bf16[256,1024]{1,0:T(8,128)(2,1)S(1)}, bf16[256,1024]{1,0:T(8,128)(2,1)}, u32[]{:S(2)}) copy-start(bf16[256,1024]{1,0:T(8,128)(2,1)} %down_ref.1) | copy-start | bytes 1572868
  75.9 45.6 %copy-start.11 = (f32[1024]{0:T(1024)S(1)}, f32[1024]{0:T(1024)}, u32[]{:S(2)}) copy-start(f32[1024]{0:T(1024)} %param.21) | copy-start | bytes 12292

commit v12 on v11

--- a/solution.py
+++ b/solution.py
@@ -13,7 +13,7 @@
 NEGATIVE = -1e30
 LOWEST = -1e29
 BOTH = ("seq", "head")
-STEPS = (0, 1, 3, 2)
+STEPS = (0, 1, 2, 3)
 F32 = jnp.float32
 BF16 = jnp.bfloat16
 MIB = 1 << 20
@@ -129,8 +129,8 @@
     kv_ref[...] = jnp.concatenate([both, jnp.zeros_like(both)], axis=1).astype(BF16)
 
 
-def keys_kernel(*refs):
-    *line_refs, w_ref, lat_ref, digits_ref, k_ref, v_ref, kv_ref, held, sems = refs
+def first_keys_kernel(*refs):
+    *line_refs, w_ref, part_ref, squares_ref, held, sems = refs
     height, tokens = line_refs[0].shape
     width = 512
     copies = []
@@ -146,18 +146,38 @@
         )
         for copy in copies[c]:
             copy.start()
-    put_keys(lat_ref[...], slice(tokens, tokens + 128), k_ref, v_ref, kv_ref)
-    kv_ref[tokens + 128 :] = digits_ref[...]
-    weights = w_ref[...]
+    weights = w_ref[:, : height * len(line_refs)]
     for c in range(tokens // width):
         cols = slice(c * width, c * width + width)
         for copy in copies[c]:
             copy.wait()
         piece = held[:, cols]
         wide = piece.astype(F32)
-        squares = jnp.sum(wide * wide, axis=0, keepdims=True)
+        squares_ref[:, cols] = jnp.sum(wide * wide, axis=0, keepdims=True)
+        part_ref[:, cols] = dot(weights, piece, NN)
+
+
+def last_keys_kernel(
+    line_ref, w_ref, part_ref, squares_ref, lat_ref, digits_ref, k_ref, v_ref, kv_ref, held, sems
+):
+    height, tokens = line_ref.shape
+    width = 512
+    copies = []
+    for c in range(tokens // width):
+        cols = slice(c * width, c * width + width)
+        copies.append(pltpu.make_async_copy(line_ref.at[:, cols], held.at[:, cols], sems.at[c]))
+        copies[c].start()
+    put_keys(lat_ref[...], slice(tokens, tokens + 128), k_ref, v_ref, kv_ref)
+    kv_ref[tokens + 128 :] = digits_ref[...]
+    weights = w_ref[:, -height:]
+    for c in range(tokens // width):
+        cols = slice(c * width, c * width + width)
+        copies[c].wait()
+        piece = held[:, cols]
+        wide = piece.astype(F32)
+        squares = squares_ref[:, cols] + jnp.sum(wide * wide, axis=0, keepdims=True)
         inverse = lax.rsqrt(squares * (1.0 / 1024) + EPSILON)
-        both = (dot(weights, piece, NN) * inverse).astype(BF16)
+        both = ((part_ref[:, cols] + dot(weights, piece, NN)) * inverse).astype(BF16)
         put_keys(both, cols, k_ref, v_ref, kv_ref)
 
 
@@ -309,12 +329,12 @@
     out_ref[...] = jnp.concatenate([packed[:, :cols], packed[:, cols:]], axis=0).astype(BF16)
 
 
-def call(kernel, outs, cost=1000, **kwargs):
+def call(kernel, outs, cost=1000, vmem_mib=40, **kwargs):
     shapes = [jax.ShapeDtypeStruct(s, t) for s, t in outs]
     return pl.pallas_call(
         kernel,
         out_shape=shapes if len(shapes) > 1 else shapes[0],
-        compiler_params=pltpu.CompilerParams(vmem_limit_bytes=40 * MIB),
+        compiler_params=pltpu.CompilerParams(vmem_limit_bytes=vmem_mib * MIB),
         cost_estimate=pl.CostEstimate(flops=cost, bytes_accessed=cost, transcendentals=0),
         **kwargs,
     )
@@ -354,7 +374,7 @@
     own = context.T
     line = jnp.concatenate([own] + [swap_lines(own, 0, step) for step in STEPS[1:]], axis=0)
     line, input_gain = lax.optimization_barrier((line, input_gain))
-    copies = call(latents_kernel, [((head_size, *block), BF16)])(latents)
+    copies = call(latents_kernel, [((head_size, *block), BF16)], vmem_mib=60)(latents)
     lat_blocks = lax.all_to_all(copies, "head", 0, 0)
     anywhere = pl.BlockSpec(memory_space=pl.ANY)
     prepared = call(
@@ -394,16 +414,26 @@
     own_queries = own_queries.reshape(rows, -1)
     own_queries, key_weights = lax.optimization_barrier((own_queries, key_weights))
 
+    features = head_size * cols
+    partial = call(
+        first_keys_kernel,
+        [((2 * cols, tokens), F32), ((1, tokens), F32)],
+        cost=10**9,
+        in_specs=[anywhere] * (side - 1) + [vmem],
+        scratch_shapes=[
+            pltpu.VMEM((features - features // side, tokens), BF16),
+            pltpu.SemaphoreType.DMA((4, side - 1)),
+        ],
+    )(*lines[:-1], key_weights)
     keys, values, both = call(
-        keys_kernel,
+        last_keys_kernel,
         [((128, key_count), BF16), ((key_count, 128), BF16), ((key_count + 96, 128), BF16)],
-        cost=10**9,
-        in_specs=[anywhere] * side + [vmem] * 3,
+        in_specs=[anywhere] + [vmem] * 5,
         scratch_shapes=[
-            pltpu.VMEM((head_size * cols, tokens), BF16),
-            pltpu.SemaphoreType.DMA((4, side)),
+            pltpu.VMEM((features // side, tokens), BF16),
+            pltpu.SemaphoreType.DMA((4,)),
         ],
-    )(*lines, key_weights, latent_kv, digits)
+    )(lines[-1], key_weights, *partial, latent_kv, digits)
     from_sibling = lax.ppermute(both, "seq", swap)
     mixed, level = call(own_kernel, [((rows, 2 * cols), F32)] * 2)(
         own_queries, query_pos, key_pos, keys, values

time: 135 us -> 135 us (level)
  Pallas kernels: 14.3 us -> 15.8 us
    all_to_all x1, blocking collectives: 22.7 us -> 20.5 us  [body(): arrived = lax.all_to_all(joined, 'seq', 0, 0, axis_index_groups=along_z)]
    all_to_all x2, blocking collectives: 22.1 us -> 23.7 us  [body(): arrived = lax.all_to_all(shares, 'head', 0, 0)]
    pallas_call x2 -> x3, Pallas kernels: 2.96 us -> 4.48 us  [the longest x1 1.63 us: body(): call(first_keys_kernel, [((2 * cols, tokens), F32), ((1, tokens), F32)],...]
  transfers between devices with their start and end apart: 8 -> 8, of which waited for: 1 -> 1; matrix products, arithmetic and copies ran while one was open for 1% -> 1% of each run, Pallas kernels for 5% -> 6%
where the time goes in v12:
time: 135 us; the launch traced here: 134 us
  blocking collectives  82.8 us (61%)
  starting transfers between devices  28.6 us (21%)
  Pallas kernels  15.8 us (12%)
  waiting for transfers between devices  5.48 us (4%)
    all_to_all x1, blocking collectives, body(): lax.all_to_all(queries, 'seq', 0, 0, axis_index_groups=along_z)  27.6 us
    all_to_all x2, blocking collectives, body(): arrived = lax.all_to_all(shares, 'head', 0, 0)  23.7 us
    all_to_all x1, blocking collectives, body(): arrived = lax.all_to_all(joined, 'seq', 0, 0, axis_index_groups=along_z)  20.5 us
    ppermute x6, starting transfers between devices, swap_lines(): return lax.ppermute(piece, BOTH, partners(seq_size, side, phase, step))  19.6 us
    all_to_all x1, blocking collectives, body(): arrived = lax.all_to_all(copies, 'head', 0, 0)  11.1 us
    all_to_all x1, starting transfers between devices, body(): lat_blocks = lax.all_to_all(copies, 'head', 0, 0)  7.03 us
    all_to_all x1, waiting for transfers between devices, body(): lat_blocks = lax.all_to_all(copies, 'head', 0, 0)  5.46 us
    pallas_call x1, Pallas kernels, body(): call(sibling_kernel, [((planes, 40, 2 * cols), BF16)], scratch_shapes=[pl...  3.85 us
  transfers between devices with their start and end apart: 8, of which 1 were waited for; matrix products, arithmetic and copies ran while one was open for 1% of the time, Pallas kernels for 6%

profile of v12, /device:TPU:32, one launch (start us, length us, event | category | flops | bytes accessed | tf_op | source)
XLA Modules:
  0.0 134.2 jit_solution(1247850678556940948)
XLA Ops:
  0.0 4.7 %collective-permute-start.2 = (bf16[64,2048]{1,0:T(8,128)(2,1)}, bf16[64,2048]{1,0:T(8,128)(2,1)S(1)}, u32[]{:S(2)}, u32[]{:S(2)}) collective-permute-start(bf16[64,2048]{1,0:T(8,128)(2,1)} %bitcast.18), channel_id=1, source_target_pairs={{0,3},{1,2},{2,1},{3,0},{4,7},{5,6},{6,5},{7,4},{8,11},{9,10},{10,... | collective-permute-start | bytes 786440 | tf_op jit(solution)/shard_map/ppermute | solution.py:372
  4.7 2.7 %collective-permute-start.1 = (bf16[64,2048]{1,0:T(8,128)(2,1)}, bf16[64,2048]{1,0:T(8,128)(2,1)S(1)}, u32[]{:S(2)}, u32[]{:S(2)}) collective-permute-start(bf16[64,2048]{1,0:T(8,128)(2,1)} %bitcast.19), channel_id=1, source_target_pairs={{0,2},{1,3},{2,0},{3,1},{4,6},{5,7},{6,4},{7,5},{8,10},{9,11},{10,... | collective-permute-start | bytes 786440 | tf_op jit(solution)/shard_map/ppermute | solution.py:372
  7.4 2.4 %collective-permute-start = (bf16[64,2048]{1,0:T(8,128)(2,1)}, bf16[64,2048]{1,0:T(8,128)(2,1)S(1)}, u32[]{:S(2)}, u32[]{:S(2)}) collective-permute-start(bf16[64,2048]{1,0:T(8,128)(2,1)} %bitcast.20), channel_id=1, source_target_pairs={{0,1},{1,0},{2,3},{3,2},{4,5},{5,4},{6,7},{7,6},{8,9},{9,8},{10,11... | collective-permute-start | bytes 786440 | tf_op jit(solution)/shard_map/ppermute | solution.py:372
  9.8 1.4 %shard_map.118 = bf16[16,32,128]{2,1,0:T(8,128)(2,1)} custom-call(bf16[64,64]{1,0:T(8,128)(2,1)} %lat_ref.3), custom_call_target="tpu_custom_call" | custom-call | flops 1000 | bytes 1000 | tf_op jit(solution)/shard_map/pallas_call | solution.py:377
  11.3 7.0 %all-to-all-start = ((bf16[16,32,128]{2,1,0:T(8,128)(2,1)}), bf16[16,32,128]{2,1,0:T(8,128)(2,1)S(1)}, u32[]{:S(2)}, u32[]{:S(2)}) async-start(bf16[16,32,128]{2,1,0:T(8,128)(2,1)} %shard_map.118), calls=%async_computation | async-start | bytes 262144 | tf_op jit(solution)/shard_map/all_to_all | solution.py:378
  18.3 0.0 copy-start.2
  18.3 0.0 copy-start.3
  18.3 0.0 copy-start.4
  18.4 0.0 copy-start.7
  18.4 0.0 copy-start.8
  18.4 0.0 copy-start.9
  18.4 0.0 collective-permute-done.2
  18.4 0.0 collective-permute-done.1
  18.4 0.0 collective-permute-done
  18.4 1.2 pad_maximum_fusion.refs_0_
  19.6 0.0 copy-done.2
  19.6 0.0 copy-done.3
  19.6 0.0 copy-done.4
  19.6 0.0 copy-done.7
  19.7 1.2 shard_map.119
  20.9 5.5 %all-to-all-done.lat_ref = bf16[16,32,128]{2,1,0:T(8,128)(2,1)S(1)} async-done(((bf16[16,32,128]{2,1,0:T(8,128)(2,1)}), bf16[16,32,128]{2,1,0:T(8,128)(2,1)S(1)}, u32[]{:S(2)}, u32[]{:S(2)}) %all-to-all-start) | async-done | bytes 131104 | tf_op jit(solution)/shard_map/all_to_all | solution.py:378
  26.3 2.9 %collective-permute-start.5 = (bf16[256,2048]{1,0:T(8,128)(2,1)S(1)}, bf16[256,2048]{1,0:T(8,128)(2,1)S(1)}, u32[]{:S(2)}, u32[]{:S(2)}) collective-permute-start(bf16[256,2048]{1,0:T(8,128)(2,1)S(1)} %pad_maximum_fusion.refs_0_), channel_id=1, source_target_pairs={{0,8},{1,9},{2,10},{3,11},{4,12},{5,13},{6,14},{7,15},{8,0},{9,1},... | collective-permute-start | bytes 3145736 | tf_op jit(solution)/shard_map/ppermute | solution.py:372
  29.2 2.7 %collective-permute-start.4 = (bf16[256,2048]{1,0:T(8,128)(2,1)S(1)}, bf16[256,2048]{1,0:T(8,128)(2,1)S(1)}, u32[]{:S(2)}, u32[]{:S(2)}) collective-permute-start(bf16[256,2048]{1,0:T(8,128)(2,1)S(1)} %pad_maximum_fusion.refs_0_), channel_id=1, source_target_pairs={{0,4},{1,5},{2,6},{3,7},{4,0},{5,1},{6,2},{7,3},{8,12},{9,13},{10,... | collective-permute-start | bytes 3145736 | tf_op jit(solution)/shard_map/ppermute | solution.py:372
  31.9 4.2 %collective-permute-start.3 = (bf16[256,2048]{1,0:T(8,128)(2,1)S(1)}, bf16[256,2048]{1,0:T(8,128)(2,1)S(1)}, u32[]{:S(2)}, u32[]{:S(2)}) collective-permute-start(bf16[256,2048]{1,0:T(8,128)(2,1)S(1)} %pad_maximum_fusion.refs_0_), channel_id=1, source_target_pairs={{0,12},{1,13},{2,14},{3,15},{4,8},{5,9},{6,10},{7,11},{8,4},{9,5},... | collective-permute-start | bytes 3145736 | tf_op jit(solution)/shard_map/ppermute | solution.py:372
  36.1 0.4 shard_map.120
  36.6 27.6 %all_to_all.30 = bf16[16,32,128]{2,1,0:T(8,128)(2,1)S(1)} all-to-all(bf16[16,32,128]{2,1,0:T(8,128)(2,1)S(1)} %get-tuple-element.41), channel_id=1, replica_groups={{0,32,64,96,128,160,192,224,256,288,320,352,384,416,448,480},{16,48,80,..., dimensions={0} | all-to-all | bytes 262144 | tf_op jit(solution)/shard_map/all_to_all | solution.py:413
  64.2 0.0 collective-permute-done.5.refs_2_
  64.2 0.0 collective-permute-done.4.refs_1_
  64.2 1.6 %shard_map.121 = (f32[128,2048]{1,0:T(8,128)S(1)}, f32[1,2048]{1,0:T(1,128)S(1)}) custom-call(bf16[256,2048]{1,0:T(8,128)(2,1)S(1)} %pad_maximum_fusion.refs_0_, bf16[256,2048]{1,0:T(8,128)(2,1)S(1)} %collective-permute-done.4.refs_1_, bf16[256,2048]{1,0:T(8,128)(2,1)S(1)} %collective-permute-done.5.refs_2_, ...), custom_call_target="tpu_custom_call" | custom-call | flops 1000000000 | bytes 1000000000 | tf_op jit(solution)/shard_map/pallas_call | solution.py:418
  65.8 0.0 collective-permute-done.3.line_ref
  65.8 1.4 %shard_map.122 = (bf16[128,2176]{1,0:T(8,128)(2,1)S(1)}, bf16[2176,128]{1,0:T(8,128)(2,1)S(1)}, bf16[2272,128]{1,0:T(8,128)(2,1)S(1)}) custom-call(bf16[256,2048]{1,0:T(8,128)(2,1)S(1)} %collective-permute-done.3.line_ref, bf16[128,1024]{1,0:T(8,128)(2,1)S(1)} %get-tuple-element.46.refs_3_.w_ref, f32[128,2048]{1,0:T(8,128)S(1)} %get-tuple-element.47.part_ref, ...), custom_call_target="tpu_custom_call" | custom-call | flops 1000 | bytes 1000 | tf_op jit(solution)/shard_map/pallas_call | solution.py:428
  67.2 1.9 %collective-permute-start.6 = (bf16[2272,128]{1,0:T(8,128)(2,1)S(1)}, bf16[2272,128]{1,0:T(8,128)(2,1)S(1)}, u32[]{:S(2)}, u32[]{:S(2)}) collective-permute-start(bf16[2272,128]{1,0:T(8,128)(2,1)S(1)} %get-tuple-element.51), channel_id=1, source_target_pairs={{0,16},{16,0},{32,48},{48,32},{64,80},{80,64},{96,112},{112,96},{1... | collective-permute-start | bytes 1744904 | tf_op jit(solution)/shard_map/ppermute | solution.py:437
  69.2 3.7 %shard_map.123 = (f32[512,128]{1,0:T(8,128)S(1)}, f32[512,128]{1,0:T(8,128)S(1)}) custom-call(bf16[512,128]{1,0:T(8,128)(2,1)S(1)} %bitcast.9, s32[2,512,128]{2,1,0:T(8,128)S(1)} %get-tuple-element.44.pos_ref, s32[1,2176]{1,0:T(1,128)S(1)} %get-tuple-element.52.kp_ref, bf16[128,2176]{1,0:T(8,128)(2,1)S(1)} %get-tuple-element.53.k_ref, ...), custom_call_target="tpu_custom_call" | custom-call | flops 1000 | bytes 1000 | tf_op jit(solution)/shard_map/pallas_call | solution.py:438
  72.8 0.0 collective-permute-done.6.kv_ref
  72.9 0.0 copy-start.5
  72.9 0.0 copy-start.6
  72.9 3.9 %shard_map.124 = bf16[16,40,128]{2,1,0:T(8,128)(2,1)S(1)} custom-call(bf16[512,128]{1,0:T(8,128)(2,1)S(1)} %bitcast.10, s32[2,512,128]{2,1,0:T(8,128)S(1)} %get-tuple-element.44.pos_ref, bf16[2272,128]{1,0:T(8,128)(2,1)S(1)} %collective-permute-done.6.kv_ref, f32[512,128]{1,0:T(8,128)S(1)} %get-tuple-element.55.mix_ref, f32[512,128]{1,0:T(8,128)S(1)} %get-tuple-element.56.lev_ref), custom_call_target="tpu_custom_call" | custom-call | flops 1000 | bytes 1000 | tf_op jit(solution)/shard_map/pallas_call | solution.py:441
  76.7 0.0 copy-start
  76.7 0.0 copy-start.1
  76.8 0.0 copy-start.10
  76.8 20.5 %all_to_all.31.arrived_ref = bf16[16,40,128]{2,1,0:T(8,128)(2,1)S(1)} all-to-all(bf16[16,40,128]{2,1,0:T(8,128)(2,1)S(1)} %shard_map.124), channel_id=1, replica_groups={{0,32,64,96,128,160,192,224,256,288,320,352,384,416,448,480},{16,48,80,..., dimensions={0} | all-to-all | bytes 327680 | tf_op jit(solution)/shard_map/all_to_all | solution.py:449
  97.2 0.7 shard_map.125
  97.9 12.7 %all_to_all.32.arrived_ref = bf16[16,32,128]{2,1,0:T(8,128)(2,1)S(1)} all-to-all(bf16[16,32,128]{2,1,0:T(8,128)(2,1)S(1)} %shard_map.125), channel_id=1, replica_groups=mesh['seq'=32,'head'=16] {'head'}, dimensions={0} | all-to-all | bytes 262144 | tf_op jit(solution)/shard_map/all_to_all | solution.py:451
  110.6 0.1 shard_map.126
  110.7 11.1 %all_to_all.33.arrived_ref = bf16[16,32,128]{2,1,0:T(8,128)(2,1)S(1)} all-to-all(bf16[16,32,128]{2,1,0:T(8,128)(2,1)S(1)} %get-tuple-element.57), channel_id=1, replica_groups=mesh['seq'=32,'head'=16] {'head'}, dimensions={0} | all-to-all | bytes 262144 | tf_op jit(solution)/shard_map/all_to_all | solution.py:455
  121.7 0.7 shard_map.127
  122.5 11.1 %all_to_all.34.arrived_ref = bf16[16,32,128]{2,1,0:T(8,128)(2,1)S(1)} all-to-all(bf16[16,32,128]{2,1,0:T(8,128)(2,1)S(1)} %shard_map.127), channel_id=1, replica_groups=mesh['seq'=32,'head'=16] {'head'}, dimensions={0} | all-to-all | bytes 262144 | tf_op jit(solution)/shard_map/all_to_all | solution.py:459
  133.5 0.7 shard_map.128
  (7 shorter events, 0.0 us)
Async XLA Ops:
  0.0 18.4 %collective-permute-start.2 = (bf16[64,2048]{1,0:T(8,128)(2,1)}, bf16[64,2048]{1,0:T(8,128)(2,1)S(1)}, u32[]{:S(2)}, u32[]{:S(2)}) collective-permute-start(bf16[64,2048]{1,0:T(8,128)(2,1)} %bitcast.18), channel_id=1, source_target_pairs={{0,3},{1,2},{2,1},{3,0},{4,7},{5,6},{6,5},{7,4},{8,11},{9,10},{10,... | collective-permute-start | bytes 786440 | tf_op jit(solution)/shard_map/ppermute | solution.py:372
  4.7 13.7 %collective-permute-start.1 = (bf16[64,2048]{1,0:T(8,128)(2,1)}, bf16[64,2048]{1,0:T(8,128)(2,1)S(1)}, u32[]{:S(2)}, u32[]{:S(2)}) collective-permute-start(bf16[64,2048]{1,0:T(8,128)(2,1)} %bitcast.19), channel_id=1, source_target_pairs={{0,2},{1,3},{2,0},{3,1},{4,6},{5,7},{6,4},{7,5},{8,10},{9,11},{10,... | collective-permute-start | bytes 786440 | tf_op jit(solution)/shard_map/ppermute | solution.py:372
  7.4 11.0 %collective-permute-start = (bf16[64,2048]{1,0:T(8,128)(2,1)}, bf16[64,2048]{1,0:T(8,128)(2,1)S(1)}, u32[]{:S(2)}, u32[]{:S(2)}) collective-permute-start(bf16[64,2048]{1,0:T(8,128)(2,1)} %bitcast.20), channel_id=1, source_target_pairs={{0,1},{1,0},{2,3},{3,2},{4,5},{5,4},{6,7},{7,6},{8,9},{9,8},{10,11... | collective-permute-start | bytes 786440 | tf_op jit(solution)/shard_map/ppermute | solution.py:372
  11.3 15.0 %all-to-all-start = ((bf16[16,32,128]{2,1,0:T(8,128)(2,1)}), bf16[16,32,128]{2,1,0:T(8,128)(2,1)S(1)}, u32[]{:S(2)}, u32[]{:S(2)}) async-start(bf16[16,32,128]{2,1,0:T(8,128)(2,1)} %shard_map.118), calls=%async_computation | async-start | bytes 262144 | tf_op jit(solution)/shard_map/all_to_all | solution.py:378
  18.3 1.3 copy-start.2
  18.3 1.3 copy-start.3
  18.3 1.3 copy-start.4
  18.4 1.3 copy-start.7
  18.4 1.3 copy-start.8
  18.4 1.3 copy-start.9
  26.3 37.8 %collective-permute-start.5 = (bf16[256,2048]{1,0:T(8,128)(2,1)S(1)}, bf16[256,2048]{1,0:T(8,128)(2,1)S(1)}, u32[]{:S(2)}, u32[]{:S(2)}) collective-permute-start(bf16[256,2048]{1,0:T(8,128)(2,1)S(1)} %pad_maximum_fusion.refs_0_), channel_id=1, source_target_pairs={{0,8},{1,9},{2,10},{3,11},{4,12},{5,13},{6,14},{7,15},{8,0},{9,1},... | collective-permute-start | bytes 3145736 | tf_op jit(solution)/shard_map/ppermute | solution.py:372
  29.2 34.9 %collective-permute-start.4 = (bf16[256,2048]{1,0:T(8,128)(2,1)S(1)}, bf16[256,2048]{1,0:T(8,128)(2,1)S(1)}, u32[]{:S(2)}, u32[]{:S(2)}) collective-permute-start(bf16[256,2048]{1,0:T(8,128)(2,1)S(1)} %pad_maximum_fusion.refs_0_), channel_id=1, source_target_pairs={{0,4},{1,5},{2,6},{3,7},{4,0},{5,1},{6,2},{7,3},{8,12},{9,13},{10,... | collective-permute-start | bytes 3145736 | tf_op jit(solution)/shard_map/ppermute | solution.py:372
  31.9 33.9 %collective-permute-start.3 = (bf16[256,2048]{1,0:T(8,128)(2,1)S(1)}, bf16[256,2048]{1,0:T(8,128)(2,1)S(1)}, u32[]{:S(2)}, u32[]{:S(2)}) collective-permute-start(bf16[256,2048]{1,0:T(8,128)(2,1)S(1)} %pad_maximum_fusion.refs_0_), channel_id=1, source_target_pairs={{0,12},{1,13},{2,14},{3,15},{4,8},{5,9},{6,10},{7,11},{8,4},{9,5},... | collective-permute-start | bytes 3145736 | tf_op jit(solution)/shard_map/ppermute | solution.py:372
  67.2 5.6 %collective-permute-start.6 = (bf16[2272,128]{1,0:T(8,128)(2,1)S(1)}, bf16[2272,128]{1,0:T(8,128)(2,1)S(1)}, u32[]{:S(2)}, u32[]{:S(2)}) collective-permute-start(bf16[2272,128]{1,0:T(8,128)(2,1)S(1)} %get-tuple-element.51), channel_id=1, source_target_pairs={{0,16},{16,0},{32,48},{48,32},{64,80},{80,64},{96,112},{112,96},{1... | collective-permute-start | bytes 1744904 | tf_op jit(solution)/shard_map/ppermute | solution.py:437
  72.9 24.4 %copy-start.5 = (bf16[64,1024]{1,0:T(8,128)(2,1)S(1)}, bf16[64,1024]{1,0:T(8,128)(2,1)}, u32[]{:S(2)}) copy-start(bf16[64,1024]{1,0:T(8,128)(2,1)} %w_ref.1) | copy-start | bytes 393220
  72.9 37.7 %copy-start.6 = (bf16[64,64]{1,0:T(8,128)(2,1)S(1)}, bf16[64,64]{1,0:T(8,128)(2,1)}, u32[]{:S(2)}) copy-start(bf16[64,64]{1,0:T(8,128)(2,1)} %lat_ref.3) | copy-start | bytes 24580
  76.7 45.0 %copy-start = (bf16[1024,256]{1,0:T(8,128)(2,1)S(1)}, bf16[1024,256]{1,0:T(8,128)(2,1)}, u32[]{:S(2)}) copy-start(bf16[1024,256]{1,0:T(8,128)(2,1)} %up_ref.1) | copy-start | bytes 1572868
  76.7 45.0 %copy-start.1 = (bf16[256,1024]{1,0:T(8,128)(2,1)S(1)}, bf16[256,1024]{1,0:T(8,128)(2,1)}, u32[]{:S(2)}) copy-start(bf16[256,1024]{1,0:T(8,128)(2,1)} %down_ref.1) | copy-start | bytes 1572868
  76.8 45.0 %copy-start.10 = (f32[1024]{0:T(1024)S(1)}, f32[1024]{0:T(1024)}, u32[]{:S(2)}) copy-start(f32[1024]{0:T(1024)} %param.21) | copy-start | bytes 12292

commit v13 on v11

--- a/solution.py
+++ b/solution.py
@@ -52,11 +52,9 @@
         out_ref[2 * g + 1] = jnp.where(low, pltpu.roll(a, 64, 1), b).astype(out_ref.dtype)
 
 
-def unpack_columns(ref):
+def unpack_columns(blocks):
     tops, bottoms = [], []
-    for g in range(ref.shape[0] // 2):
-        a = ref[2 * g].astype(F32)
-        b = ref[2 * g + 1].astype(F32)
+    for a, b in zip(blocks[::2], blocks[1::2]):
         low = low_half(a.shape)
         tops.append(jnp.where(low, a, pltpu.roll(b, 64, 1)))
         bottoms.append(jnp.where(low, pltpu.roll(a, 64, 1), b))
@@ -70,10 +68,35 @@
     return (rows * inverse * gain).astype(BF16)
 
 
-def latents_kernel(lat_ref, out_ref):
+def first_kernel(ctx_ref, w_ref, lat_any, ext_ref, out_ref, lat_ref, sems):
+    tokens = ctx_ref.shape[1]
+    copies = [
+        pltpu.make_async_copy(lat_any, lat_ref, sems.at[0]),
+        pltpu.make_async_copy(ctx_ref, ext_ref.at[:, :tokens], sems.at[1]),
+        pltpu.make_async_copy(w_ref, ext_ref.at[:, tokens:], sems.at[2]),
+    ]
+    for copy in copies:
+        copy.start()
+    copies[0].wait()
     half = lat_ref.shape[0] // 2
     packed = jnp.concatenate([lat_ref[:half, :], lat_ref[half:, :]], axis=1)
     out_ref[...] = jnp.broadcast_to(packed[None], out_ref.shape)
+    for copy in copies[1:]:
+        copy.wait()
+
+
+def lines_kernel(*refs):
+    blocks, line_ref, out_ref, sems = refs[:4], refs[4], refs[5], refs[6]
+    height, tokens = blocks[0].shape[0], line_ref.shape[1]
+    copies = []
+    for i, block in enumerate(blocks):
+        rows = slice(i * height, i * height + height)
+        copies.append(pltpu.make_async_copy(block.at[:, :tokens], line_ref.at[rows], sems.at[0, i]))
+        copies.append(pltpu.make_async_copy(block.at[:, tokens:], out_ref.at[rows], sems.at[1, i]))
+    for copy in copies:
+        copy.start()
+    for copy in copies:
+        copy.wait()
 
 
 def prepare_kernel(*refs):
@@ -118,7 +141,7 @@
 
 
 def queries_kernel(lat_ref, w_ref, q_ref, kv_ref):
-    rows = unpack_columns(lat_ref)
+    rows = unpack_columns([lat_ref[p].astype(F32) for p in range(lat_ref.shape[0])])
     inverse = lax.rsqrt(jnp.mean(rows * rows, axis=-1, keepdims=True) + EPSILON)
     normed = (rows * inverse).astype(BF16)
     q = dot(normed, w_ref[:64], NT).astype(BF16).astype(F32) * HD ** (-0.5)
@@ -272,34 +295,37 @@
     attend_all(q_ref, pos_ref, kp, k_ref, v_ref, put)
 
 
-def project_kernel(arrived_ref, w_ref, out_ref):
+def combine_kernel(arrived_ref, out_ref):
     values, levels = get_message(arrived_ref)
     groups = arrived_ref.shape[0]
     values = values.reshape(groups, 32, 128)
     levels = levels.reshape(groups, 32, 128)
     factors = jnp.exp(levels - jnp.max(levels, axis=0, keepdims=True))
     attended = jnp.sum(values * factors, axis=0) / jnp.sum(factors, axis=0)
-    low = low_half(attended.shape)
-    w = w_ref[...]
-    twice = jnp.concatenate([w, w], axis=0)
-    top = dot(jnp.where(low, attended, 0.0).astype(BF16), twice, NN)
-    bottom = dot(jnp.where(low, 0.0, attended).astype(BF16), twice, NN)
-    pack_columns(top, bottom, out_ref)
-
-
-def add_kernel(arrived_ref, lat_ref, own_ref, out_ref):
-    half = lat_ref.shape[0] // 2
-    packed = jnp.concatenate([lat_ref[:half, :], lat_ref[half:, :]], axis=1)
-    own = jnp.sum(arrived_ref[...].astype(F32), axis=0) + packed.astype(F32)
-    own_ref[...] = own
-    out_ref[...] = jnp.broadcast_to(own.astype(BF16)[None], out_ref.shape)
-
-
-def mlp_kernel(arrived_ref, gain_ref, up_ref, down_ref, out_ref):
-    normed = normalize(unpack_columns(arrived_ref), gain_ref[...])
+    out_ref[...] = jnp.broadcast_to(attended.astype(BF16)[None], out_ref.shape)
+
+
+def mlp_kernel(arrived_ref, lat_ref, *refs):
+    w_refs, (gain_ref, up_ref, down_ref, own_ref, out_ref, packed_ref) = refs[:-6], refs[-6:]
+    place, core = lax.axis_index("head"), lax.axis_index("seq") % 2
+    blocks = []
+    for i in range(4):
+        for j in range(4):
+            step = jnp.where(core == 0, 4 * i + STEPS[j], 4 * STEPS[j] + i)
+            blocks.append(arrived_ref[place ^ step].astype(F32))
+    attended = unpack_columns(blocks).astype(BF16)
+    projected = unpack_columns([lat_ref[p].astype(F32) for p in range(lat_ref.shape[0])])
+    first = 0
+    for w_ref in w_refs:
+        height = w_ref.shape[0]
+        projected = projected + dot(attended[:, first : first + height], w_ref[...], NN)
+        first += height
+    half = projected.shape[0] // 2
+    pack_columns(projected[:half], projected[half:], packed_ref)
+    own_ref[...] = packed_ref[place]
+    normed = normalize(projected, gain_ref[...])
     hidden = jax.nn.gelu(dot(normed, up_ref[...], NN), approximate=True).astype(BF16)
     share = dot(hidden, down_ref[...], NN)
-    half = share.shape[0] // 2
     pack_columns(share[:half], share[half:], out_ref)
 
 
@@ -309,12 +335,12 @@
     out_ref[...] = jnp.concatenate([packed[:, :cols], packed[:, cols:]], axis=0).astype(BF16)
 
 
-def call(kernel, outs, cost=1000, **kwargs):
+def call(kernel, outs, cost=1000, vmem_mib=40, **kwargs):
     shapes = [jax.ShapeDtypeStruct(s, t) for s, t in outs]
     return pl.pallas_call(
         kernel,
         out_shape=shapes if len(shapes) > 1 else shapes[0],
-        compiler_params=pltpu.CompilerParams(vmem_limit_bytes=40 * MIB),
+        compiler_params=pltpu.CompilerParams(vmem_limit_bytes=vmem_mib * MIB),
         cost_estimate=pl.CostEstimate(flops=cost, bytes_accessed=cost, transcendentals=0),
         **kwargs,
     )
@@ -351,12 +377,26 @@
     def swap_lines(piece, phase, step):
         return lax.ppermute(piece, BOTH, partners(seq_size, side, phase, step))
 
-    own = context.T
-    line = jnp.concatenate([own] + [swap_lines(own, 0, step) for step in STEPS[1:]], axis=0)
+    anywhere = pl.BlockSpec(memory_space=pl.ANY)
+    extended, copies = call(
+        first_kernel,
+        [((cols, tokens + w_out.shape[1]), BF16), ((head_size, *block), BF16)],
+        vmem_mib=60,
+        in_specs=[anywhere] * 3,
+        out_specs=[anywhere, vmem],
+        scratch_shapes=[pltpu.VMEM((lat_rows, cols), BF16), pltpu.SemaphoreType.DMA((3,))],
+    )(context.T, w_out, latents)
+    blocks = [extended] + [swap_lines(extended, 0, step) for step in STEPS[1:]]
+    line, out_line = call(
+        lines_kernel,
+        [((side * cols, tokens), BF16), ((side * cols, w_out.shape[1]), BF16)],
+        vmem_mib=40,
+        in_specs=[anywhere] * side,
+        out_specs=[anywhere] * 2,
+        scratch_shapes=[pltpu.SemaphoreType.DMA((2, side))],
+    )(*blocks)
     line, input_gain = lax.optimization_barrier((line, input_gain))
-    copies = call(latents_kernel, [((head_size, *block), BF16)])(latents)
     lat_blocks = lax.all_to_all(copies, "head", 0, 0)
-    anywhere = pl.BlockSpec(memory_space=pl.ANY)
     prepared = call(
         prepare_kernel,
         [
@@ -404,28 +444,33 @@
             pltpu.SemaphoreType.DMA((4, side)),
         ],
     )(*lines, key_weights, latent_kv, digits)
+    both, out_line = lax.optimization_barrier((both, out_line))
     from_sibling = lax.ppermute(both, "seq", swap)
-    mixed, level = call(own_kernel, [((rows, 2 * cols), F32)] * 2)(
+    next_line = swap_lines(out_line, 1, 1)
+    mixed, level = call(own_kernel, [((rows, 2 * cols), F32)] * 2, cost=10**8)(
         own_queries, query_pos, key_pos, keys, values
     )
+    mixed, next_line = lax.optimization_barrier((mixed, next_line))
+    out_pair = jnp.concatenate([out_line, next_line], axis=0)
+    far_pair = swap_lines(out_pair, 1, 2)
     joined = call(
         sibling_kernel,
         [((planes, 40, 2 * cols), BF16)],
+        cost=10**8,
         scratch_shapes=[
             pltpu.VMEM((128, key_count), BF16),
             pltpu.VMEM((key_count, 128), BF16),
         ],
     )(own_queries, query_pos, from_sibling, mixed, level)
     arrived = lax.all_to_all(joined, "seq", 0, 0, axis_index_groups=along_z)
-    shares = call(project_kernel, [((head_size, *block), BF16)])(arrived, w_out)
-    arrived = lax.all_to_all(shares, "head", 0, 0)
-    own_proj, copies = call(add_kernel, [(block, F32), ((head_size, *block), BF16)])(
-        arrived, latents
-    )
+    arrived, far_pair = lax.optimization_barrier((arrived, far_pair))
+    copies = call(combine_kernel, [((head_size, *block), BF16)])(arrived)
     arrived = lax.all_to_all(copies, "head", 0, 0)
-    shares = call(mlp_kernel, [((head_size, *block), BF16)])(
-        arrived, mlp_gain.reshape(1, -1), w_up, w_down
-    )
+    own_proj, shares = call(
+        mlp_kernel,
+        [(block, F32), ((head_size, *block), BF16)],
+        scratch_shapes=[pltpu.VMEM((head_size, *block), F32)],
+    )(arrived, lat_blocks, out_pair, far_pair, mlp_gain.reshape(1, -1), w_up, w_down)
     arrived = lax.all_to_all(shares, "head", 0, 0)
     return call(last_kernel, [((lat_rows, cols), BF16)])(arrived, own_proj)
 

time: 135 us -> 144 us (1.067)
  the two profiles are of different devices: /device:TPU:32 before, /device:TPU:2 now
where the time goes in v13:
time: 144 us; the launch traced here: 143 us
  blocking collectives  70.7 us (49%)
  starting transfers between devices  36.9 us (26%)
  Pallas kernels  27.5 us (19%)
  waiting for transfers between devices  5.82 us (4%)
  local copies, waits for them, and re-layouts  1.79 us (1%)
    ppermute x8, starting transfers between devices, swap_lines(): return lax.ppermute(piece, BOTH, partners(seq_size, side, phase, step))  29.5 us
    all_to_all x1, blocking collectives, body(): lax.all_to_all(queries, 'seq', 0, 0, axis_index_groups=along_z)  27.7 us
    all_to_all x1, blocking collectives, body(): arrived = lax.all_to_all(joined, 'seq', 0, 0, axis_index_groups=along_z)  19 us
    pallas_call x1, Pallas kernels, body(): call(first_kernel, [((cols, tokens + w_out.shape[1]), BF16), ((head_size,...  13.7 us
    all_to_all x1, blocking collectives, body(): arrived = lax.all_to_all(copies, 'head', 0, 0)  12.9 us
    all_to_all x1, blocking collectives, body(): arrived = lax.all_to_all(shares, 'head', 0, 0)  11.1 us
    all_to_all x1, starting transfers between devices, body(): lat_blocks = lax.all_to_all(copies, 'head', 0, 0)  5.46 us
    ppermute x8, waiting for transfers between devices, swap_lines(): return lax.ppermute(piece, BOTH, partners(seq_size, side, phase, step))  5.43 us
  transfers between devices with their start and end apart: 10, of which 3 were waited for; matrix products, arithmetic and copies ran while one was open for 0% of the time, Pallas kernels for 7%

profile of v13, /device:TPU:2, one launch (start us, length us, event | category | flops | bytes accessed | tf_op | source)
XLA Modules:
  0.0 142.9 jit_solution(3745829531162412403)
XLA Ops:
  0.0 13.7 %shard_map.118 = (bf16[64,3072]{1,0:T(8,128)(2,1)}, bf16[16,32,128]{2,1,0:T(8,128)(2,1)}) custom-call(bf16[64,2048]{1,0:T(8,128)(2,1)} %bitcast.18, bf16[64,1024]{1,0:T(8,128)(2,1)} %w_ref.1, bf16[64,64]{1,0:T(8,128)(2,1)} %lat_any.1), custom_call_target="tpu_custom_call" | custom-call | flops 1000 | bytes 1000 | tf_op jit(solution)/shard_map/pallas_call | solution.py:381
  13.7 4.0 %collective-permute-start.2 = (bf16[64,3072]{1,0:T(8,128)(2,1)}, bf16[64,3072]{1,0:T(8,128)(2,1)S(1)}, u32[]{:S(2)}, u32[]{:S(2)}) collective-permute-start(bf16[64,3072]{1,0:T(8,128)(2,1)} %get-tuple-element.40.refs_0_), channel_id=1, source_target_pairs={{0,2},{1,3},{2,0},{3,1},{4,6},{5,7},{6,4},{7,5},{8,10},{9,11},{10,... | collective-permute-start | bytes 1179656 | tf_op jit(solution)/shard_map/ppermute | solution.py:378
  17.7 7.2 %collective-permute-start.1 = (bf16[64,3072]{1,0:T(8,128)(2,1)}, bf16[64,3072]{1,0:T(8,128)(2,1)S(1)}, u32[]{:S(2)}, u32[]{:S(2)}) collective-permute-start(bf16[64,3072]{1,0:T(8,128)(2,1)} %get-tuple-element.40.refs_0_), channel_id=1, source_target_pairs={{0,3},{1,2},{2,1},{3,0},{4,7},{5,6},{6,5},{7,4},{8,11},{9,10},{10,... | collective-permute-start | bytes 1179656 | tf_op jit(solution)/shard_map/ppermute | solution.py:378
  24.9 1.9 %collective-permute-start = (bf16[64,3072]{1,0:T(8,128)(2,1)}, bf16[64,3072]{1,0:T(8,128)(2,1)S(1)}, u32[]{:S(2)}, u32[]{:S(2)}) collective-permute-start(bf16[64,3072]{1,0:T(8,128)(2,1)} %get-tuple-element.40.refs_0_), channel_id=1, source_target_pairs={{0,1},{1,0},{2,3},{3,2},{4,5},{5,4},{6,7},{7,6},{8,9},{9,8},{10,11... | collective-permute-start | bytes 1179656 | tf_op jit(solution)/shard_map/ppermute | solution.py:378
  26.8 0.0 copy-start.3
  26.8 0.0 copy-start.4
  26.8 5.5 %all-to-all-start = ((bf16[16,32,128]{2,1,0:T(8,128)(2,1)}), bf16[16,32,128]{2,1,0:T(8,128)(2,1)S(1)}, u32[]{:S(2)}, u32[]{:S(2)}) async-start(bf16[16,32,128]{2,1,0:T(8,128)(2,1)} %get-tuple-element.43), calls=%async_computation | async-start | bytes 262144 | tf_op jit(solution)/shard_map/all_to_all | solution.py:399
  32.3 0.0 collective-permute-done.2.refs_3_
  32.3 0.0 collective-permute-done.1.refs_2_
  32.3 3.2 %collective-permute-done.refs_1_ = bf16[64,3072]{1,0:T(8,128)(2,1)S(1)} collective-permute-done((bf16[64,3072]{1,0:T(8,128)(2,1)}, bf16[64,3072]{1,0:T(8,128)(2,1)S(1)}, u32[]{:S(2)}, u32[]{:S(2)}) %collective-permute-start) | collective-permute-done | bytes 393248 | tf_op jit(solution)/shard_map/ppermute | solution.py:378
  35.5 1.0 copy-done.2
  36.5 0.2 shard_map.119
  36.7 0.0 copy-start.6
  36.7 0.0 copy-start.8
  36.8 0.0 copy-done.3
  36.8 0.0 copy-done.4
  36.8 0.6 copy-done.5
  37.4 0.1 copy-done.6
  37.4 0.0 copy-done.8
  37.4 1.2 shard_map.120
  38.6 0.4 all-to-all-done.lat_ref
  39.0 2.8 %collective-permute-start.5 = (bf16[256,2048]{1,0:T(8,128)(2,1)S(1)}, bf16[256,2048]{1,0:T(8,128)(2,1)S(1)}, u32[]{:S(2)}, u32[]{:S(2)}) collective-permute-start(bf16[256,2048]{1,0:T(8,128)(2,1)S(1)} %get-tuple-element.56.refs_0_), channel_id=1, source_target_pairs={{0,8},{1,9},{2,10},{3,11},{4,12},{5,13},{6,14},{7,15},{8,0},{9,1},... | collective-permute-start | bytes 3145736 | tf_op jit(solution)/shard_map/ppermute | solution.py:378
  41.9 3.9 %collective-permute-start.4 = (bf16[256,2048]{1,0:T(8,128)(2,1)S(1)}, bf16[256,2048]{1,0:T(8,128)(2,1)S(1)}, u32[]{:S(2)}, u32[]{:S(2)}) collective-permute-start(bf16[256,2048]{1,0:T(8,128)(2,1)S(1)} %get-tuple-element.56.refs_0_), channel_id=1, source_target_pairs={{0,12},{1,13},{2,14},{3,15},{4,8},{5,9},{6,10},{7,11},{8,4},{9,5},... | collective-permute-start | bytes 3145736 | tf_op jit(solution)/shard_map/ppermute | solution.py:378
  45.8 2.5 %collective-permute-start.3 = (bf16[256,2048]{1,0:T(8,128)(2,1)S(1)}, bf16[256,2048]{1,0:T(8,128)(2,1)S(1)}, u32[]{:S(2)}, u32[]{:S(2)}) collective-permute-start(bf16[256,2048]{1,0:T(8,128)(2,1)S(1)} %get-tuple-element.56.refs_0_), channel_id=1, source_target_pairs={{0,4},{1,5},{2,6},{3,7},{4,0},{5,1},{6,2},{7,3},{8,12},{9,13},{10,... | collective-permute-start | bytes 3145736 | tf_op jit(solution)/shard_map/ppermute | solution.py:378
  48.2 0.4 shard_map.121
  48.7 27.7 %all_to_all.25 = bf16[16,32,128]{2,1,0:T(8,128)(2,1)S(1)} all-to-all(bf16[16,32,128]{2,1,0:T(8,128)(2,1)S(1)} %get-tuple-element.52), channel_id=1, replica_groups={{0,32,64,96,128,160,192,224,256,288,320,352,384,416,448,480},{16,48,80,..., dimensions={0} | all-to-all | bytes 262144 | tf_op jit(solution)/shard_map/all_to_all | solution.py:433
  76.4 0.0 collective-permute-done.5.refs_3_
  76.4 0.0 collective-permute-done.4.refs_2_
  76.4 0.0 collective-permute-done.3.refs_1_
  76.4 2.2 %shard_map.122 = (bf16[128,2176]{1,0:T(8,128)(2,1)S(1)}, bf16[2176,128]{1,0:T(8,128)(2,1)S(1)}, bf16[2272,128]{1,0:T(8,128)(2,1)S(1)}) custom-call(bf16[256,2048]{1,0:T(8,128)(2,1)S(1)} %get-tuple-element.56.refs_0_, bf16[256,2048]{1,0:T(8,128)(2,1)S(1)} %collective-permute-done.3.refs_1_, bf16[256,2048]{1,0:T(8,128)(2,1)S(1)} %collective-permute-done.4.refs_2_, ...), custom_call_target="tpu_custom_call" | custom-call | flops 1000000000 | bytes 1000000000 | tf_op jit(solution)/shard_map/pallas_call | solution.py:437
  78.7 3.2 %collective-permute-start.7 = (bf16[256,1024]{1,0:T(8,128)(2,1)S(1)}, bf16[256,1024]{1,0:T(8,128)(2,1)S(1)}, u32[]{:S(2)}, u32[]{:S(2)}) collective-permute-start(bf16[256,1024]{1,0:T(8,128)(2,1)S(1)} %get-tuple-element.67), channel_id=1, source_target_pairs={{0,4},{1,5},{2,6},{3,7},{4,0},{5,1},{6,2},{7,3},{8,12},{9,13},{10,... | collective-permute-start | bytes 1572872 | tf_op jit(solution)/shard_map/ppermute | solution.py:378
  81.8 1.9 %collective-permute-start.6 = (bf16[2272,128]{1,0:T(8,128)(2,1)S(1)}, bf16[2272,128]{1,0:T(8,128)(2,1)S(1)}, u32[]{:S(2)}, u32[]{:S(2)}) collective-permute-start(bf16[2272,128]{1,0:T(8,128)(2,1)S(1)} %get-tuple-element.62), channel_id=1, source_target_pairs={{0,16},{16,0},{32,48},{48,32},{64,80},{80,64},{96,112},{112,96},{1... | collective-permute-start | bytes 1744904 | tf_op jit(solution)/shard_map/ppermute | solution.py:448
  83.8 3.7 %shard_map.123 = (f32[512,128]{1,0:T(8,128)S(1)}, f32[512,128]{1,0:T(8,128)S(1)}) custom-call(bf16[512,128]{1,0:T(8,128)(2,1)S(1)} %bitcast.9, s32[2,512,128]{2,1,0:T(8,128)S(1)} %get-tuple-element.55.pos_ref, s32[1,2176]{1,0:T(1,128)S(1)} %get-tuple-element.63.kp_ref, bf16[128,2176]{1,0:T(8,128)(2,1)S(1)} %get-tuple-element.64.k_ref, ...), custom_call_target="tpu_custom_call" | custom-call | flops 100000000 | bytes 100000000 | tf_op jit(solution)/shard_map/pallas_call | solution.py:450
  87.5 2.3 %collective-permute-done.7 = bf16[256,1024]{1,0:T(8,128)(2,1)S(1)} collective-permute-done((bf16[256,1024]{1,0:T(8,128)(2,1)S(1)}, bf16[256,1024]{1,0:T(8,128)(2,1)S(1)}, u32[]{:S(2)}, u32[]{:S(2)}) %collective-permute-start.7) | collective-permute-done | bytes 524320 | tf_op jit(solution)/shard_map/ppermute | solution.py:378
  89.8 4.0 %collective-permute-start.8 = (bf16[512,1024]{1,0:T(8,128)(2,1)S(1)}, bf16[512,1024]{1,0:T(8,128)(2,1)S(1)}, u32[]{:S(2)}, u32[]{:S(2)}) collective-permute-start(bf16[512,1024]{1,0:T(8,128)(2,1)S(1)} %constant_dynamic-update-slice_fusion.refs_0_), channel_id=1, source_target_pairs={{0,8},{1,9},{2,10},{3,11},{4,12},{5,13},{6,14},{7,15},{8,0},{9,1},... | collective-permute-start | bytes 3145736 | tf_op jit(solution)/shard_map/ppermute | solution.py:378
  93.8 0.0 collective-permute-done.6.kv_ref
  93.8 0.0 copy-start.1
  93.8 3.8 %shard_map.124 = bf16[16,40,128]{2,1,0:T(8,128)(2,1)S(1)} custom-call(bf16[512,128]{1,0:T(8,128)(2,1)S(1)} %bitcast.10, s32[2,512,128]{2,1,0:T(8,128)S(1)} %get-tuple-element.55.pos_ref, bf16[2272,128]{1,0:T(8,128)(2,1)S(1)} %collective-permute-done.6.kv_ref, f32[512,128]{1,0:T(8,128)S(1)} %get-tuple-element.68.mix_ref, f32[512,128]{1,0:T(8,128)S(1)} %get-tuple-element.69.lev_ref), custom_call_target="tpu_custom_call" | custom-call | flops 100000000 | bytes 100000000 | tf_op jit(solution)/shard_map/pallas_call | solution.py:456
  97.7 0.0 copy-start
  97.7 19.0 %all_to_all.26.arrived_ref = bf16[16,40,128]{2,1,0:T(8,128)(2,1)S(1)} all-to-all(bf16[16,40,128]{2,1,0:T(8,128)(2,1)S(1)} %shard_map.124), channel_id=1, replica_groups={{0,32,64,96,128,160,192,224,256,288,320,352,384,416,448,480},{16,48,80,..., dimensions={0} | all-to-all | bytes 327680 | tf_op jit(solution)/shard_map/all_to_all | solution.py:465
  116.7 0.0 collective-permute-done.8.refs_1_
  116.7 0.3 shard_map.125
  117.0 0.0 copy-start.9
  117.1 12.9 %all_to_all.27.arrived_ref = bf16[16,32,128]{2,1,0:T(8,128)(2,1)S(1)} all-to-all(bf16[16,32,128]{2,1,0:T(8,128)(2,1)S(1)} %shard_map.125), channel_id=1, replica_groups=mesh['seq'=32,'head'=16] {'head'}, dimensions={0} | all-to-all | bytes 262144 | tf_op jit(solution)/shard_map/all_to_all | solution.py:468
  130.0 0.0 copy-done.1
  130.0 1.2 shard_map.126
  131.2 11.1 %all_to_all.28.arrived_ref = bf16[16,32,128]{2,1,0:T(8,128)(2,1)S(1)} all-to-all(bf16[16,32,128]{2,1,0:T(8,128)(2,1)S(1)} %get-tuple-element.73), channel_id=1, replica_groups=mesh['seq'=32,'head'=16] {'head'}, dimensions={0} | all-to-all | bytes 262144 | tf_op jit(solution)/shard_map/all_to_all | solution.py:474
  142.2 0.7 shard_map.127
  (8 shorter events, 0.1 us)
Async XLA Ops:
  13.7 18.6 %collective-permute-start.2 = (bf16[64,3072]{1,0:T(8,128)(2,1)}, bf16[64,3072]{1,0:T(8,128)(2,1)S(1)}, u32[]{:S(2)}, u32[]{:S(2)}) collective-permute-start(bf16[64,3072]{1,0:T(8,128)(2,1)} %get-tuple-element.40.refs_0_), channel_id=1, source_target_pairs={{0,2},{1,3},{2,0},{3,1},{4,6},{5,7},{6,4},{7,5},{8,10},{9,11},{10,... | collective-permute-start | bytes 1179656 | tf_op jit(solution)/shard_map/ppermute | solution.py:378
  17.7 14.6 %collective-permute-start.1 = (bf16[64,3072]{1,0:T(8,128)(2,1)}, bf16[64,3072]{1,0:T(8,128)(2,1)S(1)}, u32[]{:S(2)}, u32[]{:S(2)}) collective-permute-start(bf16[64,3072]{1,0:T(8,128)(2,1)} %get-tuple-element.40.refs_0_), channel_id=1, source_target_pairs={{0,3},{1,2},{2,1},{3,0},{4,7},{5,6},{6,5},{7,4},{8,11},{9,10},{10,... | collective-permute-start | bytes 1179656 | tf_op jit(solution)/shard_map/ppermute | solution.py:378
  24.9 10.6 %collective-permute-start = (bf16[64,3072]{1,0:T(8,128)(2,1)}, bf16[64,3072]{1,0:T(8,128)(2,1)S(1)}, u32[]{:S(2)}, u32[]{:S(2)}) collective-permute-start(bf16[64,3072]{1,0:T(8,128)(2,1)} %get-tuple-element.40.refs_0_), channel_id=1, source_target_pairs={{0,1},{1,0},{2,3},{3,2},{4,5},{5,4},{6,7},{7,6},{8,9},{9,8},{10,11... | collective-permute-start | bytes 1179656 | tf_op jit(solution)/shard_map/ppermute | solution.py:378
  26.8 9.9 %copy-start.3 = (bf16[1024,64]{0,1:T(8,128)(2,1)S(1)}, bf16[1024,64]{0,1:T(8,128)(2,1)}, u32[]{:S(2)}) copy-start(bf16[1024,64]{0,1:T(8,128)(2,1)} %param.17) | copy-start | bytes 393220
  26.8 9.9 %copy-start.4 = (bf16[1024,64]{0,1:T(8,128)(2,1)S(1)}, bf16[1024,64]{0,1:T(8,128)(2,1)}, u32[]{:S(2)}) copy-start(bf16[1024,64]{0,1:T(8,128)(2,1)} %param.18) | copy-start | bytes 393220
  26.8 12.2 %all-to-all-start = ((bf16[16,32,128]{2,1,0:T(8,128)(2,1)}), bf16[16,32,128]{2,1,0:T(8,128)(2,1)S(1)}, u32[]{:S(2)}, u32[]{:S(2)}) async-start(bf16[16,32,128]{2,1,0:T(8,128)(2,1)} %get-tuple-element.43), calls=%async_computation | async-start | bytes 262144 | tf_op jit(solution)/shard_map/all_to_all | solution.py:399
  35.5 1.0 copy-start.2
  36.5 0.9 copy-start.5
  36.5 0.9 copy-start.7
  36.7 0.7 copy-start.6
  36.7 0.7 copy-start.8
  39.0 37.4 %collective-permute-start.5 = (bf16[256,2048]{1,0:T(8,128)(2,1)S(1)}, bf16[256,2048]{1,0:T(8,128)(2,1)S(1)}, u32[]{:S(2)}, u32[]{:S(2)}) collective-permute-start(bf16[256,2048]{1,0:T(8,128)(2,1)S(1)} %get-tuple-element.56.refs_0_), channel_id=1, source_target_pairs={{0,8},{1,9},{2,10},{3,11},{4,12},{5,13},{6,14},{7,15},{8,0},{9,1},... | collective-permute-start | bytes 3145736 | tf_op jit(solution)/shard_map/ppermute | solution.py:378
  41.9 34.6 %collective-permute-start.4 = (bf16[256,2048]{1,0:T(8,128)(2,1)S(1)}, bf16[256,2048]{1,0:T(8,128)(2,1)S(1)}, u32[]{:S(2)}, u32[]{:S(2)}) collective-permute-start(bf16[256,2048]{1,0:T(8,128)(2,1)S(1)} %get-tuple-element.56.refs_0_), channel_id=1, source_target_pairs={{0,12},{1,13},{2,14},{3,15},{4,8},{5,9},{6,10},{7,11},{8,4},{9,5},... | collective-permute-start | bytes 3145736 | tf_op jit(solution)/shard_map/ppermute | solution.py:378
  45.8 30.7 %collective-permute-start.3 = (bf16[256,2048]{1,0:T(8,128)(2,1)S(1)}, bf16[256,2048]{1,0:T(8,128)(2,1)S(1)}, u32[]{:S(2)}, u32[]{:S(2)}) collective-permute-start(bf16[256,2048]{1,0:T(8,128)(2,1)S(1)} %get-tuple-element.56.refs_0_), channel_id=1, source_target_pairs={{0,4},{1,5},{2,6},{3,7},{4,0},{5,1},{6,2},{7,3},{8,12},{9,13},{10,... | collective-permute-start | bytes 3145736 | tf_op jit(solution)/shard_map/ppermute | solution.py:378
  78.7 11.1 %collective-permute-start.7 = (bf16[256,1024]{1,0:T(8,128)(2,1)S(1)}, bf16[256,1024]{1,0:T(8,128)(2,1)S(1)}, u32[]{:S(2)}, u32[]{:S(2)}) collective-permute-start(bf16[256,1024]{1,0:T(8,128)(2,1)S(1)} %get-tuple-element.67), channel_id=1, source_target_pairs={{0,4},{1,5},{2,6},{3,7},{4,0},{5,1},{6,2},{7,3},{8,12},{9,13},{10,... | collective-permute-start | bytes 1572872 | tf_op jit(solution)/shard_map/ppermute | solution.py:378
  81.8 12.0 %collective-permute-start.6 = (bf16[2272,128]{1,0:T(8,128)(2,1)S(1)}, bf16[2272,128]{1,0:T(8,128)(2,1)S(1)}, u32[]{:S(2)}, u32[]{:S(2)}) collective-permute-start(bf16[2272,128]{1,0:T(8,128)(2,1)S(1)} %get-tuple-element.62), channel_id=1, source_target_pairs={{0,16},{16,0},{32,48},{48,32},{64,80},{80,64},{96,112},{112,96},{1... | collective-permute-start | bytes 1744904 | tf_op jit(solution)/shard_map/ppermute | solution.py:448
  89.8 26.9 %collective-permute-start.8 = (bf16[512,1024]{1,0:T(8,128)(2,1)S(1)}, bf16[512,1024]{1,0:T(8,128)(2,1)S(1)}, u32[]{:S(2)}, u32[]{:S(2)}) collective-permute-start(bf16[512,1024]{1,0:T(8,128)(2,1)S(1)} %constant_dynamic-update-slice_fusion.refs_0_), channel_id=1, source_target_pairs={{0,8},{1,9},{2,10},{3,11},{4,12},{5,13},{6,14},{7,15},{8,0},{9,1},... | collective-permute-start | bytes 3145736 | tf_op jit(solution)/shard_map/ppermute | solution.py:378
  93.8 36.2 %copy-start.1 = (bf16[256,1024]{1,0:T(8,128)(2,1)S(1)}, bf16[256,1024]{1,0:T(8,128)(2,1)}, u32[]{:S(2)}) copy-start(bf16[256,1024]{1,0:T(8,128)(2,1)} %refs_4_.1) | copy-start | bytes 1572868
  97.7 32.3 %copy-start = (bf16[1024,256]{1,0:T(8,128)(2,1)S(1)}, bf16[1024,256]{1,0:T(8,128)(2,1)}, u32[]{:S(2)}) copy-start(bf16[1024,256]{1,0:T(8,128)(2,1)} %refs_3_.1) | copy-start | bytes 1572868
  117.0 12.9 %copy-start.9 = (f32[1024]{0:T(1024)S(1)}, f32[1024]{0:T(1024)}, u32[]{:S(2)}) copy-start(f32[1024]{0:T(1024)} %param.21) | copy-start | bytes 12292

commit v14 on v13

--- a/solution.py
+++ b/solution.py
@@ -13,7 +13,7 @@
 NEGATIVE = -1e30
 LOWEST = -1e29
 BOTH = ("seq", "head")
-STEPS = (0, 1, 3, 2)
+STEPS = (0, 2, 3, 1)
 F32 = jnp.float32
 BF16 = jnp.bfloat16
 MIB = 1 << 20
@@ -68,12 +68,12 @@
     return (rows * inverse * gain).astype(BF16)
 
 
-def first_kernel(ctx_ref, w_ref, lat_any, ext_ref, out_ref, lat_ref, sems):
-    tokens = ctx_ref.shape[1]
+def first_kernel(ctx_any, w_any, lat_any, ext_ref, out_ref, lat_ref, sems):
+    tokens = ctx_any.shape[1]
     copies = [
         pltpu.make_async_copy(lat_any, lat_ref, sems.at[0]),
-        pltpu.make_async_copy(ctx_ref, ext_ref.at[:, :tokens], sems.at[1]),
-        pltpu.make_async_copy(w_ref, ext_ref.at[:, tokens:], sems.at[2]),
+        pltpu.make_async_copy(ctx_any, ext_ref.at[:, :tokens], sems.at[1]),
+        pltpu.make_async_copy(w_any, ext_ref.at[:, tokens:], sems.at[2]),
     ]
     for copy in copies:
         copy.start()
@@ -383,7 +383,6 @@
         [((cols, tokens + w_out.shape[1]), BF16), ((head_size, *block), BF16)],
         vmem_mib=60,
         in_specs=[anywhere] * 3,
-        out_specs=[anywhere, vmem],
         scratch_shapes=[pltpu.VMEM((lat_rows, cols), BF16), pltpu.SemaphoreType.DMA((3,))],
     )(context.T, w_out, latents)
     blocks = [extended] + [swap_lines(extended, 0, step) for step in STEPS[1:]]
@@ -444,10 +443,10 @@
             pltpu.SemaphoreType.DMA((4, side)),
         ],
     )(*lines, key_weights, latent_kv, digits)
-    both, out_line = lax.optimization_barrier((both, out_line))
+    own_queries, out_line = lax.optimization_barrier((own_queries, out_line))
     from_sibling = lax.ppermute(both, "seq", swap)
     next_line = swap_lines(out_line, 1, 1)
-    mixed, level = call(own_kernel, [((rows, 2 * cols), F32)] * 2, cost=10**8)(
+    mixed, level = call(own_kernel, [((rows, 2 * cols), F32)] * 2)(
         own_queries, query_pos, key_pos, keys, values
     )
     mixed, next_line = lax.optimization_barrier((mixed, next_line))

time: 144 us -> 131 us (0.910)
  the two profiles are of different devices: /device:TPU:2 before, /device:TPU:32 now
where the time goes in v14:
time: 131 us
  blocking collectives  50.9 us (39%)
  starting transfers between devices  40.6 us (31%)
  waiting for transfers between devices  19.6 us (15%)
  Pallas kernels  16.4 us (13%)
  local copies, waits for them, and re-layouts  2.82 us (2%)
    all_to_all x1, blocking collectives, body(): lax.all_to_all(queries, 'seq', 0, 0, axis_index_groups=along_z)  27.6 us
    ppermute x8, starting transfers between devices, swap_lines(): return lax.ppermute(piece, BOTH, partners(seq_size, side, phase, step))  26.2 us
    all_to_all x1, blocking collectives, body(): arrived = lax.all_to_all(copies, 'head', 0, 0)  12.3 us
    all_to_all x1, blocking collectives, body(): arrived = lax.all_to_all(shares, 'head', 0, 0)  11.1 us
    all_to_all x1, waiting for transfers between devices, body(): arrived = lax.all_to_all(joined, 'seq', 0, 0, axis_index_groups=along_z)  9.53 us
    all_to_all x1, starting transfers between devices, body(): lat_blocks = lax.all_to_all(copies, 'head', 0, 0)  7.7 us
    ppermute x8, waiting for transfers between devices, swap_lines(): return lax.ppermute(piece, BOTH, partners(seq_size, side, phase, step))  5.48 us
    all_to_all x1, starting transfers between devices, body(): arrived = lax.all_to_all(joined, 'seq', 0, 0, axis_index_groups=along_z)  4.74 us
  transfers between devices with their start and end apart: 11, of which 4 were waited for; matrix products, arithmetic and copies ran while one was open for 0% of the time, Pallas kernels for 9%

profile of v14, /device:TPU:32, one launch (start us, length us, event | category | flops | bytes accessed | tf_op | source)
XLA Modules:
  0.0 130.6 jit_solution(2290641276927509265)
XLA Ops:
  0.0 1.8 %shard_map.118 = (bf16[64,3072]{1,0:T(8,128)(2,1)}, bf16[16,32,128]{2,1,0:T(8,128)(2,1)}) custom-call(bf16[64,2048]{1,0:T(8,128)(2,1)} %bitcast.18, bf16[64,1024]{1,0:T(8,128)(2,1)} %w_any.1, bf16[64,64]{1,0:T(8,128)(2,1)} %lat_any.1), custom_call_target="tpu_custom_call" | custom-call | flops 1000 | bytes 1000 | tf_op jit(solution)/shard_map/pallas_call | solution.py:381
  1.8 4.9 %collective-permute-start = (bf16[64,3072]{1,0:T(8,128)(2,1)}, bf16[64,3072]{1,0:T(8,128)(2,1)S(1)}, u32[]{:S(2)}, u32[]{:S(2)}) collective-permute-start(bf16[64,3072]{1,0:T(8,128)(2,1)} %get-tuple-element.40.refs_0_), channel_id=1, source_target_pairs={{0,2},{1,3},{2,0},{3,1},{4,6},{5,7},{6,4},{7,5},{8,10},{9,11},{10,... | collective-permute-start | bytes 1179656 | tf_op jit(solution)/shard_map/ppermute | solution.py:378
  6.8 3.0 %collective-permute-start.1 = (bf16[64,3072]{1,0:T(8,128)(2,1)}, bf16[64,3072]{1,0:T(8,128)(2,1)S(1)}, u32[]{:S(2)}, u32[]{:S(2)}) collective-permute-start(bf16[64,3072]{1,0:T(8,128)(2,1)} %get-tuple-element.40.refs_0_), channel_id=1, source_target_pairs={{0,3},{1,2},{2,1},{3,0},{4,7},{5,6},{6,5},{7,4},{8,11},{9,10},{10,... | collective-permute-start | bytes 1179656 | tf_op jit(solution)/shard_map/ppermute | solution.py:378
  9.8 1.9 %collective-permute-start.2 = (bf16[64,3072]{1,0:T(8,128)(2,1)}, bf16[64,3072]{1,0:T(8,128)(2,1)S(1)}, u32[]{:S(2)}, u32[]{:S(2)}) collective-permute-start(bf16[64,3072]{1,0:T(8,128)(2,1)} %get-tuple-element.40.refs_0_), channel_id=1, source_target_pairs={{0,1},{1,0},{2,3},{3,2},{4,5},{5,4},{6,7},{7,6},{8,9},{9,8},{10,11... | collective-permute-start | bytes 1179656 | tf_op jit(solution)/shard_map/ppermute | solution.py:378
  11.8 0.0 copy-start.3
  11.8 0.0 copy-start.4
  11.8 7.7 %all-to-all-start = ((bf16[16,32,128]{2,1,0:T(8,128)(2,1)}), bf16[16,32,128]{2,1,0:T(8,128)(2,1)S(1)}, u32[]{:S(2)}, u32[]{:S(2)}) async-start(bf16[16,32,128]{2,1,0:T(8,128)(2,1)} %get-tuple-element.43), calls=%async_computation | async-start | bytes 262144 | tf_op jit(solution)/shard_map/all_to_all | solution.py:398
  19.5 0.0 collective-permute-done.refs_1_
  19.5 0.0 collective-permute-done.1.refs_2_
  19.5 0.2 collective-permute-done.2.refs_3_
  19.7 1.0 copy-done.2
  20.7 0.2 shard_map.119
  21.0 0.0 copy-start.6
  21.0 0.0 copy-start.8
  21.0 0.0 copy-done.3
  21.0 0.0 copy-done.4
  21.0 0.6 copy-done.5
  21.6 0.1 copy-done.6
  21.7 0.0 copy-done.8
  21.7 1.2 shard_map.120
  22.9 4.6 %all-to-all-done.lat_ref = bf16[16,32,128]{2,1,0:T(8,128)(2,1)S(1)} async-done(((bf16[16,32,128]{2,1,0:T(8,128)(2,1)}), bf16[16,32,128]{2,1,0:T(8,128)(2,1)S(1)}, u32[]{:S(2)}, u32[]{:S(2)}) %all-to-all-start) | async-done | bytes 131104 | tf_op jit(solution)/shard_map/all_to_all | solution.py:398
  27.5 2.9 %collective-permute-start.3 = (bf16[256,2048]{1,0:T(8,128)(2,1)S(1)}, bf16[256,2048]{1,0:T(8,128)(2,1)S(1)}, u32[]{:S(2)}, u32[]{:S(2)}) collective-permute-start(bf16[256,2048]{1,0:T(8,128)(2,1)S(1)} %get-tuple-element.58.refs_0_), channel_id=1, source_target_pairs={{0,8},{1,9},{2,10},{3,11},{4,12},{5,13},{6,14},{7,15},{8,0},{9,1},... | collective-permute-start | bytes 3145736 | tf_op jit(solution)/shard_map/ppermute | solution.py:378
  30.4 3.9 %collective-permute-start.4 = (bf16[256,2048]{1,0:T(8,128)(2,1)S(1)}, bf16[256,2048]{1,0:T(8,128)(2,1)S(1)}, u32[]{:S(2)}, u32[]{:S(2)}) collective-permute-start(bf16[256,2048]{1,0:T(8,128)(2,1)S(1)} %get-tuple-element.58.refs_0_), channel_id=1, source_target_pairs={{0,12},{1,13},{2,14},{3,15},{4,8},{5,9},{6,10},{7,11},{8,4},{9,5},... | collective-permute-start | bytes 3145736 | tf_op jit(solution)/shard_map/ppermute | solution.py:378
  34.3 2.4 %collective-permute-start.5 = (bf16[256,2048]{1,0:T(8,128)(2,1)S(1)}, bf16[256,2048]{1,0:T(8,128)(2,1)S(1)}, u32[]{:S(2)}, u32[]{:S(2)}) collective-permute-start(bf16[256,2048]{1,0:T(8,128)(2,1)S(1)} %get-tuple-element.58.refs_0_), channel_id=1, source_target_pairs={{0,4},{1,5},{2,6},{3,7},{4,0},{5,1},{6,2},{7,3},{8,12},{9,13},{10,... | collective-permute-start | bytes 3145736 | tf_op jit(solution)/shard_map/ppermute | solution.py:378
  36.7 0.4 shard_map.121
  37.2 27.6 %all_to_all.25 = bf16[16,32,128]{2,1,0:T(8,128)(2,1)S(1)} all-to-all(bf16[16,32,128]{2,1,0:T(8,128)(2,1)S(1)} %get-tuple-element.52), channel_id=1, replica_groups={{0,32,64,96,128,160,192,224,256,288,320,352,384,416,448,480},{16,48,80,..., dimensions={0} | all-to-all | bytes 262144 | tf_op jit(solution)/shard_map/all_to_all | solution.py:432
  64.7 3.4 %collective-permute-start.7 = (bf16[256,1024]{1,0:T(8,128)(2,1)S(1)}, bf16[256,1024]{1,0:T(8,128)(2,1)S(1)}, u32[]{:S(2)}, u32[]{:S(2)}) collective-permute-start(bf16[256,1024]{1,0:T(8,128)(2,1)S(1)} %get-tuple-element.67), channel_id=1, source_target_pairs={{0,4},{1,5},{2,6},{3,7},{4,0},{5,1},{6,2},{7,3},{8,12},{9,13},{10,... | collective-permute-start | bytes 1572872 | tf_op jit(solution)/shard_map/ppermute | solution.py:378
  68.1 0.0 collective-permute-done.3.refs_1_
  68.1 0.0 collective-permute-done.4.refs_2_
  68.1 0.0 collective-permute-done.5.refs_3_
  68.2 2.3 %shard_map.122 = (bf16[128,2176]{1,0:T(8,128)(2,1)S(1)}, bf16[2176,128]{1,0:T(8,128)(2,1)S(1)}, bf16[2272,128]{1,0:T(8,128)(2,1)S(1)}) custom-call(bf16[256,2048]{1,0:T(8,128)(2,1)S(1)} %get-tuple-element.58.refs_0_, bf16[256,2048]{1,0:T(8,128)(2,1)S(1)} %collective-permute-done.3.refs_1_, bf16[256,2048]{1,0:T(8,128)(2,1)S(1)} %collective-permute-done.4.refs_2_, ...), custom_call_target="tpu_custom_call" | custom-call | flops 1000000000 | bytes 1000000000 | tf_op jit(solution)/shard_map/pallas_call | solution.py:436
  70.5 1.9 %collective-permute-start.6 = (bf16[2272,128]{1,0:T(8,128)(2,1)S(1)}, bf16[2272,128]{1,0:T(8,128)(2,1)S(1)}, u32[]{:S(2)}, u32[]{:S(2)}) collective-permute-start(bf16[2272,128]{1,0:T(8,128)(2,1)S(1)} %get-tuple-element.62), channel_id=1, source_target_pairs={{0,16},{16,0},{32,48},{48,32},{64,80},{80,64},{96,112},{112,96},{1... | collective-permute-start | bytes 1744904 | tf_op jit(solution)/shard_map/ppermute | solution.py:447
  72.5 3.7 %shard_map.123 = (f32[512,128]{1,0:T(8,128)S(1)}, f32[512,128]{1,0:T(8,128)S(1)}) custom-call(bf16[512,128]{1,0:T(8,128)(2,1)S(1)} %bitcast.9, s32[2,512,128]{2,1,0:T(8,128)S(1)} %get-tuple-element.57.pos_ref, s32[1,2176]{1,0:T(1,128)S(1)} %get-tuple-element.63.kp_ref, bf16[128,2176]{1,0:T(8,128)(2,1)S(1)} %get-tuple-element.64.k_ref, ...), custom_call_target="tpu_custom_call" | custom-call | flops 1000 | bytes 1000 | tf_op jit(solution)/shard_map/pallas_call | solution.py:449
  76.1 0.0 collective-permute-done.7
  76.2 3.7 %collective-permute-start.8 = (bf16[512,1024]{1,0:T(8,128)(2,1)S(1)}, bf16[512,1024]{1,0:T(8,128)(2,1)S(1)}, u32[]{:S(2)}, u32[]{:S(2)}) collective-permute-start(bf16[512,1024]{1,0:T(8,128)(2,1)S(1)} %constant_dynamic-update-slice_fusion.refs_0_), channel_id=1, source_target_pairs={{0,8},{1,9},{2,10},{3,11},{4,12},{5,13},{6,14},{7,15},{8,0},{9,1},... | collective-permute-start | bytes 3145736 | tf_op jit(solution)/shard_map/ppermute | solution.py:378
  79.9 0.0 collective-permute-done.6.kv_ref
  80.0 4.4 %shard_map.124 = bf16[16,40,128]{2,1,0:T(8,128)(2,1)} custom-call(bf16[512,128]{1,0:T(8,128)(2,1)S(1)} %bitcast.10, s32[2,512,128]{2,1,0:T(8,128)S(1)} %get-tuple-element.57.pos_ref, bf16[2272,128]{1,0:T(8,128)(2,1)S(1)} %collective-permute-done.6.kv_ref, f32[512,128]{1,0:T(8,128)S(1)} %get-tuple-element.68.mix_ref, f32[512,128]{1,0:T(8,128)S(1)} %get-tuple-element.69.lev_ref), custom_call_target="tpu_custom_call" | custom-call | flops 100000000 | bytes 100000000 | tf_op jit(solution)/shard_map/pallas_call | solution.py:455
  84.4 4.7 %all-to-all-start.2 = ((bf16[16,40,128]{2,1,0:T(8,128)(2,1)}), bf16[16,40,128]{2,1,0:T(8,128)(2,1)S(1)}, u32[]{:S(2)}, u32[]{:S(2)}) async-start(bf16[16,40,128]{2,1,0:T(8,128)(2,1)} %shard_map.124), calls=%async_computation.2 | async-start | bytes 327680 | tf_op jit(solution)/shard_map/all_to_all | solution.py:464
  89.1 5.3 %collective-permute-done.8.refs_1_ = bf16[512,1024]{1,0:T(8,128)(2,1)S(1)} collective-permute-done((bf16[512,1024]{1,0:T(8,128)(2,1)S(1)}, bf16[512,1024]{1,0:T(8,128)(2,1)S(1)}, u32[]{:S(2)}, u32[]{:S(2)}) %collective-permute-start.8) | collective-permute-done | bytes 1048608 | tf_op jit(solution)/shard_map/ppermute | solution.py:378
  94.4 9.5 %all-to-all-done.2.arrived_ref = bf16[16,40,128]{2,1,0:T(8,128)(2,1)S(1)} async-done(((bf16[16,40,128]{2,1,0:T(8,128)(2,1)}), bf16[16,40,128]{2,1,0:T(8,128)(2,1)S(1)}, u32[]{:S(2)}, u32[]{:S(2)}) %all-to-all-start.2) | async-done | bytes 163872 | tf_op jit(solution)/shard_map/all_to_all | solution.py:464
  103.9 0.4 shard_map.125
  104.3 0.0 copy-start.9
  104.3 12.3 %all_to_all.26.arrived_ref = bf16[16,32,128]{2,1,0:T(8,128)(2,1)S(1)} all-to-all(bf16[16,32,128]{2,1,0:T(8,128)(2,1)S(1)} %shard_map.125), channel_id=1, replica_groups=mesh['seq'=32,'head'=16] {'head'}, dimensions={0} | all-to-all | bytes 262144 | tf_op jit(solution)/shard_map/all_to_all | solution.py:467
  116.6 0.0 copy-done
  116.6 1.0 copy-done.1
  117.6 1.2 shard_map.126
  118.8 11.1 %all_to_all.27.arrived_ref = bf16[16,32,128]{2,1,0:T(8,128)(2,1)S(1)} all-to-all(bf16[16,32,128]{2,1,0:T(8,128)(2,1)S(1)} %get-tuple-element.73), channel_id=1, replica_groups=mesh['seq'=32,'head'=16] {'head'}, dimensions={0} | all-to-all | bytes 262144 | tf_op jit(solution)/shard_map/all_to_all | solution.py:473
  129.9 0.7 shard_map.127
  (9 shorter events, 0.1 us)
Async XLA Ops:
  1.8 17.7 %collective-permute-start = (bf16[64,3072]{1,0:T(8,128)(2,1)}, bf16[64,3072]{1,0:T(8,128)(2,1)S(1)}, u32[]{:S(2)}, u32[]{:S(2)}) collective-permute-start(bf16[64,3072]{1,0:T(8,128)(2,1)} %get-tuple-element.40.refs_0_), channel_id=1, source_target_pairs={{0,2},{1,3},{2,0},{3,1},{4,6},{5,7},{6,4},{7,5},{8,10},{9,11},{10,... | collective-permute-start | bytes 1179656 | tf_op jit(solution)/shard_map/ppermute | solution.py:378
  6.8 12.7 %collective-permute-start.1 = (bf16[64,3072]{1,0:T(8,128)(2,1)}, bf16[64,3072]{1,0:T(8,128)(2,1)S(1)}, u32[]{:S(2)}, u32[]{:S(2)}) collective-permute-start(bf16[64,3072]{1,0:T(8,128)(2,1)} %get-tuple-element.40.refs_0_), channel_id=1, source_target_pairs={{0,3},{1,2},{2,1},{3,0},{4,7},{5,6},{6,5},{7,4},{8,11},{9,10},{10,... | collective-permute-start | bytes 1179656 | tf_op jit(solution)/shard_map/ppermute | solution.py:378
  9.8 9.9 %collective-permute-start.2 = (bf16[64,3072]{1,0:T(8,128)(2,1)}, bf16[64,3072]{1,0:T(8,128)(2,1)S(1)}, u32[]{:S(2)}, u32[]{:S(2)}) collective-permute-start(bf16[64,3072]{1,0:T(8,128)(2,1)} %get-tuple-element.40.refs_0_), channel_id=1, source_target_pairs={{0,1},{1,0},{2,3},{3,2},{4,5},{5,4},{6,7},{7,6},{8,9},{9,8},{10,11... | collective-permute-start | bytes 1179656 | tf_op jit(solution)/shard_map/ppermute | solution.py:378
  11.8 9.2 %copy-start.3 = (bf16[1024,64]{0,1:T(8,128)(2,1)S(1)}, bf16[1024,64]{0,1:T(8,128)(2,1)}, u32[]{:S(2)}) copy-start(bf16[1024,64]{0,1:T(8,128)(2,1)} %param.17) | copy-start | bytes 393220
  11.8 9.2 %copy-start.4 = (bf16[1024,64]{0,1:T(8,128)(2,1)S(1)}, bf16[1024,64]{0,1:T(8,128)(2,1)}, u32[]{:S(2)}) copy-start(bf16[1024,64]{0,1:T(8,128)(2,1)} %param.18) | copy-start | bytes 393220
  11.8 15.7 %all-to-all-start = ((bf16[16,32,128]{2,1,0:T(8,128)(2,1)}), bf16[16,32,128]{2,1,0:T(8,128)(2,1)S(1)}, u32[]{:S(2)}, u32[]{:S(2)}) async-start(bf16[16,32,128]{2,1,0:T(8,128)(2,1)} %get-tuple-element.43), calls=%async_computation | async-start | bytes 262144 | tf_op jit(solution)/shard_map/all_to_all | solution.py:398
  19.7 1.0 copy-start.2
  20.7 0.9 copy-start.5
  20.7 0.9 copy-start.7
  21.0 0.7 copy-start.6
  21.0 0.7 copy-start.8
  27.5 40.6 %collective-permute-start.3 = (bf16[256,2048]{1,0:T(8,128)(2,1)S(1)}, bf16[256,2048]{1,0:T(8,128)(2,1)S(1)}, u32[]{:S(2)}, u32[]{:S(2)}) collective-permute-start(bf16[256,2048]{1,0:T(8,128)(2,1)S(1)} %get-tuple-element.58.refs_0_), channel_id=1, source_target_pairs={{0,8},{1,9},{2,10},{3,11},{4,12},{5,13},{6,14},{7,15},{8,0},{9,1},... | collective-permute-start | bytes 3145736 | tf_op jit(solution)/shard_map/ppermute | solution.py:378
  30.4 37.7 %collective-permute-start.4 = (bf16[256,2048]{1,0:T(8,128)(2,1)S(1)}, bf16[256,2048]{1,0:T(8,128)(2,1)S(1)}, u32[]{:S(2)}, u32[]{:S(2)}) collective-permute-start(bf16[256,2048]{1,0:T(8,128)(2,1)S(1)} %get-tuple-element.58.refs_0_), channel_id=1, source_target_pairs={{0,12},{1,13},{2,14},{3,15},{4,8},{5,9},{6,10},{7,11},{8,4},{9,5},... | collective-permute-start | bytes 3145736 | tf_op jit(solution)/shard_map/ppermute | solution.py:378
  34.3 33.9 %collective-permute-start.5 = (bf16[256,2048]{1,0:T(8,128)(2,1)S(1)}, bf16[256,2048]{1,0:T(8,128)(2,1)S(1)}, u32[]{:S(2)}, u32[]{:S(2)}) collective-permute-start(bf16[256,2048]{1,0:T(8,128)(2,1)S(1)} %get-tuple-element.58.refs_0_), channel_id=1, source_target_pairs={{0,4},{1,5},{2,6},{3,7},{4,0},{5,1},{6,2},{7,3},{8,12},{9,13},{10,... | collective-permute-start | bytes 3145736 | tf_op jit(solution)/shard_map/ppermute | solution.py:378
  64.7 11.4 %collective-permute-start.7 = (bf16[256,1024]{1,0:T(8,128)(2,1)S(1)}, bf16[256,1024]{1,0:T(8,128)(2,1)S(1)}, u32[]{:S(2)}, u32[]{:S(2)}) collective-permute-start(bf16[256,1024]{1,0:T(8,128)(2,1)S(1)} %get-tuple-element.67), channel_id=1, source_target_pairs={{0,4},{1,5},{2,6},{3,7},{4,0},{5,1},{6,2},{7,3},{8,12},{9,13},{10,... | collective-permute-start | bytes 1572872 | tf_op jit(solution)/shard_map/ppermute | solution.py:378
  70.5 9.4 %collective-permute-start.6 = (bf16[2272,128]{1,0:T(8,128)(2,1)S(1)}, bf16[2272,128]{1,0:T(8,128)(2,1)S(1)}, u32[]{:S(2)}, u32[]{:S(2)}) collective-permute-start(bf16[2272,128]{1,0:T(8,128)(2,1)S(1)} %get-tuple-element.62), channel_id=1, source_target_pairs={{0,16},{16,0},{32,48},{48,32},{64,80},{80,64},{96,112},{112,96},{1... | collective-permute-start | bytes 1744904 | tf_op jit(solution)/shard_map/ppermute | solution.py:447
  76.2 18.2 %collective-permute-start.8 = (bf16[512,1024]{1,0:T(8,128)(2,1)S(1)}, bf16[512,1024]{1,0:T(8,128)(2,1)S(1)}, u32[]{:S(2)}, u32[]{:S(2)}) collective-permute-start(bf16[512,1024]{1,0:T(8,128)(2,1)S(1)} %constant_dynamic-update-slice_fusion.refs_0_), channel_id=1, source_target_pairs={{0,8},{1,9},{2,10},{3,11},{4,12},{5,13},{6,14},{7,15},{8,0},{9,1},... | collective-permute-start | bytes 3145736 | tf_op jit(solution)/shard_map/ppermute | solution.py:378
  84.4 32.2 %copy-start = (bf16[1024,256]{1,0:T(8,128)(2,1)S(1)}, bf16[1024,256]{1,0:T(8,128)(2,1)}, u32[]{:S(2)}) copy-start(bf16[1024,256]{1,0:T(8,128)(2,1)} %refs_3_.1) | copy-start | bytes 1572868
  84.4 19.5 %all-to-all-start.2 = ((bf16[16,40,128]{2,1,0:T(8,128)(2,1)}), bf16[16,40,128]{2,1,0:T(8,128)(2,1)S(1)}, u32[]{:S(2)}, u32[]{:S(2)}) async-start(bf16[16,40,128]{2,1,0:T(8,128)(2,1)} %shard_map.124), calls=%async_computation.2 | async-start | bytes 327680 | tf_op jit(solution)/shard_map/all_to_all | solution.py:464
  104.3 12.3 %copy-start.9 = (f32[1024]{0:T(1024)S(1)}, f32[1024]{0:T(1024)}, u32[]{:S(2)}) copy-start(f32[1024]{0:T(1024)} %param.21) | copy-start | bytes 12292
  116.6 1.0 copy-start.1

commit v15 on v14

--- a/solution.py
+++ b/solution.py
@@ -14,6 +14,7 @@
 LOWEST = -1e29
 BOTH = ("seq", "head")
 STEPS = (0, 2, 3, 1)
+FAR = (0, 2, 1, 3)
 F32 = jnp.float32
 BF16 = jnp.bfloat16
 MIB = 1 << 20
@@ -311,7 +312,7 @@
     blocks = []
     for i in range(4):
         for j in range(4):
-            step = jnp.where(core == 0, 4 * i + STEPS[j], 4 * STEPS[j] + i)
+            step = jnp.where(core == 0, 4 * FAR[i] + STEPS[j], 4 * STEPS[j] + FAR[i])
             blocks.append(arrived_ref[place ^ step].astype(F32))
     attended = unpack_columns(blocks).astype(BF16)
     projected = unpack_columns([lat_ref[p].astype(F32) for p in range(lat_ref.shape[0])])
@@ -335,7 +336,7 @@
     out_ref[...] = jnp.concatenate([packed[:, :cols], packed[:, cols:]], axis=0).astype(BF16)
 
 
-def call(kernel, outs, cost=1000, vmem_mib=40, **kwargs):
+def call(kernel, outs, cost=1000, vmem_mib=24, **kwargs):
     shapes = [jax.ShapeDtypeStruct(s, t) for s, t in outs]
     return pl.pallas_call(
         kernel,
@@ -389,7 +390,6 @@
     line, out_line = call(
         lines_kernel,
         [((side * cols, tokens), BF16), ((side * cols, w_out.shape[1]), BF16)],
-        vmem_mib=40,
         in_specs=[anywhere] * side,
         out_specs=[anywhere] * 2,
         scratch_shapes=[pltpu.SemaphoreType.DMA((2, side))],
@@ -443,27 +443,26 @@
             pltpu.SemaphoreType.DMA((4, side)),
         ],
     )(*lines, key_weights, latent_kv, digits)
-    own_queries, out_line = lax.optimization_barrier((own_queries, out_line))
     from_sibling = lax.ppermute(both, "seq", swap)
-    next_line = swap_lines(out_line, 1, 1)
-    mixed, level = call(own_kernel, [((rows, 2 * cols), F32)] * 2)(
+    next_line = swap_lines(out_line, 1, FAR[1])
+    mixed, level = call(own_kernel, [((rows, 2 * cols), F32)] * 2, vmem_mib=32)(
         own_queries, query_pos, key_pos, keys, values
     )
     mixed, next_line = lax.optimization_barrier((mixed, next_line))
     out_pair = jnp.concatenate([out_line, next_line], axis=0)
-    far_pair = swap_lines(out_pair, 1, 2)
     joined = call(
         sibling_kernel,
         [((planes, 40, 2 * cols), BF16)],
-        cost=10**8,
+        vmem_mib=32,
         scratch_shapes=[
             pltpu.VMEM((128, key_count), BF16),
             pltpu.VMEM((key_count, 128), BF16),
         ],
     )(own_queries, query_pos, from_sibling, mixed, level)
+    joined, out_pair = lax.optimization_barrier((joined, out_pair))
+    far_pair = swap_lines(out_pair, 1, FAR[2])
     arrived = lax.all_to_all(joined, "seq", 0, 0, axis_index_groups=along_z)
-    arrived, far_pair = lax.optimization_barrier((arrived, far_pair))
-    copies = call(combine_kernel, [((head_size, *block), BF16)])(arrived)
+    copies = call(combine_kernel, [((head_size, *block), BF16)], cost=10**9)(arrived)
     arrived = lax.all_to_all(copies, "head", 0, 0)
     own_proj, shares = call(
         mlp_kernel,

time: 131 us -> 130 us (level)
  starting transfers between devices: 40.6 us -> 51.3 us
  blocking collectives: 50.9 us -> 42.5 us
  waiting for transfers between devices: 19.6 us -> 12.5 us
  local copies, waits for them, and re-layouts: 2.82 us -> 4.41 us
    all_to_all x1, starting transfers between devices: 4.74 us -> 15.2 us  [body(): lax.all_to_all(queries, 'seq', 0, 0, axis_index_groups=along_z)]
    all_to_all x1, blocking collectives: 27.6 us -> 19.6 us  [body(): arrived = lax.all_to_all(joined, 'seq', 0, 0, axis_index_groups=along_z)]
    ppermute x8, waiting for transfers between devices: 5.48 us -> 0.37 us  [swap_lines(): return lax.ppermute(piece, BOTH, partners(seq_size, side, phase, step))]
    unnamed x21 -> x28, local copies, waits for them, and re-layouts: 2.78 us -> 4.41 us
  transfers between devices with their start and end apart: 11 -> 11, of which waited for: 4 -> 3; matrix products, arithmetic and copies ran while one was open for 0% -> 1% of each run, Pallas kernels for 9% -> 7%
where the time goes in v15:
time: 130 us; the launch traced here: 129 us
  starting transfers between devices  51.3 us (39%)
  blocking collectives  42.5 us (33%)
  Pallas kernels  16.9 us (13%)
  waiting for transfers between devices  12.5 us (10%)
  local copies, waits for them, and re-layouts  4.41 us (3%)
    ppermute x8, starting transfers between devices, swap_lines(): return lax.ppermute(piece, BOTH, partners(seq_size, side, phase, step))  26.6 us
    all_to_all x1, blocking collectives, body(): arrived = lax.all_to_all(joined, 'seq', 0, 0, axis_index_groups=along_z)  19.6 us
    all_to_all x1, starting transfers between devices, body(): lax.all_to_all(queries, 'seq', 0, 0, axis_index_groups=along_z)  15.2 us
    all_to_all x1, blocking collectives, body(): arrived = lax.all_to_all(copies, 'head', 0, 0)  11.8 us
    all_to_all x1, blocking collectives, body(): arrived = lax.all_to_all(shares, 'head', 0, 0)  11.1 us
    all_to_all x1, waiting for transfers between devices, body(): lax.all_to_all(queries, 'seq', 0, 0, axis_index_groups=along_z)  8.43 us
    all_to_all x1, starting transfers between devices, body(): lat_blocks = lax.all_to_all(copies, 'head', 0, 0)  7.57 us
    unnamed x28, local copies, waits for them, and re-layouts  4.41 us
  transfers between devices with their start and end apart: 11, of which 3 were waited for; matrix products, arithmetic and copies ran while one was open for 1% of the time, Pallas kernels for 7%

profile of v15, /device:TPU:32, one launch (start us, length us, event | category | flops | bytes accessed | tf_op | source)
XLA Modules:
  0.0 129.0 jit_solution(5547955884662350982)
XLA Ops:
  0.0 0.0 copy-start.10
  0.0 0.0 copy-start.11
  0.0 0.0 copy-start.12
  0.0 1.9 %shard_map.118 = (bf16[64,3072]{1,0:T(8,128)(2,1)}, bf16[16,32,128]{2,1,0:T(8,128)(2,1)}) custom-call(bf16[64,2048]{1,0:T(8,128)(2,1)} %bitcast.18, bf16[64,1024]{1,0:T(8,128)(2,1)} %w_any.1, bf16[64,64]{1,0:T(8,128)(2,1)} %lat_any.1), custom_call_target="tpu_custom_call" | custom-call | flops 1000 | bytes 1000 | tf_op jit(solution)/shard_map/pallas_call | solution.py:382
  1.9 4.9 %collective-permute-start = (bf16[64,3072]{1,0:T(8,128)(2,1)}, bf16[64,3072]{1,0:T(8,128)(2,1)S(1)}, u32[]{:S(2)}, u32[]{:S(2)}) collective-permute-start(bf16[64,3072]{1,0:T(8,128)(2,1)} %get-tuple-element.38.refs_0_), channel_id=1, source_target_pairs={{0,2},{1,3},{2,0},{3,1},{4,6},{5,7},{6,4},{7,5},{8,10},{9,11},{10,... | collective-permute-start | bytes 1179656 | tf_op jit(solution)/shard_map/ppermute | solution.py:379
  6.9 3.0 %collective-permute-start.1 = (bf16[64,3072]{1,0:T(8,128)(2,1)}, bf16[64,3072]{1,0:T(8,128)(2,1)S(1)}, u32[]{:S(2)}, u32[]{:S(2)}) collective-permute-start(bf16[64,3072]{1,0:T(8,128)(2,1)} %get-tuple-element.38.refs_0_), channel_id=1, source_target_pairs={{0,3},{1,2},{2,1},{3,0},{4,7},{5,6},{6,5},{7,4},{8,11},{9,10},{10,... | collective-permute-start | bytes 1179656 | tf_op jit(solution)/shard_map/ppermute | solution.py:379
  9.9 1.9 %collective-permute-start.2 = (bf16[64,3072]{1,0:T(8,128)(2,1)}, bf16[64,3072]{1,0:T(8,128)(2,1)S(1)}, u32[]{:S(2)}, u32[]{:S(2)}) collective-permute-start(bf16[64,3072]{1,0:T(8,128)(2,1)} %get-tuple-element.38.refs_0_), channel_id=1, source_target_pairs={{0,1},{1,0},{2,3},{3,2},{4,5},{5,4},{6,7},{7,6},{8,9},{9,8},{10,11... | collective-permute-start | bytes 1179656 | tf_op jit(solution)/shard_map/ppermute | solution.py:379
  11.9 7.6 %all-to-all-start = ((bf16[16,32,128]{2,1,0:T(8,128)(2,1)}), bf16[16,32,128]{2,1,0:T(8,128)(2,1)S(1)}, u32[]{:S(2)}, u32[]{:S(2)}) async-start(bf16[16,32,128]{2,1,0:T(8,128)(2,1)} %get-tuple-element.41), calls=%async_computation | async-start | bytes 262144 | tf_op jit(solution)/shard_map/all_to_all | solution.py:398
  19.4 0.0 collective-permute-done.refs_1_
  19.4 0.0 collective-permute-done.1.refs_2_
  19.5 0.4 collective-permute-done.2.refs_3_
  19.8 1.0 copy-done.4
  20.8 0.2 shard_map.119
  21.1 0.0 copy-done.7
  21.1 0.0 copy-done.8
  21.1 0.0 copy-done.9
  21.1 1.2 shard_map.120
  22.3 0.0 copy-start.2
  22.3 0.7 copy-done.2
  23.1 0.7 copy-done.5
  23.8 3.7 %all-to-all-done.lat_ref = bf16[16,32,128]{2,1,0:T(8,128)(2,1)S(1)} async-done(((bf16[16,32,128]{2,1,0:T(8,128)(2,1)}), bf16[16,32,128]{2,1,0:T(8,128)(2,1)S(1)}, u32[]{:S(2)}, u32[]{:S(2)}) %all-to-all-start) | async-done | bytes 131104 | tf_op jit(solution)/shard_map/all_to_all | solution.py:398
  27.4 2.9 %collective-permute-start.3 = (bf16[256,2048]{1,0:T(8,128)(2,1)S(1)}, bf16[256,2048]{1,0:T(8,128)(2,1)S(1)}, u32[]{:S(2)}, u32[]{:S(2)}) collective-permute-start(bf16[256,2048]{1,0:T(8,128)(2,1)S(1)} %get-tuple-element.54.refs_0_), channel_id=1, source_target_pairs={{0,8},{1,9},{2,10},{3,11},{4,12},{5,13},{6,14},{7,15},{8,0},{9,1},... | collective-permute-start | bytes 3145736 | tf_op jit(solution)/shard_map/ppermute | solution.py:379
  30.3 3.9 %collective-permute-start.4 = (bf16[256,2048]{1,0:T(8,128)(2,1)S(1)}, bf16[256,2048]{1,0:T(8,128)(2,1)}, u32[]{:S(2)}, u32[]{:S(2)}) collective-permute-start(bf16[256,2048]{1,0:T(8,128)(2,1)S(1)} %get-tuple-element.54.refs_0_), channel_id=1, source_target_pairs={{0,12},{1,13},{2,14},{3,15},{4,8},{5,9},{6,10},{7,11},{8,4},{9,5},... | collective-permute-start | bytes 3145736 | tf_op jit(solution)/shard_map/ppermute | solution.py:379
  34.2 2.4 %collective-permute-start.5 = (bf16[256,2048]{1,0:T(8,128)(2,1)S(1)}, bf16[256,2048]{1,0:T(8,128)(2,1)}, u32[]{:S(2)}, u32[]{:S(2)}) collective-permute-start(bf16[256,2048]{1,0:T(8,128)(2,1)S(1)} %get-tuple-element.54.refs_0_), channel_id=1, source_target_pairs={{0,4},{1,5},{2,6},{3,7},{4,0},{5,1},{6,2},{7,3},{8,12},{9,13},{10,... | collective-permute-start | bytes 3145736 | tf_op jit(solution)/shard_map/ppermute | solution.py:379
  36.7 1.0 copy-done.3
  37.6 1.1 shard_map.121
  38.8 15.2 %all-to-all-start.1 = ((bf16[16,32,128]{2,1,0:T(8,128)(2,1)}), bf16[16,32,128]{2,1,0:T(8,128)(2,1)S(1)}, u32[]{:S(2)}, u32[]{:S(2)}) async-start(bf16[16,32,128]{2,1,0:T(8,128)(2,1)} %get-tuple-element.50), calls=%async_computation.1 | async-start | bytes 262144 | tf_op jit(solution)/shard_map/all_to_all | solution.py:432
  54.0 4.1 %collective-permute-start.7 = (bf16[256,1024]{1,0:T(8,128)(2,1)S(1)}, bf16[256,1024]{1,0:T(8,128)(2,1)}, u32[]{:S(2)}, u32[]{:S(2)}) collective-permute-start(bf16[256,1024]{1,0:T(8,128)(2,1)S(1)} %get-tuple-element.63), channel_id=1, source_target_pairs={{0,8},{1,9},{2,10},{3,11},{4,12},{5,13},{6,14},{7,15},{8,0},{9,1},... | collective-permute-start | bytes 1572872 | tf_op jit(solution)/shard_map/ppermute | solution.py:379
  58.1 8.4 %all-to-all-done.1 = bf16[16,32,128]{2,1,0:T(8,128)(2,1)S(1)} async-done(((bf16[16,32,128]{2,1,0:T(8,128)(2,1)}), bf16[16,32,128]{2,1,0:T(8,128)(2,1)S(1)}, u32[]{:S(2)}, u32[]{:S(2)}) %all-to-all-start.1) | async-done | bytes 131104 | tf_op jit(solution)/shard_map/all_to_all | solution.py:432
  66.5 0.0 collective-permute-done.3.refs_1_
  66.5 0.0 collective-permute-done.4.refs_2_
  66.5 0.0 collective-permute-done.5.refs_3_
  66.5 0.9 copy-done.6
  67.5 2.9 %shard_map.122 = (bf16[128,2176]{1,0:T(8,128)(2,1)S(1)}, bf16[2176,128]{1,0:T(8,128)(2,1)S(1)}, bf16[2272,128]{1,0:T(8,128)(2,1)S(1)}) custom-call(bf16[256,2048]{1,0:T(8,128)(2,1)S(1)} %get-tuple-element.54.refs_0_, bf16[256,2048]{1,0:T(8,128)(2,1)S(1)} %collective-permute-done.3.refs_1_, bf16[256,2048]{1,0:T(8,128)(2,1)} %collective-permute-done.4.refs_2_, ...), custom_call_target="tpu_custom_call" | custom-call | flops 1000000000 | bytes 1000000000 | tf_op jit(solution)/shard_map/pallas_call | solution.py:436
  70.4 1.9 %collective-permute-start.6 = (bf16[2272,128]{1,0:T(8,128)(2,1)S(1)}, bf16[2272,128]{1,0:T(8,128)(2,1)S(1)}, u32[]{:S(2)}, u32[]{:S(2)}) collective-permute-start(bf16[2272,128]{1,0:T(8,128)(2,1)S(1)} %get-tuple-element.58), channel_id=1, source_target_pairs={{0,16},{16,0},{32,48},{48,32},{64,80},{80,64},{96,112},{112,96},{1... | collective-permute-start | bytes 1744904 | tf_op jit(solution)/shard_map/ppermute | solution.py:446
  72.3 3.6 %shard_map.123 = (f32[512,128]{1,0:T(8,128)S(1)}, f32[512,128]{1,0:T(8,128)S(1)}) custom-call(bf16[512,128]{1,0:T(8,128)(2,1)S(1)} %bitcast.9, s32[2,512,128]{2,1,0:T(8,128)S(1)} %get-tuple-element.53.pos_ref, s32[1,2176]{1,0:T(1,128)S(1)} %get-tuple-element.59.kp_ref, bf16[128,2176]{1,0:T(8,128)(2,1)S(1)} %get-tuple-element.60.k_ref, ...), custom_call_target="tpu_custom_call" | custom-call | flops 1000 | bytes 1000 | tf_op jit(solution)/shard_map/pallas_call | solution.py:448
  75.9 0.0 collective-permute-done.7
  75.9 1.1 pad_maximum_fusion.refs_0_
  77.0 0.0 collective-permute-done.6.kv_ref
  77.0 3.8 %shard_map.124 = bf16[16,40,128]{2,1,0:T(8,128)(2,1)S(1)} custom-call(bf16[512,128]{1,0:T(8,128)(2,1)S(1)} %bitcast.10, s32[2,512,128]{2,1,0:T(8,128)S(1)} %get-tuple-element.53.pos_ref, bf16[2272,128]{1,0:T(8,128)(2,1)S(1)} %collective-permute-done.6.kv_ref, f32[512,128]{1,0:T(8,128)S(1)} %get-tuple-element.64.mix_ref, f32[512,128]{1,0:T(8,128)S(1)} %get-tuple-element.65.lev_ref), custom_call_target="tpu_custom_call" | custom-call | flops 1000 | bytes 1000 | tf_op jit(solution)/shard_map/pallas_call | solution.py:453
  80.8 3.4 %collective-permute-start.8 = (bf16[512,1024]{1,0:T(8,128)(2,1)S(1)}, bf16[512,1024]{1,0:T(8,128)(2,1)S(1)}, u32[]{:S(2)}, u32[]{:S(2)}) collective-permute-start(bf16[512,1024]{1,0:T(8,128)(2,1)S(1)} %pad_maximum_fusion.refs_0_), channel_id=1, source_target_pairs={{0,4},{1,5},{2,6},{3,7},{4,0},{5,1},{6,2},{7,3},{8,12},{9,13},{10,... | collective-permute-start | bytes 3145736 | tf_op jit(solution)/shard_map/ppermute | solution.py:379
  84.2 19.6 %all_to_all.25.arrived_ref = bf16[16,40,128]{2,1,0:T(8,128)(2,1)S(1)} all-to-all(bf16[16,40,128]{2,1,0:T(8,128)(2,1)S(1)} %shard_map.124), channel_id=1, replica_groups={{0,32,64,96,128,160,192,224,256,288,320,352,384,416,448,480},{16,48,80,..., dimensions={0} | all-to-all | bytes 327680 | tf_op jit(solution)/shard_map/all_to_all | solution.py:464
  103.9 0.3 shard_map.125
  104.2 11.8 %all_to_all.26.arrived_ref = bf16[16,32,128]{2,1,0:T(8,128)(2,1)S(1)} all-to-all(bf16[16,32,128]{2,1,0:T(8,128)(2,1)S(1)} %shard_map.125), channel_id=1, replica_groups=mesh['seq'=32,'head'=16] {'head'}, dimensions={0} | all-to-all | bytes 262144 | tf_op jit(solution)/shard_map/all_to_all | solution.py:466
  116.1 0.0 collective-permute-done.8.refs_1_
  116.1 1.2 shard_map.126
  117.3 11.1 %all_to_all.27.arrived_ref = bf16[16,32,128]{2,1,0:T(8,128)(2,1)S(1)} all-to-all(bf16[16,32,128]{2,1,0:T(8,128)(2,1)S(1)} %get-tuple-element.69), channel_id=1, replica_groups=mesh['seq'=32,'head'=16] {'head'}, dimensions={0} | all-to-all | bytes 262144 | tf_op jit(solution)/shard_map/all_to_all | solution.py:472
  128.3 0.7 shard_map.127
  (16 shorter events, 0.0 us)
Async XLA Ops:
  0.0 21.1 %copy-start.7 = (bf16[1024,64]{0,1:T(8,128)(2,1)S(1)}, bf16[1024,64]{0,1:T(8,128)(2,1)}, u32[]{:S(2)}) copy-start(bf16[1024,64]{0,1:T(8,128)(2,1)} %param.17) | copy-start | bytes 393220
  0.0 21.1 %copy-start.8 = (bf16[1024,64]{0,1:T(8,128)(2,1)S(1)}, bf16[1024,64]{0,1:T(8,128)(2,1)}, u32[]{:S(2)}) copy-start(bf16[1024,64]{0,1:T(8,128)(2,1)} %param.18) | copy-start | bytes 393220
  0.0 21.1 %copy-start.9 = (bf16[1024,64]{0,1:T(8,128)(2,1)S(1)}, bf16[1024,64]{0,1:T(8,128)(2,1)}, u32[]{:S(2)}) copy-start(bf16[1024,64]{0,1:T(8,128)(2,1)} %param.19) | copy-start | bytes 393220
  0.0 21.1 %copy-start.10 = (s32[2048]{0:T(1024)S(1)}, s32[2048]{0:T(1024)}, u32[]{:S(2)}) copy-start(s32[2048]{0:T(1024)} %param.14) | copy-start | bytes 24580
  0.0 21.1 %copy-start.11 = (s32[2048]{0:T(1024)S(1)}, s32[2048]{0:T(1024)}, u32[]{:S(2)}) copy-start(s32[2048]{0:T(1024)} %param.15) | copy-start | bytes 24580
  0.0 21.1 %copy-start.12 = (f32[1024]{0:T(1024)S(1)}, f32[1024]{0:T(1024)}, u32[]{:S(2)}) copy-start(f32[1024]{0:T(1024)} %param.16) | copy-start | bytes 12292
  1.9 17.5 %collective-permute-start = (bf16[64,3072]{1,0:T(8,128)(2,1)}, bf16[64,3072]{1,0:T(8,128)(2,1)S(1)}, u32[]{:S(2)}, u32[]{:S(2)}) collective-permute-start(bf16[64,3072]{1,0:T(8,128)(2,1)} %get-tuple-element.38.refs_0_), channel_id=1, source_target_pairs={{0,2},{1,3},{2,0},{3,1},{4,6},{5,7},{6,4},{7,5},{8,10},{9,11},{10,... | collective-permute-start | bytes 1179656 | tf_op jit(solution)/shard_map/ppermute | solution.py:379
  6.9 12.6 %collective-permute-start.1 = (bf16[64,3072]{1,0:T(8,128)(2,1)}, bf16[64,3072]{1,0:T(8,128)(2,1)S(1)}, u32[]{:S(2)}, u32[]{:S(2)}) collective-permute-start(bf16[64,3072]{1,0:T(8,128)(2,1)} %get-tuple-element.38.refs_0_), channel_id=1, source_target_pairs={{0,3},{1,2},{2,1},{3,0},{4,7},{5,6},{6,5},{7,4},{8,11},{9,10},{10,... | collective-permute-start | bytes 1179656 | tf_op jit(solution)/shard_map/ppermute | solution.py:379
  9.9 9.9 %collective-permute-start.2 = (bf16[64,3072]{1,0:T(8,128)(2,1)}, bf16[64,3072]{1,0:T(8,128)(2,1)S(1)}, u32[]{:S(2)}, u32[]{:S(2)}) collective-permute-start(bf16[64,3072]{1,0:T(8,128)(2,1)} %get-tuple-element.38.refs_0_), channel_id=1, source_target_pairs={{0,1},{1,0},{2,3},{3,2},{4,5},{5,4},{6,7},{7,6},{8,9},{9,8},{10,11... | collective-permute-start | bytes 1179656 | tf_op jit(solution)/shard_map/ppermute | solution.py:379
  11.9 15.6 %all-to-all-start = ((bf16[16,32,128]{2,1,0:T(8,128)(2,1)}), bf16[16,32,128]{2,1,0:T(8,128)(2,1)S(1)}, u32[]{:S(2)}, u32[]{:S(2)}) async-start(bf16[16,32,128]{2,1,0:T(8,128)(2,1)} %get-tuple-element.41), calls=%async_computation | async-start | bytes 262144 | tf_op jit(solution)/shard_map/all_to_all | solution.py:398
  19.8 1.0 copy-start.4
  22.3 0.8 copy-start.2
  23.1 0.7 copy-start.5
  27.4 39.1 %collective-permute-start.3 = (bf16[256,2048]{1,0:T(8,128)(2,1)S(1)}, bf16[256,2048]{1,0:T(8,128)(2,1)S(1)}, u32[]{:S(2)}, u32[]{:S(2)}) collective-permute-start(bf16[256,2048]{1,0:T(8,128)(2,1)S(1)} %get-tuple-element.54.refs_0_), channel_id=1, source_target_pairs={{0,8},{1,9},{2,10},{3,11},{4,12},{5,13},{6,14},{7,15},{8,0},{9,1},... | collective-permute-start | bytes 3145736 | tf_op jit(solution)/shard_map/ppermute | solution.py:379
  30.3 36.2 %collective-permute-start.4 = (bf16[256,2048]{1,0:T(8,128)(2,1)S(1)}, bf16[256,2048]{1,0:T(8,128)(2,1)}, u32[]{:S(2)}, u32[]{:S(2)}) collective-permute-start(bf16[256,2048]{1,0:T(8,128)(2,1)S(1)} %get-tuple-element.54.refs_0_), channel_id=1, source_target_pairs={{0,12},{1,13},{2,14},{3,15},{4,8},{5,9},{6,10},{7,11},{8,4},{9,5},... | collective-permute-start | bytes 3145736 | tf_op jit(solution)/shard_map/ppermute | solution.py:379
  34.2 32.3 %collective-permute-start.5 = (bf16[256,2048]{1,0:T(8,128)(2,1)S(1)}, bf16[256,2048]{1,0:T(8,128)(2,1)}, u32[]{:S(2)}, u32[]{:S(2)}) collective-permute-start(bf16[256,2048]{1,0:T(8,128)(2,1)S(1)} %get-tuple-element.54.refs_0_), channel_id=1, source_target_pairs={{0,4},{1,5},{2,6},{3,7},{4,0},{5,1},{6,2},{7,3},{8,12},{9,13},{10,... | collective-permute-start | bytes 3145736 | tf_op jit(solution)/shard_map/ppermute | solution.py:379
  36.6 1.0 copy-start.3
  38.8 27.8 %all-to-all-start.1 = ((bf16[16,32,128]{2,1,0:T(8,128)(2,1)}), bf16[16,32,128]{2,1,0:T(8,128)(2,1)S(1)}, u32[]{:S(2)}, u32[]{:S(2)}) async-start(bf16[16,32,128]{2,1,0:T(8,128)(2,1)} %get-tuple-element.50), calls=%async_computation.1 | async-start | bytes 262144 | tf_op jit(solution)/shard_map/all_to_all | solution.py:432
  54.0 21.9 %collective-permute-start.7 = (bf16[256,1024]{1,0:T(8,128)(2,1)S(1)}, bf16[256,1024]{1,0:T(8,128)(2,1)}, u32[]{:S(2)}, u32[]{:S(2)}) collective-permute-start(bf16[256,1024]{1,0:T(8,128)(2,1)S(1)} %get-tuple-element.63), channel_id=1, source_target_pairs={{0,8},{1,9},{2,10},{3,11},{4,12},{5,13},{6,14},{7,15},{8,0},{9,1},... | collective-permute-start | bytes 1572872 | tf_op jit(solution)/shard_map/ppermute | solution.py:379
  66.5 1.0 copy-start.6
  70.4 6.6 %collective-permute-start.6 = (bf16[2272,128]{1,0:T(8,128)(2,1)S(1)}, bf16[2272,128]{1,0:T(8,128)(2,1)S(1)}, u32[]{:S(2)}, u32[]{:S(2)}) collective-permute-start(bf16[2272,128]{1,0:T(8,128)(2,1)S(1)} %get-tuple-element.58), channel_id=1, source_target_pairs={{0,16},{16,0},{32,48},{48,32},{64,80},{80,64},{96,112},{112,96},{1... | collective-permute-start | bytes 1744904 | tf_op jit(solution)/shard_map/ppermute | solution.py:446
  80.8 35.2 %collective-permute-start.8 = (bf16[512,1024]{1,0:T(8,128)(2,1)S(1)}, bf16[512,1024]{1,0:T(8,128)(2,1)S(1)}, u32[]{:S(2)}, u32[]{:S(2)}) collective-permute-start(bf16[512,1024]{1,0:T(8,128)(2,1)S(1)} %pad_maximum_fusion.refs_0_), channel_id=1, source_target_pairs={{0,4},{1,5},{2,6},{3,7},{4,0},{5,1},{6,2},{7,3},{8,12},{9,13},{10,... | collective-permute-start | bytes 3145736 | tf_op jit(solution)/shard_map/ppermute | solution.py:379
  103.9 12.2 %copy-start = (bf16[1024,256]{1,0:T(8,128)(2,1)S(1)}, bf16[1024,256]{1,0:T(8,128)(2,1)}, u32[]{:S(2)}) copy-start(bf16[1024,256]{1,0:T(8,128)(2,1)} %refs_3_.1) | copy-start | bytes 1572868
  103.9 12.2 %copy-start.1 = (bf16[256,1024]{1,0:T(8,128)(2,1)S(1)}, bf16[256,1024]{1,0:T(8,128)(2,1)}, u32[]{:S(2)}) copy-start(bf16[256,1024]{1,0:T(8,128)(2,1)} %refs_4_.1) | copy-start | bytes 1572868
  103.9 12.2 %copy-start.13 = (f32[1024]{0:T(1024)S(1)}, f32[1024]{0:T(1024)}, u32[]{:S(2)}) copy-start(f32[1024]{0:T(1024)} %param.21) | copy-start | bytes 12292

commit v16 on v15

--- a/solution.py
+++ b/solution.py
@@ -443,6 +443,7 @@
             pltpu.SemaphoreType.DMA((4, side)),
         ],
     )(*lines, key_weights, latent_kv, digits)
+    own_queries, out_line = lax.optimization_barrier((own_queries, out_line))
     from_sibling = lax.ppermute(both, "seq", swap)
     next_line = swap_lines(out_line, 1, FAR[1])
     mixed, level = call(own_kernel, [((rows, 2 * cols), F32)] * 2, vmem_mib=32)(

time: 130 us -> 129 us (level)
  blocking collectives: 42.5 us -> 69.4 us
  starting transfers between devices: 51.3 us -> 36.1 us
  waiting for transfers between devices: 12.5 us -> 5.98 us
  local copies, waits for them, and re-layouts: 4.41 us -> 1.03 us
    all_to_all x0 -> x1, blocking collectives: none -> 27.5 us  [body(): lax.all_to_all(queries, 'seq', 0, 0, axis_index_groups=along_z)]
    all_to_all x1 -> x0, starting transfers between devices: 15.2 us -> none  [body(): lax.all_to_all(queries, 'seq', 0, 0, axis_index_groups=along_z)]
    all_to_all x1 -> x0, waiting for transfers between devices: 8.43 us -> none  [body(): lax.all_to_all(queries, 'seq', 0, 0, axis_index_groups=along_z)]
    unnamed x28 -> x20, local copies, waits for them, and re-layouts: 4.41 us -> 1.03 us
    all_to_all x1, waiting for transfers between devices: 3.65 us -> 5.11 us  [body(): lat_blocks = lax.all_to_all(copies, 'head', 0, 0)]
  transfers between devices with their start and end apart: 11 -> 10, of which waited for: 3 -> 3; matrix products, arithmetic and copies ran while one was open for 1% -> 0% of each run, Pallas kernels for 7% -> 6%
where the time goes in v16:
time: 129 us
  blocking collectives  69.4 us (54%)
  starting transfers between devices  36.1 us (28%)
  Pallas kernels  15.8 us (12%)
  waiting for transfers between devices  5.98 us (5%)
    all_to_all x1, blocking collectives, body(): lax.all_to_all(queries, 'seq', 0, 0, axis_index_groups=along_z)  27.5 us
    ppermute x8, starting transfers between devices, swap_lines(): return lax.ppermute(piece, BOTH, partners(seq_size, side, phase, step))  26.6 us
    all_to_all x1, blocking collectives, body(): arrived = lax.all_to_all(joined, 'seq', 0, 0, axis_index_groups=along_z)  18.5 us
    all_to_all x1, blocking collectives, body(): arrived = lax.all_to_all(copies, 'head', 0, 0)  12.3 us
    all_to_all x1, blocking collectives, body(): arrived = lax.all_to_all(shares, 'head', 0, 0)  11.1 us
    all_to_all x1, starting transfers between devices, body(): lat_blocks = lax.all_to_all(copies, 'head', 0, 0)  7.57 us
    all_to_all x1, waiting for transfers between devices, body(): lat_blocks = lax.all_to_all(copies, 'head', 0, 0)  5.11 us
    pallas_call x1, Pallas kernels, body(): call(sibling_kernel, [((planes, 40, 2 * cols), BF16)], vmem_mib=32, scrat...  3.83 us
  transfers between devices with their start and end apart: 10, of which 3 were waited for; matrix products, arithmetic and copies ran while one was open for 0% of the time, Pallas kernels for 6%

profile of v16, /device:TPU:32, one launch (start us, length us, event | category | flops | bytes accessed | tf_op | source)
XLA Modules:
  0.0 128.7 jit_solution(9958995255655372854)
XLA Ops:
  0.0 0.0 copy-start.6
  0.0 0.0 copy-start.7
  0.0 0.0 copy-start.8
  0.0 1.9 %shard_map.118 = (bf16[64,3072]{1,0:T(8,128)(2,1)}, bf16[16,32,128]{2,1,0:T(8,128)(2,1)}) custom-call(bf16[64,2048]{1,0:T(8,128)(2,1)} %bitcast.18, bf16[64,1024]{1,0:T(8,128)(2,1)} %w_any.1, bf16[64,64]{1,0:T(8,128)(2,1)} %lat_any.1), custom_call_target="tpu_custom_call" | custom-call | flops 1000 | bytes 1000 | tf_op jit(solution)/shard_map/pallas_call | solution.py:382
  1.9 4.9 %collective-permute-start = (bf16[64,3072]{1,0:T(8,128)(2,1)}, bf16[64,3072]{1,0:T(8,128)(2,1)S(1)}, u32[]{:S(2)}, u32[]{:S(2)}) collective-permute-start(bf16[64,3072]{1,0:T(8,128)(2,1)} %get-tuple-element.40.refs_0_), channel_id=1, source_target_pairs={{0,2},{1,3},{2,0},{3,1},{4,6},{5,7},{6,4},{7,5},{8,10},{9,11},{10,... | collective-permute-start | bytes 1179656 | tf_op jit(solution)/shard_map/ppermute | solution.py:379
  6.9 3.0 %collective-permute-start.1 = (bf16[64,3072]{1,0:T(8,128)(2,1)}, bf16[64,3072]{1,0:T(8,128)(2,1)S(1)}, u32[]{:S(2)}, u32[]{:S(2)}) collective-permute-start(bf16[64,3072]{1,0:T(8,128)(2,1)} %get-tuple-element.40.refs_0_), channel_id=1, source_target_pairs={{0,3},{1,2},{2,1},{3,0},{4,7},{5,6},{6,5},{7,4},{8,11},{9,10},{10,... | collective-permute-start | bytes 1179656 | tf_op jit(solution)/shard_map/ppermute | solution.py:379
  9.9 1.9 %collective-permute-start.2 = (bf16[64,3072]{1,0:T(8,128)(2,1)}, bf16[64,3072]{1,0:T(8,128)(2,1)S(1)}, u32[]{:S(2)}, u32[]{:S(2)}) collective-permute-start(bf16[64,3072]{1,0:T(8,128)(2,1)} %get-tuple-element.40.refs_0_), channel_id=1, source_target_pairs={{0,1},{1,0},{2,3},{3,2},{4,5},{5,4},{6,7},{7,6},{8,9},{9,8},{10,11... | collective-permute-start | bytes 1179656 | tf_op jit(solution)/shard_map/ppermute | solution.py:379
  11.9 7.6 %all-to-all-start = ((bf16[16,32,128]{2,1,0:T(8,128)(2,1)}), bf16[16,32,128]{2,1,0:T(8,128)(2,1)S(1)}, u32[]{:S(2)}, u32[]{:S(2)}) async-start(bf16[16,32,128]{2,1,0:T(8,128)(2,1)} %get-tuple-element.43), calls=%async_computation | async-start | bytes 262144 | tf_op jit(solution)/shard_map/all_to_all | solution.py:398
  19.4 0.0 collective-permute-done.refs_1_
  19.5 0.0 collective-permute-done.1.refs_2_
  19.5 0.4 collective-permute-done.2.refs_3_
  19.8 1.0 copy-done.2
  20.8 0.2 shard_map.119
  21.1 0.0 copy-done.3
  21.1 0.0 copy-done.4
  21.1 0.0 copy-done.5
  21.1 0.0 copy-done.6
  21.1 0.0 copy-done.7
  21.1 0.0 copy-done.8
  21.1 1.2 shard_map.120
  22.3 5.1 %all-to-all-done.lat_ref = bf16[16,32,128]{2,1,0:T(8,128)(2,1)S(1)} async-done(((bf16[16,32,128]{2,1,0:T(8,128)(2,1)}), bf16[16,32,128]{2,1,0:T(8,128)(2,1)S(1)}, u32[]{:S(2)}, u32[]{:S(2)}) %all-to-all-start) | async-done | bytes 131104 | tf_op jit(solution)/shard_map/all_to_all | solution.py:398
  27.4 2.9 %collective-permute-start.3 = (bf16[256,2048]{1,0:T(8,128)(2,1)S(1)}, bf16[256,2048]{1,0:T(8,128)(2,1)S(1)}, u32[]{:S(2)}, u32[]{:S(2)}) collective-permute-start(bf16[256,2048]{1,0:T(8,128)(2,1)S(1)} %get-tuple-element.58.refs_0_), channel_id=1, source_target_pairs={{0,8},{1,9},{2,10},{3,11},{4,12},{5,13},{6,14},{7,15},{8,0},{9,1},... | collective-permute-start | bytes 3145736 | tf_op jit(solution)/shard_map/ppermute | solution.py:379
  30.3 3.9 %collective-permute-start.4 = (bf16[256,2048]{1,0:T(8,128)(2,1)S(1)}, bf16[256,2048]{1,0:T(8,128)(2,1)S(1)}, u32[]{:S(2)}, u32[]{:S(2)}) collective-permute-start(bf16[256,2048]{1,0:T(8,128)(2,1)S(1)} %get-tuple-element.58.refs_0_), channel_id=1, source_target_pairs={{0,12},{1,13},{2,14},{3,15},{4,8},{5,9},{6,10},{7,11},{8,4},{9,5},... | collective-permute-start | bytes 3145736 | tf_op jit(solution)/shard_map/ppermute | solution.py:379
  34.2 2.4 %collective-permute-start.5 = (bf16[256,2048]{1,0:T(8,128)(2,1)S(1)}, bf16[256,2048]{1,0:T(8,128)(2,1)S(1)}, u32[]{:S(2)}, u32[]{:S(2)}) collective-permute-start(bf16[256,2048]{1,0:T(8,128)(2,1)S(1)} %get-tuple-element.58.refs_0_), channel_id=1, source_target_pairs={{0,4},{1,5},{2,6},{3,7},{4,0},{5,1},{6,2},{7,3},{8,12},{9,13},{10,... | collective-permute-start | bytes 3145736 | tf_op jit(solution)/shard_map/ppermute | solution.py:379
  36.7 0.5 shard_map.121
  37.1 27.5 %all_to_all.25 = bf16[16,32,128]{2,1,0:T(8,128)(2,1)S(1)} all-to-all(bf16[16,32,128]{2,1,0:T(8,128)(2,1)S(1)} %get-tuple-element.52), channel_id=1, replica_groups={{0,32,64,96,128,160,192,224,256,288,320,352,384,416,448,480},{16,48,80,..., dimensions={0} | all-to-all | bytes 262144 | tf_op jit(solution)/shard_map/all_to_all | solution.py:432
  64.7 4.1 %collective-permute-start.7 = (bf16[256,1024]{1,0:T(8,128)(2,1)S(1)}, bf16[256,1024]{1,0:T(8,128)(2,1)S(1)}, u32[]{:S(2)}, u32[]{:S(2)}) collective-permute-start(bf16[256,1024]{1,0:T(8,128)(2,1)S(1)} %get-tuple-element.67), channel_id=1, source_target_pairs={{0,8},{1,9},{2,10},{3,11},{4,12},{5,13},{6,14},{7,15},{8,0},{9,1},... | collective-permute-start | bytes 1572872 | tf_op jit(solution)/shard_map/ppermute | solution.py:379
  68.8 0.0 collective-permute-done.3.refs_1_
  68.8 0.0 collective-permute-done.4.refs_2_
  68.8 0.0 collective-permute-done.5.refs_3_
  68.8 2.3 %shard_map.122 = (bf16[128,2176]{1,0:T(8,128)(2,1)S(1)}, bf16[2176,128]{1,0:T(8,128)(2,1)S(1)}, bf16[2272,128]{1,0:T(8,128)(2,1)S(1)}) custom-call(bf16[256,2048]{1,0:T(8,128)(2,1)S(1)} %get-tuple-element.58.refs_0_, bf16[256,2048]{1,0:T(8,128)(2,1)S(1)} %collective-permute-done.3.refs_1_, bf16[256,2048]{1,0:T(8,128)(2,1)S(1)} %collective-permute-done.4.refs_2_, ...), custom_call_target="tpu_custom_call" | custom-call | flops 1000000000 | bytes 1000000000 | tf_op jit(solution)/shard_map/pallas_call | solution.py:436
  71.1 1.9 %collective-permute-start.6 = (bf16[2272,128]{1,0:T(8,128)(2,1)S(1)}, bf16[2272,128]{1,0:T(8,128)(2,1)S(1)}, u32[]{:S(2)}, u32[]{:S(2)}) collective-permute-start(bf16[2272,128]{1,0:T(8,128)(2,1)S(1)} %get-tuple-element.62), channel_id=1, source_target_pairs={{0,16},{16,0},{32,48},{48,32},{64,80},{80,64},{96,112},{112,96},{1... | collective-permute-start | bytes 1744904 | tf_op jit(solution)/shard_map/ppermute | solution.py:447
  73.0 3.7 %shard_map.123 = (f32[512,128]{1,0:T(8,128)S(1)}, f32[512,128]{1,0:T(8,128)S(1)}) custom-call(bf16[512,128]{1,0:T(8,128)(2,1)S(1)} %bitcast.9, s32[2,512,128]{2,1,0:T(8,128)S(1)} %get-tuple-element.57.pos_ref, s32[1,2176]{1,0:T(1,128)S(1)} %get-tuple-element.63.kp_ref, bf16[128,2176]{1,0:T(8,128)(2,1)S(1)} %get-tuple-element.64.k_ref, ...), custom_call_target="tpu_custom_call" | custom-call | flops 1000 | bytes 1000 | tf_op jit(solution)/shard_map/pallas_call | solution.py:449
  76.7 0.5 collective-permute-done.7
  77.2 0.1 pad_maximum_fusion.refs_0_
  77.3 0.0 collective-permute-done.6.kv_ref
  77.3 3.8 %shard_map.124 = bf16[16,40,128]{2,1,0:T(8,128)(2,1)S(1)} custom-call(bf16[512,128]{1,0:T(8,128)(2,1)S(1)} %bitcast.10, s32[2,512,128]{2,1,0:T(8,128)S(1)} %get-tuple-element.57.pos_ref, bf16[2272,128]{1,0:T(8,128)(2,1)S(1)} %collective-permute-done.6.kv_ref, f32[512,128]{1,0:T(8,128)S(1)} %get-tuple-element.68.mix_ref, f32[512,128]{1,0:T(8,128)S(1)} %get-tuple-element.69.lev_ref), custom_call_target="tpu_custom_call" | custom-call | flops 1000 | bytes 1000 | tf_op jit(solution)/shard_map/pallas_call | solution.py:454
  81.2 3.4 %collective-permute-start.8 = (bf16[512,1024]{1,0:T(8,128)(2,1)S(1)}, bf16[512,1024]{1,0:T(8,128)(2,1)S(1)}, u32[]{:S(2)}, u32[]{:S(2)}) collective-permute-start(bf16[512,1024]{1,0:T(8,128)(2,1)S(1)} %pad_maximum_fusion.refs_0_), channel_id=1, source_target_pairs={{0,4},{1,5},{2,6},{3,7},{4,0},{5,1},{6,2},{7,3},{8,12},{9,13},{10,... | collective-permute-start | bytes 3145736 | tf_op jit(solution)/shard_map/ppermute | solution.py:379
  84.6 18.5 %all_to_all.26.arrived_ref = bf16[16,40,128]{2,1,0:T(8,128)(2,1)S(1)} all-to-all(bf16[16,40,128]{2,1,0:T(8,128)(2,1)S(1)} %shard_map.124), channel_id=1, replica_groups={{0,32,64,96,128,160,192,224,256,288,320,352,384,416,448,480},{16,48,80,..., dimensions={0} | all-to-all | bytes 327680 | tf_op jit(solution)/shard_map/all_to_all | solution.py:465
  103.1 0.3 shard_map.125
  103.4 12.3 %all_to_all.27.arrived_ref = bf16[16,32,128]{2,1,0:T(8,128)(2,1)S(1)} all-to-all(bf16[16,32,128]{2,1,0:T(8,128)(2,1)S(1)} %shard_map.125), channel_id=1, replica_groups=mesh['seq'=32,'head'=16] {'head'}, dimensions={0} | all-to-all | bytes 262144 | tf_op jit(solution)/shard_map/all_to_all | solution.py:467
  115.8 0.0 collective-permute-done.8.refs_1_
  115.8 0.0 copy-done
  115.8 0.0 copy-done.1
  115.8 0.0 copy-done.9
  115.8 1.2 shard_map.126
  117.0 11.1 %all_to_all.28.arrived_ref = bf16[16,32,128]{2,1,0:T(8,128)(2,1)S(1)} all-to-all(bf16[16,32,128]{2,1,0:T(8,128)(2,1)S(1)} %get-tuple-element.73), channel_id=1, replica_groups=mesh['seq'=32,'head'=16] {'head'}, dimensions={0} | all-to-all | bytes 262144 | tf_op jit(solution)/shard_map/all_to_all | solution.py:473
  128.0 0.7 shard_map.127
  (7 shorter events, 0.0 us)
Async XLA Ops:
  0.0 21.1 %copy-start.3 = (bf16[1024,64]{0,1:T(8,128)(2,1)S(1)}, bf16[1024,64]{0,1:T(8,128)(2,1)}, u32[]{:S(2)}) copy-start(bf16[1024,64]{0,1:T(8,128)(2,1)} %param.17) | copy-start | bytes 393220
  0.0 21.1 %copy-start.4 = (bf16[1024,64]{0,1:T(8,128)(2,1)S(1)}, bf16[1024,64]{0,1:T(8,128)(2,1)}, u32[]{:S(2)}) copy-start(bf16[1024,64]{0,1:T(8,128)(2,1)} %param.18) | copy-start | bytes 393220
  0.0 21.1 %copy-start.5 = (bf16[1024,64]{0,1:T(8,128)(2,1)S(1)}, bf16[1024,64]{0,1:T(8,128)(2,1)}, u32[]{:S(2)}) copy-start(bf16[1024,64]{0,1:T(8,128)(2,1)} %param.19) | copy-start | bytes 393220
  0.0 21.1 %copy-start.6 = (s32[2048]{0:T(1024)S(1)}, s32[2048]{0:T(1024)}, u32[]{:S(2)}) copy-start(s32[2048]{0:T(1024)} %param.14) | copy-start | bytes 24580
  0.0 21.1 %copy-start.7 = (s32[2048]{0:T(1024)S(1)}, s32[2048]{0:T(1024)}, u32[]{:S(2)}) copy-start(s32[2048]{0:T(1024)} %param.15) | copy-start | bytes 24580
  0.0 21.1 %copy-start.8 = (f32[1024]{0:T(1024)S(1)}, f32[1024]{0:T(1024)}, u32[]{:S(2)}) copy-start(f32[1024]{0:T(1024)} %param.16) | copy-start | bytes 12292
  1.9 17.5 %collective-permute-start = (bf16[64,3072]{1,0:T(8,128)(2,1)}, bf16[64,3072]{1,0:T(8,128)(2,1)S(1)}, u32[]{:S(2)}, u32[]{:S(2)}) collective-permute-start(bf16[64,3072]{1,0:T(8,128)(2,1)} %get-tuple-element.40.refs_0_), channel_id=1, source_target_pairs={{0,2},{1,3},{2,0},{3,1},{4,6},{5,7},{6,4},{7,5},{8,10},{9,11},{10,... | collective-permute-start | bytes 1179656 | tf_op jit(solution)/shard_map/ppermute | solution.py:379
  6.9 12.6 %collective-permute-start.1 = (bf16[64,3072]{1,0:T(8,128)(2,1)}, bf16[64,3072]{1,0:T(8,128)(2,1)S(1)}, u32[]{:S(2)}, u32[]{:S(2)}) collective-permute-start(bf16[64,3072]{1,0:T(8,128)(2,1)} %get-tuple-element.40.refs_0_), channel_id=1, source_target_pairs={{0,3},{1,2},{2,1},{3,0},{4,7},{5,6},{6,5},{7,4},{8,11},{9,10},{10,... | collective-permute-start | bytes 1179656 | tf_op jit(solution)/shard_map/ppermute | solution.py:379
  9.9 9.9 %collective-permute-start.2 = (bf16[64,3072]{1,0:T(8,128)(2,1)}, bf16[64,3072]{1,0:T(8,128)(2,1)S(1)}, u32[]{:S(2)}, u32[]{:S(2)}) collective-permute-start(bf16[64,3072]{1,0:T(8,128)(2,1)} %get-tuple-element.40.refs_0_), channel_id=1, source_target_pairs={{0,1},{1,0},{2,3},{3,2},{4,5},{5,4},{6,7},{7,6},{8,9},{9,8},{10,11... | collective-permute-start | bytes 1179656 | tf_op jit(solution)/shard_map/ppermute | solution.py:379
  11.9 15.6 %all-to-all-start = ((bf16[16,32,128]{2,1,0:T(8,128)(2,1)}), bf16[16,32,128]{2,1,0:T(8,128)(2,1)S(1)}, u32[]{:S(2)}, u32[]{:S(2)}) async-start(bf16[16,32,128]{2,1,0:T(8,128)(2,1)} %get-tuple-element.43), calls=%async_computation | async-start | bytes 262144 | tf_op jit(solution)/shard_map/all_to_all | solution.py:398
  19.8 1.0 copy-start.2
  27.4 41.4 %collective-permute-start.3 = (bf16[256,2048]{1,0:T(8,128)(2,1)S(1)}, bf16[256,2048]{1,0:T(8,128)(2,1)S(1)}, u32[]{:S(2)}, u32[]{:S(2)}) collective-permute-start(bf16[256,2048]{1,0:T(8,128)(2,1)S(1)} %get-tuple-element.58.refs_0_), channel_id=1, source_target_pairs={{0,8},{1,9},{2,10},{3,11},{4,12},{5,13},{6,14},{7,15},{8,0},{9,1},... | collective-permute-start | bytes 3145736 | tf_op jit(solution)/shard_map/ppermute | solution.py:379
  30.3 38.5 %collective-permute-start.4 = (bf16[256,2048]{1,0:T(8,128)(2,1)S(1)}, bf16[256,2048]{1,0:T(8,128)(2,1)S(1)}, u32[]{:S(2)}, u32[]{:S(2)}) collective-permute-start(bf16[256,2048]{1,0:T(8,128)(2,1)S(1)} %get-tuple-element.58.refs_0_), channel_id=1, source_target_pairs={{0,12},{1,13},{2,14},{3,15},{4,8},{5,9},{6,10},{7,11},{8,4},{9,5},... | collective-permute-start | bytes 3145736 | tf_op jit(solution)/shard_map/ppermute | solution.py:379
  34.2 34.6 %collective-permute-start.5 = (bf16[256,2048]{1,0:T(8,128)(2,1)S(1)}, bf16[256,2048]{1,0:T(8,128)(2,1)S(1)}, u32[]{:S(2)}, u32[]{:S(2)}) collective-permute-start(bf16[256,2048]{1,0:T(8,128)(2,1)S(1)} %get-tuple-element.58.refs_0_), channel_id=1, source_target_pairs={{0,4},{1,5},{2,6},{3,7},{4,0},{5,1},{6,2},{7,3},{8,12},{9,13},{10,... | collective-permute-start | bytes 3145736 | tf_op jit(solution)/shard_map/ppermute | solution.py:379
  64.7 12.6 %collective-permute-start.7 = (bf16[256,1024]{1,0:T(8,128)(2,1)S(1)}, bf16[256,1024]{1,0:T(8,128)(2,1)S(1)}, u32[]{:S(2)}, u32[]{:S(2)}) collective-permute-start(bf16[256,1024]{1,0:T(8,128)(2,1)S(1)} %get-tuple-element.67), channel_id=1, source_target_pairs={{0,8},{1,9},{2,10},{3,11},{4,12},{5,13},{6,14},{7,15},{8,0},{9,1},... | collective-permute-start | bytes 1572872 | tf_op jit(solution)/shard_map/ppermute | solution.py:379
  71.1 6.2 %collective-permute-start.6 = (bf16[2272,128]{1,0:T(8,128)(2,1)S(1)}, bf16[2272,128]{1,0:T(8,128)(2,1)S(1)}, u32[]{:S(2)}, u32[]{:S(2)}) collective-permute-start(bf16[2272,128]{1,0:T(8,128)(2,1)S(1)} %get-tuple-element.62), channel_id=1, source_target_pairs={{0,16},{16,0},{32,48},{48,32},{64,80},{80,64},{96,112},{112,96},{1... | collective-permute-start | bytes 1744904 | tf_op jit(solution)/shard_map/ppermute | solution.py:447
  81.2 34.6 %collective-permute-start.8 = (bf16[512,1024]{1,0:T(8,128)(2,1)S(1)}, bf16[512,1024]{1,0:T(8,128)(2,1)S(1)}, u32[]{:S(2)}, u32[]{:S(2)}) collective-permute-start(bf16[512,1024]{1,0:T(8,128)(2,1)S(1)} %pad_maximum_fusion.refs_0_), channel_id=1, source_target_pairs={{0,4},{1,5},{2,6},{3,7},{4,0},{5,1},{6,2},{7,3},{8,12},{9,13},{10,... | collective-permute-start | bytes 3145736 | tf_op jit(solution)/shard_map/ppermute | solution.py:379
  103.1 12.7 %copy-start = (bf16[1024,256]{1,0:T(8,128)(2,1)S(1)}, bf16[1024,256]{1,0:T(8,128)(2,1)}, u32[]{:S(2)}) copy-start(bf16[1024,256]{1,0:T(8,128)(2,1)} %refs_3_.1) | copy-start | bytes 1572868
  103.1 12.7 %copy-start.1 = (bf16[256,1024]{1,0:T(8,128)(2,1)S(1)}, bf16[256,1024]{1,0:T(8,128)(2,1)}, u32[]{:S(2)}) copy-start(bf16[256,1024]{1,0:T(8,128)(2,1)} %refs_4_.1) | copy-start | bytes 1572868
  103.1 12.7 %copy-start.9 = (f32[1024]{0:T(1024)S(1)}, f32[1024]{0:T(1024)}, u32[]{:S(2)}) copy-start(f32[1024]{0:T(1024)} %param.21) | copy-start | bytes 12292

commit v17 on v16

--- a/solution.py
+++ b/solution.py
@@ -14,7 +14,7 @@
 LOWEST = -1e29
 BOTH = ("seq", "head")
 STEPS = (0, 2, 3, 1)
-FAR = (0, 2, 1, 3)
+FAR = (0, 1, 2, 3)
 F32 = jnp.float32
 BF16 = jnp.bfloat16
 MIB = 1 << 20

time: 129 us -> 129 us (level)
  transfers between devices with their start and end apart: 10 -> 10, of which waited for: 3 -> 2; matrix products, arithmetic and copies ran while one was open for 0% -> 0% of each run, Pallas kernels for 6% -> 6%
where the time goes in v17:
time: 129 us; the launch traced here: 128 us
  blocking collectives  69.9 us (54%)
  starting transfers between devices  35.8 us (28%)
  Pallas kernels  15.8 us (12%)
  waiting for transfers between devices  5.48 us (4%)
    all_to_all x1, blocking collectives, body(): lax.all_to_all(queries, 'seq', 0, 0, axis_index_groups=along_z)  27.5 us
    ppermute x8, starting transfers between devices, swap_lines(): return lax.ppermute(piece, BOTH, partners(seq_size, side, phase, step))  26.3 us
    all_to_all x1, blocking collectives, body(): arrived = lax.all_to_all(joined, 'seq', 0, 0, axis_index_groups=along_z)  19.7 us
    all_to_all x1, blocking collectives, body(): arrived = lax.all_to_all(copies, 'head', 0, 0)  11.6 us
    all_to_all x1, blocking collectives, body(): arrived = lax.all_to_all(shares, 'head', 0, 0)  11.1 us
    all_to_all x1, starting transfers between devices, body(): lat_blocks = lax.all_to_all(copies, 'head', 0, 0)  7.57 us
    all_to_all x1, waiting for transfers between devices, body(): lat_blocks = lax.all_to_all(copies, 'head', 0, 0)  5.11 us
    pallas_call x1, Pallas kernels, body(): call(sibling_kernel, [((planes, 40, 2 * cols), BF16)], vmem_mib=32, scrat...  3.83 us
  transfers between devices with their start and end apart: 10, of which 2 were waited for; matrix products, arithmetic and copies ran while one was open for 0% of the time, Pallas kernels for 6%

profile of v17, /device:TPU:32, one launch (start us, length us, event | category | flops | bytes accessed | tf_op | source)
XLA Modules:
  0.0 128.4 jit_solution(9943220050664850751)
XLA Ops:
  0.0 0.0 copy-start.6
  0.0 0.0 copy-start.7
  0.0 0.0 copy-start.8
  0.0 1.9 %shard_map.118 = (bf16[64,3072]{1,0:T(8,128)(2,1)}, bf16[16,32,128]{2,1,0:T(8,128)(2,1)}) custom-call(bf16[64,2048]{1,0:T(8,128)(2,1)} %bitcast.18, bf16[64,1024]{1,0:T(8,128)(2,1)} %w_any.1, bf16[64,64]{1,0:T(8,128)(2,1)} %lat_any.1), custom_call_target="tpu_custom_call" | custom-call | flops 1000 | bytes 1000 | tf_op jit(solution)/shard_map/pallas_call | solution.py:382
  1.9 4.9 %collective-permute-start = (bf16[64,3072]{1,0:T(8,128)(2,1)}, bf16[64,3072]{1,0:T(8,128)(2,1)S(1)}, u32[]{:S(2)}, u32[]{:S(2)}) collective-permute-start(bf16[64,3072]{1,0:T(8,128)(2,1)} %get-tuple-element.40.refs_0_), channel_id=1, source_target_pairs={{0,2},{1,3},{2,0},{3,1},{4,6},{5,7},{6,4},{7,5},{8,10},{9,11},{10,... | collective-permute-start | bytes 1179656 | tf_op jit(solution)/shard_map/ppermute | solution.py:379
  6.9 3.0 %collective-permute-start.1 = (bf16[64,3072]{1,0:T(8,128)(2,1)}, bf16[64,3072]{1,0:T(8,128)(2,1)S(1)}, u32[]{:S(2)}, u32[]{:S(2)}) collective-permute-start(bf16[64,3072]{1,0:T(8,128)(2,1)} %get-tuple-element.40.refs_0_), channel_id=1, source_target_pairs={{0,3},{1,2},{2,1},{3,0},{4,7},{5,6},{6,5},{7,4},{8,11},{9,10},{10,... | collective-permute-start | bytes 1179656 | tf_op jit(solution)/shard_map/ppermute | solution.py:379
  9.9 1.9 %collective-permute-start.2 = (bf16[64,3072]{1,0:T(8,128)(2,1)}, bf16[64,3072]{1,0:T(8,128)(2,1)S(1)}, u32[]{:S(2)}, u32[]{:S(2)}) collective-permute-start(bf16[64,3072]{1,0:T(8,128)(2,1)} %get-tuple-element.40.refs_0_), channel_id=1, source_target_pairs={{0,1},{1,0},{2,3},{3,2},{4,5},{5,4},{6,7},{7,6},{8,9},{9,8},{10,11... | collective-permute-start | bytes 1179656 | tf_op jit(solution)/shard_map/ppermute | solution.py:379
  11.9 7.6 %all-to-all-start = ((bf16[16,32,128]{2,1,0:T(8,128)(2,1)}), bf16[16,32,128]{2,1,0:T(8,128)(2,1)S(1)}, u32[]{:S(2)}, u32[]{:S(2)}) async-start(bf16[16,32,128]{2,1,0:T(8,128)(2,1)} %get-tuple-element.43), calls=%async_computation | async-start | bytes 262144 | tf_op jit(solution)/shard_map/all_to_all | solution.py:398
  19.4 0.0 collective-permute-done.refs_1_
  19.5 0.0 collective-permute-done.1.refs_2_
  19.5 0.4 collective-permute-done.2.refs_3_
  19.8 1.0 copy-done.2
  20.8 0.2 shard_map.119
  21.1 0.0 copy-done.3
  21.1 0.0 copy-done.4
  21.1 0.0 copy-done.5
  21.1 0.0 copy-done.6
  21.1 0.0 copy-done.7
  21.1 0.0 copy-done.8
  21.1 1.2 shard_map.120
  22.3 5.1 %all-to-all-done.lat_ref = bf16[16,32,128]{2,1,0:T(8,128)(2,1)S(1)} async-done(((bf16[16,32,128]{2,1,0:T(8,128)(2,1)}), bf16[16,32,128]{2,1,0:T(8,128)(2,1)S(1)}, u32[]{:S(2)}, u32[]{:S(2)}) %all-to-all-start) | async-done | bytes 131104 | tf_op jit(solution)/shard_map/all_to_all | solution.py:398
  27.4 2.9 %collective-permute-start.3 = (bf16[256,2048]{1,0:T(8,128)(2,1)S(1)}, bf16[256,2048]{1,0:T(8,128)(2,1)S(1)}, u32[]{:S(2)}, u32[]{:S(2)}) collective-permute-start(bf16[256,2048]{1,0:T(8,128)(2,1)S(1)} %get-tuple-element.58.refs_0_), channel_id=1, source_target_pairs={{0,8},{1,9},{2,10},{3,11},{4,12},{5,13},{6,14},{7,15},{8,0},{9,1},... | collective-permute-start | bytes 3145736 | tf_op jit(solution)/shard_map/ppermute | solution.py:379
  30.3 3.9 %collective-permute-start.4 = (bf16[256,2048]{1,0:T(8,128)(2,1)S(1)}, bf16[256,2048]{1,0:T(8,128)(2,1)S(1)}, u32[]{:S(2)}, u32[]{:S(2)}) collective-permute-start(bf16[256,2048]{1,0:T(8,128)(2,1)S(1)} %get-tuple-element.58.refs_0_), channel_id=1, source_target_pairs={{0,12},{1,13},{2,14},{3,15},{4,8},{5,9},{6,10},{7,11},{8,4},{9,5},... | collective-permute-start | bytes 3145736 | tf_op jit(solution)/shard_map/ppermute | solution.py:379
  34.2 2.4 %collective-permute-start.5 = (bf16[256,2048]{1,0:T(8,128)(2,1)S(1)}, bf16[256,2048]{1,0:T(8,128)(2,1)S(1)}, u32[]{:S(2)}, u32[]{:S(2)}) collective-permute-start(bf16[256,2048]{1,0:T(8,128)(2,1)S(1)} %get-tuple-element.58.refs_0_), channel_id=1, source_target_pairs={{0,4},{1,5},{2,6},{3,7},{4,0},{5,1},{6,2},{7,3},{8,12},{9,13},{10,... | collective-permute-start | bytes 3145736 | tf_op jit(solution)/shard_map/ppermute | solution.py:379
  36.7 0.5 shard_map.121
  37.1 27.5 %all_to_all.25 = bf16[16,32,128]{2,1,0:T(8,128)(2,1)S(1)} all-to-all(bf16[16,32,128]{2,1,0:T(8,128)(2,1)S(1)} %get-tuple-element.52), channel_id=1, replica_groups={{0,32,64,96,128,160,192,224,256,288,320,352,384,416,448,480},{16,48,80,..., dimensions={0} | all-to-all | bytes 262144 | tf_op jit(solution)/shard_map/all_to_all | solution.py:432
  64.7 3.4 %collective-permute-start.7 = (bf16[256,1024]{1,0:T(8,128)(2,1)S(1)}, bf16[256,1024]{1,0:T(8,128)(2,1)S(1)}, u32[]{:S(2)}, u32[]{:S(2)}) collective-permute-start(bf16[256,1024]{1,0:T(8,128)(2,1)S(1)} %get-tuple-element.67), channel_id=1, source_target_pairs={{0,4},{1,5},{2,6},{3,7},{4,0},{5,1},{6,2},{7,3},{8,12},{9,13},{10,... | collective-permute-start | bytes 1572872 | tf_op jit(solution)/shard_map/ppermute | solution.py:379
  68.1 0.0 collective-permute-done.3.refs_1_
  68.1 0.0 collective-permute-done.4.refs_2_
  68.1 0.0 collective-permute-done.5.refs_3_
  68.1 2.3 %shard_map.122 = (bf16[128,2176]{1,0:T(8,128)(2,1)S(1)}, bf16[2176,128]{1,0:T(8,128)(2,1)S(1)}, bf16[2272,128]{1,0:T(8,128)(2,1)S(1)}) custom-call(bf16[256,2048]{1,0:T(8,128)(2,1)S(1)} %get-tuple-element.58.refs_0_, bf16[256,2048]{1,0:T(8,128)(2,1)S(1)} %collective-permute-done.3.refs_1_, bf16[256,2048]{1,0:T(8,128)(2,1)S(1)} %collective-permute-done.4.refs_2_, ...), custom_call_target="tpu_custom_call" | custom-call | flops 1000000000 | bytes 1000000000 | tf_op jit(solution)/shard_map/pallas_call | solution.py:436
  70.4 1.9 %collective-permute-start.6 = (bf16[2272,128]{1,0:T(8,128)(2,1)S(1)}, bf16[2272,128]{1,0:T(8,128)(2,1)S(1)}, u32[]{:S(2)}, u32[]{:S(2)}) collective-permute-start(bf16[2272,128]{1,0:T(8,128)(2,1)S(1)} %get-tuple-element.62), channel_id=1, source_target_pairs={{0,16},{16,0},{32,48},{48,32},{64,80},{80,64},{96,112},{112,96},{1... | collective-permute-start | bytes 1744904 | tf_op jit(solution)/shard_map/ppermute | solution.py:447
  72.3 3.7 %shard_map.123 = (f32[512,128]{1,0:T(8,128)S(1)}, f32[512,128]{1,0:T(8,128)S(1)}) custom-call(bf16[512,128]{1,0:T(8,128)(2,1)S(1)} %bitcast.9, s32[2,512,128]{2,1,0:T(8,128)S(1)} %get-tuple-element.57.pos_ref, s32[1,2176]{1,0:T(1,128)S(1)} %get-tuple-element.63.kp_ref, bf16[128,2176]{1,0:T(8,128)(2,1)S(1)} %get-tuple-element.64.k_ref, ...), custom_call_target="tpu_custom_call" | custom-call | flops 1000 | bytes 1000 | tf_op jit(solution)/shard_map/pallas_call | solution.py:449
  76.0 0.0 collective-permute-done.7
  76.0 0.1 pad_maximum_fusion.refs_0_
  76.1 0.0 collective-permute-done.6.kv_ref
  76.1 3.8 %shard_map.124 = bf16[16,40,128]{2,1,0:T(8,128)(2,1)S(1)} custom-call(bf16[512,128]{1,0:T(8,128)(2,1)S(1)} %bitcast.10, s32[2,512,128]{2,1,0:T(8,128)S(1)} %get-tuple-element.57.pos_ref, bf16[2272,128]{1,0:T(8,128)(2,1)S(1)} %collective-permute-done.6.kv_ref, f32[512,128]{1,0:T(8,128)S(1)} %get-tuple-element.68.mix_ref, f32[512,128]{1,0:T(8,128)S(1)} %get-tuple-element.69.lev_ref), custom_call_target="tpu_custom_call" | custom-call | flops 1000 | bytes 1000 | tf_op jit(solution)/shard_map/pallas_call | solution.py:454
  79.9 3.8 %collective-permute-start.8 = (bf16[512,1024]{1,0:T(8,128)(2,1)S(1)}, bf16[512,1024]{1,0:T(8,128)(2,1)S(1)}, u32[]{:S(2)}, u32[]{:S(2)}) collective-permute-start(bf16[512,1024]{1,0:T(8,128)(2,1)S(1)} %pad_maximum_fusion.refs_0_), channel_id=1, source_target_pairs={{0,8},{1,9},{2,10},{3,11},{4,12},{5,13},{6,14},{7,15},{8,0},{9,1},... | collective-permute-start | bytes 3145736 | tf_op jit(solution)/shard_map/ppermute | solution.py:379
  83.8 19.7 %all_to_all.26.arrived_ref = bf16[16,40,128]{2,1,0:T(8,128)(2,1)S(1)} all-to-all(bf16[16,40,128]{2,1,0:T(8,128)(2,1)S(1)} %shard_map.124), channel_id=1, replica_groups={{0,32,64,96,128,160,192,224,256,288,320,352,384,416,448,480},{16,48,80,..., dimensions={0} | all-to-all | bytes 327680 | tf_op jit(solution)/shard_map/all_to_all | solution.py:465
  103.5 0.4 shard_map.125
  103.8 11.6 %all_to_all.27.arrived_ref = bf16[16,32,128]{2,1,0:T(8,128)(2,1)S(1)} all-to-all(bf16[16,32,128]{2,1,0:T(8,128)(2,1)S(1)} %shard_map.125), channel_id=1, replica_groups=mesh['seq'=32,'head'=16] {'head'}, dimensions={0} | all-to-all | bytes 262144 | tf_op jit(solution)/shard_map/all_to_all | solution.py:467
  115.4 0.0 collective-permute-done.8.refs_1_
  115.4 0.0 copy-done
  115.4 0.0 copy-done.1
  115.4 0.0 copy-done.9
  115.4 1.2 shard_map.126
  116.6 11.1 %all_to_all.28.arrived_ref = bf16[16,32,128]{2,1,0:T(8,128)(2,1)S(1)} all-to-all(bf16[16,32,128]{2,1,0:T(8,128)(2,1)S(1)} %get-tuple-element.73), channel_id=1, replica_groups=mesh['seq'=32,'head'=16] {'head'}, dimensions={0} | all-to-all | bytes 262144 | tf_op jit(solution)/shard_map/all_to_all | solution.py:473
  127.7 0.7 shard_map.127
  (7 shorter events, 0.0 us)
Async XLA Ops:
  0.0 21.1 %copy-start.3 = (bf16[1024,64]{0,1:T(8,128)(2,1)S(1)}, bf16[1024,64]{0,1:T(8,128)(2,1)}, u32[]{:S(2)}) copy-start(bf16[1024,64]{0,1:T(8,128)(2,1)} %param.17) | copy-start | bytes 393220
  0.0 21.1 %copy-start.4 = (bf16[1024,64]{0,1:T(8,128)(2,1)S(1)}, bf16[1024,64]{0,1:T(8,128)(2,1)}, u32[]{:S(2)}) copy-start(bf16[1024,64]{0,1:T(8,128)(2,1)} %param.18) | copy-start | bytes 393220
  0.0 21.1 %copy-start.5 = (bf16[1024,64]{0,1:T(8,128)(2,1)S(1)}, bf16[1024,64]{0,1:T(8,128)(2,1)}, u32[]{:S(2)}) copy-start(bf16[1024,64]{0,1:T(8,128)(2,1)} %param.19) | copy-start | bytes 393220
  0.0 21.1 %copy-start.6 = (s32[2048]{0:T(1024)S(1)}, s32[2048]{0:T(1024)}, u32[]{:S(2)}) copy-start(s32[2048]{0:T(1024)} %param.14) | copy-start | bytes 24580
  0.0 21.1 %copy-start.7 = (s32[2048]{0:T(1024)S(1)}, s32[2048]{0:T(1024)}, u32[]{:S(2)}) copy-start(s32[2048]{0:T(1024)} %param.15) | copy-start | bytes 24580
  0.0 21.1 %copy-start.8 = (f32[1024]{0:T(1024)S(1)}, f32[1024]{0:T(1024)}, u32[]{:S(2)}) copy-start(f32[1024]{0:T(1024)} %param.16) | copy-start | bytes 12292
  1.9 17.5 %collective-permute-start = (bf16[64,3072]{1,0:T(8,128)(2,1)}, bf16[64,3072]{1,0:T(8,128)(2,1)S(1)}, u32[]{:S(2)}, u32[]{:S(2)}) collective-permute-start(bf16[64,3072]{1,0:T(8,128)(2,1)} %get-tuple-element.40.refs_0_), channel_id=1, source_target_pairs={{0,2},{1,3},{2,0},{3,1},{4,6},{5,7},{6,4},{7,5},{8,10},{9,11},{10,... | collective-permute-start | bytes 1179656 | tf_op jit(solution)/shard_map/ppermute | solution.py:379
  6.9 12.6 %collective-permute-start.1 = (bf16[64,3072]{1,0:T(8,128)(2,1)}, bf16[64,3072]{1,0:T(8,128)(2,1)S(1)}, u32[]{:S(2)}, u32[]{:S(2)}) collective-permute-start(bf16[64,3072]{1,0:T(8,128)(2,1)} %get-tuple-element.40.refs_0_), channel_id=1, source_target_pairs={{0,3},{1,2},{2,1},{3,0},{4,7},{5,6},{6,5},{7,4},{8,11},{9,10},{10,... | collective-permute-start | bytes 1179656 | tf_op jit(solution)/shard_map/ppermute | solution.py:379
  9.9 9.9 %collective-permute-start.2 = (bf16[64,3072]{1,0:T(8,128)(2,1)}, bf16[64,3072]{1,0:T(8,128)(2,1)S(1)}, u32[]{:S(2)}, u32[]{:S(2)}) collective-permute-start(bf16[64,3072]{1,0:T(8,128)(2,1)} %get-tuple-element.40.refs_0_), channel_id=1, source_target_pairs={{0,1},{1,0},{2,3},{3,2},{4,5},{5,4},{6,7},{7,6},{8,9},{9,8},{10,11... | collective-permute-start | bytes 1179656 | tf_op jit(solution)/shard_map/ppermute | solution.py:379
  11.9 15.6 %all-to-all-start = ((bf16[16,32,128]{2,1,0:T(8,128)(2,1)}), bf16[16,32,128]{2,1,0:T(8,128)(2,1)S(1)}, u32[]{:S(2)}, u32[]{:S(2)}) async-start(bf16[16,32,128]{2,1,0:T(8,128)(2,1)} %get-tuple-element.43), calls=%async_computation | async-start | bytes 262144 | tf_op jit(solution)/shard_map/all_to_all | solution.py:398
  19.8 1.0 copy-start.2
  27.4 40.6 %collective-permute-start.3 = (bf16[256,2048]{1,0:T(8,128)(2,1)S(1)}, bf16[256,2048]{1,0:T(8,128)(2,1)S(1)}, u32[]{:S(2)}, u32[]{:S(2)}) collective-permute-start(bf16[256,2048]{1,0:T(8,128)(2,1)S(1)} %get-tuple-element.58.refs_0_), channel_id=1, source_target_pairs={{0,8},{1,9},{2,10},{3,11},{4,12},{5,13},{6,14},{7,15},{8,0},{9,1},... | collective-permute-start | bytes 3145736 | tf_op jit(solution)/shard_map/ppermute | solution.py:379
  30.3 37.7 %collective-permute-start.4 = (bf16[256,2048]{1,0:T(8,128)(2,1)S(1)}, bf16[256,2048]{1,0:T(8,128)(2,1)S(1)}, u32[]{:S(2)}, u32[]{:S(2)}) collective-permute-start(bf16[256,2048]{1,0:T(8,128)(2,1)S(1)} %get-tuple-element.58.refs_0_), channel_id=1, source_target_pairs={{0,12},{1,13},{2,14},{3,15},{4,8},{5,9},{6,10},{7,11},{8,4},{9,5},... | collective-permute-start | bytes 3145736 | tf_op jit(solution)/shard_map/ppermute | solution.py:379
  34.2 33.9 %collective-permute-start.5 = (bf16[256,2048]{1,0:T(8,128)(2,1)S(1)}, bf16[256,2048]{1,0:T(8,128)(2,1)S(1)}, u32[]{:S(2)}, u32[]{:S(2)}) collective-permute-start(bf16[256,2048]{1,0:T(8,128)(2,1)S(1)} %get-tuple-element.58.refs_0_), channel_id=1, source_target_pairs={{0,4},{1,5},{2,6},{3,7},{4,0},{5,1},{6,2},{7,3},{8,12},{9,13},{10,... | collective-permute-start | bytes 3145736 | tf_op jit(solution)/shard_map/ppermute | solution.py:379
  64.7 11.3 %collective-permute-start.7 = (bf16[256,1024]{1,0:T(8,128)(2,1)S(1)}, bf16[256,1024]{1,0:T(8,128)(2,1)S(1)}, u32[]{:S(2)}, u32[]{:S(2)}) collective-permute-start(bf16[256,1024]{1,0:T(8,128)(2,1)S(1)} %get-tuple-element.67), channel_id=1, source_target_pairs={{0,4},{1,5},{2,6},{3,7},{4,0},{5,1},{6,2},{7,3},{8,12},{9,13},{10,... | collective-permute-start | bytes 1572872 | tf_op jit(solution)/shard_map/ppermute | solution.py:379
  70.4 5.7 %collective-permute-start.6 = (bf16[2272,128]{1,0:T(8,128)(2,1)S(1)}, bf16[2272,128]{1,0:T(8,128)(2,1)S(1)}, u32[]{:S(2)}, u32[]{:S(2)}) collective-permute-start(bf16[2272,128]{1,0:T(8,128)(2,1)S(1)} %get-tuple-element.62), channel_id=1, source_target_pairs={{0,16},{16,0},{32,48},{48,32},{64,80},{80,64},{96,112},{112,96},{1... | collective-permute-start | bytes 1744904 | tf_op jit(solution)/shard_map/ppermute | solution.py:447
  79.9 35.5 %collective-permute-start.8 = (bf16[512,1024]{1,0:T(8,128)(2,1)S(1)}, bf16[512,1024]{1,0:T(8,128)(2,1)S(1)}, u32[]{:S(2)}, u32[]{:S(2)}) collective-permute-start(bf16[512,1024]{1,0:T(8,128)(2,1)S(1)} %pad_maximum_fusion.refs_0_), channel_id=1, source_target_pairs={{0,8},{1,9},{2,10},{3,11},{4,12},{5,13},{6,14},{7,15},{8,0},{9,1},... | collective-permute-start | bytes 3145736 | tf_op jit(solution)/shard_map/ppermute | solution.py:379
  103.5 12.0 %copy-start = (bf16[1024,256]{1,0:T(8,128)(2,1)S(1)}, bf16[1024,256]{1,0:T(8,128)(2,1)}, u32[]{:S(2)}) copy-start(bf16[1024,256]{1,0:T(8,128)(2,1)} %refs_3_.1) | copy-start | bytes 1572868
  103.5 12.0 %copy-start.1 = (bf16[256,1024]{1,0:T(8,128)(2,1)S(1)}, bf16[256,1024]{1,0:T(8,128)(2,1)}, u32[]{:S(2)}) copy-start(bf16[256,1024]{1,0:T(8,128)(2,1)} %refs_4_.1) | copy-start | bytes 1572868
  103.5 12.0 %copy-start.9 = (f32[1024]{0:T(1024)S(1)}, f32[1024]{0:T(1024)}, u32[]{:S(2)}) copy-start(f32[1024]{0:T(1024)} %param.21) | copy-start | bytes 12292
